TPU v7x, 32 devices: a whole 2x2x4 slice. The times are simulated.
32 devices in a mesh: dap: 16 (over z, x, core), grp: 2 (over y).
Axes of the slice: x: 2, y: 2, z: 4, core: 2. Of those that a mesh axis runs over, the one named last changes fastest.
Arguments:
- homolog_activity: bfloat16 [32, 256, 256], P(None, ('dap', 'grp')), may hold values from -6 to 6
- alignment_mask: int32 [32, 256], P(None, ('dap', 'grp')), may hold values from 0 to 1, as said below
- sequence_row_mask: int32 [32], replicated, may hold values from 0 to 1, as said below
- pairwise_bias: bfloat16 [8, 256, 256], P(None, 'dap', 'grp'), may hold values from -400 to 400
- horizontal_projection_matrix: bfloat16 [256, 4, 256], P(None, None, 'grp'), may hold values from -0.375 to 0.375
- horizontal_final_matrix: bfloat16 [256, 256], P('grp'), may hold values from -0.375 to 0.375
- column_query_weight: bfloat16 [256, 256], replicated, may hold values from -1 to 1
- column_key_weight: bfloat16 [256, 256], replicated, may hold values from -50 to 50
- vertical_content_sigmoid_matrix: bfloat16 [256, 2, 256], replicated, may hold values from -0.375 to 0.375
- vertical_final_matrix: bfloat16 [256, 256], replicated, may hold values from -0.375 to 0.375
- first_operand_matrix: bfloat16 [256, 32], replicated, may hold values from -0.375 to 0.375
- second_operand_matrix: bfloat16 [256, 32], replicated, may hold values from -0.375 to 0.375
- outer_output_weight: bfloat16 [1024, 128], replicated, may hold values from -1 to 1
Outputs:
- alignment_output: bfloat16 [32, 256, 256], P(None, ('dap', 'grp'))
- pairwise_update: bfloat16 [256, 256, 128], P(('dap', 'grp'))
Inputs may be any that keep to these rules, and one draw needn't show every extreme that they name: `alignment_mask`: row 0 is all ones. `sequence_row_mask`: entry 0 is 1; at least one entry is 0.
All inputs are finite; a program needn't handle non-finite values.
Results may differ from a plain program's by a relative error of at most 0.023.
Values may be sent and summed in bfloat16 or wider, within the bound.
No kernel may reach another device: no remote copies, remote signals or barrier semaphores. Data moves between devices by JAX's collectives and lax.ppermute only.
A program may use at most 192 MiB of HBM per device.

v0:
```python
import jax
import jax.numpy as jnp
from jax import lax
from jax.sharding import PartitionSpec as P

PER_SPLIT_DIM = 32


def layer_normalize(values):
    widened = values.astype(jnp.float32)
    centered = widened - jnp.mean(widened, axis=-1, keepdims=True)
    variance = jnp.mean(centered * centered, axis=-1, keepdims=True)
    return (centered * lax.rsqrt(variance + 1e-05)).astype(jnp.bfloat16)


def shards(
    homolog_activity,
    alignment_mask,
    sequence_row_mask,
    pairwise_bias,
    horizontal_projection_matrix,
    horizontal_final_matrix,
    column_query_weight,
    column_key_weight,
    vertical_content_sigmoid_matrix,
    vertical_final_matrix,
    first_operand_matrix,
    second_operand_matrix,
    outer_output_weight,
):
    parallel_count = lax.axis_size("dap")
    group_count = lax.axis_size("grp")
    grp_index = lax.axis_index("grp")
    sequences_overall, residues_here, alignment_width = homolog_activity.shape
    residues_overall = residues_here * parallel_count * group_count
    sequences_here = sequences_overall // parallel_count
    query_factor = PER_SPLIT_DIM ** (-0.5)
    retain_column = (alignment_mask * sequence_row_mask[:, None]).astype(jnp.float32)
    keep_wire = retain_column.astype(jnp.bfloat16)
    keep_leading = keep_wire.T
    normalized_input = layer_normalize(homolog_activity)
    left_fac = (
        jnp.dot(normalized_input, first_operand_matrix, preferred_element_type=jnp.float32)
        * retain_column[..., None]
    ).astype(jnp.bfloat16)
    right_leading = (
        jnp.einsum(
            "snc,co->nso",
            normalized_input,
            second_operand_matrix,
            preferred_element_type=jnp.float32,
        )
        * retain_column.T[..., None]
    ).astype(jnp.bfloat16)
    channels = left_fac.shape[-1]
    right_piece = lax.all_gather(right_leading, ("dap", "grp"), axis=0, tiled=True)
    keep_piece = lax.all_gather(keep_leading, ("dap", "grp"), axis=0, tiled=True)
    segment_length = right_piece.shape[0]
    outer_prod = jnp.einsum(
        "sic,jsd->ijcd", left_fac, right_piece, preferred_element_type=jnp.float32
    )
    outer_prod = outer_prod.reshape(residues_here, segment_length, channels * channels).astype(
        jnp.bfloat16
    )
    projected = jnp.dot(outer_prod, outer_output_weight, preferred_element_type=jnp.float32)
    counts = lax.dot_general(
        keep_wire, keep_piece, (((0,), (1,)), ((), ())), preferred_element_type=jnp.float32
    )
    pair_sum = projected / counts[..., None]
    pairwise_update = pair_sum.astype(jnp.bfloat16)
    transmitted_rows, sent_keep = (
        lax.all_to_all(homolog_activity, "dap", split_axis=0, concat_axis=1, tiled=True),
        lax.all_to_all(keep_wire, "dap", split_axis=0, concat_axis=1, tiled=True),
    )
    transmitted_rows = transmitted_rows.reshape(
        sequences_here, parallel_count, 1, residues_here, alignment_width
    )
    sent_keep = sent_keep.reshape(sequences_here, parallel_count, 1, residues_here)
    row_segment, row_keep = (
        lax.all_gather(transmitted_rows, "grp", axis=2, tiled=True),
        lax.all_gather(sent_keep, "grp", axis=2, tiled=True),
    )
    row_segment = row_segment.reshape(sequences_here, residues_overall, alignment_width)
    key_ok = row_keep.reshape(sequences_here, residues_overall) > 0
    normed_rows = layer_normalize(row_segment)
    projected = jnp.einsum(
        "snc,cfe->snfe",
        normed_rows,
        horizontal_projection_matrix,
        preferred_element_type=jnp.float32,
    )
    heads_local = projected.shape[-1] // PER_SPLIT_DIM
    queries = (
        (projected[:, :, 0] * query_factor)
        .astype(jnp.bfloat16)
        .reshape(sequences_here, residues_overall, heads_local, PER_SPLIT_DIM)
    )
    key_rows = (
        projected[:, :, 1]
        .astype(jnp.bfloat16)
        .reshape(sequences_here, residues_overall, heads_local, PER_SPLIT_DIM)
    )
    value_rows = (
        projected[:, :, 2]
        .astype(jnp.bfloat16)
        .reshape(sequences_here, residues_overall, heads_local, PER_SPLIT_DIM)
    )
    gating = jax.nn.sigmoid(projected[:, :, 3]).reshape(
        sequences_here, residues_overall, heads_local, PER_SPLIT_DIM
    )

    def attend(bias_piece, offset):
        segment_length = bias_piece.shape[1]
        query_part = lax.dynamic_slice_in_dim(queries, offset, segment_length, 1)
        gate_part = lax.dynamic_slice_in_dim(gating, offset, segment_length, 1)
        scores = jnp.einsum(
            "sihd,sjhd->shij", query_part, key_rows, preferred_element_type=jnp.float32
        )
        scores = scores + bias_piece.astype(jnp.float32)[None]
        scores = jnp.where(key_ok[:, None, None, :], scores, -1000000000.0)
        weights = jax.nn.softmax(scores, axis=-1).astype(jnp.bfloat16)
        mixture = (
            jnp.einsum("shij,sjhd->sihd", weights, value_rows, preferred_element_type=jnp.float32)
            * gate_part
        )
        mixture = mixture.astype(jnp.bfloat16).reshape(
            sequences_here, segment_length, heads_local * PER_SPLIT_DIM
        )
        return jnp.dot(mixture, horizontal_final_matrix, preferred_element_type=jnp.float32)

    def attend_blocks(bias_piece, offset):
        segment_length = bias_piece.shape[1]
        if segment_length <= 256 or segment_length % 256 != 0:
            return attend(bias_piece, offset)

        def one_block(block_index):
            bias_block = lax.dynamic_slice_in_dim(bias_piece, block_index * 256, 256, 1)
            return attend(bias_block, offset + block_index * 256)

        stacked_parts = lax.map(one_block, jnp.arange(segment_length // 256, dtype=jnp.int32))
        return stacked_parts.transpose(1, 0, 2, 3).reshape(
            sequences_here, segment_length, alignment_width
        )

    all_rows = lax.all_gather(pairwise_bias, "dap", axis=1, tiled=True)
    own_heads = lax.all_to_all(all_rows, "grp", split_axis=0, concat_axis=2, tiled=True)
    partial_result = attend_blocks(own_heads, 0)
    summed = lax.psum(partial_result.astype(jnp.bfloat16), "grp").astype(jnp.float32)
    row_result = (row_segment.astype(jnp.float32) + summed).astype(jnp.bfloat16)
    row_result = row_result.reshape(
        sequences_here, parallel_count, group_count * residues_here, alignment_width
    )
    regrouped_rows = lax.all_to_all(row_result, "dap", split_axis=1, concat_axis=0, tiled=True)
    regrouped_rows = regrouped_rows.reshape(
        sequences_overall, group_count * residues_here, alignment_width
    )
    column_result = lax.dynamic_slice_in_dim(
        regrouped_rows, grp_index * residues_here, residues_here, 1
    )
    column_normalized = layer_normalize(column_result)
    head_count = column_query_weight.shape[1] // PER_SPLIT_DIM
    column_query = (
        jnp.dot(column_normalized, column_query_weight, preferred_element_type=jnp.float32)
        * query_factor
    ).astype(jnp.bfloat16)
    column_query = column_query.reshape(sequences_overall, residues_here, head_count, PER_SPLIT_DIM)
    column_key = jnp.dot(
        column_normalized, column_key_weight, preferred_element_type=jnp.float32
    ).astype(jnp.bfloat16)
    column_key = column_key.reshape(sequences_overall, residues_here, head_count, PER_SPLIT_DIM)
    col_vg = jnp.einsum(
        "snc,cfe->snfe",
        column_normalized,
        vertical_content_sigmoid_matrix,
        preferred_element_type=jnp.float32,
    )
    col_v = (
        col_vg[:, :, 0]
        .astype(jnp.bfloat16)
        .reshape(sequences_overall, residues_here, head_count, PER_SPLIT_DIM)
    )
    col_gate = jax.nn.sigmoid(col_vg[:, :, 1]).reshape(
        sequences_overall, residues_here, head_count, PER_SPLIT_DIM
    )
    col_scores = jnp.einsum(
        "snhd,tnhd->nhst", column_query, column_key, preferred_element_type=jnp.float32
    )
    col_scores = jnp.where(retain_column.T[:, None, None, :] > 0, col_scores, -1000000000.0)
    col_weights = jax.nn.softmax(col_scores, axis=-1).astype(jnp.bfloat16)
    col_mix = (
        jnp.einsum("nhst,tnhd->snhd", col_weights, col_v, preferred_element_type=jnp.float32)
        * col_gate
    )
    col_mix = col_mix.astype(jnp.bfloat16).reshape(
        sequences_overall, residues_here, head_count * PER_SPLIT_DIM
    )
    vertical_mixed = jnp.dot(col_mix, vertical_final_matrix, preferred_element_type=jnp.float32)
    alignment_output = (column_result.astype(jnp.float32) + vertical_mixed).astype(jnp.bfloat16)
    return (alignment_output, pairwise_update)


def solution(mesh):
    return jax.shard_map(
        shards,
        mesh=mesh,
        in_specs=(
            P(None, ("dap", "grp"), None),
            P(None, ("dap", "grp")),
            P(),
            P(None, "dap", "grp"),
            P(None, None, "grp"),
            P("grp", None),
            P(),
            P(),
            P(),
            P(),
            P(),
            P(),
            P(),
        ),
        out_specs=(P(None, ("dap", "grp"), None), P(("dap", "grp"), None, None)),
        check_vma=False,
    )
```

profile of v0, /device:TPU:0, one launch (start us, length us, event | category | flops | bytes accessed | tf_op | source)
XLA Modules:
  0.0 269.1 jit_solution(3872166389474906189)
XLA Ops:
  7.2 0.7 broadcast_compare_fusion.1
  8.0 0.7 copy.73
  8.6 7.4 %all-to-all-start.1 = ((bf16[16,2,8]{2,1,0:T(2,128)(2,1)}), bf16[16,2,8]{2,1,0:T(2,128)(2,1)S(1)}, u32[]{:S(2)}, u32[]{:S(2)}) async-start(bf16[16,2,8]{2,1,0:T(2,128)(2,1)} %bitcast.9), calls=%async_computation.1 | async-start | bytes 16384 | tf_op jit(solution)/shard_map/all_to_all | solution.py:73
  16.1 1.0 convert_reduce_fusion.2
  17.1 1.1 fusion.33
  18.2 1.0 fusion.34
  19.3 0.9 fusion.13
  20.2 81.3 %all_gather.18 = bf16[256,32,32]{2,0,1:T(8,128)(2,1)S(1)} all-gather(bf16[8,32,32]{2,0,1:T(8,128)(2,1)S(1)} %fusion.13), channel_id=1, replica_groups=mesh['dap'=16,'grp'=2] {'dap','grp'}, dimensions={0}, use_global_device_ids=true | all-gather | bytes 540672 | tf_op jit(solution)/shard_map/all_gather | solution.py:56
  101.4 20.1 %all_gather.17 = bf16[8,256,128]{2,1,0:T(8,128)(2,1)} all-gather(bf16[8,16,128]{2,1,0:T(8,128)(2,1)S(1)} %copy-done.6), channel_id=1, replica_groups=mesh['dap'=16,'grp'=2] {'dap'}, dimensions={1}, use_global_device_ids=true | all-gather | bytes 557056 | tf_op jit(solution)/shard_map/all_gather | solution.py:145
  121.5 3.5 %all-to-all-start = ((bf16[32,8,256]{2,1,0:T(8,128)(2,1)}), bf16[32,8,256]{2,1,0:T(8,128)(2,1)S(1)}, u32[]{:S(2)}, u32[]{:S(2)}) async-start(bf16[32,8,256]{2,1,0:T(8,128)(2,1)} %param.13), calls=%async_computation | async-start | bytes 262144 | tf_op jit(solution)/shard_map/all_to_all | solution.py:72
  125.1 0.2 copy.72
  125.3 3.1 %copy.98 = bf16[256,32,32,1]{1,0,3,2:T(8,128)(2,1)} copy(bf16[256,32,32,1]{2,0,1,3:T(8,128)(2,1)S(1)} %bitcast.125) | data formatting | bytes 1048576 | tf_op jit(solution)/shard_map/all_gather | solution.py:56
  128.4 65.2 %all_gather.19 = bf16[256,32]{1,0:T(8,128)(2,1)S(1)} all-gather(bf16[8,32]{1,0:T(8,128)(2,1)S(1)} %convert_bitcast_fusion.2), channel_id=1, replica_groups=mesh['dap'=16,'grp'=2] {'dap','grp'}, dimensions={0}, use_global_device_ids=true | all-gather | bytes 16896 | tf_op jit(solution)/shard_map/all_gather | solution.py:57
  193.7 4.3 %all-gather.1 = bf16[2,16,16]{1,0,2:T(2,128)(2,1)S(1)} all-gather(bf16[2,16,8]{1,0,2:T(2,128)(2,1)S(1)} %copy.74), channel_id=3, replica_groups=mesh['dap'=16,'grp'=2] {'grp'}, dimensions={2}, use_global_device_ids=true | all-gather | bytes 1536 | tf_op jit(solution)/shard_map/all_gather | solution.py:81
  198.1 0.1 gt.22
  198.2 3.5 %all-to-all-start.2 = ((bf16[8,256,128]{2,1,0:T(8,128)(2,1)}), bf16[8,256,128]{2,1,0:T(8,128)(2,1)S(1)}, u32[]{:S(2)}, u32[]{:S(2)}) async-start(bf16[8,256,128]{2,1,0:T(8,128)(2,1)} %all_gather.17), calls=%async_computation.2 | async-start | bytes 1048576 | tf_op jit(solution)/shard_map/all_to_all | solution.py:146
  201.8 7.9 %all-gather = bf16[2,16,16,256]{3,2,1,0:T(8,128)(2,1)S(1)} all-gather(bf16[2,16,8,256]{3,2,1,0:T(8,128)(2,1)S(1)} %bitcast.139), channel_id=2, replica_groups=mesh['dap'=16,'grp'=2] {'grp'}, dimensions={2}, use_global_device_ids=true | all-gather | bytes 393216 | tf_op jit(solution)/shard_map/all_gather | solution.py:80
  209.7 0.1 convert_reduce_fusion
  210.1 0.3 fusion.20
  210.4 0.1 rsqrt.28
  210.5 0.2 fusion.22
  210.7 0.3 fusion.75
  211.2 0.3 copy.76
  211.6 2.2 fusion.76
  213.7 2.0 fusion.11
  215.8 1.0 convolution_convert_fusion
  216.8 3.4 %convert_bitcast_fusion = bf16[8,256,32,32]{1,2,0,3:T(8,128)(2,1)} fusion(bf16[256,32,32,1]{1,0,3,2:T(8,128)(2,1)S(1)} %copy-done.1, bf16[32,8,256]{2,1,0:T(8,128)(2,1)S(1)} %fusion.34, f32[32,8]{0,1:T(8,128)S(1)} %get-tuple-element.3, bf16[256,32]{0,1:T(8,128)(2,1)S(1)} %copy-done.7), kind=kOutput, calls=%fused_computation.2 | convolution fusion | flops 140525568 | bytes 4867072 | tf_op jit(solution)/shard_map/sic,jsd->ijcd/dot_general | solution.py:59
  220.2 15.8 %all-reduce.2.cloned.1.call-done = bf16[2,256,256]{2,1,0:T(8,128)(2,1)} async-done(((bf16[2,256,256]{2,1,0:T(8,128)(2,1)}), bf16[2,256,256]{2,1,0:T(8,128)(2,1)}) %all-reduce.2.cloned.1.call-update) | async-done | bytes 262160 | tf_op jit(solution)/shard_map/psum | solution.py:148
  236.0 1.0 fusion.23
  237.0 0.7 copy.79
  237.7 5.6 %all-to-all-start.3 = ((bf16[2,16,16,256]{3,2,0,1:T(8,128)(2,1)}), bf16[2,16,16,256]{3,2,0,1:T(8,128)(2,1)S(1)}, u32[]{:S(2)}, u32[]{:S(2)}) async-start(bf16[2,16,16,256]{3,2,0,1:T(8,128)(2,1)} %copy.79), calls=%async_computation.3 | async-start | bytes 524288 | tf_op jit(solution)/shard_map/all_to_all | solution.py:153
  243.4 0.1 fusion.82
  243.5 6.7 %copy.91 = bf16[8,256,32,32]{1,3,2,0:T(8,128)(2,1)} copy(bf16[8,256,32,32]{1,2,0,3:T(8,128)(2,1)} %convert_bitcast_fusion) | data formatting | bytes 8388608 | tf_op jit(solution)/shard_map/convert_element_type | solution.py:62
  250.2 4.5 %fusion.6 = bf16[8,256,128]{2,1,0:T(8,128)(2,1)} fusion(bf16[8,256,1024]{1,2,0:T(8,128)(2,1)} %bitcast.126, f32[8,256]{1,0:T(8,128)S(1)} %fusion.82, bf16[1024,128]{1,0:T(8,128)(2,1)S(1)} %copy-done), kind=kOutput, calls=%fused_computation.13 | convolution fusion | flops 537395200 | bytes 4988928 | tf_op jit(solution)/shard_map/dot_general | solution.py:65
  254.7 0.1 convert_reduce_fusion.1
  254.8 0.2 fusion.31
  255.1 0.3 fusion.9
  255.3 0.2 reshape.154
  255.6 0.2 convolution_convert_fusion.1
  255.8 0.2 reshape.155
  256.1 0.8 convolution_select_fusion
  256.9 1.0 fusion.77
  257.9 0.3 fusion.45
  258.3 0.4 copy.102
  258.7 0.3 copy.101
  259.0 1.2 fusion.7
  260.2 1.2 copy.86
  261.4 0.9 fusion.10
  (47 shorter events, 1.0 us)
Async XLA Ops:
  7.2 243.1 %copy-start = (bf16[1024,128]{1,0:T(8,128)(2,1)S(1)}, bf16[1024,128]{1,0:T(8,128)(2,1)}, u32[]{:S(2)}) copy-start(bf16[1024,128]{1,0:T(8,128)(2,1)} %param.25) | copy-start | bytes 786436
  7.2 94.2 %copy-start.6 = (bf16[8,16,128]{2,1,0:T(8,128)(2,1)S(1)}, bf16[8,16,128]{2,1,0:T(8,128)(2,1)}, u32[]{:S(2)}) copy-start(bf16[8,16,128]{2,1,0:T(8,128)(2,1)} %param.16) | copy-start | bytes 98308
  7.2 117.9 %copy-start.3 = (bf16[256,4,128]{2,1,0:T(4,128)(2,1)S(1)}, bf16[256,4,128]{2,1,0:T(4,128)(2,1)}, u32[]{:S(2)}) copy-start(bf16[256,4,128]{2,1,0:T(4,128)(2,1)} %param.17) | copy-start | bytes 786436
  8.6 112.9 %all-to-all-start.1 = ((bf16[16,2,8]{2,1,0:T(2,128)(2,1)}), bf16[16,2,8]{2,1,0:T(2,128)(2,1)S(1)}, u32[]{:S(2)}, u32[]{:S(2)}) async-start(bf16[16,2,8]{2,1,0:T(2,128)(2,1)} %bitcast.9), calls=%async_computation.1 | async-start | bytes 16384 | tf_op jit(solution)/shard_map/all_to_all | solution.py:73
  121.5 76.6 %all-to-all-start = ((bf16[32,8,256]{2,1,0:T(8,128)(2,1)}), bf16[32,8,256]{2,1,0:T(8,128)(2,1)S(1)}, u32[]{:S(2)}, u32[]{:S(2)}) async-start(bf16[32,8,256]{2,1,0:T(8,128)(2,1)} %param.13), calls=%async_computation | async-start | bytes 262144 | tf_op jit(solution)/shard_map/all_to_all | solution.py:72
  198.2 12.9 %all-to-all-start.2 = ((bf16[8,256,128]{2,1,0:T(8,128)(2,1)}), bf16[8,256,128]{2,1,0:T(8,128)(2,1)S(1)}, u32[]{:S(2)}, u32[]{:S(2)}) async-start(bf16[8,256,128]{2,1,0:T(8,128)(2,1)} %all_gather.17), calls=%async_computation.2 | async-start | bytes 1048576 | tf_op jit(solution)/shard_map/all_to_all | solution.py:146
  201.7 34.3 %all-reduce.2.cloned.1.call-start = ((), (), s32[]{:S(2)}) async-start(), calls=%async_computation.4 | async-start | bytes 524288 | tf_op jit(solution)/shard_map/psum | solution.py:148
  213.7 2.1 copy-start.5
  213.7 3.0 %copy-start.1 = (bf16[256,32,32,1]{1,0,3,2:T(8,128)(2,1)S(1)}, bf16[256,32,32,1]{1,0,3,2:T(8,128)(2,1)}, u32[]{:S(2)}) copy-start(bf16[256,32,32,1]{1,0,3,2:T(8,128)(2,1)} %copy.98) | copy-start | bytes 1572868
  213.7 3.1 %copy-start.7 = (bf16[256,32]{0,1:T(8,128)(2,1)S(1)}, bf16[256,32]{0,1:T(8,128)(2,1)}, u32[]{:S(2)}) copy-start(bf16[256,32]{0,1:T(8,128)(2,1)} %param.23) | copy-start | bytes 49156
  237.7 17.0 %all-to-all-start.3 = ((bf16[2,16,16,256]{3,2,0,1:T(8,128)(2,1)}), bf16[2,16,16,256]{3,2,0,1:T(8,128)(2,1)S(1)}, u32[]{:S(2)}, u32[]{:S(2)}) async-start(bf16[2,16,16,256]{3,2,0,1:T(8,128)(2,1)} %copy.79), calls=%async_computation.3 | async-start | bytes 524288 | tf_op jit(solution)/shard_map/all_to_all | solution.py:153
  250.2 4.8 %copy-start.8 = (bf16[256,256]{1,0:T(8,128)(2,1)S(1)}, bf16[256,256]{1,0:T(8,128)(2,1)}, u32[]{:S(2)}) copy-start(bf16[256,256]{1,0:T(8,128)(2,1)} %param.19) | copy-start | bytes 393220
  250.2 5.3 %copy-start.9 = (bf16[256,256]{1,0:T(8,128)(2,1)S(1)}, bf16[256,256]{1,0:T(8,128)(2,1)}, u32[]{:S(2)}) copy-start(bf16[256,256]{1,0:T(8,128)(2,1)} %param.20) | copy-start | bytes 393220
  256.1 1.8 copy-start.2
  259.0 2.5 copy-start.4
Sparse Core Ops, SparseCore 0:
  216.9 19.0 all-reduce.1
where the time goes:
time: 270 us; the launch traced here: 269 us
  blocking collectives  179 us (66%)
  starting transfers between devices  20 us (7%)
  matrix products  19 us (7%)
  waiting for transfers between devices  15.8 us (6%)
  local copies, waits for them, and re-layouts  14.9 us (6%)
  between operations  14.4 us (5%)
  other arithmetic  6.11 us (2%)
    all_gather x1, blocking collectives, shards(): lax.all_gather(right_leading, ('dap', 'grp'), axis=0, tiled=True)  81.3 us
    all_gather x1, blocking collectives, shards(): lax.all_gather(keep_leading, ('dap', 'grp'), axis=0, tiled=True)  65.2 us
    all_gather x1, blocking collectives, shards(): all_rows = lax.all_gather(pairwise_bias, 'dap', axis=1, tiled=True)  20.1 us
    psum x1, waiting for transfers between devices, shards(): lax.psum(partial_result.astype(jnp.bfloat16), 'grp').astype(jnp.float32)  15.8 us
    all_gather x1, blocking collectives, shards(): lax.all_gather(transmitted_rows, 'grp', axis=2, tiled=True)  7.9 us
    all_to_all x1, starting transfers between devices, shards(): lax.all_to_all(keep_wire, 'dap', split_axis=0, concat_axis=1, tiled=True)  7.36 us
    convert_element_type x1, local copies, waits for them, and re-layouts, shards(): outer_prod.reshape(residues_here, segment_length, channels * channels)  6.74 us
    all_to_all x1, starting transfers between devices, shards(): lax.all_to_all(row_result, 'dap', split_axis=1, concat_axis=0, tiled=True)  5.62 us
  transfers between devices with their start and end apart: 5, of which 1 were waited for; matrix products, arithmetic and copies ran while one was open for 9% of the time, Pallas kernels for 0%

commit v1 on v0

v1 whole, which is shorter than its diff:
```python
import functools

import jax
import jax.numpy as jnp
from jax import lax
from jax.experimental import pallas as pl
from jax.experimental.pallas import tpu as pltpu
from jax.sharding import PartitionSpec as P

PER_SPLIT_DIM = 32
LANES = 128
MASKED = -1000000000.0
F32 = jnp.float32
BF16 = jnp.bfloat16


def matmul(lhs, rhs):
    return jnp.dot(lhs, rhs, preferred_element_type=F32)


def matmul_nt(lhs, rhs):
    return lax.dot_general(lhs, rhs, (((1,), (1,)), ((), ())), preferred_element_type=F32)


def matmul_tn(lhs, rhs):
    return lax.dot_general(lhs, rhs, (((0,), (0,)), ((), ())), preferred_element_type=F32)


def rows_of(shape):
    return lax.broadcasted_iota(jnp.int32, shape, 0)


def lanes_of(shape):
    return lax.broadcasted_iota(jnp.int32, shape, 1)


def quotient(values, divisor):
    return lax.shift_right_logical(values, divisor.bit_length() - 1)


def remainder(values, divisor):
    return values & (divisor - 1)


def one_hot(condition):
    return condition.astype(F32).astype(BF16)


def flat_rows(tiles):
    blocks, sublanes, lanes = tiles.shape
    return tiles.astype(F32).reshape(blocks * sublanes, lanes).astype(BF16)


def layer_normalize(widened):
    centered = widened - jnp.mean(widened, axis=-1, keepdims=True)
    variance = jnp.mean(centered * centered, axis=-1, keepdims=True)
    return (centered * lax.rsqrt(variance + 1e-05)).astype(BF16)


def residue_major(sequences, residues):
    total = sequences * residues
    row, lane = rows_of((total, total)), lanes_of((total, total))
    return one_hot(lane == remainder(row, sequences) * residues + quotient(row, sequences))


def prepare_kernel(
    sizes, x_ref, mask_ref, present_ref, bias_ref, left_w_ref, right_w_ref,
    rows_ref, right_ref, left_ref, keep_ref,
):
    groups, sequences_here = sizes
    sequences, residues, width = x_ref.shape
    total = sequences * residues
    channels = left_w_ref.shape[1]
    keep = (mask_ref[...] * present_ref[...]).astype(F32)
    keep_padded = jnp.pad(keep, ((0, 0), (0, LANES - sequences))) if sequences < LANES else keep
    keep_ref[...] = keep_padded
    normed = layer_normalize(x_ref[...].astype(F32).reshape(total, width))
    normed_tiles = normed.astype(F32).reshape(sequences, residues, width).astype(BF16)
    halves = width // LANES
    heads, bias_rows, bias_columns = bias_ref.shape
    heads_here = heads // groups
    keep_tile = keep_padded.astype(BF16)
    for group in range(groups):
        for part in range(sequences // sequences_here):
            target = part * groups + group
            for own in range(sequences_here):
                for half in range(halves):
                    rows_ref[target, own * halves + half] = normed_tiles[
                        part * sequences_here + own, :, half * LANES : (half + 1) * LANES
                    ]
            rows_ref[target, sequences_here * halves] = keep_tile
            slot = sequences_here * halves + 1
            for head in range(heads_here):
                for block in range(bias_rows // residues):
                    for half in range(bias_columns // LANES):
                        rows_ref[target, slot] = bias_ref[
                            group * heads_here + head,
                            block * residues : (block + 1) * residues,
                            half * LANES : (half + 1) * LANES,
                        ]
                        slot += 1

    to_residue_major = residue_major(sequences, residues)
    left = matmul(normed, left_w_ref[...]).astype(BF16)
    left = matmul(to_residue_major, left)
    pick = one_hot(
        quotient(rows_of((total, residues)), sequences) == lanes_of((total, residues))
    )
    own_keep = matmul(pick, keep.astype(BF16))
    at_sequence = remainder(rows_of((total, sequences)), sequences) == lanes_of((total, sequences))
    own_keep = jnp.sum(jnp.where(at_sequence, own_keep, 0.0), axis=1, keepdims=True)
    left_ref[...] = (left * own_keep).astype(BF16)

    right = matmul(normed, right_w_ref[...]).astype(BF16)
    residue_pick = one_hot(
        remainder(lanes_of((residues, total)), residues) == rows_of((residues, total))
    )
    per_tile = LANES // sequences
    spread = one_hot(
        remainder(lanes_of((sequences, LANES)), sequences) == rows_of((sequences, LANES))
    )
    keep_spread = matmul(keep.astype(BF16), spread)
    same_sequence = quotient(rows_of((total, LANES)), residues) == remainder(
        lanes_of((total, LANES)), sequences
    )
    for tile in range(channels // per_tile):
        select = one_hot(
            rows_of((channels, LANES))
            == tile * per_tile + quotient(lanes_of((channels, LANES)), sequences)
        )
        expanded = jnp.where(same_sequence, matmul(right, select), 0.0).astype(BF16)
        result = (matmul(residue_pick, expanded) * keep_spread).astype(BF16)
        for target in range(right_ref.shape[0]):
            right_ref[target, tile] = result


def row_kernel(sizes, place_ref, rows_ref, weight_ref, mix_ref, query_s, key_s, value_s, gate_s):
    parallel, groups, sequences_here, heads_here = sizes
    blocks, tiles, residues, _ = rows_ref.shape
    residues_overall = blocks * residues
    halves = weight_ref.shape[1] // LANES
    head_lanes = heads_here * PER_SPLIT_DIM
    bias_row_blocks = residues_overall // parallel // residues
    bias_column_blocks = residues_overall // groups // LANES
    query_factor = PER_SPLIT_DIM ** (-0.5)
    block_rows = min(residues_overall, 256)

    keep_all = flat_rows(rows_ref[:, sequences_here * halves])
    chosen = one_hot(
        lanes_of((8, LANES)) == place_ref[0] * sequences_here + rows_of((8, LANES))
    )
    key_keep = matmul_nt(chosen, keep_all)

    for own in range(sequences_here):
        normed = jnp.concatenate(
            [flat_rows(rows_ref[:, own * halves + half]) for half in range(halves)], axis=1
        )
        query_s[own] = (matmul(normed, weight_ref[0]) * query_factor).astype(BF16)
        key_s[own] = matmul(normed, weight_ref[1]).astype(BF16)
        value_s[own] = matmul(normed, weight_ref[2]).astype(BF16)
        gate_s[own] = jax.nn.sigmoid(matmul(normed, weight_ref[3]))

    def attend(block):
        start = block * block_rows
        first_part = block * (block_rows // (bias_row_blocks * residues))
        parts = block_rows // (bias_row_blocks * residues)
        head_of = quotient(lanes_of((residues_overall, head_lanes)), PER_SPLIT_DIM)
        query_head = quotient(lanes_of((block_rows, head_lanes)), PER_SPLIT_DIM)
        biases = []
        for head in range(heads_here):
            columns = []
            for group in range(groups):
                for half in range(bias_column_blocks):
                    pieces = []
                    for part in range(parts):
                        for row_block in range(bias_row_blocks):
                            slot = (
                                sequences_here * halves
                                + 1
                                + (head * bias_row_blocks + row_block) * bias_column_blocks
                                + half
                            )
                            pieces.append(
                                rows_ref[(first_part + part) * groups + group, slot].astype(F32)
                            )
                    columns.append(jnp.concatenate(pieces, axis=0))
            biases.append(jnp.concatenate(columns, axis=1))
        for own in range(sequences_here):
            queries = query_s[own, pl.ds(start, block_rows), :]
            keys, values = key_s[own], value_s[own]
            keep_row = key_keep[own : own + 1, :] > 0.5
            total = jnp.zeros((block_rows, 2 * head_lanes), F32)
            for head in range(heads_here):
                query_part = jnp.where(query_head == head, queries, jnp.zeros_like(queries))
                scores = matmul_nt(query_part, keys) + biases[head]
                scores = jnp.where(keep_row, scores, MASKED)
                scores = scores - jnp.max(scores, axis=1, keepdims=True)
                weights = jnp.exp(scores).astype(BF16)
                mine = head_of == head
                value_part = jnp.where(mine, values, jnp.zeros_like(values))
                total = total + matmul(
                    weights, jnp.concatenate([value_part, one_hot(mine)], axis=1)
                )
            mixed = total[:, :head_lanes] / total[:, head_lanes:]
            mixed = mixed * gate_s[own, pl.ds(start, block_rows), :]
            mix_ref[pl.ds(block * (block_rows // residues), block_rows // residues), own] = (
                mixed.reshape(block_rows // residues, residues, head_lanes).astype(BF16)
            )

    if residues_overall == block_rows:
        attend(0)
    else:
        pl.loop(0, residues_overall // block_rows)(attend)


def outer_kernel(sizes, rows_ref, right_ref, left_ref, keep_ref, weight_ref, out_ref, mixed_s):
    keep_slot, sequences, pair = sizes
    blocks, right_tiles, residues, _ = right_ref.shape
    segment = blocks * residues
    channels, _, depth = weight_ref.shape
    left = left_ref[...]
    per_step = 2 if depth == LANES else 1
    for channel in range(0, channels, per_step):
        weights = jnp.concatenate(
            [weight_ref[channel + at] for at in range(per_step)], axis=1
        )
        product = matmul(left, weights).astype(BF16)
        for residue in range(residues):
            for at in range(per_step):
                mixed_s[
                    residue, (channel + at) * sequences : (channel + at + 1) * sequences, :
                ] = product[
                    residue * sequences : (residue + 1) * sequences, at * depth : (at + 1) * depth
                ]
    right = jnp.concatenate(
        [flat_rows(right_ref[:, tile]) for tile in range(right_tiles)], axis=1
    )
    keep_all = flat_rows(rows_ref[:, keep_slot])
    for first in range(0, residues, pair):
        members = range(first, first + pair)
        mixed = jnp.concatenate([mixed_s[residue] for residue in members], axis=1)
        keep_rows = jnp.concatenate(
            [
                jnp.broadcast_to(keep_ref[residue : residue + 1, :], (depth, LANES))
                for residue in members
            ],
            axis=0,
        ).astype(BF16)
        result = matmul(right, mixed) / matmul_nt(keep_all, keep_rows)
        for at, residue in enumerate(members):
            out_ref[residue] = result[:, at * depth : (at + 1) * depth].astype(BF16)
    del segment


def column_kernel(
    sizes, place_ref, x_ref, mix_ref, keep_ref, row_out_ref, query_w_ref, key_w_ref, vg_w_ref,
    out_w_ref, out_ref,
):
    groups = sizes
    sequences, residues, width = x_ref.shape
    total = sequences * residues
    heads = query_w_ref.shape[1] // PER_SPLIT_DIM
    query_factor = PER_SPLIT_DIM ** (-0.5)
    own_group = place_ref[1]
    after = x_ref[...].astype(F32).reshape(total, width)
    for at in range(groups):
        group = own_group + at
        group = jnp.where(group >= groups, group - groups, group)
        mixed = mix_ref[:, pl.ds(group, 1)]
        mixed = mixed.astype(F32).reshape(total, mixed.shape[-1]).astype(BF16)
        after = after + matmul(mixed, row_out_ref[at])
    after = after.astype(BF16).astype(F32)
    permutation = residue_major(sequences, residues)
    normed = matmul(permutation, layer_normalize(after)).astype(BF16)
    queries = (matmul(normed, query_w_ref[...]) * query_factor).astype(BF16)
    keys = matmul(normed, key_w_ref[...]).astype(BF16)
    values = matmul(normed, vg_w_ref[0]).astype(BF16)
    gate = jax.nn.sigmoid(matmul(normed, vg_w_ref[1]))

    together = max(1, min(residues, 256 // sequences))
    span = together * sequences
    head_rows = heads * sequences
    inner = heads * PER_SPLIT_DIM
    block_diagonal = quotient(rows_of((head_rows, inner)), sequences) == quotient(
        lanes_of((head_rows, inner)), PER_SPLIT_DIM
    )
    zero = jnp.zeros((head_rows, inner), BF16)

    def by_head(part):
        return jnp.where(block_diagonal, jnp.concatenate([part] * heads, axis=0), zero)

    mixes = []
    for first in range(0, residues, together):
        base = first * sequences
        query_span = queries[base : base + span]
        owner = quotient(rows_of((span, inner)), sequences)
        scores = jnp.zeros((head_rows, span), F32)
        for at in range(together):
            key_part = by_head(keys[base + at * sequences : base + (at + 1) * sequences])
            query_part = jnp.where(owner == at, query_span, jnp.zeros_like(query_span))
            scores = scores + matmul_nt(key_part, query_part)
        spread = one_hot(
            rows_of((residues, span)) == first + quotient(lanes_of((residues, span)), sequences)
        )
        key_keep = matmul_tn(keep_ref[...].astype(BF16), spread)[:sequences]
        scores = scores.reshape(heads, sequences, span)
        scores = jnp.where(key_keep[None] > 0.5, scores, MASKED)
        scores = jnp.exp(scores - jnp.max(scores, axis=1, keepdims=True))
        weights = scores / jnp.sum(scores, axis=1, keepdims=True)
        weights = weights.reshape(head_rows, span).T.astype(BF16)
        for at in range(together):
            value_part = by_head(values[base + at * sequences : base + (at + 1) * sequences])
            mixes.append(matmul(weights[at * sequences : (at + 1) * sequences], value_part))
    mixed = (jnp.concatenate(mixes, axis=0) * gate).astype(BF16)
    mixed = matmul_tn(permutation, mixed).astype(BF16)
    result = after + matmul(mixed, out_w_ref[...])
    out_ref[...] = result.reshape(sequences, residues, width).astype(BF16)


def call(kernel, outs, scratch=(), scalars=0, arguments=(), mib=32):
    vmem = pl.BlockSpec(memory_space=pltpu.VMEM)
    smem = pl.BlockSpec(memory_space=pltpu.SMEM)
    return pl.pallas_call(
        kernel,
        out_shape=outs,
        in_specs=[smem] * scalars + [vmem] * (len(arguments) - scalars),
        out_specs=jax.tree.map(lambda _: vmem, outs),
        scratch_shapes=list(scratch),
        compiler_params=pltpu.CompilerParams(vmem_limit_bytes=mib * 1024 * 1024),
    )(*arguments)


def shards(
    homolog_activity,
    alignment_mask,
    sequence_row_mask,
    pairwise_bias,
    horizontal_projection_matrix,
    horizontal_final_matrix,
    column_query_weight,
    column_key_weight,
    vertical_content_sigmoid_matrix,
    vertical_final_matrix,
    first_operand_matrix,
    second_operand_matrix,
    outer_output_weight,
):
    parallel = lax.axis_size("dap")
    groups = lax.axis_size("grp")
    devices = parallel * groups
    sequences, residues, width = homolog_activity.shape
    residues_overall = residues * devices
    sequences_here = sequences // parallel
    heads, bias_rows, bias_columns = pairwise_bias.shape
    heads_here = heads // groups
    head_lanes = heads_here * PER_SPLIT_DIM
    channels = first_operand_matrix.shape[1]
    depth = outer_output_weight.shape[1]
    large = residues_overall > 256
    place = jnp.stack([lax.axis_index("dap"), lax.axis_index("grp")]).astype(jnp.int32)

    keep_slot = sequences_here * (width // LANES)
    tiles = keep_slot + 1 + heads_here * (bias_rows // residues) * (bias_columns // LANES)
    right_tiles = channels * sequences // LANES
    shape = jax.ShapeDtypeStruct
    rows_out, right_out, left, keep = call(
        functools.partial(prepare_kernel, (groups, sequences_here)),
        (
            shape((devices, tiles, residues, LANES), BF16),
            shape((devices, right_tiles, residues, LANES), BF16),
            shape((sequences * residues, channels), BF16),
            shape((residues, LANES), F32),
        ),
        arguments=(
            homolog_activity,
            alignment_mask.T,
            sequence_row_mask.reshape(1, sequences),
            pairwise_bias,
            first_operand_matrix,
            second_operand_matrix,
        ),
        mib=56 if large else 32,
    )
    both = ("dap", "grp")
    final_parts = [horizontal_final_matrix]
    for step in range(1, groups):
        final_parts.append(
            lax.ppermute(
                horizontal_final_matrix,
                "grp",
                [(source, (source - step) % groups) for source in range(groups)],
            )
        )
    row_out_weight = jnp.stack(final_parts)
    rows_in = lax.all_to_all(rows_out, both, split_axis=0, concat_axis=0, tiled=True)
    right_in = lax.all_to_all(right_out, both, split_axis=0, concat_axis=0, tiled=True)

    mix_out = call(
        functools.partial(row_kernel, (parallel, groups, sequences_here, heads_here)),
        shape((devices, sequences_here, residues, head_lanes), BF16),
        scratch=[pltpu.VMEM((sequences_here, residues_overall, head_lanes), BF16)] * 3
        + [pltpu.VMEM((sequences_here, residues_overall, head_lanes), F32)],
        scalars=1,
        arguments=(place, rows_in, horizontal_projection_matrix.transpose(1, 0, 2)),
        mib=56 if large else 32,
    )
    mix_in = lax.all_to_all(mix_out, both, split_axis=0, concat_axis=0, tiled=True)

    pairwise_update = call(
        functools.partial(outer_kernel, (keep_slot, sequences, 2)),
        shape((residues, residues_overall, depth), BF16),
        scratch=[pltpu.VMEM((residues, channels * sequences, depth), BF16)],
        arguments=(
            rows_in,
            right_in,
            left,
            keep,
            outer_output_weight.reshape(channels, channels, depth).transpose(1, 0, 2),
        ),
        mib=60 if large else 32,
    )

    alignment_output = call(
        functools.partial(column_kernel, groups),
        shape((sequences, residues, width), BF16),
        scalars=1,
        arguments=(
            place,
            homolog_activity,
            mix_in.reshape(parallel, groups, sequences_here, residues, head_lanes),
            keep,
            row_out_weight,
            column_query_weight,
            column_key_weight,
            vertical_content_sigmoid_matrix.transpose(1, 0, 2),
            vertical_final_matrix,
        ),
        mib=56 if large else 32,
    )
    return (alignment_output, pairwise_update)


def solution(mesh):
    return jax.shard_map(
        shards,
        mesh=mesh,
        in_specs=(
            P(None, ("dap", "grp"), None),
            P(None, ("dap", "grp")),
            P(),
            P(None, "dap", "grp"),
            P(None, None, "grp"),
            P("grp", None),
            P(),
            P(),
            P(),
            P(),
            P(),
            P(),
            P(),
        ),
        out_specs=(P(None, ("dap", "grp"), None), P(("dap", "grp"), None, None)),
        check_vma=False,
    )
```

time: 270 us -> 70.4 us (0.26)
  blocking collectives: 179 us -> 29.1 us
  matrix products: 19 us -> 0 us
  between operations: 14.4 us -> 0.76 us
  starting transfers between devices: 20 us -> 9.07 us
  Pallas kernels: 0 us -> 10.9 us
  local copies, waits for them, and re-layouts: 14.9 us -> 4.08 us
  other arithmetic: 6.11 us -> 0.09 us
    all_gather x5 -> x0, blocking collectives: 179 us -> none  [the longest x1 81.3 us: shards(): lax.all_gather(right_leading, ('dap', 'grp'), axis=0, tiled=True)]
    all_to_all x0 -> x1, blocking collectives: none -> 29.1 us  [shards(): lax.all_to_all(rows_out, both, split_axis=0, concat_axis=0, tiled=True)]
    dot_general x13 -> x0, matrix products: 15.9 us -> none  [the longest x1 4.48 us: shards(): jnp.dot(outer_prod, outer_output_weight, preferred_element_type=jnp.float32)]
    psum x1 -> x0, waiting for transfers between devices: 15.8 us -> none  [shards(): lax.psum(partial_result.astype(jnp.bfloat16), 'grp').astype(jnp.float32)]
    all_to_all x4 -> x2, waiting for transfers between devices: 0.01 us -> 13.8 us  [the longest x1 12.3 us: shards(): lax.all_to_all(right_out, both, split_axis=0, concat_axis=0, tiled=True)]
    all_to_all x4 -> x2, starting transfers between devices: 20 us -> 7.24 us  [the longest x1 3.62 us: shards(): lax.all_to_all(right_out, both, split_axis=0, concat_axis=0, tiled=True)]
    pallas_call x0 -> x4, Pallas kernels: none -> 10.9 us  [call(): pl.pallas_call(kernel, out_shape=outs, in_specs=[smem] * scalars + [vmem]...]
    convert_element_type x4 -> x0, local copies, waits for them, and re-layouts: 8.04 us -> none  [the longest x1 6.74 us: shards(): outer_prod.reshape(residues_here, segment_length, channels * channels)]
  transfers between devices with their start and end apart: 5 -> 3, of which waited for: 1 -> 3; matrix products, arithmetic and copies ran while one was open for 9% -> 0% of each run, Pallas kernels for 0% -> 7%
where the time goes in v1:
time: 70.4 us; the launch traced here: 69.9 us
  blocking collectives  29.1 us (41%)
  waiting for transfers between devices  15.8 us (22%)
  Pallas kernels  10.9 us (15%)
  starting transfers between devices  9.07 us (13%)
  local copies, waits for them, and re-layouts  4.08 us (6%)
  between operations  0.76 us (1%)
    all_to_all x1, blocking collectives, shards(): lax.all_to_all(rows_out, both, split_axis=0, concat_axis=0, tiled=True)  29.1 us
    all_to_all x1, waiting for transfers between devices, shards(): lax.all_to_all(right_out, both, split_axis=0, concat_axis=0, tiled=True)  12.3 us
    pallas_call x4, Pallas kernels, call(): pl.pallas_call(kernel, out_shape=outs, in_specs=[smem] * scalars + [vmem]...  10.9 us
    unnamed x26, local copies, waits for them, and re-layouts  3.98 us
    all_to_all x1, starting transfers between devices, shards(): lax.all_to_all(right_out, both, split_axis=0, concat_axis=0, tiled=True)  3.62 us
    all_to_all x1, starting transfers between devices, shards(): lax.all_to_all(mix_out, both, split_axis=0, concat_axis=0, tiled=True)  3.62 us
    ppermute x1, waiting for transfers between devices, shards(): lax.ppermute(horizontal_final_matrix, 'grp', [(source, (source - step) %...  2.07 us
    ppermute x1, starting transfers between devices, shards(): lax.ppermute(horizontal_final_matrix, 'grp', [(source, (source - step) %...  1.83 us
  transfers between devices with their start and end apart: 3, of which 3 were waited for; matrix products, arithmetic and copies ran while one was open for 0% of the time, Pallas kernels for 7%

profile of v1, /device:TPU:0, one launch (start us, length us, event | category | flops | bytes accessed | tf_op | source)
XLA Modules:
  0.0 69.9 jit_solution(13058298021274403368)
XLA Ops:
  0.6 0.0 copy-start
  0.6 0.9 %copy.19.left_w_ref = bf16[256,32]{1,0:T(8,128)(2,1)S(1)} copy(bf16[256,32]{0,1:T(8,128)(2,1)} %param.23) | data formatting | bytes 32768 | tf_op args[10]
  1.5 0.0 copy-start.4
  1.5 0.8 %copy.20.right_w_ref = bf16[256,32]{1,0:T(8,128)(2,1)S(1)} copy(bf16[256,32]{0,1:T(8,128)(2,1)} %param.24) | data formatting | bytes 32768 | tf_op args[11]
  2.4 0.0 copy-start.6
  2.4 0.0 copy-done
  2.4 0.0 copy-done.4
  2.4 0.6 copy-done.6
  3.0 0.0 copy-start.5
  3.0 0.7 copy-done.5
  3.7 2.8 %shard_map.140 = (bf16[32,13,8,128]{3,2,1,0:T(8,128)(2,1)S(1)}, bf16[32,8,8,128]{3,2,1,0:T(8,128)(2,1)}, bf16[256,32]{1,0:T(8,128)(2,1)S(1)}, f32[8,128]{1,0:T(8,128)S(1)}) custom-call(bf16[32,8,256]{2,1,0:T(8,128)(2,1)S(1)} %copy-done, s32[8,32]{1,0:T(8,128)S(1)} %bitcast.21, s32[1,32]{1,0:T(1,128)S(1)} %bitcast.22, bf16[8,16,128]{2,1,0:T(8,128)(2,1)S(1)} %copy-done.4, ...), custom_call_target="tpu_custom_call" | custom-call | tf_op jit(solution)/shard_map/pallas_call | solution.py:323
  6.5 29.1 %all_to_all.15.rows_ref = bf16[32,13,8,128]{3,2,1,0:T(8,128)(2,1)S(1)} all-to-all(bf16[32,13,8,128]{3,2,1,0:T(8,128)(2,1)S(1)} %get-tuple-element.6), channel_id=1, replica_groups=mesh['dap'=16,'grp'=2] {'dap','grp'}, dimensions={0} | all-to-all | bytes 1703936 | tf_op jit(solution)/shard_map/all_to_all | solution.py:395
  35.6 0.0 copy-start.7
  35.6 3.6 %all-to-all-start.2 = ((bf16[32,8,8,128]{3,2,1,0:T(8,128)(2,1)}), bf16[32,8,8,128]{3,2,1,0:T(8,128)(2,1)S(1)}, u32[]{:S(2)}, u32[]{:S(2)}) async-start(bf16[32,8,8,128]{3,2,1,0:T(8,128)(2,1)} %get-tuple-element.8), calls=%async_computation.2 | async-start | bytes 1048576 | tf_op jit(solution)/shard_map/all_to_all | solution.py:396
  39.2 0.0 copy-done.7
  39.3 0.1 pad_add_fusion.place_ref
  39.4 0.0 copy-start.10
  39.4 2.6 %shard_map.141 = bf16[32,2,8,128]{3,2,1,0:T(8,128)(2,1)} custom-call(s32[2]{0:T(128)S(1)} %pad_add_fusion.place_ref, bf16[32,13,8,128]{3,2,1,0:T(8,128)(2,1)S(1)} %all_to_all.15.rows_ref, bf16[4,256,128]{2,1,0:T(8,128)(2,1)S(1)} %bitcast.19), custom_call_target="tpu_custom_call" | custom-call | tf_op jit(solution)/shard_map/pallas_call | solution.py:323
  42.0 0.0 copy-start.8
  42.0 12.3 %all-to-all-done.2.right_ref = bf16[32,8,8,128]{3,2,1,0:T(8,128)(2,1)S(1)} async-done(((bf16[32,8,8,128]{3,2,1,0:T(8,128)(2,1)}), bf16[32,8,8,128]{3,2,1,0:T(8,128)(2,1)S(1)}, u32[]{:S(2)}, u32[]{:S(2)}) %all-to-all-start.2) | async-done | bytes 524320 | tf_op jit(solution)/shard_map/all_to_all | solution.py:396
  54.2 3.6 %all-to-all-start.1 = ((bf16[32,2,8,128]{3,2,1,0:T(8,128)(2,1)}), bf16[32,2,8,128]{3,2,1,0:T(8,128)(2,1)S(1)}, u32[]{:S(2)}, u32[]{:S(2)}) async-start(bf16[32,2,8,128]{3,2,1,0:T(8,128)(2,1)} %shard_map.141), calls=%async_computation.1 | async-start | bytes 262144 | tf_op jit(solution)/shard_map/all_to_all | solution.py:407
  57.9 0.0 copy-done.10
  57.9 1.8 %collective-permute-start = (bf16[128,256]{1,0:T(8,128)(2,1)S(1)}, bf16[128,256]{1,0:T(8,128)(2,1)S(1)}, u32[]{:S(2)}, u32[]{:S(2)}) collective-permute-start(bf16[128,256]{1,0:T(8,128)(2,1)S(1)} %copy-done.10), channel_id=1, source_target_pairs={{0,1},{1,0},{2,3},{3,2},{4,5},{5,4},{6,7},{7,6},{8,9},{9,8},{10,11... | collective-permute-start | bytes 196616 | tf_op jit(solution)/shard_map/ppermute | solution.py:388
  59.7 0.0 copy-done.8
  59.7 0.0 copy-start.9
  59.7 0.1 copy.27
  59.8 0.8 %copy-done.9 = bf16[256,2,256]{2,1,0:T(2,128)(2,1)S(1)} copy-done((bf16[256,2,256]{2,1,0:T(2,128)(2,1)S(1)}, bf16[256,2,256]{2,1,0:T(2,128)(2,1)}, u32[]{:S(2)}) %copy-start.9) | copy-done | bytes 262168
  60.7 2.1 %collective-permute-done = bf16[128,256]{1,0:T(8,128)(2,1)S(1)} collective-permute-done((bf16[128,256]{1,0:T(8,128)(2,1)S(1)}, bf16[128,256]{1,0:T(8,128)(2,1)S(1)}, u32[]{:S(2)}, u32[]{:S(2)}) %collective-permute-start) | collective-permute-done | bytes 65568 | tf_op jit(solution)/shard_map/ppermute | solution.py:388
  62.8 0.0 copy-start.1
  62.8 0.0 copy-start.2
  62.8 0.0 copy-start.3
  62.8 2.2 %shard_map.143 = bf16[8,256,128]{2,1,0:T(8,128)(2,1)} custom-call(bf16[32,13,8,128]{3,2,1,0:T(8,128)(2,1)S(1)} %all_to_all.15.rows_ref, bf16[32,8,8,128]{3,2,1,0:T(8,128)(2,1)S(1)} %all-to-all-done.2.right_ref, bf16[256,32]{1,0:T(8,128)(2,1)S(1)} %get-tuple-element.9.left_ref, f32[8,128]{1,0:T(8,128)S(1)} %get-tuple-element.7.keep_ref, ...), custom_call_target="tpu_custom_call" | custom-call | tf_op jit(solution)/shard_map/pallas_call | solution.py:323
  65.0 1.5 %all-to-all-done.1 = bf16[32,2,8,128]{3,2,1,0:T(8,128)(2,1)S(1)} async-done(((bf16[32,2,8,128]{3,2,1,0:T(8,128)(2,1)}), bf16[32,2,8,128]{3,2,1,0:T(8,128)(2,1)S(1)}, u32[]{:S(2)}, u32[]{:S(2)}) %all-to-all-start.1) | async-done | bytes 131104 | tf_op jit(solution)/shard_map/all_to_all | solution.py:407
  66.5 0.0 copy-done.1
  66.5 0.0 copy-done.2
  66.5 0.0 copy-done.3
  66.5 3.4 %shard_map.142 = bf16[32,8,256]{2,1,0:T(8,128)(2,1)} custom-call(s32[2]{0:T(128)S(1)} %pad_add_fusion.place_ref, bf16[32,8,256]{2,1,0:T(8,128)(2,1)S(1)} %copy-done, bf16[16,2,2,8,128]{4,3,2,1,0:T(8,128)(2,1)S(1)} %bitcast.20, f32[8,128]{1,0:T(8,128)S(1)} %get-tuple-element.7.keep_ref, bf16[2,128,256]{2,1,0:T(8,128)(2,1)S(1)} %pad_maximum_fusion.row_out_ref, ...), custom_call_target="tpu_custom_call" | custom-call | tf_op jit(solution)/shard_map/pallas_call | solution.py:323
  (3 shorter events, 0.1 us)
Async XLA Ops:
  0.6 1.7 %copy-start = (bf16[32,8,256]{2,1,0:T(8,128)(2,1)S(1)}, bf16[32,8,256]{2,1,0:T(8,128)(2,1)}, u32[]{:S(2)}) copy-start(bf16[32,8,256]{2,1,0:T(8,128)(2,1)} %x_ref.3) | copy-start | bytes 393220
  1.5 0.9 %copy-start.4 = (bf16[8,16,128]{2,1,0:T(8,128)(2,1)S(1)}, bf16[8,16,128]{2,1,0:T(8,128)(2,1)}, u32[]{:S(2)}) copy-start(bf16[8,16,128]{2,1,0:T(8,128)(2,1)} %bias_ref.1) | copy-start | bytes 98308
  2.4 0.7 copy-start.6
  3.0 0.7 copy-start.5
  35.6 3.6 %copy-start.7 = (bf16[256,4,128]{2,1,0:T(4,128)(2,1)S(1)}, bf16[256,4,128]{2,1,0:T(4,128)(2,1)}, u32[]{:S(2)}) copy-start(bf16[256,4,128]{2,1,0:T(4,128)(2,1)} %param.17) | copy-start | bytes 786436
  35.6 18.6 %all-to-all-start.2 = ((bf16[32,8,8,128]{3,2,1,0:T(8,128)(2,1)}), bf16[32,8,8,128]{3,2,1,0:T(8,128)(2,1)S(1)}, u32[]{:S(2)}, u32[]{:S(2)}) async-start(bf16[32,8,8,128]{3,2,1,0:T(8,128)(2,1)} %get-tuple-element.8), calls=%async_computation.2 | async-start | bytes 1048576 | tf_op jit(solution)/shard_map/all_to_all | solution.py:396
  39.4 18.5 %copy-start.10 = (bf16[128,256]{1,0:T(8,128)(2,1)S(1)}, bf16[128,256]{1,0:T(8,128)(2,1)}, u32[]{:S(2)}) copy-start(bf16[128,256]{1,0:T(8,128)(2,1)} %param.18) | copy-start | bytes 196612
  42.0 17.7 %copy-start.8 = (bf16[1024,128]{1,0:T(8,128)(2,1)S(1)}, bf16[1024,128]{1,0:T(8,128)(2,1)}, u32[]{:S(2)}) copy-start(bf16[1024,128]{1,0:T(8,128)(2,1)} %param.25) | copy-start | bytes 786436
  54.2 12.3 %all-to-all-start.1 = ((bf16[32,2,8,128]{3,2,1,0:T(8,128)(2,1)}), bf16[32,2,8,128]{3,2,1,0:T(8,128)(2,1)S(1)}, u32[]{:S(2)}, u32[]{:S(2)}) async-start(bf16[32,2,8,128]{3,2,1,0:T(8,128)(2,1)} %shard_map.141), calls=%async_computation.1 | async-start | bytes 262144 | tf_op jit(solution)/shard_map/all_to_all | solution.py:407
  57.9 4.9 %collective-permute-start = (bf16[128,256]{1,0:T(8,128)(2,1)S(1)}, bf16[128,256]{1,0:T(8,128)(2,1)S(1)}, u32[]{:S(2)}, u32[]{:S(2)}) collective-permute-start(bf16[128,256]{1,0:T(8,128)(2,1)S(1)} %copy-done.10), channel_id=1, source_target_pairs={{0,1},{1,0},{2,3},{3,2},{4,5},{5,4},{6,7},{7,6},{8,9},{9,8},{10,11... | collective-permute-start | bytes 196616 | tf_op jit(solution)/shard_map/ppermute | solution.py:388
  59.7 1.0 %copy-start.9 = (bf16[256,2,256]{2,1,0:T(2,128)(2,1)S(1)}, bf16[256,2,256]{2,1,0:T(2,128)(2,1)}, u32[]{:S(2)}) copy-start(bf16[256,2,256]{2,1,0:T(2,128)(2,1)} %param.21) | copy-start | bytes 786436
  62.8 3.7 %copy-start.1 = (bf16[256,256]{1,0:T(8,128)(2,1)S(1)}, bf16[256,256]{1,0:T(8,128)(2,1)}, u32[]{:S(2)}) copy-start(bf16[256,256]{1,0:T(8,128)(2,1)} %query_w_ref.1) | copy-start | bytes 393220
  62.8 3.7 %copy-start.2 = (bf16[256,256]{1,0:T(8,128)(2,1)S(1)}, bf16[256,256]{1,0:T(8,128)(2,1)}, u32[]{:S(2)}) copy-start(bf16[256,256]{1,0:T(8,128)(2,1)} %key_w_ref.1) | copy-start | bytes 393220
  62.8 3.7 %copy-start.3 = (bf16[256,256]{1,0:T(8,128)(2,1)S(1)}, bf16[256,256]{1,0:T(8,128)(2,1)}, u32[]{:S(2)}) copy-start(bf16[256,256]{1,0:T(8,128)(2,1)} %out_w_ref.1) | copy-start | bytes 393220

commit v2 on v1

--- a/solution.py
+++ b/solution.py
@@ -63,45 +63,56 @@
     return one_hot(lane == remainder(row, sequences) * residues + quotient(row, sequences))
 
 
+def tile_count(bias_shape, groups):
+    heads, bias_rows, bias_columns = bias_shape
+    return heads // groups, bias_rows // 8, bias_columns // LANES
+
+
+def share_kernel(groups, place_ref, mask_ref, present_ref, bias_ref, *out_refs):
+    *piece_refs, keep_ref = out_refs
+    heads_here, row_tiles, column_tiles = tile_count(bias_ref.shape, groups)
+    sequences = mask_ref.shape[1]
+    keep = (mask_ref[...] * present_ref[...]).astype(F32)
+    if sequences < LANES:
+        keep = jnp.pad(keep, ((0, 0), (0, LANES - sequences)))
+    keep_ref[...] = keep
+    own_group = place_ref[0] & (groups - 1)
+    for relative, piece_ref in enumerate(piece_refs):
+        group = own_group ^ relative
+        slot = 0
+        for head in range(heads_here):
+            for row in range(row_tiles):
+                for column in range(column_tiles):
+                    piece_ref[slot] = bias_ref[
+                        group * heads_here + head,
+                        row * 8 : (row + 1) * 8,
+                        column * LANES : (column + 1) * LANES,
+                    ]
+                    slot += 1
+        piece_ref[slot] = keep.astype(BF16)
+
+
 def prepare_kernel(
-    sizes, x_ref, mask_ref, present_ref, bias_ref, left_w_ref, right_w_ref,
-    rows_ref, right_ref, left_ref, keep_ref,
+    sizes, x_ref, keep_ref, left_w_ref, right_w_ref, rows_ref, right_ref, left_ref
 ):
     groups, sequences_here = sizes
     sequences, residues, width = x_ref.shape
     total = sequences * residues
-    channels = left_w_ref.shape[1]
-    keep = (mask_ref[...] * present_ref[...]).astype(F32)
-    keep_padded = jnp.pad(keep, ((0, 0), (0, LANES - sequences))) if sequences < LANES else keep
-    keep_ref[...] = keep_padded
+    channels = left_w_ref.shape[0]
+    keep = keep_ref[:, :sequences]
     normed = layer_normalize(x_ref[...].astype(F32).reshape(total, width))
     normed_tiles = normed.astype(F32).reshape(sequences, residues, width).astype(BF16)
     halves = width // LANES
-    heads, bias_rows, bias_columns = bias_ref.shape
-    heads_here = heads // groups
-    keep_tile = keep_padded.astype(BF16)
-    for group in range(groups):
-        for part in range(sequences // sequences_here):
-            target = part * groups + group
-            for own in range(sequences_here):
-                for half in range(halves):
-                    rows_ref[target, own * halves + half] = normed_tiles[
+    for part in range(sequences // sequences_here):
+        for own in range(sequences_here):
+            for half in range(halves):
+                for group in range(groups):
+                    rows_ref[part * groups + group, own * halves + half] = normed_tiles[
                         part * sequences_here + own, :, half * LANES : (half + 1) * LANES
                     ]
-            rows_ref[target, sequences_here * halves] = keep_tile
-            slot = sequences_here * halves + 1
-            for head in range(heads_here):
-                for block in range(bias_rows // residues):
-                    for half in range(bias_columns // LANES):
-                        rows_ref[target, slot] = bias_ref[
-                            group * heads_here + head,
-                            block * residues : (block + 1) * residues,
-                            half * LANES : (half + 1) * LANES,
-                        ]
-                        slot += 1
 
     to_residue_major = residue_major(sequences, residues)
-    left = matmul(normed, left_w_ref[...]).astype(BF16)
+    left = matmul_nt(normed, left_w_ref[...]).astype(BF16)
     left = matmul(to_residue_major, left)
     pick = one_hot(
         quotient(rows_of((total, residues)), sequences) == lanes_of((total, residues))
@@ -111,7 +122,7 @@
     own_keep = jnp.sum(jnp.where(at_sequence, own_keep, 0.0), axis=1, keepdims=True)
     left_ref[...] = (left * own_keep).astype(BF16)
 
-    right = matmul(normed, right_w_ref[...]).astype(BF16)
+    right = matmul_nt(normed, right_w_ref[...]).astype(BF16)
     residue_pick = one_hot(
         remainder(lanes_of((residues, total)), residues) == rows_of((residues, total))
     )
@@ -129,27 +140,35 @@
             == tile * per_tile + quotient(lanes_of((channels, LANES)), sequences)
         )
         expanded = jnp.where(same_sequence, matmul(right, select), 0.0).astype(BF16)
-        result = (matmul(residue_pick, expanded) * keep_spread).astype(BF16)
-        for target in range(right_ref.shape[0]):
-            right_ref[target, tile] = result
-
-
-def row_kernel(sizes, place_ref, rows_ref, weight_ref, mix_ref, query_s, key_s, value_s, gate_s):
-    parallel, groups, sequences_here, heads_here = sizes
+        right_ref[tile] = (matmul(residue_pick, expanded) * keep_spread).astype(BF16)
+
+
+def sources(place, groups, pieces):
+    for across in range(2):
+        for core in range(2):
+            for near in range(pieces):
+                mask = near // groups * 4 * groups + near % groups
+                yield across * 2 + core, near, place ^ (
+                    mask + across * 2 * groups + core * groups
+                )
+
+
+def row_kernel(
+    sizes, place_ref, rows_ref, piece0, piece1, piece2, piece3, weight_ref,
+    mix_ref, keep_all_ref, bias_s, keep_s, query_s, key_s, value_s, gate_s,
+):
+    groups, sequences_here = sizes
     blocks, tiles, residues, _ = rows_ref.shape
     residues_overall = blocks * residues
     halves = weight_ref.shape[1] // LANES
+    heads_here, all_columns, all_rows = bias_s.shape[:3]
+    row_tiles = all_rows // (blocks // groups)
+    column_tiles = all_columns // groups
     head_lanes = heads_here * PER_SPLIT_DIM
-    bias_row_blocks = residues_overall // parallel // residues
-    bias_column_blocks = residues_overall // groups // LANES
     query_factor = PER_SPLIT_DIM ** (-0.5)
     block_rows = min(residues_overall, 256)
-
-    keep_all = flat_rows(rows_ref[:, sequences_here * halves])
-    chosen = one_hot(
-        lanes_of((8, LANES)) == place_ref[0] * sequences_here + rows_of((8, LANES))
-    )
-    key_keep = matmul_nt(chosen, keep_all)
+    place = place_ref[0]
+    pieces = (piece0, piece1, piece2, piece3)
 
     for own in range(sequences_here):
         normed = jnp.concatenate(
@@ -160,30 +179,39 @@
         value_s[own] = matmul(normed, weight_ref[2]).astype(BF16)
         gate_s[own] = jax.nn.sigmoid(matmul(normed, weight_ref[3]))
 
+    for stack, near, source in sources(place, groups, piece0.shape[0]):
+        group = source & (groups - 1)
+        part = quotient(source, groups)
+        slot = 0
+        for head in range(heads_here):
+            for row in range(row_tiles):
+                for column in range(column_tiles):
+                    bias_s[head, group * column_tiles + column, part * row_tiles + row] = pieces[
+                        stack
+                    ][near, slot]
+                    slot += 1
+        keep_s[source] = pieces[stack][near, slot]
+
+    keep_all = flat_rows(keep_s[...])
+    keep_all_ref[...] = keep_all
+    chosen = one_hot(
+        lanes_of((8, LANES)) == quotient(place, groups) * sequences_here + rows_of((8, LANES))
+    )
+    key_keep = matmul_nt(chosen, keep_all)
+
     def attend(block):
         start = block * block_rows
-        first_part = block * (block_rows // (bias_row_blocks * residues))
-        parts = block_rows // (bias_row_blocks * residues)
+        count = block_rows // 8
         head_of = quotient(lanes_of((residues_overall, head_lanes)), PER_SPLIT_DIM)
         query_head = quotient(lanes_of((block_rows, head_lanes)), PER_SPLIT_DIM)
         biases = []
         for head in range(heads_here):
-            columns = []
-            for group in range(groups):
-                for half in range(bias_column_blocks):
-                    pieces = []
-                    for part in range(parts):
-                        for row_block in range(bias_row_blocks):
-                            slot = (
-                                sequences_here * halves
-                                + 1
-                                + (head * bias_row_blocks + row_block) * bias_column_blocks
-                                + half
-                            )
-                            pieces.append(
-                                rows_ref[(first_part + part) * groups + group, slot].astype(F32)
-                            )
-                    columns.append(jnp.concatenate(pieces, axis=0))
+            columns = [
+                bias_s[head, column, pl.ds(block * count, count)]
+                .astype(F32)
+                .reshape(block_rows, LANES)
+                for column in range(all_columns)
+            ]
             biases.append(jnp.concatenate(columns, axis=1))
         for own in range(sequences_here):
             queries = query_s[own, pl.ds(start, block_rows), :]
@@ -213,10 +241,13 @@
         pl.loop(0, residues_overall // block_rows)(attend)
 
 
-def outer_kernel(sizes, rows_ref, right_ref, left_ref, keep_ref, weight_ref, out_ref, mixed_s):
-    keep_slot, sequences, pair = sizes
-    blocks, right_tiles, residues, _ = right_ref.shape
-    segment = blocks * residues
+def outer_kernel(
+    sizes, place_ref, keep_all_ref, piece0, piece1, piece2, piece3, left_ref, keep_ref,
+    weight_ref, out_ref, mixed_s, right_s,
+):
+    groups, sequences, pair = sizes
+    right_tiles = right_s.shape[1]
+    residues = keep_ref.shape[0]
     channels, _, depth = weight_ref.shape
     left = left_ref[...]
     per_step = 2 if depth == LANES else 1
@@ -232,10 +263,13 @@
                 ] = product[
                     residue * sequences : (residue + 1) * sequences, at * depth : (at + 1) * depth
                 ]
+    pieces = (piece0, piece1, piece2, piece3)
+    for stack, near, source in sources(place_ref[0], groups, piece0.shape[0]):
+        right_s[source] = pieces[stack][near]
     right = jnp.concatenate(
-        [flat_rows(right_ref[:, tile]) for tile in range(right_tiles)], axis=1
-    )
-    keep_all = flat_rows(rows_ref[:, keep_slot])
+        [flat_rows(right_s[:, tile]) for tile in range(right_tiles)], axis=1
+    )
+    keep_all = keep_all_ref[...]
     for first in range(0, residues, pair):
         members = range(first, first + pair)
         mixed = jnp.concatenate([mixed_s[residue] for residue in members], axis=1)
@@ -249,7 +283,6 @@
         result = matmul(right, mixed) / matmul_nt(keep_all, keep_rows)
         for at, residue in enumerate(members):
             out_ref[residue] = result[:, at * depth : (at + 1) * depth].astype(BF16)
-    del segment
 
 
 def column_kernel(
@@ -261,11 +294,10 @@
     total = sequences * residues
     heads = query_w_ref.shape[1] // PER_SPLIT_DIM
     query_factor = PER_SPLIT_DIM ** (-0.5)
-    own_group = place_ref[1]
+    own_group = place_ref[0] & (groups - 1)
     after = x_ref[...].astype(F32).reshape(total, width)
     for at in range(groups):
-        group = own_group + at
-        group = jnp.where(group >= groups, group - groups, group)
+        group = own_group ^ at
         mixed = mix_ref[:, pl.ds(group, 1)]
         mixed = mixed.astype(F32).reshape(total, mixed.shape[-1]).astype(BF16)
         after = after + matmul(mixed, row_out_ref[at])
@@ -317,7 +349,7 @@
     out_ref[...] = result.reshape(sequences, residues, width).astype(BF16)
 
 
-def call(kernel, outs, scratch=(), scalars=0, arguments=(), mib=32):
+def call(kernel, outs, arguments, scratch=(), scalars=0, mib=32, micros=2):
     vmem = pl.BlockSpec(memory_space=pltpu.VMEM)
     smem = pl.BlockSpec(memory_space=pltpu.SMEM)
     return pl.pallas_call(
@@ -327,6 +359,9 @@
         out_specs=jax.tree.map(lambda _: vmem, outs),
         scratch_shapes=list(scratch),
         compiler_params=pltpu.CompilerParams(vmem_limit_bytes=mib * 1024 * 1024),
+        cost_estimate=pl.CostEstimate(
+            flops=micros * 1_000_000_000, bytes_accessed=micros * 1_000_000, transcendentals=0
+        ),
     )(*arguments)
 
 
@@ -348,83 +383,102 @@
     parallel = lax.axis_size("dap")
     groups = lax.axis_size("grp")
     devices = parallel * groups
+    both = ("dap", "grp")
     sequences, residues, width = homolog_activity.shape
     residues_overall = residues * devices
     sequences_here = sequences // parallel
-    heads, bias_rows, bias_columns = pairwise_bias.shape
-    heads_here = heads // groups
-    head_lanes = heads_here * PER_SPLIT_DIM
     channels = first_operand_matrix.shape[1]
     depth = outer_output_weight.shape[1]
+    heads_here, row_tiles, column_tiles = tile_count(pairwise_bias.shape, groups)
+    head_lanes = heads_here * PER_SPLIT_DIM
     large = residues_overall > 256
-    place = jnp.stack([lax.axis_index("dap"), lax.axis_index("grp")]).astype(jnp.int32)
-
-    keep_slot = sequences_here * (width // LANES)
-    tiles = keep_slot + 1 + heads_here * (bias_rows // residues) * (bias_columns // LANES)
+    near_pieces = parallel // 4 * groups
+    place = (lax.axis_index("dap") * groups + lax.axis_index("grp")).astype(jnp.int32).reshape(1)
+    shape = jax.ShapeDtypeStruct
+
+    def exchange(value, mask):
+        return lax.ppermute(value, both, [(at, at ^ mask) for at in range(devices)])
+
+    def gather(pieces):
+        parts = [pieces[0]]
+        for near in range(1, near_pieces):
+            mask = near // groups * 4 * groups + near % groups
+            parts.append(exchange(pieces[near % groups], mask))
+        own = jnp.stack(parts)
+        across = exchange(own, 2 * groups)
+        return own, exchange(own, groups), across, exchange(across, groups)
+
+    bias_tiles = heads_here * row_tiles * column_tiles
+    *bias_pieces, keep = call(
+        functools.partial(share_kernel, groups),
+        tuple([shape((bias_tiles + 1, 8, LANES), BF16)] * groups + [shape((8, LANES), F32)]),
+        (place, alignment_mask.T, sequence_row_mask.reshape(1, sequences), pairwise_bias),
+        scalars=1,
+        micros=1,
+    )
+    bias_stacks = gather(bias_pieces)
+    row_out_weight = jnp.stack(
+        [horizontal_final_matrix]
+        + [exchange(horizontal_final_matrix, relative) for relative in range(1, groups)]
+    )
+
     right_tiles = channels * sequences // LANES
-    shape = jax.ShapeDtypeStruct
-    rows_out, right_out, left, keep = call(
+    rows_out, right_piece, left = call(
         functools.partial(prepare_kernel, (groups, sequences_here)),
         (
-            shape((devices, tiles, residues, LANES), BF16),
-            shape((devices, right_tiles, residues, LANES), BF16),
+            shape((devices, sequences_here * (width // LANES), residues, LANES), BF16),
+            shape((right_tiles, residues, LANES), BF16),
             shape((sequences * residues, channels), BF16),
-            shape((residues, LANES), F32),
         ),
-        arguments=(
-            homolog_activity,
-            alignment_mask.T,
-            sequence_row_mask.reshape(1, sequences),
-            pairwise_bias,
-            first_operand_matrix,
-            second_operand_matrix,
+        (homolog_activity, keep, first_operand_matrix.T, second_operand_matrix.T),
+        mib=56 if large else 32,
+    )
+    rows_in = lax.all_to_all(rows_out, both, split_axis=0, concat_axis=0, tiled=True)
+    right_stacks = gather([right_piece] * groups)
+
+    mix_out, keep_all = call(
+        functools.partial(row_kernel, (groups, sequences_here)),
+        (
+            shape((devices, sequences_here, residues, head_lanes), BF16),
+            shape((residues_overall, LANES), BF16),
         ),
-        mib=56 if large else 32,
-    )
-    both = ("dap", "grp")
-    final_parts = [horizontal_final_matrix]
-    for step in range(1, groups):
-        final_parts.append(
-            lax.ppermute(
-                horizontal_final_matrix,
-                "grp",
-                [(source, (source - step) % groups) for source in range(groups)],
-            )
-        )
-    row_out_weight = jnp.stack(final_parts)
-    rows_in = lax.all_to_all(rows_out, both, split_axis=0, concat_axis=0, tiled=True)
-    right_in = lax.all_to_all(right_out, both, split_axis=0, concat_axis=0, tiled=True)
-
-    mix_out = call(
-        functools.partial(row_kernel, (parallel, groups, sequences_here, heads_here)),
-        shape((devices, sequences_here, residues, head_lanes), BF16),
-        scratch=[pltpu.VMEM((sequences_here, residues_overall, head_lanes), BF16)] * 3
+        (place, rows_in, *bias_stacks, horizontal_projection_matrix.transpose(1, 0, 2)),
+        scratch=[
+            pltpu.VMEM(
+                (heads_here, groups * column_tiles, parallel * row_tiles, 8, LANES), BF16
+            ),
+            pltpu.VMEM((devices, 8, LANES), BF16),
+        ]
+        + [pltpu.VMEM((sequences_here, residues_overall, head_lanes), BF16)] * 3
         + [pltpu.VMEM((sequences_here, residues_overall, head_lanes), F32)],
         scalars=1,
-        arguments=(place, rows_in, horizontal_projection_matrix.transpose(1, 0, 2)),
-        mib=56 if large else 32,
+        mib=60 if large else 32,
     )
     mix_in = lax.all_to_all(mix_out, both, split_axis=0, concat_axis=0, tiled=True)
 
     pairwise_update = call(
-        functools.partial(outer_kernel, (keep_slot, sequences, 2)),
+        functools.partial(outer_kernel, (groups, sequences, 2)),
         shape((residues, residues_overall, depth), BF16),
-        scratch=[pltpu.VMEM((residues, channels * sequences, depth), BF16)],
-        arguments=(
-            rows_in,
-            right_in,
+        (
+            place,
+            keep_all,
+            *right_stacks,
             left,
             keep,
             outer_output_weight.reshape(channels, channels, depth).transpose(1, 0, 2),
         ),
+        scratch=[
+            pltpu.VMEM((residues, channels * sequences, depth), BF16),
+            pltpu.VMEM((devices, right_tiles, residues, LANES), BF16),
+        ],
+        scalars=1,
         mib=60 if large else 32,
     )
 
     alignment_output = call(
         functools.partial(column_kernel, groups),
         shape((sequences, residues, width), BF16),
-        scalars=1,
-        arguments=(
+        (
             place,
             homolog_activity,
             mix_in.reshape(parallel, groups, sequences_here, residues, head_lanes),
@@ -435,7 +489,9 @@
             vertical_content_sigmoid_matrix.transpose(1, 0, 2),
             vertical_final_matrix,
         ),
+        scalars=1,
         mib=56 if large else 32,
+        micros=3,
     )
     return (alignment_output, pairwise_update)
 

time: 70.4 us -> 78.8 us (1.12)
  starting transfers between devices: 9.07 us -> 43 us
  blocking collectives: 29.1 us -> 0 us
  waiting for transfers between devices: 15.8 us -> 22.8 us
  Pallas kernels: 10.9 us -> 9.04 us
  local copies, waits for them, and re-layouts: 4.08 us -> 2.68 us
    ppermute x1 -> x21, starting transfers between devices: 1.83 us -> 36.4 us  [exchange(): return lax.ppermute(value, both, [(at, at ^ mask) for at in range(devices)])]
    all_to_all x1 -> x0, blocking collectives: 29.1 us -> none  [shards(): lax.all_to_all(rows_out, both, split_axis=0, concat_axis=0, tiled=True)]
    ppermute x1 -> x21, waiting for transfers between devices: 2.07 us -> 16.5 us  [exchange(): return lax.ppermute(value, both, [(at, at ^ mask) for at in range(devices)])]
    all_to_all x1, waiting for transfers between devices: 12.3 us -> 0.01 us  [shards(): lax.all_to_all(rows_out, both, split_axis=0, concat_axis=0, tiled=True)]
    all_to_all x1, waiting for transfers between devices: 1.51 us -> 6.37 us  [shards(): lax.all_to_all(mix_out, both, split_axis=0, concat_axis=0, tiled=True)]
    pallas_call x4 -> x5, Pallas kernels: 10.9 us -> 9.04 us  [call(): pl.pallas_call(kernel, out_shape=outs, in_specs=[smem] * scalars + [vmem]...]
    unnamed x26 -> x42, local copies, waits for them, and re-layouts: 3.98 us -> 2.55 us
    all_to_all x1, starting transfers between devices: 3.62 us -> 2.73 us  [shards(): lax.all_to_all(mix_out, both, split_axis=0, concat_axis=0, tiled=True)]
  transfers between devices with their start and end apart: 3 -> 23, of which waited for: 3 -> 8; matrix products, arithmetic and copies ran while one was open for 0% -> 0% of each run, Pallas kernels for 7% -> 8%
where the time goes in v2:
time: 78.8 us; the launch traced here: 78.4 us
  starting transfers between devices  43 us (55%)
  waiting for transfers between devices  22.8 us (29%)
  Pallas kernels  9.04 us (11%)
  local copies, waits for them, and re-layouts  2.68 us (3%)
  between operations  0.86 us (1%)
    ppermute x21, starting transfers between devices, exchange(): return lax.ppermute(value, both, [(at, at ^ mask) for at in range(devices)])  36.4 us
    ppermute x21, waiting for transfers between devices, exchange(): return lax.ppermute(value, both, [(at, at ^ mask) for at in range(devices)])  16.5 us
    pallas_call x5, Pallas kernels, call(): pl.pallas_call(kernel, out_shape=outs, in_specs=[smem] * scalars + [vmem]...  9.04 us
    all_to_all x1, waiting for transfers between devices, shards(): lax.all_to_all(mix_out, both, split_axis=0, concat_axis=0, tiled=True)  6.37 us
    all_to_all x1, starting transfers between devices, shards(): lax.all_to_all(rows_out, both, split_axis=0, concat_axis=0, tiled=True)  3.83 us
    all_to_all x1, starting transfers between devices, shards(): lax.all_to_all(mix_out, both, split_axis=0, concat_axis=0, tiled=True)  2.73 us
    unnamed x42, local copies, waits for them, and re-layouts  2.55 us
  transfers between devices with their start and end apart: 23, of which 8 were waited for; matrix products, arithmetic and copies ran while one was open for 0% of the time, Pallas kernels for 8%

profile of v2, /device:TPU:0, one launch (start us, length us, event | category | flops | bytes accessed | tf_op | source)
XLA Modules:
  0.0 78.4 jit_solution(2672418953117861239)
XLA Ops:
  0.7 0.7 copy-done.7
  1.3 0.8 copy-done.4
  2.1 3.0 %collective-permute-start = (bf16[9,8,128]{2,1,0:T(8,128)(2,1)S(1)}, bf16[9,8,128]{2,1,0:T(8,128)(2,1)S(1)}, u32[]{:S(2)}, u32[]{:S(2)}) collective-permute-start(bf16[9,8,128]{2,1,0:T(8,128)(2,1)S(1)} %get-tuple-element.13), channel_id=1, source_target_pairs={{0,1},{1,0},{2,3},{3,2},{4,5},{5,4},{6,7},{7,6},{8,9},{9,8},{10,11... | collective-permute-start | bytes 55304 | tf_op jit(solution)/shard_map/ppermute | solution.py:400
  5.1 1.5 %collective-permute-start.2 = (bf16[9,8,128]{2,1,0:T(8,128)(2,1)S(1)}, bf16[9,8,128]{2,1,0:T(8,128)(2,1)S(1)}, u32[]{:S(2)}, u32[]{:S(2)}) collective-permute-start(bf16[9,8,128]{2,1,0:T(8,128)(2,1)S(1)} %get-tuple-element.13), channel_id=1, source_target_pairs={{0,9},{1,8},{2,11},{3,10},{4,13},{5,12},{6,15},{7,14},{8,1},{9,0},... | collective-permute-start | bytes 55304 | tf_op jit(solution)/shard_map/ppermute | solution.py:400
  6.7 0.1 collective-permute-start.1
  6.7 3.0 %collective-permute-start.3 = (bf16[9,8,128]{2,1,0:T(8,128)(2,1)S(1)}, bf16[9,8,128]{2,1,0:T(8,128)(2,1)S(1)}, u32[]{:S(2)}, u32[]{:S(2)}) collective-permute-start(bf16[9,8,128]{2,1,0:T(8,128)(2,1)S(1)} %get-tuple-element.12), channel_id=1, source_target_pairs={{0,16},{1,17},{2,18},{3,19},{4,20},{5,21},{6,22},{7,23},{8,24},{9,... | collective-permute-start | bytes 55304 | tf_op jit(solution)/shard_map/ppermute | solution.py:400
  9.7 2.0 %shard_map.141 = (bf16[32,4,8,128]{3,2,1,0:T(8,128)(2,1)}, bf16[8,8,128]{2,1,0:T(8,128)(2,1)S(1)}, bf16[256,32]{1,0:T(8,128)(2,1)S(1)}) custom-call(bf16[32,8,256]{2,1,0:T(8,128)(2,1)S(1)} %copy-done, f32[8,128]{1,0:T(8,128)S(1)} %get-tuple-element.10.keep_ref, bf16[32,256]{1,0:T(8,128)(2,1)S(1)} %bitcast.54, bf16[32,256]{1,0:T(8,128)(2,1)S(1)} %bitcast.55), custom_call_target="tpu_custom_call" | custom-call | flops 2000000000 | bytes 2000000 | tf_op jit(solution)/shard_map/pallas_call | solution.py:355
  11.7 3.8 %all-to-all-start = ((bf16[32,4,8,128]{3,2,1,0:T(8,128)(2,1)}), bf16[32,4,8,128]{3,2,1,0:T(8,128)(2,1)S(1)}, u32[]{:S(2)}, u32[]{:S(2)}) async-start(bf16[32,4,8,128]{3,2,1,0:T(8,128)(2,1)} %get-tuple-element.11), calls=%async_computation | async-start | bytes 524288 | tf_op jit(solution)/shard_map/all_to_all | solution.py:436
  15.5 1.8 %collective-permute-start.11 = (bf16[8,8,128]{2,1,0:T(8,128)(2,1)S(1)}, bf16[8,8,128]{2,1,0:T(8,128)(2,1)S(1)}, u32[]{:S(2)}, u32[]{:S(2)}) collective-permute-start(bf16[8,8,128]{2,1,0:T(8,128)(2,1)S(1)} %get-tuple-element.16), channel_id=1, source_target_pairs={{0,1},{1,0},{2,3},{3,2},{4,5},{5,4},{6,7},{7,6},{8,9},{9,8},{10,11... | collective-permute-start | bytes 49160 | tf_op jit(solution)/shard_map/ppermute | solution.py:400
  17.3 2.0 %collective-permute-done.11 = bf16[8,8,128]{2,1,0:T(8,128)(2,1)S(1)} collective-permute-done((bf16[8,8,128]{2,1,0:T(8,128)(2,1)S(1)}, bf16[8,8,128]{2,1,0:T(8,128)(2,1)S(1)}, u32[]{:S(2)}, u32[]{:S(2)}) %collective-permute-start.11) | collective-permute-done | bytes 16416 | tf_op jit(solution)/shard_map/ppermute | solution.py:400
  19.3 1.8 %collective-permute-start.12 = (bf16[8,8,128]{2,1,0:T(8,128)(2,1)S(1)}, bf16[8,8,128]{2,1,0:T(8,128)(2,1)S(1)}, u32[]{:S(2)}, u32[]{:S(2)}) collective-permute-start(bf16[8,8,128]{2,1,0:T(8,128)(2,1)S(1)} %get-tuple-element.16), channel_id=1, source_target_pairs={{0,8},{1,9},{2,10},{3,11},{4,12},{5,13},{6,14},{7,15},{8,0},{9,1},... | collective-permute-start | bytes 49160 | tf_op jit(solution)/shard_map/ppermute | solution.py:400
  21.1 2.2 %collective-permute-done.12 = bf16[8,8,128]{2,1,0:T(8,128)(2,1)S(1)} collective-permute-done((bf16[8,8,128]{2,1,0:T(8,128)(2,1)S(1)}, bf16[8,8,128]{2,1,0:T(8,128)(2,1)S(1)}, u32[]{:S(2)}, u32[]{:S(2)}) %collective-permute-start.12) | collective-permute-done | bytes 16416 | tf_op jit(solution)/shard_map/ppermute | solution.py:400
  23.3 2.5 %collective-permute-start.13 = (bf16[8,8,128]{2,1,0:T(8,128)(2,1)S(1)}, bf16[8,8,128]{2,1,0:T(8,128)(2,1)S(1)}, u32[]{:S(2)}, u32[]{:S(2)}) collective-permute-start(bf16[8,8,128]{2,1,0:T(8,128)(2,1)S(1)} %get-tuple-element.16), channel_id=1, source_target_pairs={{0,9},{1,8},{2,11},{3,10},{4,13},{5,12},{6,15},{7,14},{8,1},{9,0},... | collective-permute-start | bytes 49160 | tf_op jit(solution)/shard_map/ppermute | solution.py:400
  25.8 2.1 %collective-permute-done.13 = bf16[8,8,128]{2,1,0:T(8,128)(2,1)S(1)} collective-permute-done((bf16[8,8,128]{2,1,0:T(8,128)(2,1)S(1)}, bf16[8,8,128]{2,1,0:T(8,128)(2,1)S(1)}, u32[]{:S(2)}, u32[]{:S(2)}) %collective-permute-start.13) | collective-permute-done | bytes 16416 | tf_op jit(solution)/shard_map/ppermute | solution.py:400
  28.0 2.9 %collective-permute-start.14 = (bf16[8,8,128]{2,1,0:T(8,128)(2,1)S(1)}, bf16[8,8,128]{2,1,0:T(8,128)(2,1)S(1)}, u32[]{:S(2)}, u32[]{:S(2)}) collective-permute-start(bf16[8,8,128]{2,1,0:T(8,128)(2,1)S(1)} %get-tuple-element.16), channel_id=1, source_target_pairs={{0,16},{1,17},{2,18},{3,19},{4,20},{5,21},{6,22},{7,23},{8,24},{9,... | collective-permute-start | bytes 49160 | tf_op jit(solution)/shard_map/ppermute | solution.py:400
  30.9 1.7 %collective-permute-done.14 = bf16[8,8,128]{2,1,0:T(8,128)(2,1)S(1)} collective-permute-done((bf16[8,8,128]{2,1,0:T(8,128)(2,1)S(1)}, bf16[8,8,128]{2,1,0:T(8,128)(2,1)S(1)}, u32[]{:S(2)}, u32[]{:S(2)}) %collective-permute-start.14) | collective-permute-done | bytes 16416 | tf_op jit(solution)/shard_map/ppermute | solution.py:400
  32.6 3.7 %collective-permute-start.15 = (bf16[8,8,128]{2,1,0:T(8,128)(2,1)S(1)}, bf16[8,8,128]{2,1,0:T(8,128)(2,1)S(1)}, u32[]{:S(2)}, u32[]{:S(2)}) collective-permute-start(bf16[8,8,128]{2,1,0:T(8,128)(2,1)S(1)} %get-tuple-element.16), channel_id=1, source_target_pairs={{0,17},{1,16},{2,19},{3,18},{4,21},{5,20},{6,23},{7,22},{8,25},{9,... | collective-permute-start | bytes 49160 | tf_op jit(solution)/shard_map/ppermute | solution.py:400
  36.3 1.9 %collective-permute-done.15 = bf16[8,8,128]{2,1,0:T(8,128)(2,1)S(1)} collective-permute-done((bf16[8,8,128]{2,1,0:T(8,128)(2,1)S(1)}, bf16[8,8,128]{2,1,0:T(8,128)(2,1)S(1)}, u32[]{:S(2)}, u32[]{:S(2)}) %collective-permute-start.15) | collective-permute-done | bytes 16416 | tf_op jit(solution)/shard_map/ppermute | solution.py:400
  38.2 3.8 %collective-permute-start.4 = (bf16[9,8,128]{2,1,0:T(8,128)(2,1)S(1)}, bf16[9,8,128]{2,1,0:T(8,128)(2,1)S(1)}, u32[]{:S(2)}, u32[]{:S(2)}) collective-permute-start(bf16[9,8,128]{2,1,0:T(8,128)(2,1)S(1)} %get-tuple-element.13), channel_id=1, source_target_pairs={{0,17},{1,16},{2,19},{3,18},{4,21},{5,20},{6,23},{7,22},{8,25},{9,... | collective-permute-start | bytes 55304 | tf_op jit(solution)/shard_map/ppermute | solution.py:400
  42.0 1.1 %collective-permute-start.5 = (bf16[9,8,128]{2,1,0:T(8,128)(2,1)S(1)}, bf16[9,8,128]{2,1,0:T(8,128)(2,1)S(1)}, u32[]{:S(2)}, u32[]{:S(2)}) collective-permute-start(bf16[9,8,128]{2,1,0:T(8,128)(2,1)S(1)} %get-tuple-element.12), channel_id=1, source_target_pairs={{0,24},{1,25},{2,26},{3,27},{4,28},{5,29},{6,30},{7,31},{8,16},{9,... | collective-permute-start | bytes 55304 | tf_op jit(solution)/shard_map/ppermute | solution.py:400
  43.1 2.9 %collective-permute-start.6 = (bf16[9,8,128]{2,1,0:T(8,128)(2,1)S(1)}, bf16[9,8,128]{2,1,0:T(8,128)(2,1)S(1)}, u32[]{:S(2)}, u32[]{:S(2)}) collective-permute-start(bf16[9,8,128]{2,1,0:T(8,128)(2,1)S(1)} %get-tuple-element.13), channel_id=1, source_target_pairs={{0,25},{1,24},{2,27},{3,26},{4,29},{5,28},{6,31},{7,30},{8,17},{9,... | collective-permute-start | bytes 55304 | tf_op jit(solution)/shard_map/ppermute | solution.py:400
  46.0 0.0 collective-permute-done.2
  46.0 1.5 %collective-permute-start.16 = (bf16[8,8,128]{2,1,0:T(8,128)(2,1)S(1)}, bf16[8,8,128]{2,1,0:T(8,128)(2,1)S(1)}, u32[]{:S(2)}, u32[]{:S(2)}) collective-permute-start(bf16[8,8,128]{2,1,0:T(8,128)(2,1)S(1)} %get-tuple-element.16), channel_id=1, source_target_pairs={{0,24},{1,25},{2,26},{3,27},{4,28},{5,29},{6,30},{7,31},{8,16},{9,... | collective-permute-start | bytes 49160 | tf_op jit(solution)/shard_map/ppermute | solution.py:400
  47.5 0.0 collective-permute-done.3
  47.5 3.3 %collective-permute-start.17 = (bf16[8,8,128]{2,1,0:T(8,128)(2,1)S(1)}, bf16[8,8,128]{2,1,0:T(8,128)(2,1)S(1)}, u32[]{:S(2)}, u32[]{:S(2)}) collective-permute-start(bf16[8,8,128]{2,1,0:T(8,128)(2,1)S(1)} %get-tuple-element.16), channel_id=1, source_target_pairs={{0,25},{1,24},{2,27},{3,26},{4,29},{5,28},{6,31},{7,30},{8,17},{9,... | collective-permute-start | bytes 49160 | tf_op jit(solution)/shard_map/ppermute | solution.py:400
  50.8 0.0 collective-permute-done.4
  50.8 0.0 copy-start.12
  50.8 0.0 collective-permute-done.5
  50.9 0.0 collective-permute-done.6
  50.9 1.4 %collective-permute-start.8 = (bf16[8,9,8,128]{3,2,1,0:T(8,128)(2,1)S(1)}, bf16[8,9,8,128]{3,2,1,0:T(8,128)(2,1)S(1)}, u32[]{:S(2)}, u32[]{:S(2)}) collective-permute-start(bf16[8,9,8,128]{3,2,1,0:T(8,128)(2,1)S(1)} %constant_dynamic-update-slice_fusion.piece0), channel_id=1, source_target_pairs={{0,4},{1,5},{2,6},{3,7},{4,0},{5,1},{6,2},{7,3},{8,12},{9,13},{10,... | collective-permute-start | bytes 442376 | tf_op jit(solution)/shard_map/ppermute | solution.py:400
  52.3 0.0 collective-permute-done.16
  52.3 3.8 %collective-permute-done.8.piece2 = bf16[8,9,8,128]{3,2,1,0:T(8,128)(2,1)S(1)} collective-permute-done((bf16[8,9,8,128]{3,2,1,0:T(8,128)(2,1)S(1)}, bf16[8,9,8,128]{3,2,1,0:T(8,128)(2,1)S(1)}, u32[]{:S(2)}, u32[]{:S(2)}) %collective-permute-start.8) | collective-permute-done | bytes 147488 | tf_op jit(solution)/shard_map/ppermute | solution.py:400
  56.1 0.0 copy-start.10
  56.1 1.4 %collective-permute-start.19 = (bf16[8,8,8,128]{3,2,1,0:T(8,128)(2,1)S(1)}, bf16[8,8,8,128]{3,2,1,0:T(8,128)(2,1)S(1)}, u32[]{:S(2)}, u32[]{:S(2)}) collective-permute-start(bf16[8,8,8,128]{3,2,1,0:T(8,128)(2,1)S(1)} %constant_dynamic-update-slice_fusion.8.piece0), channel_id=1, source_target_pairs={{0,4},{1,5},{2,6},{3,7},{4,0},{5,1},{6,2},{7,3},{8,12},{9,13},{10,... | collective-permute-start | bytes 393224 | tf_op jit(solution)/shard_map/ppermute | solution.py:400
  57.5 0.6 collective-permute-start.10
  58.2 0.0 copy-start.11
  58.2 0.9 %copy-done.11 = bf16[1024,128]{1,0:T(8,128)(2,1)S(1)} copy-done((bf16[1024,128]{1,0:T(8,128)(2,1)S(1)}, bf16[1024,128]{1,0:T(8,128)(2,1)}, u32[]{:S(2)}) %copy-start.11) | copy-done | bytes 262168
  59.1 0.1 copy.23
  59.2 0.1 collective-permute-start.18
  59.3 2.8 %collective-permute-done.19.piece2 = bf16[8,8,8,128]{3,2,1,0:T(8,128)(2,1)S(1)} collective-permute-done((bf16[8,8,8,128]{3,2,1,0:T(8,128)(2,1)S(1)}, bf16[8,8,8,128]{3,2,1,0:T(8,128)(2,1)S(1)}, u32[]{:S(2)}, u32[]{:S(2)}) %collective-permute-start.19) | collective-permute-done | bytes 131104 | tf_op jit(solution)/shard_map/ppermute | solution.py:400
  62.1 2.1 %shard_map.142 = (bf16[32,2,8,128]{3,2,1,0:T(8,128)(2,1)}, bf16[256,128]{1,0:T(8,128)(2,1)S(1)}) custom-call(s32[1]{0:T(128)} %bitcast.place_ref, bf16[32,4,8,128]{3,2,1,0:T(8,128)(2,1)S(1)} %all-to-all-done.rows_ref, bf16[8,9,8,128]{3,2,1,0:T(8,128)(2,1)S(1)} %constant_dynamic-update-slice_fusion.piece0, ...), custom_call_target="tpu_custom_call" | custom-call | flops 2000000000 | bytes 2000000 | tf_op jit(solution)/shard_map/pallas_call | solution.py:355
  64.2 2.7 %all-to-all-start.1 = ((bf16[32,2,8,128]{3,2,1,0:T(8,128)(2,1)}), bf16[32,2,8,128]{3,2,1,0:T(8,128)(2,1)S(1)}, u32[]{:S(2)}, u32[]{:S(2)}) async-start(bf16[32,2,8,128]{3,2,1,0:T(8,128)(2,1)} %get-tuple-element.14), calls=%async_computation.1 | async-start | bytes 262144 | tf_op jit(solution)/shard_map/all_to_all | solution.py:457
  67.0 0.0 copy-start.1
  67.0 0.0 copy-start.2
  67.0 0.0 copy-start.3
  67.0 2.2 %shard_map.144 = bf16[8,256,128]{2,1,0:T(8,128)(2,1)} custom-call(s32[1]{0:T(128)} %bitcast.place_ref, bf16[256,128]{1,0:T(8,128)(2,1)S(1)} %get-tuple-element.15.keep_all_ref, bf16[8,8,8,128]{3,2,1,0:T(8,128)(2,1)S(1)} %constant_dynamic-update-slice_fusion.8.piece0, bf16[8,8,8,128]{3,2,1,0:T(8,128)(2,1)S(1)} %collective-permute-done.18.piece1, ...), custom_call_target="tpu_custom_call" | custom-call | flops 2000000000 | bytes 2000000 | tf_op jit(solution)/shard_map/pallas_call | solution.py:355
  69.2 6.4 %all-to-all-done.1 = bf16[32,2,8,128]{3,2,1,0:T(8,128)(2,1)S(1)} async-done(((bf16[32,2,8,128]{3,2,1,0:T(8,128)(2,1)}), bf16[32,2,8,128]{3,2,1,0:T(8,128)(2,1)S(1)}, u32[]{:S(2)}, u32[]{:S(2)}) %all-to-all-start.1) | async-done | bytes 131104 | tf_op jit(solution)/shard_map/all_to_all | solution.py:457
  75.6 2.8 %shard_map.143 = bf16[32,8,256]{2,1,0:T(8,128)(2,1)} custom-call(s32[1]{0:T(128)} %bitcast.place_ref, bf16[32,8,256]{2,1,0:T(8,128)(2,1)S(1)} %copy-done, bf16[16,2,2,8,128]{4,3,2,1,0:T(8,128)(2,1)S(1)} %bitcast.53, f32[8,128]{1,0:T(8,128)S(1)} %get-tuple-element.10.keep_ref, bf16[2,128,256]{2,1,0:T(8,128)(2,1)S(1)} %pad_maximum_fusion.row_out_ref, ...), custom_call_target="tpu_custom_call" | custom-call | flops 3000000000 | bytes 3000000 | tf_op jit(solution)/shard_map/pallas_call | solution.py:355
  (49 shorter events, 0.3 us)
Async XLA Ops:
  0.6 0.7 copy-start.7
  0.6 0.7 copy-start.8
  1.3 0.8 copy-start.4
  2.1 7.6 %copy-start = (bf16[32,8,256]{2,1,0:T(8,128)(2,1)S(1)}, bf16[32,8,256]{2,1,0:T(8,128)(2,1)}, u32[]{:S(2)}) copy-start(bf16[32,8,256]{2,1,0:T(8,128)(2,1)} %x_ref.3) | copy-start | bytes 393220
  2.1 7.6 %copy-start.5 = (bf16[256,32]{0,1:T(8,128)(2,1)S(1)}, bf16[256,32]{0,1:T(8,128)(2,1)}, u32[]{:S(2)}) copy-start(bf16[256,32]{0,1:T(8,128)(2,1)} %param.23) | copy-start | bytes 49156
  2.1 7.6 %copy-start.6 = (bf16[256,32]{0,1:T(8,128)(2,1)S(1)}, bf16[256,32]{0,1:T(8,128)(2,1)}, u32[]{:S(2)}) copy-start(bf16[256,32]{0,1:T(8,128)(2,1)} %param.24) | copy-start | bytes 49156
  2.1 39.9 %collective-permute-start = (bf16[9,8,128]{2,1,0:T(8,128)(2,1)S(1)}, bf16[9,8,128]{2,1,0:T(8,128)(2,1)S(1)}, u32[]{:S(2)}, u32[]{:S(2)}) collective-permute-start(bf16[9,8,128]{2,1,0:T(8,128)(2,1)S(1)} %get-tuple-element.13), channel_id=1, source_target_pairs={{0,1},{1,0},{2,3},{3,2},{4,5},{5,4},{6,7},{7,6},{8,9},{9,8},{10,11... | collective-permute-start | bytes 55304 | tf_op jit(solution)/shard_map/ppermute | solution.py:400
  5.1 40.8 %collective-permute-start.2 = (bf16[9,8,128]{2,1,0:T(8,128)(2,1)S(1)}, bf16[9,8,128]{2,1,0:T(8,128)(2,1)S(1)}, u32[]{:S(2)}, u32[]{:S(2)}) collective-permute-start(bf16[9,8,128]{2,1,0:T(8,128)(2,1)S(1)} %get-tuple-element.13), channel_id=1, source_target_pairs={{0,9},{1,8},{2,11},{3,10},{4,13},{5,12},{6,15},{7,14},{8,1},{9,0},... | collective-permute-start | bytes 55304 | tf_op jit(solution)/shard_map/ppermute | solution.py:400
  6.7 36.4 %collective-permute-start.1 = (bf16[9,8,128]{2,1,0:T(8,128)(2,1)S(1)}, bf16[9,8,128]{2,1,0:T(8,128)(2,1)S(1)}, u32[]{:S(2)}, u32[]{:S(2)}) collective-permute-start(bf16[9,8,128]{2,1,0:T(8,128)(2,1)S(1)} %get-tuple-element.12), channel_id=1, source_target_pairs={{0,8},{1,9},{2,10},{3,11},{4,12},{5,13},{6,14},{7,15},{8,0},{9,1},... | collective-permute-start | bytes 55304 | tf_op jit(solution)/shard_map/ppermute | solution.py:400
  6.7 40.7 %collective-permute-start.3 = (bf16[9,8,128]{2,1,0:T(8,128)(2,1)S(1)}, bf16[9,8,128]{2,1,0:T(8,128)(2,1)S(1)}, u32[]{:S(2)}, u32[]{:S(2)}) collective-permute-start(bf16[9,8,128]{2,1,0:T(8,128)(2,1)S(1)} %get-tuple-element.12), channel_id=1, source_target_pairs={{0,16},{1,17},{2,18},{3,19},{4,20},{5,21},{6,22},{7,23},{8,24},{9,... | collective-permute-start | bytes 55304 | tf_op jit(solution)/shard_map/ppermute | solution.py:400
  11.7 50.4 %all-to-all-start = ((bf16[32,4,8,128]{3,2,1,0:T(8,128)(2,1)}), bf16[32,4,8,128]{3,2,1,0:T(8,128)(2,1)S(1)}, u32[]{:S(2)}, u32[]{:S(2)}) async-start(bf16[32,4,8,128]{3,2,1,0:T(8,128)(2,1)} %get-tuple-element.11), calls=%async_computation | async-start | bytes 524288 | tf_op jit(solution)/shard_map/all_to_all | solution.py:436
  15.5 3.8 %collective-permute-start.11 = (bf16[8,8,128]{2,1,0:T(8,128)(2,1)S(1)}, bf16[8,8,128]{2,1,0:T(8,128)(2,1)S(1)}, u32[]{:S(2)}, u32[]{:S(2)}) collective-permute-start(bf16[8,8,128]{2,1,0:T(8,128)(2,1)S(1)} %get-tuple-element.16), channel_id=1, source_target_pairs={{0,1},{1,0},{2,3},{3,2},{4,5},{5,4},{6,7},{7,6},{8,9},{9,8},{10,11... | collective-permute-start | bytes 49160 | tf_op jit(solution)/shard_map/ppermute | solution.py:400
  17.3 40.8 %copy-start.9 = (bf16[256,4,128]{2,1,0:T(4,128)(2,1)S(1)}, bf16[256,4,128]{2,1,0:T(4,128)(2,1)}, u32[]{:S(2)}) copy-start(bf16[256,4,128]{2,1,0:T(4,128)(2,1)} %param.17) | copy-start | bytes 786436
  19.3 4.0 %collective-permute-start.12 = (bf16[8,8,128]{2,1,0:T(8,128)(2,1)S(1)}, bf16[8,8,128]{2,1,0:T(8,128)(2,1)S(1)}, u32[]{:S(2)}, u32[]{:S(2)}) collective-permute-start(bf16[8,8,128]{2,1,0:T(8,128)(2,1)S(1)} %get-tuple-element.16), channel_id=1, source_target_pairs={{0,8},{1,9},{2,10},{3,11},{4,12},{5,13},{6,14},{7,15},{8,0},{9,1},... | collective-permute-start | bytes 49160 | tf_op jit(solution)/shard_map/ppermute | solution.py:400
  23.3 4.6 %collective-permute-start.13 = (bf16[8,8,128]{2,1,0:T(8,128)(2,1)S(1)}, bf16[8,8,128]{2,1,0:T(8,128)(2,1)S(1)}, u32[]{:S(2)}, u32[]{:S(2)}) collective-permute-start(bf16[8,8,128]{2,1,0:T(8,128)(2,1)S(1)} %get-tuple-element.16), channel_id=1, source_target_pairs={{0,9},{1,8},{2,11},{3,10},{4,13},{5,12},{6,15},{7,14},{8,1},{9,0},... | collective-permute-start | bytes 49160 | tf_op jit(solution)/shard_map/ppermute | solution.py:400
  28.0 4.7 %collective-permute-start.14 = (bf16[8,8,128]{2,1,0:T(8,128)(2,1)S(1)}, bf16[8,8,128]{2,1,0:T(8,128)(2,1)S(1)}, u32[]{:S(2)}, u32[]{:S(2)}) collective-permute-start(bf16[8,8,128]{2,1,0:T(8,128)(2,1)S(1)} %get-tuple-element.16), channel_id=1, source_target_pairs={{0,16},{1,17},{2,18},{3,19},{4,20},{5,21},{6,22},{7,23},{8,24},{9,... | collective-permute-start | bytes 49160 | tf_op jit(solution)/shard_map/ppermute | solution.py:400
  32.6 5.5 %collective-permute-start.15 = (bf16[8,8,128]{2,1,0:T(8,128)(2,1)S(1)}, bf16[8,8,128]{2,1,0:T(8,128)(2,1)S(1)}, u32[]{:S(2)}, u32[]{:S(2)}) collective-permute-start(bf16[8,8,128]{2,1,0:T(8,128)(2,1)S(1)} %get-tuple-element.16), channel_id=1, source_target_pairs={{0,17},{1,16},{2,19},{3,18},{4,21},{5,20},{6,23},{7,22},{8,25},{9,... | collective-permute-start | bytes 49160 | tf_op jit(solution)/shard_map/ppermute | solution.py:400
  38.2 12.6 %collective-permute-start.4 = (bf16[9,8,128]{2,1,0:T(8,128)(2,1)S(1)}, bf16[9,8,128]{2,1,0:T(8,128)(2,1)S(1)}, u32[]{:S(2)}, u32[]{:S(2)}) collective-permute-start(bf16[9,8,128]{2,1,0:T(8,128)(2,1)S(1)} %get-tuple-element.13), channel_id=1, source_target_pairs={{0,17},{1,16},{2,19},{3,18},{4,21},{5,20},{6,23},{7,22},{8,25},{9,... | collective-permute-start | bytes 55304 | tf_op jit(solution)/shard_map/ppermute | solution.py:400
  42.0 8.8 %collective-permute-start.5 = (bf16[9,8,128]{2,1,0:T(8,128)(2,1)S(1)}, bf16[9,8,128]{2,1,0:T(8,128)(2,1)S(1)}, u32[]{:S(2)}, u32[]{:S(2)}) collective-permute-start(bf16[9,8,128]{2,1,0:T(8,128)(2,1)S(1)} %get-tuple-element.12), channel_id=1, source_target_pairs={{0,24},{1,25},{2,26},{3,27},{4,28},{5,29},{6,30},{7,31},{8,16},{9,... | collective-permute-start | bytes 55304 | tf_op jit(solution)/shard_map/ppermute | solution.py:400
  43.1 7.8 %collective-permute-start.6 = (bf16[9,8,128]{2,1,0:T(8,128)(2,1)S(1)}, bf16[9,8,128]{2,1,0:T(8,128)(2,1)S(1)}, u32[]{:S(2)}, u32[]{:S(2)}) collective-permute-start(bf16[9,8,128]{2,1,0:T(8,128)(2,1)S(1)} %get-tuple-element.13), channel_id=1, source_target_pairs={{0,25},{1,24},{2,27},{3,26},{4,29},{5,28},{6,31},{7,30},{8,17},{9,... | collective-permute-start | bytes 55304 | tf_op jit(solution)/shard_map/ppermute | solution.py:400
  46.0 6.3 %collective-permute-start.16 = (bf16[8,8,128]{2,1,0:T(8,128)(2,1)S(1)}, bf16[8,8,128]{2,1,0:T(8,128)(2,1)S(1)}, u32[]{:S(2)}, u32[]{:S(2)}) collective-permute-start(bf16[8,8,128]{2,1,0:T(8,128)(2,1)S(1)} %get-tuple-element.16), channel_id=1, source_target_pairs={{0,24},{1,25},{2,26},{3,27},{4,28},{5,29},{6,30},{7,31},{8,16},{9,... | collective-permute-start | bytes 49160 | tf_op jit(solution)/shard_map/ppermute | solution.py:400
  47.5 8.6 %collective-permute-start.17 = (bf16[8,8,128]{2,1,0:T(8,128)(2,1)S(1)}, bf16[8,8,128]{2,1,0:T(8,128)(2,1)S(1)}, u32[]{:S(2)}, u32[]{:S(2)}) collective-permute-start(bf16[8,8,128]{2,1,0:T(8,128)(2,1)S(1)} %get-tuple-element.16), channel_id=1, source_target_pairs={{0,25},{1,24},{2,27},{3,26},{4,29},{5,28},{6,31},{7,30},{8,17},{9,... | collective-permute-start | bytes 49160 | tf_op jit(solution)/shard_map/ppermute | solution.py:400
  50.8 6.7 %copy-start.12 = (bf16[128,256]{1,0:T(8,128)(2,1)S(1)}, bf16[128,256]{1,0:T(8,128)(2,1)}, u32[]{:S(2)}) copy-start(bf16[128,256]{1,0:T(8,128)(2,1)} %param.18) | copy-start | bytes 196612
  50.9 5.2 %collective-permute-start.8 = (bf16[8,9,8,128]{3,2,1,0:T(8,128)(2,1)S(1)}, bf16[8,9,8,128]{3,2,1,0:T(8,128)(2,1)S(1)}, u32[]{:S(2)}, u32[]{:S(2)}) collective-permute-start(bf16[8,9,8,128]{3,2,1,0:T(8,128)(2,1)S(1)} %constant_dynamic-update-slice_fusion.piece0), channel_id=1, source_target_pairs={{0,4},{1,5},{2,6},{3,7},{4,0},{5,1},{6,2},{7,3},{8,12},{9,13},{10,... | collective-permute-start | bytes 442376 | tf_op jit(solution)/shard_map/ppermute | solution.py:400
  52.3 9.8 %collective-permute-start.7 = (bf16[8,9,8,128]{3,2,1,0:T(8,128)(2,1)S(1)}, bf16[8,9,8,128]{3,2,1,0:T(8,128)(2,1)S(1)}, u32[]{:S(2)}, u32[]{:S(2)}) collective-permute-start(bf16[8,9,8,128]{3,2,1,0:T(8,128)(2,1)S(1)} %constant_dynamic-update-slice_fusion.piece0), channel_id=1, source_target_pairs={{0,2},{1,3},{2,0},{3,1},{4,6},{5,7},{6,4},{7,5},{8,10},{9,11},{10,... | collective-permute-start | bytes 442376 | tf_op jit(solution)/shard_map/ppermute | solution.py:400
  56.1 6.0 %collective-permute-start.9 = (bf16[8,9,8,128]{3,2,1,0:T(8,128)(2,1)S(1)}, bf16[8,9,8,128]{3,2,1,0:T(8,128)(2,1)S(1)}, u32[]{:S(2)}, u32[]{:S(2)}) collective-permute-start(bf16[8,9,8,128]{3,2,1,0:T(8,128)(2,1)S(1)} %collective-permute-done.8.piece2), channel_id=1, source_target_pairs={{0,2},{1,3},{2,0},{3,1},{4,6},{5,7},{6,4},{7,5},{8,10},{9,11},{10,... | collective-permute-start | bytes 442376 | tf_op jit(solution)/shard_map/ppermute | solution.py:400
  56.1 2.1 %copy-start.10 = (bf16[256,2,256]{2,1,0:T(2,128)(2,1)S(1)}, bf16[256,2,256]{2,1,0:T(2,128)(2,1)}, u32[]{:S(2)}) copy-start(bf16[256,2,256]{2,1,0:T(2,128)(2,1)} %param.21) | copy-start | bytes 786436
  56.1 6.0 %collective-permute-start.19 = (bf16[8,8,8,128]{3,2,1,0:T(8,128)(2,1)S(1)}, bf16[8,8,8,128]{3,2,1,0:T(8,128)(2,1)S(1)}, u32[]{:S(2)}, u32[]{:S(2)}) collective-permute-start(bf16[8,8,8,128]{3,2,1,0:T(8,128)(2,1)S(1)} %constant_dynamic-update-slice_fusion.8.piece0), channel_id=1, source_target_pairs={{0,4},{1,5},{2,6},{3,7},{4,0},{5,1},{6,2},{7,3},{8,12},{9,13},{10,... | collective-permute-start | bytes 393224 | tf_op jit(solution)/shard_map/ppermute | solution.py:400
  57.5 9.4 %collective-permute-start.10 = (bf16[128,256]{1,0:T(8,128)(2,1)S(1)}, bf16[128,256]{1,0:T(8,128)(2,1)S(1)}, u32[]{:S(2)}, u32[]{:S(2)}) collective-permute-start(bf16[128,256]{1,0:T(8,128)(2,1)S(1)} %copy-done.12), channel_id=1, source_target_pairs={{0,1},{1,0},{2,3},{3,2},{4,5},{5,4},{6,7},{7,6},{8,9},{9,8},{10,11... | collective-permute-start | bytes 196616 | tf_op jit(solution)/shard_map/ppermute | solution.py:400
  58.2 1.0 %copy-start.11 = (bf16[1024,128]{1,0:T(8,128)(2,1)S(1)}, bf16[1024,128]{1,0:T(8,128)(2,1)}, u32[]{:S(2)}) copy-start(bf16[1024,128]{1,0:T(8,128)(2,1)} %param.25) | copy-start | bytes 786436
  59.2 7.7 %collective-permute-start.18 = (bf16[8,8,8,128]{3,2,1,0:T(8,128)(2,1)S(1)}, bf16[8,8,8,128]{3,2,1,0:T(8,128)(2,1)S(1)}, u32[]{:S(2)}, u32[]{:S(2)}) collective-permute-start(bf16[8,8,8,128]{3,2,1,0:T(8,128)(2,1)S(1)} %constant_dynamic-update-slice_fusion.8.piece0), channel_id=1, source_target_pairs={{0,2},{1,3},{2,0},{3,1},{4,6},{5,7},{6,4},{7,5},{8,10},{9,11},{10,... | collective-permute-start | bytes 393224 | tf_op jit(solution)/shard_map/ppermute | solution.py:400
  62.1 4.9 %collective-permute-start.20 = (bf16[8,8,8,128]{3,2,1,0:T(8,128)(2,1)S(1)}, bf16[8,8,8,128]{3,2,1,0:T(8,128)(2,1)S(1)}, u32[]{:S(2)}, u32[]{:S(2)}) collective-permute-start(bf16[8,8,8,128]{3,2,1,0:T(8,128)(2,1)S(1)} %collective-permute-done.19.piece2), channel_id=1, source_target_pairs={{0,2},{1,3},{2,0},{3,1},{4,6},{5,7},{6,4},{7,5},{8,10},{9,11},{10,... | collective-permute-start | bytes 393224 | tf_op jit(solution)/shard_map/ppermute | solution.py:400
  64.2 11.4 %all-to-all-start.1 = ((bf16[32,2,8,128]{3,2,1,0:T(8,128)(2,1)}), bf16[32,2,8,128]{3,2,1,0:T(8,128)(2,1)S(1)}, u32[]{:S(2)}, u32[]{:S(2)}) async-start(bf16[32,2,8,128]{3,2,1,0:T(8,128)(2,1)} %get-tuple-element.14), calls=%async_computation.1 | async-start | bytes 262144 | tf_op jit(solution)/shard_map/all_to_all | solution.py:457
  67.0 8.6 %copy-start.1 = (bf16[256,256]{1,0:T(8,128)(2,1)S(1)}, bf16[256,256]{1,0:T(8,128)(2,1)}, u32[]{:S(2)}) copy-start(bf16[256,256]{1,0:T(8,128)(2,1)} %query_w_ref.1) | copy-start | bytes 393220
  67.0 8.6 %copy-start.2 = (bf16[256,256]{1,0:T(8,128)(2,1)S(1)}, bf16[256,256]{1,0:T(8,128)(2,1)}, u32[]{:S(2)}) copy-start(bf16[256,256]{1,0:T(8,128)(2,1)} %key_w_ref.1) | copy-start | bytes 393220
  67.0 8.6 %copy-start.3 = (bf16[256,256]{1,0:T(8,128)(2,1)S(1)}, bf16[256,256]{1,0:T(8,128)(2,1)}, u32[]{:S(2)}) copy-start(bf16[256,256]{1,0:T(8,128)(2,1)} %out_w_ref.1) | copy-start | bytes 393220

commit v3 on v2

--- a/solution.py
+++ b/solution.py
@@ -68,28 +68,28 @@
     return heads // groups, bias_rows // 8, bias_columns // LANES
 
 
-def share_kernel(groups, place_ref, mask_ref, present_ref, bias_ref, *out_refs):
-    *piece_refs, keep_ref = out_refs
+def share_kernel(groups, mask_ref, present_ref, bias_ref, out_ref, keep_ref):
     heads_here, row_tiles, column_tiles = tile_count(bias_ref.shape, groups)
+    half_heads = heads_here // 2
     sequences = mask_ref.shape[1]
     keep = (mask_ref[...] * present_ref[...]).astype(F32)
     if sequences < LANES:
         keep = jnp.pad(keep, ((0, 0), (0, LANES - sequences)))
     keep_ref[...] = keep
-    own_group = place_ref[0] & (groups - 1)
-    for relative, piece_ref in enumerate(piece_refs):
-        group = own_group ^ relative
+    keep_tile = keep.astype(BF16)
+    for target in range(out_ref.shape[0]):
+        part, group = divmod(target, groups)
         slot = 0
-        for head in range(heads_here):
+        for head in range(half_heads):
             for row in range(row_tiles):
                 for column in range(column_tiles):
-                    piece_ref[slot] = bias_ref[
-                        group * heads_here + head,
+                    out_ref[target, slot] = bias_ref[
+                        group * heads_here + part % 2 * half_heads + head,
                         row * 8 : (row + 1) * 8,
                         column * LANES : (column + 1) * LANES,
                     ]
                     slot += 1
-        piece_ref[slot] = keep.astype(BF16)
+        out_ref[target, slot] = keep_tile
 
 
 def prepare_kernel(
@@ -140,35 +140,27 @@
             == tile * per_tile + quotient(lanes_of((channels, LANES)), sequences)
         )
         expanded = jnp.where(same_sequence, matmul(right, select), 0.0).astype(BF16)
-        right_ref[tile] = (matmul(residue_pick, expanded) * keep_spread).astype(BF16)
-
-
-def sources(place, groups, pieces):
-    for across in range(2):
-        for core in range(2):
-            for near in range(pieces):
-                mask = near // groups * 4 * groups + near % groups
-                yield across * 2 + core, near, place ^ (
-                    mask + across * 2 * groups + core * groups
-                )
+        result = (matmul(residue_pick, expanded) * keep_spread).astype(BF16)
+        core, slot = divmod(tile, right_ref.shape[1])
+        for target in range(right_ref.shape[0]):
+            if target // groups % 2 == core:
+                right_ref[target, slot] = result
 
 
 def row_kernel(
-    sizes, place_ref, rows_ref, piece0, piece1, piece2, piece3, weight_ref,
-    mix_ref, keep_all_ref, bias_s, keep_s, query_s, key_s, value_s, gate_s,
+    sizes, place_ref, own_bias_ref, other_bias_ref, rows_ref, weight_ref,
+    mix_ref, keep_all_ref, query_s, key_s, value_s, gate_s,
 ):
-    groups, sequences_here = sizes
+    groups, sequences_here, row_tiles, column_tiles = sizes
     blocks, tiles, residues, _ = rows_ref.shape
     residues_overall = blocks * residues
     halves = weight_ref.shape[1] // LANES
-    heads_here, all_columns, all_rows = bias_s.shape[:3]
-    row_tiles = all_rows // (blocks // groups)
-    column_tiles = all_columns // groups
-    head_lanes = heads_here * PER_SPLIT_DIM
+    head_lanes = weight_ref.shape[2]
+    half_heads = head_lanes // PER_SPLIT_DIM // 2
     query_factor = PER_SPLIT_DIM ** (-0.5)
     block_rows = min(residues_overall, 256)
-    place = place_ref[0]
-    pieces = (piece0, piece1, piece2, piece3)
+    part = quotient(place_ref[0], groups)
+    core = part & 1
 
     for own in range(sequences_here):
         normed = jnp.concatenate(
@@ -179,48 +171,39 @@
         value_s[own] = matmul(normed, weight_ref[2]).astype(BF16)
         gate_s[own] = jax.nn.sigmoid(matmul(normed, weight_ref[3]))
 
-    for stack, near, source in sources(place, groups, piece0.shape[0]):
-        group = source & (groups - 1)
-        part = quotient(source, groups)
-        slot = 0
-        for head in range(heads_here):
-            for row in range(row_tiles):
-                for column in range(column_tiles):
-                    bias_s[head, group * column_tiles + column, part * row_tiles + row] = pieces[
-                        stack
-                    ][near, slot]
-                    slot += 1
-        keep_s[source] = pieces[stack][near, slot]
-
-    keep_all = flat_rows(keep_s[...])
+    keep_all = flat_rows(own_bias_ref[:, half_heads * row_tiles * column_tiles])
     keep_all_ref[...] = keep_all
-    chosen = one_hot(
-        lanes_of((8, LANES)) == quotient(place, groups) * sequences_here + rows_of((8, LANES))
-    )
+    chosen = one_hot(lanes_of((8, LANES)) == part * sequences_here + rows_of((8, LANES)))
     key_keep = matmul_nt(chosen, keep_all)
 
     def attend(block):
         start = block * block_rows
-        count = block_rows // 8
+        parts = block_rows // (row_tiles * 8)
         head_of = quotient(lanes_of((residues_overall, head_lanes)), PER_SPLIT_DIM)
         query_head = quotient(lanes_of((block_rows, head_lanes)), PER_SPLIT_DIM)
         biases = []
-        for head in range(heads_here):
-            columns = [
-                bias_s[head, column, pl.ds(block * count, count)]
-                .astype(F32)
-                .reshape(block_rows, LANES)
-                for column in range(all_columns)
-            ]
-            biases.append(jnp.concatenate(columns, axis=1))
+        for bias_ref in (own_bias_ref, other_bias_ref):
+            for head in range(half_heads):
+                columns = []
+                for group in range(groups):
+                    for column in range(column_tiles):
+                        pieces = []
+                        for at in range(parts):
+                            for row in range(row_tiles):
+                                slot = (head * row_tiles + row) * column_tiles + column
+                                source = (block * parts + at) * groups + group
+                                pieces.append(bias_ref[source, slot].astype(F32))
+                        columns.append(jnp.concatenate(pieces, axis=0))
+                biases.append(jnp.concatenate(columns, axis=1))
         for own in range(sequences_here):
             queries = query_s[own, pl.ds(start, block_rows), :]
             keys, values = key_s[own], value_s[own]
             keep_row = key_keep[own : own + 1, :] > 0.5
             total = jnp.zeros((block_rows, 2 * head_lanes), F32)
-            for head in range(heads_here):
+            for at in range(2 * half_heads):
+                head = (core ^ (at // half_heads)) * half_heads + at % half_heads
                 query_part = jnp.where(query_head == head, queries, jnp.zeros_like(queries))
-                scores = matmul_nt(query_part, keys) + biases[head]
+                scores = matmul_nt(query_part, keys) + biases[at]
                 scores = jnp.where(keep_row, scores, MASKED)
                 scores = scores - jnp.max(scores, axis=1, keepdims=True)
                 weights = jnp.exp(scores).astype(BF16)
@@ -242,32 +225,32 @@
 
 
 def outer_kernel(
-    sizes, place_ref, keep_all_ref, piece0, piece1, piece2, piece3, left_ref, keep_ref,
-    weight_ref, out_ref, mixed_s, right_s,
+    sizes, place_ref, keep_all_ref, own_right_ref, other_right_ref, left_ref, keep_ref,
+    weight_ref, out_ref, mixed_s,
 ):
     groups, sequences, pair = sizes
-    right_tiles = right_s.shape[1]
     residues = keep_ref.shape[0]
     channels, _, depth = weight_ref.shape
+    core = quotient(place_ref[0], groups) & 1
     left = left_ref[...]
-    per_step = 2 if depth == LANES else 1
-    for channel in range(0, channels, per_step):
-        weights = jnp.concatenate(
-            [weight_ref[channel + at] for at in range(per_step)], axis=1
-        )
+    half_channels = channels // 2
+    for at in range(0, channels, 2):
+        channel = (core ^ (at // half_channels)) * half_channels + at % half_channels
+        weights = jnp.concatenate([weight_ref[channel], weight_ref[channel + 1]], axis=1)
         product = matmul(left, weights).astype(BF16)
         for residue in range(residues):
-            for at in range(per_step):
-                mixed_s[
-                    residue, (channel + at) * sequences : (channel + at + 1) * sequences, :
-                ] = product[
-                    residue * sequences : (residue + 1) * sequences, at * depth : (at + 1) * depth
+            for step in range(2):
+                mixed_s[residue, (at + step) * sequences : (at + step + 1) * sequences, :] = product[
+                    residue * sequences : (residue + 1) * sequences,
+                    step * depth : (step + 1) * depth,
                 ]
-    pieces = (piece0, piece1, piece2, piece3)
-    for stack, near, source in sources(place_ref[0], groups, piece0.shape[0]):
-        right_s[source] = pieces[stack][near]
     right = jnp.concatenate(
-        [flat_rows(right_s[:, tile]) for tile in range(right_tiles)], axis=1
+        [
+            flat_rows(right_ref[:, tile])
+            for right_ref in (own_right_ref, other_right_ref)
+            for tile in range(right_ref.shape[1])
+        ],
+        axis=1,
     )
     keep_all = keep_all_ref[...]
     for first in range(0, residues, pair):
@@ -349,13 +332,14 @@
     out_ref[...] = result.reshape(sequences, residues, width).astype(BF16)
 
 
-def call(kernel, outs, arguments, scratch=(), scalars=0, mib=32, micros=2):
+def call(kernel, outs, arguments, scratch=(), scalars=0, mib=32, micros=2, loose=False):
     vmem = pl.BlockSpec(memory_space=pltpu.VMEM)
+    read = pl.BlockSpec() if loose else vmem
     smem = pl.BlockSpec(memory_space=pltpu.SMEM)
     return pl.pallas_call(
         kernel,
         out_shape=outs,
-        in_specs=[smem] * scalars + [vmem] * (len(arguments) - scalars),
+        in_specs=[smem] * scalars + [read] * (len(arguments) - scalars),
         out_specs=jax.tree.map(lambda _: vmem, outs),
         scratch_shapes=list(scratch),
         compiler_params=pltpu.CompilerParams(vmem_limit_bytes=mib * 1024 * 1024),
@@ -392,69 +376,64 @@
     heads_here, row_tiles, column_tiles = tile_count(pairwise_bias.shape, groups)
     head_lanes = heads_here * PER_SPLIT_DIM
     large = residues_overall > 256
-    near_pieces = parallel // 4 * groups
     place = (lax.axis_index("dap") * groups + lax.axis_index("grp")).astype(jnp.int32).reshape(1)
     shape = jax.ShapeDtypeStruct
 
     def exchange(value, mask):
         return lax.ppermute(value, both, [(at, at ^ mask) for at in range(devices)])
 
-    def gather(pieces):
-        parts = [pieces[0]]
-        for near in range(1, near_pieces):
-            mask = near // groups * 4 * groups + near % groups
-            parts.append(exchange(pieces[near % groups], mask))
-        own = jnp.stack(parts)
-        across = exchange(own, 2 * groups)
-        return own, exchange(own, groups), across, exchange(across, groups)
-
-    bias_tiles = heads_here * row_tiles * column_tiles
-    *bias_pieces, keep = call(
+    def to_all(value):
+        return lax.all_to_all(value, both, split_axis=0, concat_axis=0, tiled=True)
+
+    half_tiles = heads_here // 2 * row_tiles * column_tiles
+    bias_out, keep = call(
         functools.partial(share_kernel, groups),
-        tuple([shape((bias_tiles + 1, 8, LANES), BF16)] * groups + [shape((8, LANES), F32)]),
-        (place, alignment_mask.T, sequence_row_mask.reshape(1, sequences), pairwise_bias),
-        scalars=1,
+        (shape((devices, half_tiles + 1, 8, LANES), BF16), shape((8, LANES), F32)),
+        (alignment_mask.T, sequence_row_mask.reshape(1, sequences), pairwise_bias),
         micros=1,
-    )
-    bias_stacks = gather(bias_pieces)
+        loose=True,
+    )
+    own_bias = to_all(bias_out)
+    other_bias = exchange(own_bias, groups)
     row_out_weight = jnp.stack(
         [horizontal_final_matrix]
         + [exchange(horizontal_final_matrix, relative) for relative in range(1, groups)]
     )
 
     right_tiles = channels * sequences // LANES
-    rows_out, right_piece, left = call(
+    rows_out, right_out, left = call(
         functools.partial(prepare_kernel, (groups, sequences_here)),
         (
             shape((devices, sequences_here * (width // LANES), residues, LANES), BF16),
-            shape((right_tiles, residues, LANES), BF16),
+            shape((devices, right_tiles // 2, residues, LANES), BF16),
             shape((sequences * residues, channels), BF16),
         ),
         (homolog_activity, keep, first_operand_matrix.T, second_operand_matrix.T),
         mib=56 if large else 32,
     )
-    rows_in = lax.all_to_all(rows_out, both, split_axis=0, concat_axis=0, tiled=True)
-    right_stacks = gather([right_piece] * groups)
+    rows_in = to_all(rows_out)
+    own_right = to_all(right_out)
+    other_right = exchange(own_right, groups)
 
     mix_out, keep_all = call(
-        functools.partial(row_kernel, (groups, sequences_here)),
+        functools.partial(row_kernel, (groups, sequences_here, row_tiles, column_tiles)),
         (
             shape((devices, sequences_here, residues, head_lanes), BF16),
             shape((residues_overall, LANES), BF16),
         ),
-        (place, rows_in, *bias_stacks, horizontal_projection_matrix.transpose(1, 0, 2)),
-        scratch=[
-            pltpu.VMEM(
-                (heads_here, groups * column_tiles, parallel * row_tiles, 8, LANES), BF16
-            ),
-            pltpu.VMEM((devices, 8, LANES), BF16),
-        ]
-        + [pltpu.VMEM((sequences_here, residues_overall, head_lanes), BF16)] * 3
+        (
+            place,
+            own_bias,
+            other_bias,
+            rows_in,
+            horizontal_projection_matrix.transpose(1, 0, 2),
+        ),
+        scratch=[pltpu.VMEM((sequences_here, residues_overall, head_lanes), BF16)] * 3
         + [pltpu.VMEM((sequences_here, residues_overall, head_lanes), F32)],
         scalars=1,
         mib=60 if large else 32,
     )
-    mix_in = lax.all_to_all(mix_out, both, split_axis=0, concat_axis=0, tiled=True)
+    mix_in = to_all(mix_out)
 
     pairwise_update = call(
         functools.partial(outer_kernel, (groups, sequences, 2)),
@@ -462,15 +441,13 @@
         (
             place,
             keep_all,
-            *right_stacks,
+            own_right,
+            other_right,
             left,
             keep,
             outer_output_weight.reshape(channels, channels, depth).transpose(1, 0, 2),
         ),
-        scratch=[
-            pltpu.VMEM((residues, channels * sequences, depth), BF16),
-            pltpu.VMEM((devices, right_tiles, residues, LANES), BF16),
-        ],
+        scratch=[pltpu.VMEM((residues, channels * sequences, depth), BF16)],
         scalars=1,
         mib=60 if large else 32,
     )

time: 78.8 us -> 67.2 us (0.85)
  starting transfers between devices: 43 us -> 7.39 us
  blocking collectives: 0 us -> 31.6 us
  waiting for transfers between devices: 22.8 us -> 13 us
  local copies, waits for them, and re-layouts: 2.68 us -> 4.9 us
    ppermute x21 -> x3, starting transfers between devices: 36.4 us -> 2.1 us  [exchange(): return lax.ppermute(value, both, [(at, at ^ mask) for at in range(devices)])]
    all_to_all x0 -> x2, blocking collectives: none -> 31.6 us  [to_all(): return lax.all_to_all(value, both, split_axis=0, concat_axis=0, tiled=True)]
    ppermute x21 -> x3, waiting for transfers between devices: 16.5 us -> 0.01 us  [exchange(): return lax.ppermute(value, both, [(at, at ^ mask) for at in range(devices)])]
    all_to_all x2, waiting for transfers between devices: 6.37 us -> 13 us  [to_all(): return lax.all_to_all(value, both, split_axis=0, concat_axis=0, tiled=True)]
    unnamed x42 -> x28, local copies, waits for them, and re-layouts: 2.55 us -> 4.8 us
    all_to_all x2, starting transfers between devices: 6.56 us -> 5.29 us  [to_all(): return lax.all_to_all(value, both, split_axis=0, concat_axis=0, tiled=True)]
  transfers between devices with their start and end apart: 23 -> 5, of which waited for: 8 -> 2; matrix products, arithmetic and copies ran while one was open for 0% -> 0% of each run, Pallas kernels for 8% -> 6%
where the time goes in v3:
time: 67.2 us; the launch traced here: 66.8 us
  blocking collectives  31.6 us (47%)
  waiting for transfers between devices  13 us (19%)
  Pallas kernels  9.09 us (14%)
  starting transfers between devices  7.39 us (11%)
  local copies, waits for them, and re-layouts  4.9 us (7%)
  between operations  0.74 us (1%)
    all_to_all x2, blocking collectives, to_all(): return lax.all_to_all(value, both, split_axis=0, concat_axis=0, tiled=True)  31.6 us
    all_to_all x2, waiting for transfers between devices, to_all(): return lax.all_to_all(value, both, split_axis=0, concat_axis=0, tiled=True)  13 us
    pallas_call x5, Pallas kernels, call(): pl.pallas_call(kernel, out_shape=outs, in_specs=[smem] * scalars + [read]...  9.09 us
    all_to_all x2, starting transfers between devices, to_all(): return lax.all_to_all(value, both, split_axis=0, concat_axis=0, tiled=True)  5.29 us
    unnamed x28, local copies, waits for them, and re-layouts  4.8 us
    ppermute x3, starting transfers between devices, exchange(): return lax.ppermute(value, both, [(at, at ^ mask) for at in range(devices)])  2.1 us
  transfers between devices with their start and end apart: 5, of which 2 were waited for; matrix products, arithmetic and copies ran while one was open for 0% of the time, Pallas kernels for 6%

profile of v3, /device:TPU:0, one launch (start us, length us, event | category | flops | bytes accessed | tf_op | source)
XLA Modules:
  0.0 66.8 jit_solution(1230280123110169903)
XLA Ops:
  0.6 0.0 copy-start.8
  0.6 0.6 copy-done.8
  1.3 0.0 copy-start.4
  1.3 0.8 %copy-done.4 = bf16[8,16,128]{2,1,0:T(8,128)(2,1)S(1)} copy-done((bf16[8,16,128]{2,1,0:T(8,128)(2,1)S(1)}, bf16[8,16,128]{2,1,0:T(8,128)(2,1)}, u32[]{:S(2)}) %copy-start.4) | copy-done | bytes 32792
  2.0 0.0 copy-start.7
  2.0 0.7 %copy-done.7 = s32[32,8]{0,1:T(8,128)S(1)} copy-done((s32[32,8]{0,1:T(8,128)S(1)}, s32[32,8]{0,1:T(8,128)}, u32[]{:S(2)}) %copy-start.7) | copy-done | bytes 1048
  2.7 0.0 copy-start
  2.7 0.0 copy-start.5
  2.7 0.0 copy-start.6
  2.8 0.8 %copy-done = bf16[32,8,256]{2,1,0:T(8,128)(2,1)S(1)} copy-done((bf16[32,8,256]{2,1,0:T(8,128)(2,1)S(1)}, bf16[32,8,256]{2,1,0:T(8,128)(2,1)}, u32[]{:S(2)}) %copy-start) | copy-done | bytes 131096
  3.6 0.0 copy-done.5
  3.6 0.0 copy-done.6
  3.6 2.0 %shard_map.141 = (bf16[32,4,8,128]{3,2,1,0:T(8,128)(2,1)}, bf16[32,4,8,128]{3,2,1,0:T(8,128)(2,1)S(1)}, bf16[256,32]{1,0:T(8,128)(2,1)S(1)}) custom-call(bf16[32,8,256]{2,1,0:T(8,128)(2,1)S(1)} %copy-done, f32[8,128]{1,0:T(8,128)S(1)} %get-tuple-element.10.keep_ref, bf16[32,256]{1,0:T(8,128)(2,1)S(1)} %bitcast.22, bf16[32,256]{1,0:T(8,128)(2,1)S(1)} %bitcast.23), custom_call_target="tpu_custom_call" | custom-call | flops 2000000000 | bytes 2000000 | tf_op jit(solution)/shard_map/pallas_call | solution.py:339
  5.6 17.8 %all_to_all.20.own_right_ref = bf16[32,4,8,128]{3,2,1,0:T(8,128)(2,1)S(1)} all-to-all(bf16[32,4,8,128]{3,2,1,0:T(8,128)(2,1)S(1)} %get-tuple-element.14), channel_id=1, replica_groups=mesh['dap'=16,'grp'=2] {'dap','grp'}, dimensions={0} | all-to-all | bytes 524288 | tf_op jit(solution)/shard_map/all_to_all | solution.py:386
  23.4 13.8 %all_to_all.21.own_bias_ref = bf16[32,5,8,128]{3,2,1,0:T(8,128)(2,1)S(1)} all-to-all(bf16[32,5,8,128]{3,2,1,0:T(8,128)(2,1)S(1)} %get-tuple-element.9), channel_id=1, replica_groups=mesh['dap'=16,'grp'=2] {'dap','grp'}, dimensions={0} | all-to-all | bytes 655360 | tf_op jit(solution)/shard_map/all_to_all | solution.py:386
  37.2 0.0 copy-start.12
  37.2 0.0 copy-start.9
  37.2 2.7 %all-to-all-start.1 = ((bf16[32,4,8,128]{3,2,1,0:T(8,128)(2,1)}), bf16[32,4,8,128]{3,2,1,0:T(8,128)(2,1)S(1)}, u32[]{:S(2)}, u32[]{:S(2)}) async-start(bf16[32,4,8,128]{3,2,1,0:T(8,128)(2,1)} %get-tuple-element.11), calls=%async_computation.1 | async-start | bytes 524288 | tf_op jit(solution)/shard_map/all_to_all | solution.py:386
  40.0 0.3 collective-permute-start
  40.2 0.0 copy-done.12
  40.2 1.7 %collective-permute-start.1 = (bf16[128,256]{1,0:T(8,128)(2,1)S(1)}, bf16[128,256]{1,0:T(8,128)(2,1)S(1)}, u32[]{:S(2)}, u32[]{:S(2)}) collective-permute-start(bf16[128,256]{1,0:T(8,128)(2,1)S(1)} %copy-done.12), channel_id=1, source_target_pairs={{0,1},{1,0},{2,3},{3,2},{4,5},{5,4},{6,7},{7,6},{8,9},{9,8},{10,11... | collective-permute-start | bytes 196616 | tf_op jit(solution)/shard_map/ppermute | solution.py:383
  41.9 0.0 copy-done.9
  41.9 0.0 copy-start.10
  42.0 0.9 %copy-done.10 = bf16[1024,128]{1,0:T(8,128)(2,1)S(1)} copy-done((bf16[1024,128]{1,0:T(8,128)(2,1)S(1)}, bf16[1024,128]{1,0:T(8,128)(2,1)}, u32[]{:S(2)}) %copy-start.10) | copy-done | bytes 262168
  42.9 0.0 copy-start.11
  42.9 0.1 copy.23
  43.0 0.8 %copy-done.11 = bf16[256,2,256]{2,1,0:T(2,128)(2,1)S(1)} copy-done((bf16[256,2,256]{2,1,0:T(2,128)(2,1)S(1)}, bf16[256,2,256]{2,1,0:T(2,128)(2,1)}, u32[]{:S(2)}) %copy-start.11) | copy-done | bytes 262168
  43.9 0.1 collective-permute-start.2
  44.0 6.6 %all-to-all-done.1.rows_ref = bf16[32,4,8,128]{3,2,1,0:T(8,128)(2,1)S(1)} async-done(((bf16[32,4,8,128]{3,2,1,0:T(8,128)(2,1)}), bf16[32,4,8,128]{3,2,1,0:T(8,128)(2,1)S(1)}, u32[]{:S(2)}, u32[]{:S(2)}) %all-to-all-start.1) | async-done | bytes 262176 | tf_op jit(solution)/shard_map/all_to_all | solution.py:386
  50.6 0.0 collective-permute-done.other_bias_ref
  50.6 2.1 %shard_map.142 = (bf16[32,2,8,128]{3,2,1,0:T(8,128)(2,1)}, bf16[256,128]{1,0:T(8,128)(2,1)S(1)}) custom-call(s32[1]{0:T(128)} %bitcast.place_ref, bf16[32,5,8,128]{3,2,1,0:T(8,128)(2,1)S(1)} %all_to_all.21.own_bias_ref, bf16[32,5,8,128]{3,2,1,0:T(8,128)(2,1)S(1)} %collective-permute-done.other_bias_ref, bf16[32,4,8,128]{3,2,1,0:T(8,128)(2,1)S(1)} %all-to-all-done.1.rows_ref, ...), custom_call_target="tpu_custom_call" | custom-call | flops 2000000000 | bytes 2000000 | tf_op jit(solution)/shard_map/pallas_call | solution.py:339
  52.7 2.6 %all-to-all-start.2 = ((bf16[32,2,8,128]{3,2,1,0:T(8,128)(2,1)}), bf16[32,2,8,128]{3,2,1,0:T(8,128)(2,1)S(1)}, u32[]{:S(2)}, u32[]{:S(2)}) async-start(bf16[32,2,8,128]{3,2,1,0:T(8,128)(2,1)} %get-tuple-element.12), calls=%async_computation.2 | async-start | bytes 262144 | tf_op jit(solution)/shard_map/all_to_all | solution.py:386
  55.3 0.0 collective-permute-done.1
  55.4 0.0 collective-permute-done.2.other_right_ref
  55.4 0.0 copy-start.1
  55.4 0.0 copy-start.2
  55.4 0.0 copy-start.3
  55.4 2.2 %shard_map.144 = bf16[8,256,128]{2,1,0:T(8,128)(2,1)} custom-call(s32[1]{0:T(128)} %bitcast.place_ref, bf16[256,128]{1,0:T(8,128)(2,1)S(1)} %get-tuple-element.13.keep_all_ref, bf16[32,4,8,128]{3,2,1,0:T(8,128)(2,1)S(1)} %all_to_all.20.own_right_ref, bf16[32,4,8,128]{3,2,1,0:T(8,128)(2,1)S(1)} %collective-permute-done.2.other_right_ref, ...), custom_call_target="tpu_custom_call" | custom-call | flops 2000000000 | bytes 2000000 | tf_op jit(solution)/shard_map/pallas_call | solution.py:339
  57.6 6.4 %all-to-all-done.2 = bf16[32,2,8,128]{3,2,1,0:T(8,128)(2,1)S(1)} async-done(((bf16[32,2,8,128]{3,2,1,0:T(8,128)(2,1)}), bf16[32,2,8,128]{3,2,1,0:T(8,128)(2,1)S(1)}, u32[]{:S(2)}, u32[]{:S(2)}) %all-to-all-start.2) | async-done | bytes 131104 | tf_op jit(solution)/shard_map/all_to_all | solution.py:386
  64.0 0.0 copy-done.1
  64.0 0.0 copy-done.2
  64.0 0.0 copy-done.3
  64.0 2.8 %shard_map.143 = bf16[32,8,256]{2,1,0:T(8,128)(2,1)} custom-call(s32[1]{0:T(128)} %bitcast.place_ref, bf16[32,8,256]{2,1,0:T(8,128)(2,1)S(1)} %copy-done, bf16[16,2,2,8,128]{4,3,2,1,0:T(8,128)(2,1)S(1)} %bitcast.21, f32[8,128]{1,0:T(8,128)S(1)} %get-tuple-element.10.keep_ref, bf16[2,128,256]{2,1,0:T(8,128)(2,1)S(1)} %pad_maximum_fusion.row_out_ref, ...), custom_call_target="tpu_custom_call" | custom-call | flops 3000000000 | bytes 3000000 | tf_op jit(solution)/shard_map/pallas_call | solution.py:339
  (4 shorter events, 0.1 us)
Async XLA Ops:
  0.6 0.7 copy-start.8
  1.3 0.8 %copy-start.4 = (bf16[8,16,128]{2,1,0:T(8,128)(2,1)S(1)}, bf16[8,16,128]{2,1,0:T(8,128)(2,1)}, u32[]{:S(2)}) copy-start(bf16[8,16,128]{2,1,0:T(8,128)(2,1)} %bias_ref.1) | copy-start | bytes 98308
  2.0 0.7 %copy-start.7 = (s32[32,8]{0,1:T(8,128)S(1)}, s32[32,8]{0,1:T(8,128)}, u32[]{:S(2)}) copy-start(s32[32,8]{0,1:T(8,128)} %param.14) | copy-start | bytes 3076
  2.7 0.9 %copy-start = (bf16[32,8,256]{2,1,0:T(8,128)(2,1)S(1)}, bf16[32,8,256]{2,1,0:T(8,128)(2,1)}, u32[]{:S(2)}) copy-start(bf16[32,8,256]{2,1,0:T(8,128)(2,1)} %x_ref.3) | copy-start | bytes 393220
  2.7 0.9 %copy-start.5 = (bf16[256,32]{0,1:T(8,128)(2,1)S(1)}, bf16[256,32]{0,1:T(8,128)(2,1)}, u32[]{:S(2)}) copy-start(bf16[256,32]{0,1:T(8,128)(2,1)} %param.23) | copy-start | bytes 49156
  2.7 0.9 %copy-start.6 = (bf16[256,32]{0,1:T(8,128)(2,1)S(1)}, bf16[256,32]{0,1:T(8,128)(2,1)}, u32[]{:S(2)}) copy-start(bf16[256,32]{0,1:T(8,128)(2,1)} %param.24) | copy-start | bytes 49156
  37.2 3.0 %copy-start.12 = (bf16[128,256]{1,0:T(8,128)(2,1)S(1)}, bf16[128,256]{1,0:T(8,128)(2,1)}, u32[]{:S(2)}) copy-start(bf16[128,256]{1,0:T(8,128)(2,1)} %param.18) | copy-start | bytes 196612
  37.2 4.7 %copy-start.9 = (bf16[256,4,128]{2,1,0:T(4,128)(2,1)S(1)}, bf16[256,4,128]{2,1,0:T(4,128)(2,1)}, u32[]{:S(2)}) copy-start(bf16[256,4,128]{2,1,0:T(4,128)(2,1)} %param.17) | copy-start | bytes 786436
  37.2 13.4 %all-to-all-start.1 = ((bf16[32,4,8,128]{3,2,1,0:T(8,128)(2,1)}), bf16[32,4,8,128]{3,2,1,0:T(8,128)(2,1)S(1)}, u32[]{:S(2)}, u32[]{:S(2)}) async-start(bf16[32,4,8,128]{3,2,1,0:T(8,128)(2,1)} %get-tuple-element.11), calls=%async_computation.1 | async-start | bytes 524288 | tf_op jit(solution)/shard_map/all_to_all | solution.py:386
  40.0 10.7 %collective-permute-start = (bf16[32,5,8,128]{3,2,1,0:T(8,128)(2,1)S(1)}, bf16[32,5,8,128]{3,2,1,0:T(8,128)(2,1)S(1)}, u32[]{:S(2)}, u32[]{:S(2)}) collective-permute-start(bf16[32,5,8,128]{3,2,1,0:T(8,128)(2,1)S(1)} %all_to_all.21.own_bias_ref), channel_id=1, source_target_pairs={{0,2},{1,3},{2,0},{3,1},{4,6},{5,7},{6,4},{7,5},{8,10},{9,11},{10,... | collective-permute-start | bytes 983048 | tf_op jit(solution)/shard_map/ppermute | solution.py:383
  40.2 15.1 %collective-permute-start.1 = (bf16[128,256]{1,0:T(8,128)(2,1)S(1)}, bf16[128,256]{1,0:T(8,128)(2,1)S(1)}, u32[]{:S(2)}, u32[]{:S(2)}) collective-permute-start(bf16[128,256]{1,0:T(8,128)(2,1)S(1)} %copy-done.12), channel_id=1, source_target_pairs={{0,1},{1,0},{2,3},{3,2},{4,5},{5,4},{6,7},{7,6},{8,9},{9,8},{10,11... | collective-permute-start | bytes 196616 | tf_op jit(solution)/shard_map/ppermute | solution.py:383
  41.9 1.0 %copy-start.10 = (bf16[1024,128]{1,0:T(8,128)(2,1)S(1)}, bf16[1024,128]{1,0:T(8,128)(2,1)}, u32[]{:S(2)}) copy-start(bf16[1024,128]{1,0:T(8,128)(2,1)} %param.25) | copy-start | bytes 786436
  42.9 0.9 %copy-start.11 = (bf16[256,2,256]{2,1,0:T(2,128)(2,1)S(1)}, bf16[256,2,256]{2,1,0:T(2,128)(2,1)}, u32[]{:S(2)}) copy-start(bf16[256,2,256]{2,1,0:T(2,128)(2,1)} %param.21) | copy-start | bytes 786436
  43.9 11.5 %collective-permute-start.2 = (bf16[32,4,8,128]{3,2,1,0:T(8,128)(2,1)S(1)}, bf16[32,4,8,128]{3,2,1,0:T(8,128)(2,1)S(1)}, u32[]{:S(2)}, u32[]{:S(2)}) collective-permute-start(bf16[32,4,8,128]{3,2,1,0:T(8,128)(2,1)S(1)} %all_to_all.20.own_right_ref), channel_id=1, source_target_pairs={{0,2},{1,3},{2,0},{3,1},{4,6},{5,7},{6,4},{7,5},{8,10},{9,11},{10,... | collective-permute-start | bytes 786440 | tf_op jit(solution)/shard_map/ppermute | solution.py:383
  52.7 11.2 %all-to-all-start.2 = ((bf16[32,2,8,128]{3,2,1,0:T(8,128)(2,1)}), bf16[32,2,8,128]{3,2,1,0:T(8,128)(2,1)S(1)}, u32[]{:S(2)}, u32[]{:S(2)}) async-start(bf16[32,2,8,128]{3,2,1,0:T(8,128)(2,1)} %get-tuple-element.12), calls=%async_computation.2 | async-start | bytes 262144 | tf_op jit(solution)/shard_map/all_to_all | solution.py:386
  55.4 8.6 %copy-start.1 = (bf16[256,256]{1,0:T(8,128)(2,1)S(1)}, bf16[256,256]{1,0:T(8,128)(2,1)}, u32[]{:S(2)}) copy-start(bf16[256,256]{1,0:T(8,128)(2,1)} %query_w_ref.1) | copy-start | bytes 393220
  55.4 8.6 %copy-start.2 = (bf16[256,256]{1,0:T(8,128)(2,1)S(1)}, bf16[256,256]{1,0:T(8,128)(2,1)}, u32[]{:S(2)}) copy-start(bf16[256,256]{1,0:T(8,128)(2,1)} %key_w_ref.1) | copy-start | bytes 393220
  55.4 8.6 %copy-start.3 = (bf16[256,256]{1,0:T(8,128)(2,1)S(1)}, bf16[256,256]{1,0:T(8,128)(2,1)}, u32[]{:S(2)}) copy-start(bf16[256,256]{1,0:T(8,128)(2,1)} %out_w_ref.1) | copy-start | bytes 393220

commit v4 on v3

--- a/solution.py
+++ b/solution.py
@@ -68,7 +68,19 @@
     return heads // groups, bias_rows // 8, bias_columns // LANES
 
 
-def share_kernel(groups, mask_ref, present_ref, bias_ref, out_ref, keep_ref):
+def share_kernel(
+    groups, mask_hbm, present_hbm, bias_hbm, out_ref, keep_ref, mask_ref, present_ref, bias_ref,
+    sems,
+):
+    pairs = ((bias_hbm, bias_ref), (mask_hbm, mask_ref), (present_hbm, present_ref))
+    copies = [
+        pltpu.make_async_copy(source, target, sems.at[at])
+        for at, (source, target) in enumerate(pairs)
+    ]
+    for copy in copies:
+        copy.start()
+    for copy in copies:
+        copy.wait()
     heads_here, row_tiles, column_tiles = tile_count(bias_ref.shape, groups)
     half_heads = heads_here // 2
     sequences = mask_ref.shape[1]
@@ -93,7 +105,7 @@
 
 
 def prepare_kernel(
-    sizes, x_ref, keep_ref, left_w_ref, right_w_ref, rows_ref, right_ref, left_ref
+    sizes, x_ref, keep_ref, left_w_ref, right_w_ref, rows_ref, left_ref
 ):
     groups, sequences_here = sizes
     sequences, residues, width = x_ref.shape
@@ -141,10 +153,10 @@
         )
         expanded = jnp.where(same_sequence, matmul(right, select), 0.0).astype(BF16)
         result = (matmul(residue_pick, expanded) * keep_spread).astype(BF16)
-        core, slot = divmod(tile, right_ref.shape[1])
-        for target in range(right_ref.shape[0]):
-            if target // groups % 2 == core:
-                right_ref[target, slot] = result
+        quarter, slot = divmod(tile, channels // per_tile // 4)
+        for target in range(rows_ref.shape[0]):
+            if target // groups % 4 == quarter:
+                rows_ref[target, sequences_here * halves + slot] = result
 
 
 def row_kernel(
@@ -225,17 +237,17 @@
 
 
 def outer_kernel(
-    sizes, place_ref, keep_all_ref, own_right_ref, other_right_ref, left_ref, keep_ref,
+    sizes, place_ref, keep_all_ref, right0, right1, right2, right3, left_ref, keep_ref,
     weight_ref, out_ref, mixed_s,
 ):
     groups, sequences, pair = sizes
     residues = keep_ref.shape[0]
     channels, _, depth = weight_ref.shape
-    core = quotient(place_ref[0], groups) & 1
+    quarter = quotient(place_ref[0], groups) & 3
     left = left_ref[...]
-    half_channels = channels // 2
+    quarter_channels = channels // 4
     for at in range(0, channels, 2):
-        channel = (core ^ (at // half_channels)) * half_channels + at % half_channels
+        channel = (quarter ^ (at // quarter_channels)) * quarter_channels + at % quarter_channels
         weights = jnp.concatenate([weight_ref[channel], weight_ref[channel + 1]], axis=1)
         product = matmul(left, weights).astype(BF16)
         for residue in range(residues):
@@ -247,7 +259,7 @@
     right = jnp.concatenate(
         [
             flat_rows(right_ref[:, tile])
-            for right_ref in (own_right_ref, other_right_ref)
+            for right_ref in (right0, right1, right2, right3)
             for tile in range(right_ref.shape[1])
         ],
         axis=1,
@@ -332,9 +344,9 @@
     out_ref[...] = result.reshape(sequences, residues, width).astype(BF16)
 
 
-def call(kernel, outs, arguments, scratch=(), scalars=0, mib=32, micros=2, loose=False):
+def call(kernel, outs, arguments, scratch=(), scalars=0, mib=32, micros=2, fetch=False):
     vmem = pl.BlockSpec(memory_space=pltpu.VMEM)
-    read = pl.BlockSpec() if loose else vmem
+    read = pl.BlockSpec(memory_space=pltpu.HBM) if fetch else vmem
     smem = pl.BlockSpec(memory_space=pltpu.SMEM)
     return pl.pallas_call(
         kernel,
@@ -390,8 +402,14 @@
         functools.partial(share_kernel, groups),
         (shape((devices, half_tiles + 1, 8, LANES), BF16), shape((8, LANES), F32)),
         (alignment_mask.T, sequence_row_mask.reshape(1, sequences), pairwise_bias),
+        scratch=[
+            pltpu.VMEM((residues, sequences), jnp.int32),
+            pltpu.VMEM((1, sequences), jnp.int32),
+            pltpu.VMEM(pairwise_bias.shape, BF16),
+            pltpu.SemaphoreType.DMA((3,)),
+        ],
         micros=1,
-        loose=True,
+        fetch=True,
     )
     own_bias = to_all(bias_out)
     other_bias = exchange(own_bias, groups)
@@ -401,19 +419,20 @@
     )
 
     right_tiles = channels * sequences // LANES
-    rows_out, right_out, left = call(
+    row_slots = sequences_here * (width // LANES)
+    rows_out, left = call(
         functools.partial(prepare_kernel, (groups, sequences_here)),
         (
-            shape((devices, sequences_here * (width // LANES), residues, LANES), BF16),
-            shape((devices, right_tiles // 2, residues, LANES), BF16),
+            shape((devices, row_slots + right_tiles // 4, residues, LANES), BF16),
             shape((sequences * residues, channels), BF16),
         ),
         (homolog_activity, keep, first_operand_matrix.T, second_operand_matrix.T),
         mib=56 if large else 32,
     )
     rows_in = to_all(rows_out)
-    own_right = to_all(right_out)
-    other_right = exchange(own_right, groups)
+    right = rows_in[:, row_slots:]
+    right_across = exchange(right, 2 * groups)
+    right_parts = (right, exchange(right, groups), right_across, exchange(right_across, groups))
 
     mix_out, keep_all = call(
         functools.partial(row_kernel, (groups, sequences_here, row_tiles, column_tiles)),
@@ -441,8 +460,7 @@
         (
             place,
             keep_all,
-            own_right,
-            other_right,
+            *right_parts,
             left,
             keep,
             outer_output_weight.reshape(channels, channels, depth).transpose(1, 0, 2),

time: 67.2 us -> 60.9 us (0.906)
  blocking collectives: 31.6 us -> 0 us
  waiting for transfers between devices: 13 us -> 29.5 us
  starting transfers between devices: 7.39 us -> 15.4 us
  Pallas kernels: 9.09 us -> 10.6 us
  local copies, waits for them, and re-layouts: 4.9 us -> 4.07 us
    all_to_all x2 -> x0, blocking collectives: 31.6 us -> none  [to_all(): return lax.all_to_all(value, both, split_axis=0, concat_axis=0, tiled=True)]
    all_to_all x2 -> x3, waiting for transfers between devices: 13 us -> 27.8 us  [to_all(): return lax.all_to_all(value, both, split_axis=0, concat_axis=0, tiled=True)]
    all_to_all x2 -> x3, starting transfers between devices: 5.29 us -> 12.6 us  [to_all(): return lax.all_to_all(value, both, split_axis=0, concat_axis=0, tiled=True)]
    ppermute x3 -> x5, waiting for transfers between devices: 0.01 us -> 1.68 us  [exchange(): return lax.ppermute(value, both, [(at, at ^ mask) for at in range(devices)])]
    pallas_call x5, Pallas kernels: 9.09 us -> 10.6 us  [call(): pl.pallas_call(kernel, out_shape=outs, in_specs=[smem] * scalars + [read]...]
    unnamed x28, local copies, waits for them, and re-layouts: 4.8 us -> 3.96 us
    ppermute x3 -> x5, starting transfers between devices: 2.1 us -> 2.81 us  [exchange(): return lax.ppermute(value, both, [(at, at ^ mask) for at in range(devices)])]
  transfers between devices with their start and end apart: 5 -> 8, of which waited for: 2 -> 4; matrix products, arithmetic and copies ran while one was open for 0% -> 0% of each run, Pallas kernels for 6% -> 12%
where the time goes in v4:
time: 60.9 us; the launch traced here: 60.4 us
  waiting for transfers between devices  29.5 us (48%)
  starting transfers between devices  15.4 us (25%)
  Pallas kernels  10.6 us (17%)
  local copies, waits for them, and re-layouts  4.07 us (7%)
  between operations  0.83 us (1%)
    all_to_all x3, waiting for transfers between devices, to_all(): return lax.all_to_all(value, both, split_axis=0, concat_axis=0, tiled=True)  27.8 us
    all_to_all x3, starting transfers between devices, to_all(): return lax.all_to_all(value, both, split_axis=0, concat_axis=0, tiled=True)  12.6 us
    pallas_call x5, Pallas kernels, call(): pl.pallas_call(kernel, out_shape=outs, in_specs=[smem] * scalars + [read]...  10.6 us
    unnamed x28, local copies, waits for them, and re-layouts  3.96 us
    ppermute x5, starting transfers between devices, exchange(): return lax.ppermute(value, both, [(at, at ^ mask) for at in range(devices)])  2.81 us
    ppermute x5, waiting for transfers between devices, exchange(): return lax.ppermute(value, both, [(at, at ^ mask) for at in range(devices)])  1.68 us
  transfers between devices with their start and end apart: 8, of which 4 were waited for; matrix products, arithmetic and copies ran while one was open for 0% of the time, Pallas kernels for 12%

profile of v4, /device:TPU:0, one launch (start us, length us, event | category | flops | bytes accessed | tf_op | source)
XLA Modules:
  0.0 60.4 jit_solution(16811648870995871351)
XLA Ops:
  0.6 0.0 copy-start.8
  0.6 0.6 %copy-done.8 = s32[32]{0:T(128)S(1)} copy-done((s32[32]{0:T(128)S(1)}, s32[32]{0:T(128)}, u32[]{:S(2)}) %copy-start.8) | copy-done | bytes 152
  1.3 0.0 copy-start.4
  1.3 0.8 %copy-done.4 = bf16[8,16,128]{2,1,0:T(8,128)(2,1)S(1)} copy-done((bf16[8,16,128]{2,1,0:T(8,128)(2,1)S(1)}, bf16[8,16,128]{2,1,0:T(8,128)(2,1)}, u32[]{:S(2)}) %copy-start.4) | copy-done | bytes 32792
  2.0 0.0 copy-start.7
  2.0 0.7 %copy-done.7 = s32[32,8]{0,1:T(8,128)S(1)} copy-done((s32[32,8]{0,1:T(8,128)S(1)}, s32[32,8]{0,1:T(8,128)}, u32[]{:S(2)}) %copy-start.7) | copy-done | bytes 1048
  2.7 0.8 %shard_map.140 = (bf16[32,5,8,128]{3,2,1,0:T(8,128)(2,1)}, f32[8,128]{1,0:T(8,128)S(1)}) custom-call(s32[8,32]{1,0:T(8,128)S(1)} %bitcast.24, s32[1,32]{1,0:T(1,128)S(1)} %bitcast.25, bf16[8,16,128]{2,1,0:T(8,128)(2,1)S(1)} %copy-done.4), custom_call_target="tpu_custom_call" | custom-call | flops 1000000000 | bytes 1000000 | tf_op jit(solution)/shard_map/pallas_call | solution.py:351
  3.6 0.0 copy-start
  3.6 0.0 copy-start.5
  3.6 0.0 copy-start.6
  3.6 7.3 %all-to-all-start = ((bf16[32,5,8,128]{3,2,1,0:T(8,128)(2,1)}), bf16[32,5,8,128]{3,2,1,0:T(8,128)(2,1)S(1)}, u32[]{:S(2)}, u32[]{:S(2)}) async-start(bf16[32,5,8,128]{3,2,1,0:T(8,128)(2,1)} %get-tuple-element.8), calls=%async_computation | async-start | bytes 655360 | tf_op jit(solution)/shard_map/all_to_all | solution.py:398
  10.9 0.0 copy-done
  10.9 0.0 copy-done.5
  10.9 0.0 copy-done.6
  10.9 2.7 %shard_map.141 = (bf16[32,6,8,128]{3,2,1,0:T(8,128)(2,1)}, bf16[256,32]{1,0:T(8,128)(2,1)S(1)}) custom-call(bf16[32,8,256]{2,1,0:T(8,128)(2,1)S(1)} %copy-done, f32[8,128]{1,0:T(8,128)S(1)} %get-tuple-element.9.keep_ref, bf16[32,256]{1,0:T(8,128)(2,1)S(1)} %bitcast.22, bf16[32,256]{1,0:T(8,128)(2,1)S(1)} %bitcast.23), custom_call_target="tpu_custom_call" | custom-call | flops 2000000000 | bytes 2000000 | tf_op jit(solution)/shard_map/pallas_call | solution.py:351
  13.6 9.0 %all-to-all-done.own_bias_ref = bf16[32,5,8,128]{3,2,1,0:T(8,128)(2,1)S(1)} async-done(((bf16[32,5,8,128]{3,2,1,0:T(8,128)(2,1)}), bf16[32,5,8,128]{3,2,1,0:T(8,128)(2,1)S(1)}, u32[]{:S(2)}, u32[]{:S(2)}) %all-to-all-start) | async-done | bytes 327712 | tf_op jit(solution)/shard_map/all_to_all | solution.py:398
  22.6 0.0 copy-start.12
  22.6 2.7 %all-to-all-start.1 = ((bf16[32,6,8,128]{3,2,1,0:T(8,128)(2,1)}), bf16[32,6,8,128]{3,2,1,0:T(8,128)(2,1)S(1)}, u32[]{:S(2)}, u32[]{:S(2)}) async-start(bf16[32,6,8,128]{3,2,1,0:T(8,128)(2,1)} %get-tuple-element.10), calls=%async_computation.1 | async-start | bytes 786432 | tf_op jit(solution)/shard_map/all_to_all | solution.py:398
  25.4 0.0 copy-start.9
  25.4 0.3 collective-permute-start
  25.7 12.5 %all-to-all-done.1.rows_ref = bf16[32,6,8,128]{3,2,1,0:T(8,128)(2,1)S(1)} async-done(((bf16[32,6,8,128]{3,2,1,0:T(8,128)(2,1)}), bf16[32,6,8,128]{3,2,1,0:T(8,128)(2,1)S(1)}, u32[]{:S(2)}, u32[]{:S(2)}) %all-to-all-start.1) | async-done | bytes 393248 | tf_op jit(solution)/shard_map/all_to_all | solution.py:398
  38.1 1.0 %collective-permute-start.3 = (bf16[32,2,8,128]{3,2,1,0:T(8,128)(2,1)S(1)}, bf16[32,2,8,128]{3,2,1,0:T(8,128)(2,1)S(1)}, u32[]{:S(2)}, u32[]{:S(2)}) collective-permute-start(bf16[32,2,8,128]{3,2,1,0:T(8,128)(2,1)S(1)} %slice.4.right0), channel_id=1, source_target_pairs={{0,4},{1,5},{2,6},{3,7},{4,0},{5,1},{6,2},{7,3},{8,12},{9,13},{10,... | collective-permute-start | bytes 393224 | tf_op jit(solution)/shard_map/ppermute | solution.py:395
  39.1 0.0 copy-done.12
  39.1 1.5 %collective-permute-start.1 = (bf16[128,256]{1,0:T(8,128)(2,1)S(1)}, bf16[128,256]{1,0:T(8,128)(2,1)S(1)}, u32[]{:S(2)}, u32[]{:S(2)}) collective-permute-start(bf16[128,256]{1,0:T(8,128)(2,1)S(1)} %copy-done.12), channel_id=1, source_target_pairs={{0,1},{1,0},{2,3},{3,2},{4,5},{5,4},{6,7},{7,6},{8,9},{9,8},{10,11... | collective-permute-start | bytes 196616 | tf_op jit(solution)/shard_map/ppermute | solution.py:395
  40.6 0.0 copy-done.9
  40.6 0.0 copy-start.10
  40.6 0.9 %copy-done.10 = bf16[1024,128]{1,0:T(8,128)(2,1)S(1)} copy-done((bf16[1024,128]{1,0:T(8,128)(2,1)S(1)}, bf16[1024,128]{1,0:T(8,128)(2,1)}, u32[]{:S(2)}) %copy-start.10) | copy-done | bytes 262168
  41.6 0.0 copy-start.11
  41.6 0.1 copy.23
  41.7 0.8 %copy-done.11 = bf16[256,2,256]{2,1,0:T(2,128)(2,1)S(1)} copy-done((bf16[256,2,256]{2,1,0:T(2,128)(2,1)S(1)}, bf16[256,2,256]{2,1,0:T(2,128)(2,1)}, u32[]{:S(2)}) %copy-start.11) | copy-done | bytes 262168
  42.5 0.1 collective-permute-start.2
  42.6 1.7 %collective-permute-done.3.right2 = bf16[32,2,8,128]{3,2,1,0:T(8,128)(2,1)S(1)} collective-permute-done((bf16[32,2,8,128]{3,2,1,0:T(8,128)(2,1)S(1)}, bf16[32,2,8,128]{3,2,1,0:T(8,128)(2,1)S(1)}, u32[]{:S(2)}, u32[]{:S(2)}) %collective-permute-start.3) | collective-permute-done | bytes 131104 | tf_op jit(solution)/shard_map/ppermute | solution.py:395
  44.3 0.0 collective-permute-start.4
  44.3 0.0 collective-permute-done.other_bias_ref
  44.3 2.1 %shard_map.142 = (bf16[32,2,8,128]{3,2,1,0:T(8,128)(2,1)}, bf16[256,128]{1,0:T(8,128)(2,1)S(1)}) custom-call(s32[1]{0:T(128)} %bitcast.place_ref, bf16[32,5,8,128]{3,2,1,0:T(8,128)(2,1)S(1)} %all-to-all-done.own_bias_ref, bf16[32,5,8,128]{3,2,1,0:T(8,128)(2,1)S(1)} %collective-permute-done.other_bias_ref, ...), custom_call_target="tpu_custom_call" | custom-call | flops 2000000000 | bytes 2000000 | tf_op jit(solution)/shard_map/pallas_call | solution.py:351
  46.4 2.6 %all-to-all-start.2 = ((bf16[32,2,8,128]{3,2,1,0:T(8,128)(2,1)}), bf16[32,2,8,128]{3,2,1,0:T(8,128)(2,1)S(1)}, u32[]{:S(2)}, u32[]{:S(2)}) async-start(bf16[32,2,8,128]{3,2,1,0:T(8,128)(2,1)} %get-tuple-element.11), calls=%async_computation.2 | async-start | bytes 262144 | tf_op jit(solution)/shard_map/all_to_all | solution.py:398
  49.0 0.0 collective-permute-done.1
  49.0 0.0 collective-permute-done.2.right1
  49.0 0.0 collective-permute-done.4.right3
  49.0 0.0 copy-start.1
  49.1 0.0 copy-start.2
  49.1 0.0 copy-start.3
  49.1 2.2 %shard_map.144 = bf16[8,256,128]{2,1,0:T(8,128)(2,1)} custom-call(s32[1]{0:T(128)} %bitcast.place_ref, bf16[256,128]{1,0:T(8,128)(2,1)S(1)} %get-tuple-element.12.keep_all_ref, bf16[32,2,8,128]{3,2,1,0:T(8,128)(2,1)S(1)} %slice.4.right0, bf16[32,2,8,128]{3,2,1,0:T(8,128)(2,1)S(1)} %collective-permute-done.2.right1, ...), custom_call_target="tpu_custom_call" | custom-call | flops 2000000000 | bytes 2000000 | tf_op jit(solution)/shard_map/pallas_call | solution.py:351
  51.2 6.4 %all-to-all-done.2 = bf16[32,2,8,128]{3,2,1,0:T(8,128)(2,1)S(1)} async-done(((bf16[32,2,8,128]{3,2,1,0:T(8,128)(2,1)}), bf16[32,2,8,128]{3,2,1,0:T(8,128)(2,1)S(1)}, u32[]{:S(2)}, u32[]{:S(2)}) %all-to-all-start.2) | async-done | bytes 131104 | tf_op jit(solution)/shard_map/all_to_all | solution.py:398
  57.6 0.0 copy-done.1
  57.6 0.0 copy-done.2
  57.6 0.0 copy-done.3
  57.6 2.8 %shard_map.143 = bf16[32,8,256]{2,1,0:T(8,128)(2,1)} custom-call(s32[1]{0:T(128)} %bitcast.place_ref, bf16[32,8,256]{2,1,0:T(8,128)(2,1)S(1)} %copy-done, bf16[16,2,2,8,128]{4,3,2,1,0:T(8,128)(2,1)S(1)} %bitcast.21, f32[8,128]{1,0:T(8,128)S(1)} %get-tuple-element.9.keep_ref, bf16[2,128,256]{2,1,0:T(8,128)(2,1)S(1)} %pad_maximum_fusion.row_out_ref, ...), custom_call_target="tpu_custom_call" | custom-call | flops 3000000000 | bytes 3000000 | tf_op jit(solution)/shard_map/pallas_call | solution.py:351
  (4 shorter events, 0.1 us)
Async XLA Ops:
  0.6 0.7 %copy-start.8 = (s32[32]{0:T(128)S(1)}, s32[32]{0:T(128)}, u32[]{:S(2)}) copy-start(s32[32]{0:T(128)} %param.15) | copy-start | bytes 388
  1.3 0.8 %copy-start.4 = (bf16[8,16,128]{2,1,0:T(8,128)(2,1)S(1)}, bf16[8,16,128]{2,1,0:T(8,128)(2,1)}, u32[]{:S(2)}) copy-start(bf16[8,16,128]{2,1,0:T(8,128)(2,1)} %bias_hbm.1) | copy-start | bytes 98308
  2.0 0.7 %copy-start.7 = (s32[32,8]{0,1:T(8,128)S(1)}, s32[32,8]{0,1:T(8,128)}, u32[]{:S(2)}) copy-start(s32[32,8]{0,1:T(8,128)} %param.14) | copy-start | bytes 3076
  3.6 7.3 %copy-start = (bf16[32,8,256]{2,1,0:T(8,128)(2,1)S(1)}, bf16[32,8,256]{2,1,0:T(8,128)(2,1)}, u32[]{:S(2)}) copy-start(bf16[32,8,256]{2,1,0:T(8,128)(2,1)} %x_ref.3) | copy-start | bytes 393220
  3.6 7.3 %copy-start.5 = (bf16[256,32]{0,1:T(8,128)(2,1)S(1)}, bf16[256,32]{0,1:T(8,128)(2,1)}, u32[]{:S(2)}) copy-start(bf16[256,32]{0,1:T(8,128)(2,1)} %param.23) | copy-start | bytes 49156
  3.6 7.3 %copy-start.6 = (bf16[256,32]{0,1:T(8,128)(2,1)S(1)}, bf16[256,32]{0,1:T(8,128)(2,1)}, u32[]{:S(2)}) copy-start(bf16[256,32]{0,1:T(8,128)(2,1)} %param.24) | copy-start | bytes 49156
  3.6 19.0 %all-to-all-start = ((bf16[32,5,8,128]{3,2,1,0:T(8,128)(2,1)}), bf16[32,5,8,128]{3,2,1,0:T(8,128)(2,1)S(1)}, u32[]{:S(2)}, u32[]{:S(2)}) async-start(bf16[32,5,8,128]{3,2,1,0:T(8,128)(2,1)} %get-tuple-element.8), calls=%async_computation | async-start | bytes 655360 | tf_op jit(solution)/shard_map/all_to_all | solution.py:398
  22.6 16.5 %copy-start.12 = (bf16[128,256]{1,0:T(8,128)(2,1)S(1)}, bf16[128,256]{1,0:T(8,128)(2,1)}, u32[]{:S(2)}) copy-start(bf16[128,256]{1,0:T(8,128)(2,1)} %param.18) | copy-start | bytes 196612
  22.6 15.5 %all-to-all-start.1 = ((bf16[32,6,8,128]{3,2,1,0:T(8,128)(2,1)}), bf16[32,6,8,128]{3,2,1,0:T(8,128)(2,1)S(1)}, u32[]{:S(2)}, u32[]{:S(2)}) async-start(bf16[32,6,8,128]{3,2,1,0:T(8,128)(2,1)} %get-tuple-element.10), calls=%async_computation.1 | async-start | bytes 786432 | tf_op jit(solution)/shard_map/all_to_all | solution.py:398
  25.4 15.2 %copy-start.9 = (bf16[256,4,128]{2,1,0:T(4,128)(2,1)S(1)}, bf16[256,4,128]{2,1,0:T(4,128)(2,1)}, u32[]{:S(2)}) copy-start(bf16[256,4,128]{2,1,0:T(4,128)(2,1)} %param.17) | copy-start | bytes 786436
  25.4 18.9 %collective-permute-start = (bf16[32,5,8,128]{3,2,1,0:T(8,128)(2,1)S(1)}, bf16[32,5,8,128]{3,2,1,0:T(8,128)(2,1)S(1)}, u32[]{:S(2)}, u32[]{:S(2)}) collective-permute-start(bf16[32,5,8,128]{3,2,1,0:T(8,128)(2,1)S(1)} %all-to-all-done.own_bias_ref), channel_id=1, source_target_pairs={{0,2},{1,3},{2,0},{3,1},{4,6},{5,7},{6,4},{7,5},{8,10},{9,11},{10,... | collective-permute-start | bytes 983048 | tf_op jit(solution)/shard_map/ppermute | solution.py:395
  38.1 6.2 %collective-permute-start.3 = (bf16[32,2,8,128]{3,2,1,0:T(8,128)(2,1)S(1)}, bf16[32,2,8,128]{3,2,1,0:T(8,128)(2,1)S(1)}, u32[]{:S(2)}, u32[]{:S(2)}) collective-permute-start(bf16[32,2,8,128]{3,2,1,0:T(8,128)(2,1)S(1)} %slice.4.right0), channel_id=1, source_target_pairs={{0,4},{1,5},{2,6},{3,7},{4,0},{5,1},{6,2},{7,3},{8,12},{9,13},{10,... | collective-permute-start | bytes 393224 | tf_op jit(solution)/shard_map/ppermute | solution.py:395
  39.1 9.9 %collective-permute-start.1 = (bf16[128,256]{1,0:T(8,128)(2,1)S(1)}, bf16[128,256]{1,0:T(8,128)(2,1)S(1)}, u32[]{:S(2)}, u32[]{:S(2)}) collective-permute-start(bf16[128,256]{1,0:T(8,128)(2,1)S(1)} %copy-done.12), channel_id=1, source_target_pairs={{0,1},{1,0},{2,3},{3,2},{4,5},{5,4},{6,7},{7,6},{8,9},{9,8},{10,11... | collective-permute-start | bytes 196616 | tf_op jit(solution)/shard_map/ppermute | solution.py:395
  40.6 1.0 %copy-start.10 = (bf16[1024,128]{1,0:T(8,128)(2,1)S(1)}, bf16[1024,128]{1,0:T(8,128)(2,1)}, u32[]{:S(2)}) copy-start(bf16[1024,128]{1,0:T(8,128)(2,1)} %param.25) | copy-start | bytes 786436
  41.6 0.9 %copy-start.11 = (bf16[256,2,256]{2,1,0:T(2,128)(2,1)S(1)}, bf16[256,2,256]{2,1,0:T(2,128)(2,1)}, u32[]{:S(2)}) copy-start(bf16[256,2,256]{2,1,0:T(2,128)(2,1)} %param.21) | copy-start | bytes 786436
  42.5 6.5 %collective-permute-start.2 = (bf16[32,2,8,128]{3,2,1,0:T(8,128)(2,1)S(1)}, bf16[32,2,8,128]{3,2,1,0:T(8,128)(2,1)S(1)}, u32[]{:S(2)}, u32[]{:S(2)}) collective-permute-start(bf16[32,2,8,128]{3,2,1,0:T(8,128)(2,1)S(1)} %slice.4.right0), channel_id=1, source_target_pairs={{0,2},{1,3},{2,0},{3,1},{4,6},{5,7},{6,4},{7,5},{8,10},{9,11},{10,... | collective-permute-start | bytes 393224 | tf_op jit(solution)/shard_map/ppermute | solution.py:395
  44.3 4.7 %collective-permute-start.4 = (bf16[32,2,8,128]{3,2,1,0:T(8,128)(2,1)S(1)}, bf16[32,2,8,128]{3,2,1,0:T(8,128)(2,1)S(1)}, u32[]{:S(2)}, u32[]{:S(2)}) collective-permute-start(bf16[32,2,8,128]{3,2,1,0:T(8,128)(2,1)S(1)} %collective-permute-done.3.right2), channel_id=1, source_target_pairs={{0,2},{1,3},{2,0},{3,1},{4,6},{5,7},{6,4},{7,5},{8,10},{9,11},{10,... | collective-permute-start | bytes 393224 | tf_op jit(solution)/shard_map/ppermute | solution.py:395
  46.4 11.2 %all-to-all-start.2 = ((bf16[32,2,8,128]{3,2,1,0:T(8,128)(2,1)}), bf16[32,2,8,128]{3,2,1,0:T(8,128)(2,1)S(1)}, u32[]{:S(2)}, u32[]{:S(2)}) async-start(bf16[32,2,8,128]{3,2,1,0:T(8,128)(2,1)} %get-tuple-element.11), calls=%async_computation.2 | async-start | bytes 262144 | tf_op jit(solution)/shard_map/all_to_all | solution.py:398
  49.0 8.6 %copy-start.1 = (bf16[256,256]{1,0:T(8,128)(2,1)S(1)}, bf16[256,256]{1,0:T(8,128)(2,1)}, u32[]{:S(2)}) copy-start(bf16[256,256]{1,0:T(8,128)(2,1)} %query_w_ref.1) | copy-start | bytes 393220
  49.1 8.6 %copy-start.2 = (bf16[256,256]{1,0:T(8,128)(2,1)S(1)}, bf16[256,256]{1,0:T(8,128)(2,1)}, u32[]{:S(2)}) copy-start(bf16[256,256]{1,0:T(8,128)(2,1)} %key_w_ref.1) | copy-start | bytes 393220
  49.1 8.6 %copy-start.3 = (bf16[256,256]{1,0:T(8,128)(2,1)S(1)}, bf16[256,256]{1,0:T(8,128)(2,1)}, u32[]{:S(2)}) copy-start(bf16[256,256]{1,0:T(8,128)(2,1)} %out_w_ref.1) | copy-start | bytes 393220

commit v5 on v4

--- a/solution.py
+++ b/solution.py
@@ -159,34 +159,14 @@
                 rows_ref[target, sequences_here * halves + slot] = result
 
 
-def row_kernel(
-    sizes, place_ref, own_bias_ref, other_bias_ref, rows_ref, weight_ref,
-    mix_ref, keep_all_ref, query_s, key_s, value_s, gate_s,
-):
-    groups, sequences_here, row_tiles, column_tiles = sizes
-    blocks, tiles, residues, _ = rows_ref.shape
-    residues_overall = blocks * residues
-    halves = weight_ref.shape[1] // LANES
-    head_lanes = weight_ref.shape[2]
+def attend_half(
+    sizes, place_ref, bias_ref, key_keep_ref, query_ref, key_ref, value_ref, other, block_rows,
+    finish,
+):
+    groups, row_tiles, column_tiles = sizes
+    sequences_here, residues_overall, head_lanes = query_ref.shape
     half_heads = head_lanes // PER_SPLIT_DIM // 2
-    query_factor = PER_SPLIT_DIM ** (-0.5)
-    block_rows = min(residues_overall, 256)
-    part = quotient(place_ref[0], groups)
-    core = part & 1
-
-    for own in range(sequences_here):
-        normed = jnp.concatenate(
-            [flat_rows(rows_ref[:, own * halves + half]) for half in range(halves)], axis=1
-        )
-        query_s[own] = (matmul(normed, weight_ref[0]) * query_factor).astype(BF16)
-        key_s[own] = matmul(normed, weight_ref[1]).astype(BF16)
-        value_s[own] = matmul(normed, weight_ref[2]).astype(BF16)
-        gate_s[own] = jax.nn.sigmoid(matmul(normed, weight_ref[3]))
-
-    keep_all = flat_rows(own_bias_ref[:, half_heads * row_tiles * column_tiles])
-    keep_all_ref[...] = keep_all
-    chosen = one_hot(lanes_of((8, LANES)) == part * sequences_here + rows_of((8, LANES)))
-    key_keep = matmul_nt(chosen, keep_all)
+    side = (quotient(place_ref[0], groups) & 1) ^ other
 
     def attend(block):
         start = block * block_rows
@@ -194,26 +174,25 @@
         head_of = quotient(lanes_of((residues_overall, head_lanes)), PER_SPLIT_DIM)
         query_head = quotient(lanes_of((block_rows, head_lanes)), PER_SPLIT_DIM)
         biases = []
-        for bias_ref in (own_bias_ref, other_bias_ref):
-            for head in range(half_heads):
-                columns = []
-                for group in range(groups):
-                    for column in range(column_tiles):
-                        pieces = []
-                        for at in range(parts):
-                            for row in range(row_tiles):
-                                slot = (head * row_tiles + row) * column_tiles + column
-                                source = (block * parts + at) * groups + group
-                                pieces.append(bias_ref[source, slot].astype(F32))
-                        columns.append(jnp.concatenate(pieces, axis=0))
-                biases.append(jnp.concatenate(columns, axis=1))
+        for head in range(half_heads):
+            columns = []
+            for group in range(groups):
+                for column in range(column_tiles):
+                    pieces = []
+                    for at in range(parts):
+                        for row in range(row_tiles):
+                            slot = (head * row_tiles + row) * column_tiles + column
+                            source = (block * parts + at) * groups + group
+                            pieces.append(bias_ref[source, slot].astype(F32))
+                    columns.append(jnp.concatenate(pieces, axis=0))
+            biases.append(jnp.concatenate(columns, axis=1))
         for own in range(sequences_here):
-            queries = query_s[own, pl.ds(start, block_rows), :]
-            keys, values = key_s[own], value_s[own]
-            keep_row = key_keep[own : own + 1, :] > 0.5
+            queries = query_ref[own, pl.ds(start, block_rows), :]
+            keys, values = key_ref[own], value_ref[own]
+            keep_row = key_keep_ref[own : own + 1, :] > 0.5
             total = jnp.zeros((block_rows, 2 * head_lanes), F32)
-            for at in range(2 * half_heads):
-                head = (core ^ (at // half_heads)) * half_heads + at % half_heads
+            for at in range(half_heads):
+                head = side * half_heads + at
                 query_part = jnp.where(query_head == head, queries, jnp.zeros_like(queries))
                 scores = matmul_nt(query_part, keys) + biases[at]
                 scores = jnp.where(keep_row, scores, MASKED)
@@ -224,16 +203,71 @@
                 total = total + matmul(
                     weights, jnp.concatenate([value_part, one_hot(mine)], axis=1)
                 )
-            mixed = total[:, :head_lanes] / total[:, head_lanes:]
-            mixed = mixed * gate_s[own, pl.ds(start, block_rows), :]
-            mix_ref[pl.ds(block * (block_rows // residues), block_rows // residues), own] = (
-                mixed.reshape(block_rows // residues, residues, head_lanes).astype(BF16)
-            )
+            here = quotient(query_head, half_heads) == side
+            mixed = total[:, :head_lanes] / jnp.where(here, total[:, head_lanes:], 1.0)
+            finish(block, own, start, mixed)
 
     if residues_overall == block_rows:
         attend(0)
     else:
         pl.loop(0, residues_overall // block_rows)(attend)
+
+
+def first_row_kernel(
+    sizes, place_ref, bias_ref, rows_ref, weight_ref,
+    part_ref, keep_all_ref, key_keep_ref, query_ref, key_ref, value_ref, gate_ref,
+):
+    groups, row_tiles, column_tiles = sizes
+    sequences_here = query_ref.shape[0]
+    halves = weight_ref.shape[1] // LANES
+    half_heads = weight_ref.shape[2] // PER_SPLIT_DIM // 2
+    query_factor = PER_SPLIT_DIM ** (-0.5)
+    for own in range(sequences_here):
+        normed = jnp.concatenate(
+            [flat_rows(rows_ref[:, own * halves + half]) for half in range(halves)], axis=1
+        )
+        query_ref[own] = (matmul(normed, weight_ref[0]) * query_factor).astype(BF16)
+        key_ref[own] = matmul(normed, weight_ref[1]).astype(BF16)
+        value_ref[own] = matmul(normed, weight_ref[2]).astype(BF16)
+        gate_ref[own] = jax.nn.sigmoid(matmul(normed, weight_ref[3]))
+
+    keep_all = flat_rows(bias_ref[:, half_heads * row_tiles * column_tiles])
+    keep_all_ref[...] = keep_all
+    part = quotient(place_ref[0], groups)
+    chosen = one_hot(lanes_of((8, LANES)) == part * sequences_here + rows_of((8, LANES)))
+    key_keep_ref[...] = matmul_nt(chosen, keep_all)
+    block_rows = min(query_ref.shape[1], 256)
+
+    def finish(block, own, start, mixed):
+        part_ref[own, pl.ds(start, block_rows), :] = mixed
+
+    attend_half(
+        sizes, place_ref, bias_ref, key_keep_ref, query_ref, key_ref, value_ref, 0, block_rows,
+        finish,
+    )
+
+
+def second_row_kernel(
+    sizes, place_ref, bias_ref, rows_ref, part_ref, key_keep_ref, query_ref, key_ref, value_ref,
+    gate_ref, mix_ref, right_ref,
+):
+    _, _, residues, head_lanes = mix_ref.shape
+    block_rows = min(query_ref.shape[1], 256)
+    count = block_rows // residues
+
+    def finish(block, own, start, mixed):
+        rows = pl.ds(start, block_rows)
+        mixed = (part_ref[own, rows, :] + mixed) * gate_ref[own, rows, :]
+        mix_ref[pl.ds(block * count, count), own] = mixed.reshape(
+            count, residues, head_lanes
+        ).astype(BF16)
+
+    attend_half(
+        sizes, place_ref, bias_ref, key_keep_ref, query_ref, key_ref, value_ref, 1, block_rows,
+        finish,
+    )
+    tiles = right_ref.shape[1]
+    right_ref[...] = rows_ref[:, rows_ref.shape[1] - tiles :]
 
 
 def outer_kernel(
@@ -410,9 +444,9 @@
         ],
         micros=1,
         fetch=True,
+        mib=62,
     )
     own_bias = to_all(bias_out)
-    other_bias = exchange(own_bias, groups)
     row_out_weight = jnp.stack(
         [horizontal_final_matrix]
         + [exchange(horizontal_final_matrix, relative) for relative in range(1, groups)]
@@ -430,28 +464,45 @@
         mib=56 if large else 32,
     )
     rows_in = to_all(rows_out)
-    right = rows_in[:, row_slots:]
+    row_weight = horizontal_projection_matrix.transpose(1, 0, 2)
+    outer_weight = outer_output_weight.reshape(channels, channels, depth).transpose(1, 0, 2)
+    content_weight = vertical_content_sigmoid_matrix.transpose(1, 0, 2)
+    own_bias, rows_in, row_weight, outer_weight, content_weight, row_out_weight = (
+        lax.optimization_barrier(
+            (own_bias, rows_in, row_weight, outer_weight, content_weight, row_out_weight)
+        )
+    )
+    other_bias = exchange(own_bias, groups)
+
+    row_sizes = (groups, row_tiles, column_tiles)
+    here = (sequences_here, residues_overall, head_lanes)
+    part, keep_all, *projected = call(
+        functools.partial(first_row_kernel, row_sizes),
+        (
+            shape(here, F32),
+            shape((residues_overall, LANES), BF16),
+            shape((8, residues_overall), F32),
+            shape(here, BF16),
+            shape(here, BF16),
+            shape(here, BF16),
+            shape(here, F32),
+        ),
+        (place, own_bias, rows_in, row_weight),
+        scalars=1,
+        mib=60 if large else 32,
+    )
+    mix_out, right = call(
+        functools.partial(second_row_kernel, row_sizes),
+        (
+            shape((devices, sequences_here, residues, head_lanes), BF16),
+            shape((devices, right_tiles // 4, residues, LANES), BF16),
+        ),
+        (place, other_bias, rows_in, part, *projected),
+        scalars=1,
+        mib=60 if large else 32,
+    )
     right_across = exchange(right, 2 * groups)
     right_parts = (right, exchange(right, groups), right_across, exchange(right_across, groups))
-
-    mix_out, keep_all = call(
-        functools.partial(row_kernel, (groups, sequences_here, row_tiles, column_tiles)),
-        (
-            shape((devices, sequences_here, residues, head_lanes), BF16),
-            shape((residues_overall, LANES), BF16),
-        ),
-        (
-            place,
-            own_bias,
-            other_bias,
-            rows_in,
-            horizontal_projection_matrix.transpose(1, 0, 2),
-        ),
-        scratch=[pltpu.VMEM((sequences_here, residues_overall, head_lanes), BF16)] * 3
-        + [pltpu.VMEM((sequences_here, residues_overall, head_lanes), F32)],
-        scalars=1,
-        mib=60 if large else 32,
-    )
     mix_in = to_all(mix_out)
 
     pairwise_update = call(
@@ -463,7 +514,7 @@
             *right_parts,
             left,
             keep,
-            outer_output_weight.reshape(channels, channels, depth).transpose(1, 0, 2),
+            outer_weight,
         ),
         scratch=[pltpu.VMEM((residues, channels * sequences, depth), BF16)],
         scalars=1,
@@ -481,7 +532,7 @@
             row_out_weight,
             column_query_weight,
             column_key_weight,
-            vertical_content_sigmoid_matrix.transpose(1, 0, 2),
+            content_weight,
             vertical_final_matrix,
         ),
         scalars=1,

time: 60.9 us -> 56.9 us (0.934)
  waiting for transfers between devices: 29.5 us -> 25.2 us
  local copies, waits for them, and re-layouts: 4.07 us -> 1.7 us
  starting transfers between devices: 15.4 us -> 17.1 us
  Pallas kernels: 10.6 us -> 11.7 us
    all_to_all x3, waiting for transfers between devices: 27.8 us -> 16.2 us  [to_all(): return lax.all_to_all(value, both, split_axis=0, concat_axis=0, tiled=True)]
    ppermute x5, waiting for transfers between devices: 1.68 us -> 8.99 us  [exchange(): return lax.ppermute(value, both, [(at, at ^ mask) for at in range(devices)])]
    unnamed x28 -> x24, local copies, waits for them, and re-layouts: 3.96 us -> 1.59 us
    ppermute x5, starting transfers between devices: 2.81 us -> 4.31 us  [exchange(): return lax.ppermute(value, both, [(at, at ^ mask) for at in range(devices)])]
    pallas_call x5 -> x6, Pallas kernels: 10.6 us -> 11.7 us  [call(): pl.pallas_call(kernel, out_shape=outs, in_specs=[smem] * scalars + [read]...]
  transfers between devices with their start and end apart: 8 -> 8, of which waited for: 4 -> 6; matrix products, arithmetic and copies ran while one was open for 0% -> 0% of each run, Pallas kernels for 12% -> 12%
where the time goes in v5:
time: 56.9 us; the launch traced here: 56.4 us
  waiting for transfers between devices  25.2 us (44%)
  starting transfers between devices  17.1 us (30%)
  Pallas kernels  11.7 us (21%)
  local copies, waits for them, and re-layouts  1.7 us (3%)
  between operations  0.79 us (1%)
    all_to_all x3, waiting for transfers between devices, to_all(): return lax.all_to_all(value, both, split_axis=0, concat_axis=0, tiled=True)  16.2 us
    all_to_all x3, starting transfers between devices, to_all(): return lax.all_to_all(value, both, split_axis=0, concat_axis=0, tiled=True)  12.7 us
    pallas_call x6, Pallas kernels, call(): pl.pallas_call(kernel, out_shape=outs, in_specs=[smem] * scalars + [read]...  11.7 us
    ppermute x5, waiting for transfers between devices, exchange(): return lax.ppermute(value, both, [(at, at ^ mask) for at in range(devices)])  8.99 us
    ppermute x5, starting transfers between devices, exchange(): return lax.ppermute(value, both, [(at, at ^ mask) for at in range(devices)])  4.31 us
    unnamed x24, local copies, waits for them, and re-layouts  1.59 us
  transfers between devices with their start and end apart: 8, of which 6 were waited for; matrix products, arithmetic and copies ran while one was open for 0% of the time, Pallas kernels for 12%

profile of v5, /device:TPU:0, one launch (start us, length us, event | category | flops | bytes accessed | tf_op | source)
XLA Modules:
  0.0 56.4 jit_solution(9502179364831243317)
XLA Ops:
  0.6 1.6 %shard_map.140 = (bf16[32,5,8,128]{3,2,1,0:T(8,128)(2,1)}, f32[8,128]{1,0:T(8,128)}) custom-call(s32[8,32]{1,0:T(8,128)} %bitcast.27, s32[1,32]{1,0:T(1,128)} %bitcast.28, bf16[8,16,128]{2,1,0:T(8,128)(2,1)} %bias_hbm.1), custom_call_target="tpu_custom_call" | custom-call | flops 1000000000 | bytes 1000000 | tf_op jit(solution)/shard_map/pallas_call | solution.py:385
  2.2 0.0 copy-start
  2.2 0.0 copy-start.4
  2.2 0.0 copy-start.5
  2.2 7.3 %all-to-all-start = ((bf16[32,5,8,128]{3,2,1,0:T(8,128)(2,1)}), bf16[32,5,8,128]{3,2,1,0:T(8,128)(2,1)S(1)}, u32[]{:S(2)}, u32[]{:S(2)}) async-start(bf16[32,5,8,128]{3,2,1,0:T(8,128)(2,1)} %get-tuple-element.21), calls=%async_computation | async-start | bytes 655360 | tf_op jit(solution)/shard_map/all_to_all | solution.py:432
  9.5 0.0 copy-start.6
  9.6 0.0 copy-done
  9.6 0.0 copy-done.4
  9.6 0.0 copy-done.5
  9.6 0.6 %copy-done.6 = f32[8,128]{1,0:T(8,128)S(1)} copy-done((f32[8,128]{1,0:T(8,128)S(1)}, f32[8,128]{1,0:T(8,128)}, u32[]{:S(2)}) %copy-start.6) | copy-done | bytes 4120
  10.2 2.7 %shard_map.141 = (bf16[32,6,8,128]{3,2,1,0:T(8,128)(2,1)}, bf16[256,32]{1,0:T(8,128)(2,1)S(1)}) custom-call(bf16[32,8,256]{2,1,0:T(8,128)(2,1)S(1)} %copy-done, f32[8,128]{1,0:T(8,128)S(1)} %copy-done.6, bf16[32,256]{1,0:T(8,128)(2,1)S(1)} %bitcast.22, bf16[32,256]{1,0:T(8,128)(2,1)S(1)} %bitcast.23), custom_call_target="tpu_custom_call" | custom-call | flops 2000000000 | bytes 2000000 | tf_op jit(solution)/shard_map/pallas_call | solution.py:385
  12.9 8.3 %all-to-all-done.bias_ref = bf16[32,5,8,128]{3,2,1,0:T(8,128)(2,1)S(1)} async-done(((bf16[32,5,8,128]{3,2,1,0:T(8,128)(2,1)}), bf16[32,5,8,128]{3,2,1,0:T(8,128)(2,1)S(1)}, u32[]{:S(2)}, u32[]{:S(2)}) %all-to-all-start) | async-done | bytes 327712 | tf_op jit(solution)/shard_map/all_to_all | solution.py:432
  21.3 0.0 copy-start.10
  21.3 0.0 copy-start.7
  21.3 2.7 %all-to-all-start.1 = ((bf16[32,6,8,128]{3,2,1,0:T(8,128)(2,1)}), bf16[32,6,8,128]{3,2,1,0:T(8,128)(2,1)S(1)}, u32[]{:S(2)}, u32[]{:S(2)}) async-start(bf16[32,6,8,128]{3,2,1,0:T(8,128)(2,1)} %get-tuple-element.23), calls=%async_computation.1 | async-start | bytes 786432 | tf_op jit(solution)/shard_map/all_to_all | solution.py:432
  24.0 0.0 copy-done.10
  24.0 0.0 copy-start.8
  24.0 1.8 %collective-permute-start = (bf16[128,256]{1,0:T(8,128)(2,1)S(1)}, bf16[128,256]{1,0:T(8,128)(2,1)S(1)}, u32[]{:S(2)}, u32[]{:S(2)}) collective-permute-start(bf16[128,256]{1,0:T(8,128)(2,1)S(1)} %copy-done.10), channel_id=1, source_target_pairs={{0,1},{1,0},{2,3},{3,2},{4,5},{5,4},{6,7},{7,6},{8,9},{9,8},{10,11... | collective-permute-start | bytes 196616 | tf_op jit(solution)/shard_map/ppermute | solution.py:429
  25.8 0.0 copy-done.7
  25.9 0.0 copy-done.8
  25.9 0.0 copy-start.9
  25.9 0.1 copy.24
  26.0 0.8 %copy-done.9 = bf16[256,4,128]{2,1,0:T(4,128)(2,1)S(1)} copy-done((bf16[256,4,128]{2,1,0:T(4,128)(2,1)S(1)}, bf16[256,4,128]{2,1,0:T(4,128)(2,1)}, u32[]{:S(2)}) %copy-start.9) | copy-done | bytes 262168
  26.9 3.7 %collective-permute-done = bf16[128,256]{1,0:T(8,128)(2,1)S(1)} collective-permute-done((bf16[128,256]{1,0:T(8,128)(2,1)S(1)}, bf16[128,256]{1,0:T(8,128)(2,1)S(1)}, u32[]{:S(2)}, u32[]{:S(2)}) %collective-permute-start) | collective-permute-done | bytes 65568 | tf_op jit(solution)/shard_map/ppermute | solution.py:429
  30.6 6.1 %all-to-all-done.1.rows_ref = bf16[32,6,8,128]{3,2,1,0:T(8,128)(2,1)S(1)} async-done(((bf16[32,6,8,128]{3,2,1,0:T(8,128)(2,1)}), bf16[32,6,8,128]{3,2,1,0:T(8,128)(2,1)S(1)}, u32[]{:S(2)}, u32[]{:S(2)}) %all-to-all-start.1) | async-done | bytes 393248 | tf_op jit(solution)/shard_map/all_to_all | solution.py:432
  36.8 0.7 %collective-permute-start.1 = (bf16[32,5,8,128]{3,2,1,0:T(8,128)(2,1)S(1)}, bf16[32,5,8,128]{3,2,1,0:T(8,128)(2,1)S(1)}, u32[]{:S(2)}, u32[]{:S(2)}) collective-permute-start(bf16[32,5,8,128]{3,2,1,0:T(8,128)(2,1)S(1)} %all-to-all-done.bias_ref), channel_id=1, source_target_pairs={{0,2},{1,3},{2,0},{3,1},{4,6},{5,7},{6,4},{7,5},{8,10},{9,11},{10,... | collective-permute-start | bytes 983048 | tf_op jit(solution)/shard_map/ppermute | solution.py:429
  37.4 1.1 %shard_map.142 = (f32[2,256,128]{2,1,0:T(8,128)S(1)}, bf16[256,128]{1,0:T(8,128)(2,1)S(1)}, f32[8,256]{1,0:T(8,128)S(1)}, bf16[2,256,128]{2,1,0:T(8,128)(2,1)S(1...) custom-call(s32[1]{0:T(128)} %bitcast.place_ref, ...), custom_call_target="tpu_custom_call" | custom-call | flops 2000000000 | bytes 2000000 | tf_op jit(solution)/shard_map/pallas_call | solution.py:385
  38.6 0.1 collective-permute-done.1.bias_ref
  38.7 0.0 copy-start.3
  38.7 1.4 %shard_map.143 = (bf16[32,2,8,128]{3,2,1,0:T(8,128)(2,1)}, bf16[32,2,8,128]{3,2,1,0:T(8,128)(2,1)S(1)}) custom-call(s32[1]{0:T(128)} %bitcast.place_ref, bf16[32,5,8,128]{3,2,1,0:T(8,128)(2,1)S(1)} %collective-permute-done.1.bias_ref, bf16[32,6,8,128]{3,2,1,0:T(8,128)(2,1)S(1)} %all-to-all-done.1.rows_ref, f32[2,256,128]{2,1,0:T(8,128)S(1)} %get-tuple-element.27.part_ref, ...), custom_call_target="tpu_custom_call" | custom-call | flops 2000000000 | bytes 2000000 | tf_op jit(solution)/shard_map/pallas_call | solution.py:385
  40.1 0.0 copy-start.1
  40.1 0.0 copy-start.2
  40.1 2.7 %all-to-all-start.2 = ((bf16[32,2,8,128]{3,2,1,0:T(8,128)(2,1)}), bf16[32,2,8,128]{3,2,1,0:T(8,128)(2,1)S(1)}, u32[]{:S(2)}, u32[]{:S(2)}) async-start(bf16[32,2,8,128]{3,2,1,0:T(8,128)(2,1)} %get-tuple-element.33), calls=%async_computation.2 | async-start | bytes 262144 | tf_op jit(solution)/shard_map/all_to_all | solution.py:432
  42.8 1.8 %collective-permute-start.3 = (bf16[32,2,8,128]{3,2,1,0:T(8,128)(2,1)S(1)}, bf16[32,2,8,128]{3,2,1,0:T(8,128)(2,1)S(1)}, u32[]{:S(2)}, u32[]{:S(2)}) collective-permute-start(bf16[32,2,8,128]{3,2,1,0:T(8,128)(2,1)S(1)} %get-tuple-element.37.right0), channel_id=1, source_target_pairs={{0,4},{1,5},{2,6},{3,7},{4,0},{5,1},{6,2},{7,3},{8,12},{9,13},{10,... | collective-permute-start | bytes 393224 | tf_op jit(solution)/shard_map/ppermute | solution.py:429
  44.6 0.0 collective-permute-start.2
  44.6 5.1 %collective-permute-done.3.right2 = bf16[32,2,8,128]{3,2,1,0:T(8,128)(2,1)S(1)} collective-permute-done((bf16[32,2,8,128]{3,2,1,0:T(8,128)(2,1)S(1)}, bf16[32,2,8,128]{3,2,1,0:T(8,128)(2,1)S(1)}, u32[]{:S(2)}, u32[]{:S(2)}) %collective-permute-start.3) | collective-permute-done | bytes 131104 | tf_op jit(solution)/shard_map/ppermute | solution.py:429
  49.7 0.0 collective-permute-start.4
  49.7 1.7 %all-to-all-done.2 = bf16[32,2,8,128]{3,2,1,0:T(8,128)(2,1)S(1)} async-done(((bf16[32,2,8,128]{3,2,1,0:T(8,128)(2,1)}), bf16[32,2,8,128]{3,2,1,0:T(8,128)(2,1)S(1)}, u32[]{:S(2)}, u32[]{:S(2)}) %all-to-all-start.2) | async-done | bytes 131104 | tf_op jit(solution)/shard_map/all_to_all | solution.py:432
  51.4 0.0 copy-done.3
  51.4 0.0 copy-done.1
  51.4 0.0 copy-done.2
  51.4 2.8 %shard_map.144 = bf16[32,8,256]{2,1,0:T(8,128)(2,1)} custom-call(s32[1]{0:T(128)} %bitcast.place_ref, bf16[32,8,256]{2,1,0:T(8,128)(2,1)S(1)} %copy-done, bf16[16,2,2,8,128]{4,3,2,1,0:T(8,128)(2,1)S(1)} %bitcast.21, f32[8,128]{1,0:T(8,128)S(1)} %copy-done.6, bf16[2,128,256]{2,1,0:T(8,128)(2,1)S(1)} %pad_maximum_fusion.row_out_ref, ...), custom_call_target="tpu_custom_call" | custom-call | flops 3000000000 | bytes 3000000 | tf_op jit(solution)/shard_map/pallas_call | solution.py:385
  54.3 0.0 collective-permute-done.2.right1
  54.3 0.0 collective-permute-done.4.right3
  54.3 2.2 %shard_map.145 = bf16[8,256,128]{2,1,0:T(8,128)(2,1)} custom-call(s32[1]{0:T(128)} %bitcast.place_ref, bf16[256,128]{1,0:T(8,128)(2,1)S(1)} %get-tuple-element.36.keep_all_ref, bf16[32,2,8,128]{3,2,1,0:T(8,128)(2,1)S(1)} %get-tuple-element.37.right0, bf16[32,2,8,128]{3,2,1,0:T(8,128)(2,1)S(1)} %collective-permute-done.2.right1, ...), custom_call_target="tpu_custom_call" | custom-call | flops 2000000000 | bytes 2000000 | tf_op jit(solution)/shard_map/pallas_call | solution.py:385
  (3 shorter events, 0.1 us)
Async XLA Ops:
  2.2 7.4 %copy-start = (bf16[32,8,256]{2,1,0:T(8,128)(2,1)S(1)}, bf16[32,8,256]{2,1,0:T(8,128)(2,1)}, u32[]{:S(2)}) copy-start(bf16[32,8,256]{2,1,0:T(8,128)(2,1)} %x_ref.3) | copy-start | bytes 393220
  2.2 7.4 %copy-start.4 = (bf16[256,32]{0,1:T(8,128)(2,1)S(1)}, bf16[256,32]{0,1:T(8,128)(2,1)}, u32[]{:S(2)}) copy-start(bf16[256,32]{0,1:T(8,128)(2,1)} %param.23) | copy-start | bytes 49156
  2.2 7.4 %copy-start.5 = (bf16[256,32]{0,1:T(8,128)(2,1)S(1)}, bf16[256,32]{0,1:T(8,128)(2,1)}, u32[]{:S(2)}) copy-start(bf16[256,32]{0,1:T(8,128)(2,1)} %param.24) | copy-start | bytes 49156
  2.2 19.0 %all-to-all-start = ((bf16[32,5,8,128]{3,2,1,0:T(8,128)(2,1)}), bf16[32,5,8,128]{3,2,1,0:T(8,128)(2,1)S(1)}, u32[]{:S(2)}, u32[]{:S(2)}) async-start(bf16[32,5,8,128]{3,2,1,0:T(8,128)(2,1)} %get-tuple-element.21), calls=%async_computation | async-start | bytes 655360 | tf_op jit(solution)/shard_map/all_to_all | solution.py:432
  9.5 0.7 %copy-start.6 = (f32[8,128]{1,0:T(8,128)S(1)}, f32[8,128]{1,0:T(8,128)}, u32[]{:S(2)}) copy-start(f32[8,128]{1,0:T(8,128)} %get-tuple-element.22.keep_ref) | copy-start | bytes 12292
  21.3 2.7 %copy-start.10 = (bf16[128,256]{1,0:T(8,128)(2,1)S(1)}, bf16[128,256]{1,0:T(8,128)(2,1)}, u32[]{:S(2)}) copy-start(bf16[128,256]{1,0:T(8,128)(2,1)} %param.18) | copy-start | bytes 196612
  21.3 4.6 %copy-start.7 = (bf16[256,2,256]{2,1,0:T(2,128)(2,1)S(1)}, bf16[256,2,256]{2,1,0:T(2,128)(2,1)}, u32[]{:S(2)}) copy-start(bf16[256,2,256]{2,1,0:T(2,128)(2,1)} %param.21) | copy-start | bytes 786436
  21.3 15.5 %all-to-all-start.1 = ((bf16[32,6,8,128]{3,2,1,0:T(8,128)(2,1)}), bf16[32,6,8,128]{3,2,1,0:T(8,128)(2,1)S(1)}, u32[]{:S(2)}, u32[]{:S(2)}) async-start(bf16[32,6,8,128]{3,2,1,0:T(8,128)(2,1)} %get-tuple-element.23), calls=%async_computation.1 | async-start | bytes 786432 | tf_op jit(solution)/shard_map/all_to_all | solution.py:432
  24.0 1.8 %copy-start.8 = (bf16[1024,128]{1,0:T(8,128)(2,1)S(1)}, bf16[1024,128]{1,0:T(8,128)(2,1)}, u32[]{:S(2)}) copy-start(bf16[1024,128]{1,0:T(8,128)(2,1)} %param.25) | copy-start | bytes 786436
  24.0 6.6 %collective-permute-start = (bf16[128,256]{1,0:T(8,128)(2,1)S(1)}, bf16[128,256]{1,0:T(8,128)(2,1)S(1)}, u32[]{:S(2)}, u32[]{:S(2)}) collective-permute-start(bf16[128,256]{1,0:T(8,128)(2,1)S(1)} %copy-done.10), channel_id=1, source_target_pairs={{0,1},{1,0},{2,3},{3,2},{4,5},{5,4},{6,7},{7,6},{8,9},{9,8},{10,11... | collective-permute-start | bytes 196616 | tf_op jit(solution)/shard_map/ppermute | solution.py:429
  25.9 1.0 %copy-start.9 = (bf16[256,4,128]{2,1,0:T(4,128)(2,1)S(1)}, bf16[256,4,128]{2,1,0:T(4,128)(2,1)}, u32[]{:S(2)}) copy-start(bf16[256,4,128]{2,1,0:T(4,128)(2,1)} %param.17) | copy-start | bytes 786436
  36.8 1.9 %collective-permute-start.1 = (bf16[32,5,8,128]{3,2,1,0:T(8,128)(2,1)S(1)}, bf16[32,5,8,128]{3,2,1,0:T(8,128)(2,1)S(1)}, u32[]{:S(2)}, u32[]{:S(2)}) collective-permute-start(bf16[32,5,8,128]{3,2,1,0:T(8,128)(2,1)S(1)} %all-to-all-done.bias_ref), channel_id=1, source_target_pairs={{0,2},{1,3},{2,0},{3,1},{4,6},{5,7},{6,4},{7,5},{8,10},{9,11},{10,... | collective-permute-start | bytes 983048 | tf_op jit(solution)/shard_map/ppermute | solution.py:429
  38.7 12.7 %copy-start.3 = (bf16[256,256]{1,0:T(8,128)(2,1)S(1)}, bf16[256,256]{1,0:T(8,128)(2,1)}, u32[]{:S(2)}) copy-start(bf16[256,256]{1,0:T(8,128)(2,1)} %out_w_ref.1) | copy-start | bytes 393220
  40.1 11.4 %copy-start.1 = (bf16[256,256]{1,0:T(8,128)(2,1)S(1)}, bf16[256,256]{1,0:T(8,128)(2,1)}, u32[]{:S(2)}) copy-start(bf16[256,256]{1,0:T(8,128)(2,1)} %query_w_ref.1) | copy-start | bytes 393220
  40.1 11.4 %copy-start.2 = (bf16[256,256]{1,0:T(8,128)(2,1)S(1)}, bf16[256,256]{1,0:T(8,128)(2,1)}, u32[]{:S(2)}) copy-start(bf16[256,256]{1,0:T(8,128)(2,1)} %key_w_ref.1) | copy-start | bytes 393220
  40.1 11.3 %all-to-all-start.2 = ((bf16[32,2,8,128]{3,2,1,0:T(8,128)(2,1)}), bf16[32,2,8,128]{3,2,1,0:T(8,128)(2,1)S(1)}, u32[]{:S(2)}, u32[]{:S(2)}) async-start(bf16[32,2,8,128]{3,2,1,0:T(8,128)(2,1)} %get-tuple-element.33), calls=%async_computation.2 | async-start | bytes 262144 | tf_op jit(solution)/shard_map/all_to_all | solution.py:432
  42.8 6.9 %collective-permute-start.3 = (bf16[32,2,8,128]{3,2,1,0:T(8,128)(2,1)S(1)}, bf16[32,2,8,128]{3,2,1,0:T(8,128)(2,1)S(1)}, u32[]{:S(2)}, u32[]{:S(2)}) collective-permute-start(bf16[32,2,8,128]{3,2,1,0:T(8,128)(2,1)S(1)} %get-tuple-element.37.right0), channel_id=1, source_target_pairs={{0,4},{1,5},{2,6},{3,7},{4,0},{5,1},{6,2},{7,3},{8,12},{9,13},{10,... | collective-permute-start | bytes 393224 | tf_op jit(solution)/shard_map/ppermute | solution.py:429
  44.6 9.6 %collective-permute-start.2 = (bf16[32,2,8,128]{3,2,1,0:T(8,128)(2,1)S(1)}, bf16[32,2,8,128]{3,2,1,0:T(8,128)(2,1)S(1)}, u32[]{:S(2)}, u32[]{:S(2)}) collective-permute-start(bf16[32,2,8,128]{3,2,1,0:T(8,128)(2,1)S(1)} %get-tuple-element.37.right0), channel_id=1, source_target_pairs={{0,2},{1,3},{2,0},{3,1},{4,6},{5,7},{6,4},{7,5},{8,10},{9,11},{10,... | collective-permute-start | bytes 393224 | tf_op jit(solution)/shard_map/ppermute | solution.py:429
  49.7 4.5 %collective-permute-start.4 = (bf16[32,2,8,128]{3,2,1,0:T(8,128)(2,1)S(1)}, bf16[32,2,8,128]{3,2,1,0:T(8,128)(2,1)S(1)}, u32[]{:S(2)}, u32[]{:S(2)}) collective-permute-start(bf16[32,2,8,128]{3,2,1,0:T(8,128)(2,1)S(1)} %collective-permute-done.3.right2), channel_id=1, source_target_pairs={{0,2},{1,3},{2,0},{3,1},{4,6},{5,7},{6,4},{7,5},{8,10},{9,11},{10,... | collective-permute-start | bytes 393224 | tf_op jit(solution)/shard_map/ppermute | solution.py:429

commit v6 on v5

--- a/solution.py
+++ b/solution.py
@@ -68,50 +68,48 @@
     return heads // groups, bias_rows // 8, bias_columns // LANES
 
 
-def share_kernel(
-    groups, mask_hbm, present_hbm, bias_hbm, out_ref, keep_ref, mask_ref, present_ref, bias_ref,
-    sems,
-):
-    pairs = ((bias_hbm, bias_ref), (mask_hbm, mask_ref), (present_hbm, present_ref))
+def prepare_kernel(
+    sizes, bias_hbm, mask_hbm, present_hbm, x_hbm, left_w_hbm, right_w_hbm,
+    rows_ref, left_ref, keep_ref,
+    bias_ref, mask_ref, present_ref, x_ref, left_w_ref, right_w_ref, sems,
+):
+    groups, sequences_here = sizes
+    sources = (bias_hbm, mask_hbm, present_hbm, x_hbm, left_w_hbm, right_w_hbm)
+    targets = (bias_ref, mask_ref, present_ref, x_ref, left_w_ref, right_w_ref)
     copies = [
         pltpu.make_async_copy(source, target, sems.at[at])
-        for at, (source, target) in enumerate(pairs)
+        for at, (source, target) in enumerate(zip(sources, targets))
     ]
     for copy in copies:
         copy.start()
-    for copy in copies:
+    for copy in copies[:3]:
         copy.wait()
+    sequences, residues, width = x_ref.shape
+    total = sequences * residues
+    channels = left_w_ref.shape[0]
     heads_here, row_tiles, column_tiles = tile_count(bias_ref.shape, groups)
     half_heads = heads_here // 2
-    sequences = mask_ref.shape[1]
     keep = (mask_ref[...] * present_ref[...]).astype(F32)
-    if sequences < LANES:
-        keep = jnp.pad(keep, ((0, 0), (0, LANES - sequences)))
-    keep_ref[...] = keep
-    keep_tile = keep.astype(BF16)
-    for target in range(out_ref.shape[0]):
+    keep_padded = jnp.pad(keep, ((0, 0), (0, LANES - sequences))) if sequences < LANES else keep
+    keep_ref[...] = keep_padded
+    keep_tile = keep_padded.astype(BF16)
+    last = rows_ref.shape[1] - 1
+    for target in range(rows_ref.shape[0]):
         part, group = divmod(target, groups)
-        slot = 0
+        slot = last - half_heads * row_tiles * column_tiles
         for head in range(half_heads):
             for row in range(row_tiles):
                 for column in range(column_tiles):
-                    out_ref[target, slot] = bias_ref[
+                    rows_ref[target, slot] = bias_ref[
                         group * heads_here + part % 2 * half_heads + head,
                         row * 8 : (row + 1) * 8,
                         column * LANES : (column + 1) * LANES,
                     ]
                     slot += 1
-        out_ref[target, slot] = keep_tile
-
-
-def prepare_kernel(
-    sizes, x_ref, keep_ref, left_w_ref, right_w_ref, rows_ref, left_ref
-):
-    groups, sequences_here = sizes
-    sequences, residues, width = x_ref.shape
-    total = sequences * residues
-    channels = left_w_ref.shape[0]
-    keep = keep_ref[:, :sequences]
+        rows_ref[target, last] = keep_tile
+    for copy in copies[3:]:
+        copy.wait()
+
     normed = layer_normalize(x_ref[...].astype(F32).reshape(total, width))
     normed_tiles = normed.astype(F32).reshape(sequences, residues, width).astype(BF16)
     halves = width // LANES
@@ -160,8 +158,8 @@
 
 
 def attend_half(
-    sizes, place_ref, bias_ref, key_keep_ref, query_ref, key_ref, value_ref, other, block_rows,
-    finish,
+    sizes, place_ref, bias_ref, first_slot, key_keep_ref, query_ref, key_ref, value_ref, other,
+    block_rows, finish,
 ):
     groups, row_tiles, column_tiles = sizes
     sequences_here, residues_overall, head_lanes = query_ref.shape
@@ -182,6 +180,7 @@
                     for at in range(parts):
                         for row in range(row_tiles):
                             slot = (head * row_tiles + row) * column_tiles + column
+                            slot += first_slot
                             source = (block * parts + at) * groups + group
                             pieces.append(bias_ref[source, slot].astype(F32))
                     columns.append(jnp.concatenate(pieces, axis=0))
@@ -214,13 +213,12 @@
 
 
 def first_row_kernel(
-    sizes, place_ref, bias_ref, rows_ref, weight_ref,
-    part_ref, keep_all_ref, key_keep_ref, query_ref, key_ref, value_ref, gate_ref,
-):
-    groups, row_tiles, column_tiles = sizes
+    sizes, place_ref, rows_ref, weight_ref,
+    right_ref, part_ref, keep_all_ref, key_keep_ref, query_ref, key_ref, value_ref, gate_ref,
+):
+    groups = sizes[0]
     sequences_here = query_ref.shape[0]
     halves = weight_ref.shape[1] // LANES
-    half_heads = weight_ref.shape[2] // PER_SPLIT_DIM // 2
     query_factor = PER_SPLIT_DIM ** (-0.5)
     for own in range(sequences_here):
         normed = jnp.concatenate(
@@ -231,7 +229,10 @@
         value_ref[own] = matmul(normed, weight_ref[2]).astype(BF16)
         gate_ref[own] = jax.nn.sigmoid(matmul(normed, weight_ref[3]))
 
-    keep_all = flat_rows(bias_ref[:, half_heads * row_tiles * column_tiles])
+    first = sequences_here * halves
+    tiles = right_ref.shape[1]
+    right_ref[...] = rows_ref[:, first : first + tiles]
+    keep_all = flat_rows(rows_ref[:, rows_ref.shape[1] - 1])
     keep_all_ref[...] = keep_all
     part = quotient(place_ref[0], groups)
     chosen = one_hot(lanes_of((8, LANES)) == part * sequences_here + rows_of((8, LANES)))
@@ -242,14 +243,14 @@
         part_ref[own, pl.ds(start, block_rows), :] = mixed
 
     attend_half(
-        sizes, place_ref, bias_ref, key_keep_ref, query_ref, key_ref, value_ref, 0, block_rows,
-        finish,
+        sizes, place_ref, rows_ref, first + tiles, key_keep_ref, query_ref, key_ref, value_ref, 0,
+        block_rows, finish,
     )
 
 
 def second_row_kernel(
-    sizes, place_ref, bias_ref, rows_ref, part_ref, key_keep_ref, query_ref, key_ref, value_ref,
-    gate_ref, mix_ref, right_ref,
+    sizes, place_ref, swapped_ref, part_ref, key_keep_ref, query_ref, key_ref, value_ref,
+    gate_ref, mix_ref,
 ):
     _, _, residues, head_lanes = mix_ref.shape
     block_rows = min(query_ref.shape[1], 256)
@@ -262,12 +263,11 @@
             count, residues, head_lanes
         ).astype(BF16)
 
+    tiles = swapped_ref.shape[1] - head_lanes // PER_SPLIT_DIM // 2 * sizes[1] * sizes[2]
     attend_half(
-        sizes, place_ref, bias_ref, key_keep_ref, query_ref, key_ref, value_ref, 1, block_rows,
-        finish,
-    )
-    tiles = right_ref.shape[1]
-    right_ref[...] = rows_ref[:, rows_ref.shape[1] - tiles :]
+        sizes, place_ref, swapped_ref, tiles, key_keep_ref, query_ref, key_ref, value_ref, 1,
+        block_rows, finish,
+    )
 
 
 def outer_kernel(
@@ -294,7 +294,7 @@
         [
             flat_rows(right_ref[:, tile])
             for right_ref in (right0, right1, right2, right3)
-            for tile in range(right_ref.shape[1])
+            for tile in range(right0.shape[1])
         ],
         axis=1,
     )
@@ -431,22 +431,6 @@
     def to_all(value):
         return lax.all_to_all(value, both, split_axis=0, concat_axis=0, tiled=True)
 
-    half_tiles = heads_here // 2 * row_tiles * column_tiles
-    bias_out, keep = call(
-        functools.partial(share_kernel, groups),
-        (shape((devices, half_tiles + 1, 8, LANES), BF16), shape((8, LANES), F32)),
-        (alignment_mask.T, sequence_row_mask.reshape(1, sequences), pairwise_bias),
-        scratch=[
-            pltpu.VMEM((residues, sequences), jnp.int32),
-            pltpu.VMEM((1, sequences), jnp.int32),
-            pltpu.VMEM(pairwise_bias.shape, BF16),
-            pltpu.SemaphoreType.DMA((3,)),
-        ],
-        micros=1,
-        fetch=True,
-        mib=62,
-    )
-    own_bias = to_all(bias_out)
     row_out_weight = jnp.stack(
         [horizontal_final_matrix]
         + [exchange(horizontal_final_matrix, relative) for relative in range(1, groups)]
@@ -454,31 +438,46 @@
 
     right_tiles = channels * sequences // LANES
     row_slots = sequences_here * (width // LANES)
-    rows_out, left = call(
+    half_tiles = heads_here // 2 * row_tiles * column_tiles
+    operands = (
+        pairwise_bias,
+        alignment_mask.T,
+        sequence_row_mask.reshape(1, sequences),
+        homolog_activity,
+        first_operand_matrix.T,
+        second_operand_matrix.T,
+    )
+    rows_out, left, keep = call(
         functools.partial(prepare_kernel, (groups, sequences_here)),
         (
-            shape((devices, row_slots + right_tiles // 4, residues, LANES), BF16),
+            shape(
+                (devices, row_slots + right_tiles // 4 + half_tiles + 1, residues, LANES), BF16
+            ),
             shape((sequences * residues, channels), BF16),
+            shape((residues, LANES), F32),
         ),
-        (homolog_activity, keep, first_operand_matrix.T, second_operand_matrix.T),
-        mib=56 if large else 32,
+        operands,
+        scratch=[pltpu.VMEM(operand.shape, operand.dtype) for operand in operands]
+        + [pltpu.SemaphoreType.DMA((len(operands),))],
+        fetch=True,
+        mib=62,
     )
     rows_in = to_all(rows_out)
+
     row_weight = horizontal_projection_matrix.transpose(1, 0, 2)
     outer_weight = outer_output_weight.reshape(channels, channels, depth).transpose(1, 0, 2)
     content_weight = vertical_content_sigmoid_matrix.transpose(1, 0, 2)
-    own_bias, rows_in, row_weight, outer_weight, content_weight, row_out_weight = (
-        lax.optimization_barrier(
-            (own_bias, rows_in, row_weight, outer_weight, content_weight, row_out_weight)
-        )
-    )
-    other_bias = exchange(own_bias, groups)
+    rows_in, row_weight, outer_weight, content_weight, row_out_weight = lax.optimization_barrier(
+        (rows_in, row_weight, outer_weight, content_weight, row_out_weight)
+    )
+    swapped = exchange(rows_in[:, row_slots:-1], groups)
 
     row_sizes = (groups, row_tiles, column_tiles)
     here = (sequences_here, residues_overall, head_lanes)
-    part, keep_all, *projected = call(
+    right, part, keep_all, *projected = call(
         functools.partial(first_row_kernel, row_sizes),
         (
+            shape((devices, right_tiles // 4, residues, LANES), BF16),
             shape(here, F32),
             shape((residues_overall, LANES), BF16),
             shape((8, residues_overall), F32),
@@ -487,22 +486,18 @@
             shape(here, BF16),
             shape(here, F32),
         ),
-        (place, own_bias, rows_in, row_weight),
+        (place, rows_in, row_weight),
         scalars=1,
         mib=60 if large else 32,
     )
-    mix_out, right = call(
+    right_across = exchange(right, 2 * groups)
+    mix_out = call(
         functools.partial(second_row_kernel, row_sizes),
-        (
-            shape((devices, sequences_here, residues, head_lanes), BF16),
-            shape((devices, right_tiles // 4, residues, LANES), BF16),
-        ),
-        (place, other_bias, rows_in, part, *projected),
+        shape((devices, sequences_here, residues, head_lanes), BF16),
+        (place, swapped, part, *projected),
         scalars=1,
         mib=60 if large else 32,
     )
-    right_across = exchange(right, 2 * groups)
-    right_parts = (right, exchange(right, groups), right_across, exchange(right_across, groups))
     mix_in = to_all(mix_out)
 
     pairwise_update = call(
@@ -511,7 +506,10 @@
         (
             place,
             keep_all,
-            *right_parts,
+            right,
+            swapped,
+            right_across,
+            exchange(right_across, groups),
             left,
             keep,
             outer_weight,

time: 56.9 us -> 55.2 us (0.970)
  starting transfers between devices: 17.1 us -> 14.8 us
  waiting for transfers between devices: 25.2 us -> 26.1 us
    all_to_all x3 -> x2, starting transfers between devices: 12.7 us -> 10.8 us  [to_all(): return lax.all_to_all(value, both, split_axis=0, concat_axis=0, tiled=True)]
    all_to_all x3 -> x2, waiting for transfers between devices: 16.2 us -> 17.2 us  [to_all(): return lax.all_to_all(value, both, split_axis=0, concat_axis=0, tiled=True)]
    pallas_call x6 -> x5, Pallas kernels: 11.7 us -> 11.3 us  [call(): pl.pallas_call(kernel, out_shape=outs, in_specs=[smem] * scalars + [read]...]
    ppermute x5 -> x4, starting transfers between devices: 4.31 us -> 3.92 us  [exchange(): return lax.ppermute(value, both, [(at, at ^ mask) for at in range(devices)])]
    ppermute x5 -> x4, waiting for transfers between devices: 8.99 us -> 8.92 us  [exchange(): return lax.ppermute(value, both, [(at, at ^ mask) for at in range(devices)])]
    unnamed x24 -> x22, local copies, waits for them, and re-layouts: 1.59 us -> 1.66 us
  transfers between devices with their start and end apart: 8 -> 6, of which waited for: 6 -> 4; matrix products, arithmetic and copies ran while one was open for 0% -> 0% of each run, Pallas kernels for 12% -> 8%
where the time goes in v6:
time: 55.2 us; the launch traced here: 54.8 us
  waiting for transfers between devices  26.1 us (47%)
  starting transfers between devices  14.8 us (27%)
  Pallas kernels  11.3 us (20%)
  local copies, waits for them, and re-layouts  1.79 us (3%)
  between operations  0.78 us (1%)
    all_to_all x2, waiting for transfers between devices, to_all(): return lax.all_to_all(value, both, split_axis=0, concat_axis=0, tiled=True)  17.2 us
    pallas_call x5, Pallas kernels, call(): pl.pallas_call(kernel, out_shape=outs, in_specs=[smem] * scalars + [read]...  11.3 us
    all_to_all x2, starting transfers between devices, to_all(): return lax.all_to_all(value, both, split_axis=0, concat_axis=0, tiled=True)  10.8 us
    ppermute x4, waiting for transfers between devices, exchange(): return lax.ppermute(value, both, [(at, at ^ mask) for at in range(devices)])  8.92 us
    ppermute x4, starting transfers between devices, exchange(): return lax.ppermute(value, both, [(at, at ^ mask) for at in range(devices)])  3.92 us
    unnamed x22, local copies, waits for them, and re-layouts  1.66 us
  transfers between devices with their start and end apart: 6, of which 4 were waited for; matrix products, arithmetic and copies ran while one was open for 0% of the time, Pallas kernels for 8%

profile of v6, /device:TPU:0, one launch (start us, length us, event | category | flops | bytes accessed | tf_op | source)
XLA Modules:
  0.0 54.8 jit_solution(3988657552431489563)
XLA Ops:
  0.6 3.9 %shard_map.140 = (bf16[32,11,8,128]{3,2,1,0:T(8,128)(2,1)}, bf16[256,32]{1,0:T(8,128)(2,1)}, f32[8,128]{1,0:T(8,128)}) custom-call(bf16[8,16,128]{2,1,0:T(8,128)(2,1)} %bias_hbm.1, s32[8,32]{1,0:T(8,128)} %bitcast.27, s32[1,32]{1,0:T(1,128)} %bitcast.28, bf16[32,8,256]{2,1,0:T(8,128)(2,1)} %x_ref.1, bf16[32,256]{1,0:T(8,128)(2,1)} %bitcast.25, ...), custom_call_target="tpu_custom_call" | custom-call | flops 2000000000 | bytes 2000000 | tf_op jit(solution)/shard_map/pallas_call | solution.py:385
  4.5 0.0 copy-start.9
  4.5 0.0 copy-start.6
  4.5 7.3 %all-to-all-start = ((bf16[32,11,8,128]{3,2,1,0:T(8,128)(2,1)}), bf16[32,11,8,128]{3,2,1,0:T(8,128)(2,1)S(1)}, u32[]{:S(2)}, u32[]{:S(2)}) async-start(bf16[32,11,8,128]{3,2,1,0:T(8,128)(2,1)} %get-tuple-element.18), calls=%async_computation | async-start | bytes 1441792 | tf_op jit(solution)/shard_map/all_to_all | solution.py:432
  11.8 0.0 copy-done.9
  11.8 0.0 copy-start.7
  11.9 1.8 %collective-permute-start = (bf16[128,256]{1,0:T(8,128)(2,1)S(1)}, bf16[128,256]{1,0:T(8,128)(2,1)S(1)}, u32[]{:S(2)}, u32[]{:S(2)}) collective-permute-start(bf16[128,256]{1,0:T(8,128)(2,1)S(1)} %copy-done.9), channel_id=1, source_target_pairs={{0,1},{1,0},{2,3},{3,2},{4,5},{5,4},{6,7},{7,6},{8,9},{9,8},{10,11... | collective-permute-start | bytes 196616 | tf_op jit(solution)/shard_map/ppermute | solution.py:429
  13.7 0.0 copy-done.6
  13.7 0.0 copy-done.7
  13.7 0.0 copy-start.8
  13.8 0.9 %copy-done.8 = bf16[1024,128]{1,0:T(8,128)(2,1)S(1)} copy-done((bf16[1024,128]{1,0:T(8,128)(2,1)S(1)}, bf16[1024,128]{1,0:T(8,128)(2,1)}, u32[]{:S(2)}) %copy-start.8) | copy-done | bytes 262168
  14.7 0.1 copy.24
  14.8 4.8 %collective-permute-done = bf16[128,256]{1,0:T(8,128)(2,1)S(1)} collective-permute-done((bf16[128,256]{1,0:T(8,128)(2,1)S(1)}, bf16[128,256]{1,0:T(8,128)(2,1)S(1)}, u32[]{:S(2)}, u32[]{:S(2)}) %collective-permute-start) | collective-permute-done | bytes 65568 | tf_op jit(solution)/shard_map/ppermute | solution.py:429
  19.6 11.5 %all-to-all-done.rows_ref = bf16[32,11,8,128]{3,2,1,0:T(8,128)(2,1)S(1)} async-done(((bf16[32,11,8,128]{3,2,1,0:T(8,128)(2,1)}), bf16[32,11,8,128]{3,2,1,0:T(8,128)(2,1)S(1)}, u32[]{:S(2)}, u32[]{:S(2)}) %all-to-all-start) | async-done | bytes 720928 | tf_op jit(solution)/shard_map/all_to_all | solution.py:432
  31.1 0.7 %collective-permute-start.1 = (bf16[32,6,8,128]{3,2,1,0:T(8,128)(2,1)S(1)}, bf16[32,6,8,128]{3,2,1,0:T(8,128)(2,1)S(1)}, u32[]{:S(2)}, u32[]{:S(2)}) collective-permute-start(bf16[32,6,8,128]{3,2,1,0:T(8,128)(2,1)S(1)} %slice.3), channel_id=1, source_target_pairs={{0,2},{1,3},{2,0},{3,1},{4,6},{5,7},{6,4},{7,5},{8,10},{9,11},{10,... | collective-permute-start | bytes 1179656 | tf_op jit(solution)/shard_map/ppermute | solution.py:429
  31.8 1.1 %shard_map.141 = (bf16[32,2,8,128]{3,2,1,0:T(8,128)(2,1)S(1)}, f32[2,256,128]{2,1,0:T(8,128)S(1)}, bf16[256,128]{1,0:T(8,128)(2,1)S(1)}, f32[8,256]{1,0:T(8,128)...) custom-call(s32[1]{0:T(128)} %bitcast.place_ref, ...), custom_call_target="tpu_custom_call" | custom-call | flops 2000000000 | bytes 2000000 | tf_op jit(solution)/shard_map/pallas_call | solution.py:385
  32.9 1.3 %collective-permute-start.2 = (bf16[32,2,8,128]{3,2,1,0:T(8,128)(2,1)S(1)}, bf16[32,2,8,128]{3,2,1,0:T(8,128)(2,1)S(1)}, u32[]{:S(2)}, u32[]{:S(2)}) collective-permute-start(bf16[32,2,8,128]{3,2,1,0:T(8,128)(2,1)S(1)} %get-tuple-element.31.right0), channel_id=1, source_target_pairs={{0,4},{1,5},{2,6},{3,7},{4,0},{5,1},{6,2},{7,3},{8,12},{9,13},{10,... | collective-permute-start | bytes 393224 | tf_op jit(solution)/shard_map/ppermute | solution.py:429
  34.3 4.1 %collective-permute-done.2.right2 = bf16[32,2,8,128]{3,2,1,0:T(8,128)(2,1)S(1)} collective-permute-done((bf16[32,2,8,128]{3,2,1,0:T(8,128)(2,1)S(1)}, bf16[32,2,8,128]{3,2,1,0:T(8,128)(2,1)S(1)}, u32[]{:S(2)}, u32[]{:S(2)}) %collective-permute-start.2) | collective-permute-done | bytes 131104 | tf_op jit(solution)/shard_map/ppermute | solution.py:429
  38.4 0.0 collective-permute-start.3
  38.4 0.0 collective-permute-done.1.swapped_ref.right1
  38.4 1.4 %shard_map.142 = bf16[32,2,8,128]{3,2,1,0:T(8,128)(2,1)} custom-call(s32[1]{0:T(128)} %bitcast.place_ref, bf16[32,6,8,128]{3,2,1,0:T(8,128)(2,1)S(1)} %collective-permute-done.1.swapped_ref.right1, f32[2,256,128]{2,1,0:T(8,128)S(1)} %get-tuple-element.21.part_ref, f32[8,256]{1,0:T(8,128)S(1)} %get-tuple-element.22.key_keep_ref, ...), custom_call_target="tpu_custom_call" | custom-call | flops 2000000000 | bytes 2000000 | tf_op jit(solution)/shard_map/pallas_call | solution.py:385
  39.8 0.0 copy-start.4
  39.8 3.5 %all-to-all-start.1 = ((bf16[32,2,8,128]{3,2,1,0:T(8,128)(2,1)}), bf16[32,2,8,128]{3,2,1,0:T(8,128)(2,1)S(1)}, u32[]{:S(2)}, u32[]{:S(2)}) async-start(bf16[32,2,8,128]{3,2,1,0:T(8,128)(2,1)} %shard_map.142), calls=%async_computation.1 | async-start | bytes 262144 | tf_op jit(solution)/shard_map/all_to_all | solution.py:432
  43.4 0.0 copy-start.5
  43.4 0.0 collective-permute-done.3.right3
  43.4 0.0 copy-done.4
  43.4 0.6 %copy-done.5 = f32[8,128]{1,0:T(8,128)S(1)} copy-done((f32[8,128]{1,0:T(8,128)S(1)}, f32[8,128]{1,0:T(8,128)}, u32[]{:S(2)}) %copy-start.5) | copy-done | bytes 4120
  44.0 0.0 copy-start
  44.0 0.0 copy-start.1
  44.1 0.0 copy-start.2
  44.1 0.0 copy-start.3
  44.1 2.2 %shard_map.144 = bf16[8,256,128]{2,1,0:T(8,128)(2,1)} custom-call(s32[1]{0:T(128)} %bitcast.place_ref, bf16[256,128]{1,0:T(8,128)(2,1)S(1)} %get-tuple-element.30.keep_all_ref, bf16[32,2,8,128]{3,2,1,0:T(8,128)(2,1)S(1)} %get-tuple-element.31.right0, bf16[32,6,8,128]{3,2,1,0:T(8,128)(2,1)S(1)} %collective-permute-done.1.swapped_ref.right1, ...), custom_call_target="tpu_custom_call" | custom-call | flops 2000000000 | bytes 2000000 | tf_op jit(solution)/shard_map/pallas_call | solution.py:385
  46.2 5.8 %all-to-all-done.1 = bf16[32,2,8,128]{3,2,1,0:T(8,128)(2,1)S(1)} async-done(((bf16[32,2,8,128]{3,2,1,0:T(8,128)(2,1)}), bf16[32,2,8,128]{3,2,1,0:T(8,128)(2,1)S(1)}, u32[]{:S(2)}, u32[]{:S(2)}) %all-to-all-start.1) | async-done | bytes 131104 | tf_op jit(solution)/shard_map/all_to_all | solution.py:432
  52.0 0.0 copy-done
  52.0 0.0 copy-done.1
  52.0 0.0 copy-done.2
  52.0 0.0 copy-done.3
  52.0 2.8 %shard_map.143 = bf16[32,8,256]{2,1,0:T(8,128)(2,1)} custom-call(s32[1]{0:T(128)} %bitcast.place_ref, bf16[32,8,256]{2,1,0:T(8,128)(2,1)S(1)} %copy-done, bf16[16,2,2,8,128]{4,3,2,1,0:T(8,128)(2,1)S(1)} %bitcast.21, f32[8,128]{1,0:T(8,128)S(1)} %copy-done.5, bf16[2,128,256]{2,1,0:T(8,128)(2,1)S(1)} %pad_maximum_fusion.row_out_ref, ...), custom_call_target="tpu_custom_call" | custom-call | flops 3000000000 | bytes 3000000 | tf_op jit(solution)/shard_map/pallas_call | solution.py:385
  (4 shorter events, 0.1 us)
Async XLA Ops:
  4.5 7.3 %copy-start.9 = (bf16[128,256]{1,0:T(8,128)(2,1)S(1)}, bf16[128,256]{1,0:T(8,128)(2,1)}, u32[]{:S(2)}) copy-start(bf16[128,256]{1,0:T(8,128)(2,1)} %param.18) | copy-start | bytes 196612
  4.5 9.2 %copy-start.6 = (bf16[256,4,128]{2,1,0:T(4,128)(2,1)S(1)}, bf16[256,4,128]{2,1,0:T(4,128)(2,1)}, u32[]{:S(2)}) copy-start(bf16[256,4,128]{2,1,0:T(4,128)(2,1)} %param.17) | copy-start | bytes 786436
  4.5 26.5 %all-to-all-start = ((bf16[32,11,8,128]{3,2,1,0:T(8,128)(2,1)}), bf16[32,11,8,128]{3,2,1,0:T(8,128)(2,1)S(1)}, u32[]{:S(2)}, u32[]{:S(2)}) async-start(bf16[32,11,8,128]{3,2,1,0:T(8,128)(2,1)} %get-tuple-element.18), calls=%async_computation | async-start | bytes 1441792 | tf_op jit(solution)/shard_map/all_to_all | solution.py:432
  11.8 1.9 %copy-start.7 = (bf16[256,2,256]{2,1,0:T(2,128)(2,1)S(1)}, bf16[256,2,256]{2,1,0:T(2,128)(2,1)}, u32[]{:S(2)}) copy-start(bf16[256,2,256]{2,1,0:T(2,128)(2,1)} %param.21) | copy-start | bytes 786436
  11.9 7.7 %collective-permute-start = (bf16[128,256]{1,0:T(8,128)(2,1)S(1)}, bf16[128,256]{1,0:T(8,128)(2,1)S(1)}, u32[]{:S(2)}, u32[]{:S(2)}) collective-permute-start(bf16[128,256]{1,0:T(8,128)(2,1)S(1)} %copy-done.9), channel_id=1, source_target_pairs={{0,1},{1,0},{2,3},{3,2},{4,5},{5,4},{6,7},{7,6},{8,9},{9,8},{10,11... | collective-permute-start | bytes 196616 | tf_op jit(solution)/shard_map/ppermute | solution.py:429
  13.7 1.0 %copy-start.8 = (bf16[1024,128]{1,0:T(8,128)(2,1)S(1)}, bf16[1024,128]{1,0:T(8,128)(2,1)}, u32[]{:S(2)}) copy-start(bf16[1024,128]{1,0:T(8,128)(2,1)} %param.25) | copy-start | bytes 786436
  31.1 7.4 %collective-permute-start.1 = (bf16[32,6,8,128]{3,2,1,0:T(8,128)(2,1)S(1)}, bf16[32,6,8,128]{3,2,1,0:T(8,128)(2,1)S(1)}, u32[]{:S(2)}, u32[]{:S(2)}) collective-permute-start(bf16[32,6,8,128]{3,2,1,0:T(8,128)(2,1)S(1)} %slice.3), channel_id=1, source_target_pairs={{0,2},{1,3},{2,0},{3,1},{4,6},{5,7},{6,4},{7,5},{8,10},{9,11},{10,... | collective-permute-start | bytes 1179656 | tf_op jit(solution)/shard_map/ppermute | solution.py:429
  32.9 5.5 %collective-permute-start.2 = (bf16[32,2,8,128]{3,2,1,0:T(8,128)(2,1)S(1)}, bf16[32,2,8,128]{3,2,1,0:T(8,128)(2,1)S(1)}, u32[]{:S(2)}, u32[]{:S(2)}) collective-permute-start(bf16[32,2,8,128]{3,2,1,0:T(8,128)(2,1)S(1)} %get-tuple-element.31.right0), channel_id=1, source_target_pairs={{0,4},{1,5},{2,6},{3,7},{4,0},{5,1},{6,2},{7,3},{8,12},{9,13},{10,... | collective-permute-start | bytes 393224 | tf_op jit(solution)/shard_map/ppermute | solution.py:429
  38.4 5.0 %collective-permute-start.3 = (bf16[32,2,8,128]{3,2,1,0:T(8,128)(2,1)S(1)}, bf16[32,2,8,128]{3,2,1,0:T(8,128)(2,1)S(1)}, u32[]{:S(2)}, u32[]{:S(2)}) collective-permute-start(bf16[32,2,8,128]{3,2,1,0:T(8,128)(2,1)S(1)} %collective-permute-done.2.right2), channel_id=1, source_target_pairs={{0,2},{1,3},{2,0},{3,1},{4,6},{5,7},{6,4},{7,5},{8,10},{9,11},{10,... | collective-permute-start | bytes 393224 | tf_op jit(solution)/shard_map/ppermute | solution.py:429
  39.8 3.6 %copy-start.4 = (bf16[256,32]{1,0:T(8,128)(2,1)S(1)}, bf16[256,32]{1,0:T(8,128)(2,1)}, u32[]{:S(2)}) copy-start(bf16[256,32]{1,0:T(8,128)(2,1)} %get-tuple-element.32.left_ref) | copy-start | bytes 49156
  39.8 12.2 %all-to-all-start.1 = ((bf16[32,2,8,128]{3,2,1,0:T(8,128)(2,1)}), bf16[32,2,8,128]{3,2,1,0:T(8,128)(2,1)S(1)}, u32[]{:S(2)}, u32[]{:S(2)}) async-start(bf16[32,2,8,128]{3,2,1,0:T(8,128)(2,1)} %shard_map.142), calls=%async_computation.1 | async-start | bytes 262144 | tf_op jit(solution)/shard_map/all_to_all | solution.py:432
  43.4 0.7 %copy-start.5 = (f32[8,128]{1,0:T(8,128)S(1)}, f32[8,128]{1,0:T(8,128)}, u32[]{:S(2)}) copy-start(f32[8,128]{1,0:T(8,128)} %get-tuple-element.27.keep_ref) | copy-start | bytes 12292
  44.0 8.0 %copy-start = (bf16[32,8,256]{2,1,0:T(8,128)(2,1)S(1)}, bf16[32,8,256]{2,1,0:T(8,128)(2,1)}, u32[]{:S(2)}) copy-start(bf16[32,8,256]{2,1,0:T(8,128)(2,1)} %x_ref.1) | copy-start | bytes 393220
  44.0 8.0 %copy-start.1 = (bf16[256,256]{1,0:T(8,128)(2,1)S(1)}, bf16[256,256]{1,0:T(8,128)(2,1)}, u32[]{:S(2)}) copy-start(bf16[256,256]{1,0:T(8,128)(2,1)} %query_w_ref.1) | copy-start | bytes 393220
  44.1 8.0 %copy-start.2 = (bf16[256,256]{1,0:T(8,128)(2,1)S(1)}, bf16[256,256]{1,0:T(8,128)(2,1)}, u32[]{:S(2)}) copy-start(bf16[256,256]{1,0:T(8,128)(2,1)} %key_w_ref.1) | copy-start | bytes 393220
  44.1 8.0 %copy-start.3 = (bf16[256,256]{1,0:T(8,128)(2,1)S(1)}, bf16[256,256]{1,0:T(8,128)(2,1)}, u32[]{:S(2)}) copy-start(bf16[256,256]{1,0:T(8,128)(2,1)} %out_w_ref.1) | copy-start | bytes 393220

commit v7 on v6

--- a/solution.py
+++ b/solution.py
@@ -68,14 +68,13 @@
     return heads // groups, bias_rows // 8, bias_columns // LANES
 
 
-def prepare_kernel(
-    sizes, bias_hbm, mask_hbm, present_hbm, x_hbm, left_w_hbm, right_w_hbm,
-    rows_ref, left_ref, keep_ref,
-    bias_ref, mask_ref, present_ref, x_ref, left_w_ref, right_w_ref, sems,
+def share_kernel(
+    sizes, bias_hbm, mask_hbm, present_hbm, x_hbm, rows_ref, keep_ref,
+    bias_ref, mask_ref, present_ref, x_ref, sems,
 ):
     groups, sequences_here = sizes
-    sources = (bias_hbm, mask_hbm, present_hbm, x_hbm, left_w_hbm, right_w_hbm)
-    targets = (bias_ref, mask_ref, present_ref, x_ref, left_w_ref, right_w_ref)
+    sources = (bias_hbm, mask_hbm, present_hbm, x_hbm)
+    targets = (bias_ref, mask_ref, present_ref, x_ref)
     copies = [
         pltpu.make_async_copy(source, target, sems.at[at])
         for at, (source, target) in enumerate(zip(sources, targets))
@@ -85,8 +84,6 @@
     for copy in copies[:3]:
         copy.wait()
     sequences, residues, width = x_ref.shape
-    total = sequences * residues
-    channels = left_w_ref.shape[0]
     heads_here, row_tiles, column_tiles = tile_count(bias_ref.shape, groups)
     half_heads = heads_here // 2
     keep = (mask_ref[...] * present_ref[...]).astype(F32)
@@ -107,23 +104,26 @@
                     ]
                     slot += 1
         rows_ref[target, last] = keep_tile
-    for copy in copies[3:]:
-        copy.wait()
-
-    normed = layer_normalize(x_ref[...].astype(F32).reshape(total, width))
-    normed_tiles = normed.astype(F32).reshape(sequences, residues, width).astype(BF16)
+    copies[3].wait()
     halves = width // LANES
     for part in range(sequences // sequences_here):
         for own in range(sequences_here):
             for half in range(halves):
+                tile = x_ref[
+                    part * sequences_here + own, :, half * LANES : (half + 1) * LANES
+                ]
                 for group in range(groups):
-                    rows_ref[part * groups + group, own * halves + half] = normed_tiles[
-                        part * sequences_here + own, :, half * LANES : (half + 1) * LANES
-                    ]
-
-    to_residue_major = residue_major(sequences, residues)
+                    rows_ref[part * groups + group, own * halves + half] = tile
+
+
+def factor_kernel(groups, x_ref, keep_ref, left_w_ref, right_w_ref, right_ref, left_ref):
+    sequences, residues, width = x_ref.shape
+    total = sequences * residues
+    channels = left_w_ref.shape[0]
+    keep = keep_ref[:, :sequences]
+    normed = layer_normalize(x_ref[...].astype(F32).reshape(total, width))
     left = matmul_nt(normed, left_w_ref[...]).astype(BF16)
-    left = matmul(to_residue_major, left)
+    left = matmul(residue_major(sequences, residues), left)
     pick = one_hot(
         quotient(rows_of((total, residues)), sequences) == lanes_of((total, residues))
     )
@@ -151,10 +151,10 @@
         )
         expanded = jnp.where(same_sequence, matmul(right, select), 0.0).astype(BF16)
         result = (matmul(residue_pick, expanded) * keep_spread).astype(BF16)
-        quarter, slot = divmod(tile, channels // per_tile // 4)
-        for target in range(rows_ref.shape[0]):
-            if target // groups % 4 == quarter:
-                rows_ref[target, sequences_here * halves + slot] = result
+        core, slot = divmod(tile, right_ref.shape[1])
+        for target in range(right_ref.shape[0]):
+            if target // groups % 2 == core:
+                right_ref[target, slot] = result
 
 
 def attend_half(
@@ -214,24 +214,22 @@
 
 def first_row_kernel(
     sizes, place_ref, rows_ref, weight_ref,
-    right_ref, part_ref, keep_all_ref, key_keep_ref, query_ref, key_ref, value_ref, gate_ref,
+    part_ref, keep_all_ref, key_keep_ref, query_ref, key_ref, value_ref, gate_ref,
 ):
     groups = sizes[0]
     sequences_here = query_ref.shape[0]
     halves = weight_ref.shape[1] // LANES
     query_factor = PER_SPLIT_DIM ** (-0.5)
     for own in range(sequences_here):
-        normed = jnp.concatenate(
-            [flat_rows(rows_ref[:, own * halves + half]) for half in range(halves)], axis=1
+        tiles = [rows_ref[:, own * halves + half].astype(F32) for half in range(halves)]
+        normed = layer_normalize(
+            jnp.concatenate([tile.reshape(-1, LANES) for tile in tiles], axis=1)
         )
         query_ref[own] = (matmul(normed, weight_ref[0]) * query_factor).astype(BF16)
         key_ref[own] = matmul(normed, weight_ref[1]).astype(BF16)
         value_ref[own] = matmul(normed, weight_ref[2]).astype(BF16)
         gate_ref[own] = jax.nn.sigmoid(matmul(normed, weight_ref[3]))
 
-    first = sequences_here * halves
-    tiles = right_ref.shape[1]
-    right_ref[...] = rows_ref[:, first : first + tiles]
     keep_all = flat_rows(rows_ref[:, rows_ref.shape[1] - 1])
     keep_all_ref[...] = keep_all
     part = quotient(place_ref[0], groups)
@@ -243,8 +241,8 @@
         part_ref[own, pl.ds(start, block_rows), :] = mixed
 
     attend_half(
-        sizes, place_ref, rows_ref, first + tiles, key_keep_ref, query_ref, key_ref, value_ref, 0,
-        block_rows, finish,
+        sizes, place_ref, rows_ref, sequences_here * halves, key_keep_ref, query_ref, key_ref,
+        value_ref, 0, block_rows, finish,
     )
 
 
@@ -263,25 +261,24 @@
             count, residues, head_lanes
         ).astype(BF16)
 
-    tiles = swapped_ref.shape[1] - head_lanes // PER_SPLIT_DIM // 2 * sizes[1] * sizes[2]
     attend_half(
-        sizes, place_ref, swapped_ref, tiles, key_keep_ref, query_ref, key_ref, value_ref, 1,
+        sizes, place_ref, swapped_ref, 0, key_keep_ref, query_ref, key_ref, value_ref, 1,
         block_rows, finish,
     )
 
 
 def outer_kernel(
-    sizes, place_ref, keep_all_ref, right0, right1, right2, right3, left_ref, keep_ref,
+    sizes, place_ref, keep_all_ref, own_right_ref, other_right_ref, left_ref, keep_ref,
     weight_ref, out_ref, mixed_s,
 ):
     groups, sequences, pair = sizes
     residues = keep_ref.shape[0]
     channels, _, depth = weight_ref.shape
-    quarter = quotient(place_ref[0], groups) & 3
+    core = quotient(place_ref[0], groups) & 1
     left = left_ref[...]
-    quarter_channels = channels // 4
+    half_channels = channels // 2
     for at in range(0, channels, 2):
-        channel = (quarter ^ (at // quarter_channels)) * quarter_channels + at % quarter_channels
+        channel = (core ^ (at // half_channels)) * half_channels + at % half_channels
         weights = jnp.concatenate([weight_ref[channel], weight_ref[channel + 1]], axis=1)
         product = matmul(left, weights).astype(BF16)
         for residue in range(residues):
@@ -293,8 +290,8 @@
     right = jnp.concatenate(
         [
             flat_rows(right_ref[:, tile])
-            for right_ref in (right0, right1, right2, right3)
-            for tile in range(right0.shape[1])
+            for right_ref in (own_right_ref, other_right_ref)
+            for tile in range(right_ref.shape[1])
         ],
         axis=1,
     )
@@ -390,7 +387,7 @@
         scratch_shapes=list(scratch),
         compiler_params=pltpu.CompilerParams(vmem_limit_bytes=mib * 1024 * 1024),
         cost_estimate=pl.CostEstimate(
-            flops=micros * 1_000_000_000, bytes_accessed=micros * 1_000_000, transcendentals=0
+            flops=int(micros * 1e9), bytes_accessed=int(micros * 1e6), transcendentals=0
         ),
     )(*arguments)
 
@@ -444,16 +441,11 @@
         alignment_mask.T,
         sequence_row_mask.reshape(1, sequences),
         homolog_activity,
-        first_operand_matrix.T,
-        second_operand_matrix.T,
-    )
-    rows_out, left, keep = call(
-        functools.partial(prepare_kernel, (groups, sequences_here)),
+    )
+    rows_out, keep = call(
+        functools.partial(share_kernel, (groups, sequences_here)),
         (
-            shape(
-                (devices, row_slots + right_tiles // 4 + half_tiles + 1, residues, LANES), BF16
-            ),
-            shape((sequences * residues, channels), BF16),
+            shape((devices, row_slots + half_tiles + 1, residues, LANES), BF16),
             shape((residues, LANES), F32),
         ),
         operands,
@@ -463,6 +455,16 @@
         mib=62,
     )
     rows_in = to_all(rows_out)
+    right_out, left = call(
+        functools.partial(factor_kernel, groups),
+        (
+            shape((devices, right_tiles // 2, residues, LANES), BF16),
+            shape((sequences * residues, channels), BF16),
+        ),
+        (homolog_activity, keep, first_operand_matrix.T, second_operand_matrix.T),
+        mib=56 if large else 32,
+    )
+    own_right = to_all(right_out)
 
     row_weight = horizontal_projection_matrix.transpose(1, 0, 2)
     outer_weight = outer_output_weight.reshape(channels, channels, depth).transpose(1, 0, 2)
@@ -470,14 +472,13 @@
     rows_in, row_weight, outer_weight, content_weight, row_out_weight = lax.optimization_barrier(
         (rows_in, row_weight, outer_weight, content_weight, row_out_weight)
     )
-    swapped = exchange(rows_in[:, row_slots:-1], groups)
+    other_bias = exchange(rows_in[:, row_slots:-1], groups)
 
     row_sizes = (groups, row_tiles, column_tiles)
     here = (sequences_here, residues_overall, head_lanes)
-    right, part, keep_all, *projected = call(
+    part, keep_all, *projected = call(
         functools.partial(first_row_kernel, row_sizes),
         (
-            shape((devices, right_tiles // 4, residues, LANES), BF16),
             shape(here, F32),
             shape((residues_overall, LANES), BF16),
             shape((8, residues_overall), F32),
@@ -489,16 +490,19 @@
         (place, rows_in, row_weight),
         scalars=1,
         mib=60 if large else 32,
-    )
-    right_across = exchange(right, 2 * groups)
+        micros=0.1,
+    )
     mix_out = call(
         functools.partial(second_row_kernel, row_sizes),
         shape((devices, sequences_here, residues, head_lanes), BF16),
-        (place, swapped, part, *projected),
+        (place, other_bias, part, *projected),
         scalars=1,
         mib=60 if large else 32,
+        micros=0.1,
     )
     mix_in = to_all(mix_out)
+    late_right, _ = lax.optimization_barrier((own_right, mix_out))
+    other_right = exchange(late_right, groups)
 
     pairwise_update = call(
         functools.partial(outer_kernel, (groups, sequences, 2)),
@@ -506,10 +510,8 @@
         (
             place,
             keep_all,
-            right,
-            swapped,
-            right_across,
-            exchange(right_across, groups),
+            own_right,
+            other_right,
             left,
             keep,
             outer_weight,

time: 55.2 us -> 58.2 us (1.054)
  starting transfers between devices: 14.8 us -> 16.8 us
  Pallas kernels: 11.3 us -> 12.2 us
    all_to_all x2 -> x3, waiting for transfers between devices: 17.2 us -> 23.4 us  [to_all(): return lax.all_to_all(value, both, split_axis=0, concat_axis=0, tiled=True)]
    ppermute x4 -> x3, waiting for transfers between devices: 8.92 us -> 2.91 us  [exchange(): return lax.ppermute(value, both, [(at, at ^ mask) for at in range(devices)])]
    all_to_all x2 -> x3, starting transfers between devices: 10.8 us -> 14.5 us  [to_all(): return lax.all_to_all(value, both, split_axis=0, concat_axis=0, tiled=True)]
    ppermute x4 -> x3, starting transfers between devices: 3.92 us -> 2.22 us  [exchange(): return lax.ppermute(value, both, [(at, at ^ mask) for at in range(devices)])]
    pallas_call x5 -> x6, Pallas kernels: 11.3 us -> 12.2 us  [call(): pl.pallas_call(kernel, out_shape=outs, in_specs=[smem] * scalars + [read]...]
    unnamed x22 -> x24, local copies, waits for them, and re-layouts: 1.66 us -> 1.59 us
  transfers between devices with their start and end apart: 6 -> 6, of which waited for: 4 -> 5; matrix products, arithmetic and copies ran while one was open for 0% -> 0% of each run, Pallas kernels for 8% -> 14%
where the time goes in v7:
time: 58.2 us; the launch traced here: 57.8 us
  waiting for transfers between devices  26.3 us (45%)
  starting transfers between devices  16.8 us (29%)
  Pallas kernels  12.2 us (21%)
  local copies, waits for them, and re-layouts  1.72 us (3%)
  between operations  0.81 us (1%)
    all_to_all x3, waiting for transfers between devices, to_all(): return lax.all_to_all(value, both, split_axis=0, concat_axis=0, tiled=True)  23.4 us
    all_to_all x3, starting transfers between devices, to_all(): return lax.all_to_all(value, both, split_axis=0, concat_axis=0, tiled=True)  14.5 us
    pallas_call x6, Pallas kernels, call(): pl.pallas_call(kernel, out_shape=outs, in_specs=[smem] * scalars + [read]...  12.2 us
    ppermute x3, waiting for transfers between devices, exchange(): return lax.ppermute(value, both, [(at, at ^ mask) for at in range(devices)])  2.91 us
    ppermute x3, starting transfers between devices, exchange(): return lax.ppermute(value, both, [(at, at ^ mask) for at in range(devices)])  2.22 us
    unnamed x24, local copies, waits for them, and re-layouts  1.59 us
  transfers between devices with their start and end apart: 6, of which 5 were waited for; matrix products, arithmetic and copies ran while one was open for 0% of the time, Pallas kernels for 14%

profile of v7, /device:TPU:0, one launch (start us, length us, event | category | flops | bytes accessed | tf_op | source)
XLA Modules:
  0.0 57.8 jit_solution(6426251604008840648)
XLA Ops:
  0.6 1.8 %shard_map.140 = (bf16[32,9,8,128]{3,2,1,0:T(8,128)(2,1)}, f32[8,128]{1,0:T(8,128)}) custom-call(bf16[8,16,128]{2,1,0:T(8,128)(2,1)} %bias_hbm.1, s32[8,32]{1,0:T(8,128)} %bitcast.27, s32[1,32]{1,0:T(1,128)} %bitcast.28, bf16[32,8,256]{2,1,0:T(8,128)(2,1)} %x_ref.3), custom_call_target="tpu_custom_call" | custom-call | flops 2000000000 | bytes 2000000 | tf_op jit(solution)/shard_map/pallas_call | solution.py:382
  2.5 0.0 copy-start
  2.5 0.0 copy-start.4
  2.5 0.0 copy-start.5
  2.5 7.3 %all-to-all-start = ((bf16[32,9,8,128]{3,2,1,0:T(8,128)(2,1)}), bf16[32,9,8,128]{3,2,1,0:T(8,128)(2,1)S(1)}, u32[]{:S(2)}, u32[]{:S(2)}) async-start(bf16[32,9,8,128]{3,2,1,0:T(8,128)(2,1)} %get-tuple-element.19), calls=%async_computation | async-start | bytes 1179648 | tf_op jit(solution)/shard_map/all_to_all | solution.py:429
  9.8 0.0 copy-start.6
  9.8 0.0 copy-done
  9.9 0.0 copy-done.4
  9.9 0.0 copy-done.5
  9.9 0.6 %copy-done.6 = f32[8,128]{1,0:T(8,128)S(1)} copy-done((f32[8,128]{1,0:T(8,128)S(1)}, f32[8,128]{1,0:T(8,128)}, u32[]{:S(2)}) %copy-start.6) | copy-done | bytes 4120
  10.5 2.7 %shard_map.144 = (bf16[32,4,8,128]{3,2,1,0:T(8,128)(2,1)}, bf16[256,32]{1,0:T(8,128)(2,1)S(1)}) custom-call(bf16[32,8,256]{2,1,0:T(8,128)(2,1)S(1)} %copy-done, f32[8,128]{1,0:T(8,128)S(1)} %copy-done.6, bf16[32,256]{1,0:T(8,128)(2,1)S(1)} %bitcast.22, bf16[32,256]{1,0:T(8,128)(2,1)S(1)} %bitcast.23), custom_call_target="tpu_custom_call" | custom-call | flops 2000000000 | bytes 2000000 | tf_op jit(solution)/shard_map/pallas_call | solution.py:382
  13.2 13.1 %all-to-all-done.rows_ref = bf16[32,9,8,128]{3,2,1,0:T(8,128)(2,1)S(1)} async-done(((bf16[32,9,8,128]{3,2,1,0:T(8,128)(2,1)}), bf16[32,9,8,128]{3,2,1,0:T(8,128)(2,1)S(1)}, u32[]{:S(2)}, u32[]{:S(2)}) %all-to-all-start) | async-done | bytes 589856 | tf_op jit(solution)/shard_map/all_to_all | solution.py:429
  26.2 0.0 copy-start.10
  26.2 0.0 copy-start.7
  26.2 3.6 %all-to-all-start.2 = ((bf16[32,4,8,128]{3,2,1,0:T(8,128)(2,1)}), bf16[32,4,8,128]{3,2,1,0:T(8,128)(2,1)S(1)}, u32[]{:S(2)}, u32[]{:S(2)}) async-start(bf16[32,4,8,128]{3,2,1,0:T(8,128)(2,1)} %get-tuple-element.32), calls=%async_computation.2 | async-start | bytes 524288 | tf_op jit(solution)/shard_map/all_to_all | solution.py:429
  29.9 0.0 copy-done.10
  29.9 0.0 copy-start.8
  29.9 1.8 %collective-permute-start = (bf16[128,256]{1,0:T(8,128)(2,1)S(1)}, bf16[128,256]{1,0:T(8,128)(2,1)S(1)}, u32[]{:S(2)}, u32[]{:S(2)}) collective-permute-start(bf16[128,256]{1,0:T(8,128)(2,1)S(1)} %copy-done.10), channel_id=1, source_target_pairs={{0,1},{1,0},{2,3},{3,2},{4,5},{5,4},{6,7},{7,6},{8,9},{9,8},{10,11... | collective-permute-start | bytes 196616 | tf_op jit(solution)/shard_map/ppermute | solution.py:426
  31.7 0.0 copy-done.7
  31.8 0.0 copy-done.8
  31.8 0.0 copy-start.9
  31.8 0.1 copy.24
  31.9 0.8 %copy-done.9 = bf16[256,4,128]{2,1,0:T(4,128)(2,1)S(1)} copy-done((bf16[256,4,128]{2,1,0:T(4,128)(2,1)S(1)}, bf16[256,4,128]{2,1,0:T(4,128)(2,1)}, u32[]{:S(2)}) %copy-start.9) | copy-done | bytes 262168
  32.8 2.7 %collective-permute-done = bf16[128,256]{1,0:T(8,128)(2,1)S(1)} collective-permute-done((bf16[128,256]{1,0:T(8,128)(2,1)S(1)}, bf16[128,256]{1,0:T(8,128)(2,1)S(1)}, u32[]{:S(2)}, u32[]{:S(2)}) %collective-permute-start) | collective-permute-done | bytes 65568 | tf_op jit(solution)/shard_map/ppermute | solution.py:426
  35.5 0.1 collective-permute-start.1
  35.6 1.3 %shard_map.141 = (f32[2,256,128]{2,1,0:T(8,128)S(1)}, bf16[256,128]{1,0:T(8,128)(2,1)S(1)}, f32[8,256]{1,0:T(8,128)S(1)}, bf16[2,256,128]{2,1,0:T(8,128)(2,1)S(1...) custom-call(s32[1]{0:T(128)} %bitcast.place_ref, ...), custom_call_target="tpu_custom_call" | custom-call | flops 100000000 | bytes 100000 | tf_op jit(solution)/shard_map/pallas_call | solution.py:382
  36.9 0.2 collective-permute-done.1.swapped_ref
  37.1 0.0 copy-start.3
  37.1 1.4 %shard_map.142 = bf16[32,2,8,128]{3,2,1,0:T(8,128)(2,1)} custom-call(s32[1]{0:T(128)} %bitcast.place_ref, bf16[32,4,8,128]{3,2,1,0:T(8,128)(2,1)S(1)} %collective-permute-done.1.swapped_ref, f32[2,256,128]{2,1,0:T(8,128)S(1)} %get-tuple-element.22.part_ref, f32[8,256]{1,0:T(8,128)S(1)} %get-tuple-element.23.key_keep_ref, ...), custom_call_target="tpu_custom_call" | custom-call | flops 100000000 | bytes 100000 | tf_op jit(solution)/shard_map/pallas_call | solution.py:382
  38.5 0.0 copy-start.1
  38.5 0.0 copy-start.2
  38.5 2.1 %all-to-all-done.2.own_right_ref = bf16[32,4,8,128]{3,2,1,0:T(8,128)(2,1)S(1)} async-done(((bf16[32,4,8,128]{3,2,1,0:T(8,128)(2,1)}), bf16[32,4,8,128]{3,2,1,0:T(8,128)(2,1)S(1)}, u32[]{:S(2)}, u32[]{:S(2)}) %all-to-all-start.2) | async-done | bytes 262176 | tf_op jit(solution)/shard_map/all_to_all | solution.py:429
  40.6 3.6 %all-to-all-start.1 = ((bf16[32,2,8,128]{3,2,1,0:T(8,128)(2,1)}), bf16[32,2,8,128]{3,2,1,0:T(8,128)(2,1)S(1)}, u32[]{:S(2)}, u32[]{:S(2)}) async-start(bf16[32,2,8,128]{3,2,1,0:T(8,128)(2,1)} %shard_map.142), calls=%async_computation.1 | async-start | bytes 262144 | tf_op jit(solution)/shard_map/all_to_all | solution.py:429
  44.2 0.3 collective-permute-start.2
  44.5 8.3 %all-to-all-done.1 = bf16[32,2,8,128]{3,2,1,0:T(8,128)(2,1)S(1)} async-done(((bf16[32,2,8,128]{3,2,1,0:T(8,128)(2,1)}), bf16[32,2,8,128]{3,2,1,0:T(8,128)(2,1)S(1)}, u32[]{:S(2)}, u32[]{:S(2)}) %all-to-all-start.1) | async-done | bytes 131104 | tf_op jit(solution)/shard_map/all_to_all | solution.py:429
  52.8 0.0 copy-done.3
  52.8 0.0 copy-done.1
  52.8 0.0 copy-done.2
  52.8 2.8 %shard_map.143 = bf16[32,8,256]{2,1,0:T(8,128)(2,1)} custom-call(s32[1]{0:T(128)} %bitcast.place_ref, bf16[32,8,256]{2,1,0:T(8,128)(2,1)S(1)} %copy-done, bf16[16,2,2,8,128]{4,3,2,1,0:T(8,128)(2,1)S(1)} %bitcast.21, f32[8,128]{1,0:T(8,128)S(1)} %copy-done.6, bf16[2,128,256]{2,1,0:T(8,128)(2,1)S(1)} %pad_maximum_fusion.row_out_ref, ...), custom_call_target="tpu_custom_call" | custom-call | flops 3000000000 | bytes 3000000 | tf_op jit(solution)/shard_map/pallas_call | solution.py:382
  55.6 0.0 collective-permute-done.2.other_right_ref
  55.6 2.2 %shard_map.145 = bf16[8,256,128]{2,1,0:T(8,128)(2,1)} custom-call(s32[1]{0:T(128)} %bitcast.place_ref, bf16[256,128]{1,0:T(8,128)(2,1)S(1)} %get-tuple-element.31.keep_all_ref, bf16[32,4,8,128]{3,2,1,0:T(8,128)(2,1)S(1)} %all-to-all-done.2.own_right_ref, bf16[32,4,8,128]{3,2,1,0:T(8,128)(2,1)S(1)} %collective-permute-done.2.other_right_ref, ...), custom_call_target="tpu_custom_call" | custom-call | flops 2000000000 | bytes 2000000 | tf_op jit(solution)/shard_map/pallas_call | solution.py:382
  (4 shorter events, 0.1 us)
Async XLA Ops:
  2.5 7.4 %copy-start = (bf16[32,8,256]{2,1,0:T(8,128)(2,1)S(1)}, bf16[32,8,256]{2,1,0:T(8,128)(2,1)}, u32[]{:S(2)}) copy-start(bf16[32,8,256]{2,1,0:T(8,128)(2,1)} %x_ref.3) | copy-start | bytes 393220
  2.5 7.4 %copy-start.4 = (bf16[256,32]{0,1:T(8,128)(2,1)S(1)}, bf16[256,32]{0,1:T(8,128)(2,1)}, u32[]{:S(2)}) copy-start(bf16[256,32]{0,1:T(8,128)(2,1)} %param.23) | copy-start | bytes 49156
  2.5 7.4 %copy-start.5 = (bf16[256,32]{0,1:T(8,128)(2,1)S(1)}, bf16[256,32]{0,1:T(8,128)(2,1)}, u32[]{:S(2)}) copy-start(bf16[256,32]{0,1:T(8,128)(2,1)} %param.24) | copy-start | bytes 49156
  2.5 23.7 %all-to-all-start = ((bf16[32,9,8,128]{3,2,1,0:T(8,128)(2,1)}), bf16[32,9,8,128]{3,2,1,0:T(8,128)(2,1)S(1)}, u32[]{:S(2)}, u32[]{:S(2)}) async-start(bf16[32,9,8,128]{3,2,1,0:T(8,128)(2,1)} %get-tuple-element.19), calls=%async_computation | async-start | bytes 1179648 | tf_op jit(solution)/shard_map/all_to_all | solution.py:429
  9.8 0.7 %copy-start.6 = (f32[8,128]{1,0:T(8,128)S(1)}, f32[8,128]{1,0:T(8,128)}, u32[]{:S(2)}) copy-start(f32[8,128]{1,0:T(8,128)} %get-tuple-element.28.keep_ref) | copy-start | bytes 12292
  26.2 3.6 %copy-start.10 = (bf16[128,256]{1,0:T(8,128)(2,1)S(1)}, bf16[128,256]{1,0:T(8,128)(2,1)}, u32[]{:S(2)}) copy-start(bf16[128,256]{1,0:T(8,128)(2,1)} %param.18) | copy-start | bytes 196612
  26.2 5.5 %copy-start.7 = (bf16[256,2,256]{2,1,0:T(2,128)(2,1)S(1)}, bf16[256,2,256]{2,1,0:T(2,128)(2,1)}, u32[]{:S(2)}) copy-start(bf16[256,2,256]{2,1,0:T(2,128)(2,1)} %param.21) | copy-start | bytes 786436
  26.2 14.3 %all-to-all-start.2 = ((bf16[32,4,8,128]{3,2,1,0:T(8,128)(2,1)}), bf16[32,4,8,128]{3,2,1,0:T(8,128)(2,1)S(1)}, u32[]{:S(2)}, u32[]{:S(2)}) async-start(bf16[32,4,8,128]{3,2,1,0:T(8,128)(2,1)} %get-tuple-element.32), calls=%async_computation.2 | async-start | bytes 524288 | tf_op jit(solution)/shard_map/all_to_all | solution.py:429
  29.9 1.9 %copy-start.8 = (bf16[1024,128]{1,0:T(8,128)(2,1)S(1)}, bf16[1024,128]{1,0:T(8,128)(2,1)}, u32[]{:S(2)}) copy-start(bf16[1024,128]{1,0:T(8,128)(2,1)} %param.25) | copy-start | bytes 786436
  29.9 5.6 %collective-permute-start = (bf16[128,256]{1,0:T(8,128)(2,1)S(1)}, bf16[128,256]{1,0:T(8,128)(2,1)S(1)}, u32[]{:S(2)}, u32[]{:S(2)}) collective-permute-start(bf16[128,256]{1,0:T(8,128)(2,1)S(1)} %copy-done.10), channel_id=1, source_target_pairs={{0,1},{1,0},{2,3},{3,2},{4,5},{5,4},{6,7},{7,6},{8,9},{9,8},{10,11... | collective-permute-start | bytes 196616 | tf_op jit(solution)/shard_map/ppermute | solution.py:426
  31.8 1.0 %copy-start.9 = (bf16[256,4,128]{2,1,0:T(4,128)(2,1)S(1)}, bf16[256,4,128]{2,1,0:T(4,128)(2,1)}, u32[]{:S(2)}) copy-start(bf16[256,4,128]{2,1,0:T(4,128)(2,1)} %param.17) | copy-start | bytes 786436
  35.5 1.6 %collective-permute-start.1 = (bf16[32,4,8,128]{3,2,1,0:T(8,128)(2,1)S(1)}, bf16[32,4,8,128]{3,2,1,0:T(8,128)(2,1)S(1)}, u32[]{:S(2)}, u32[]{:S(2)}) collective-permute-start(bf16[32,4,8,128]{3,2,1,0:T(8,128)(2,1)S(1)} %slice.3), channel_id=1, source_target_pairs={{0,2},{1,3},{2,0},{3,1},{4,6},{5,7},{6,4},{7,5},{8,10},{9,11},{10,... | collective-permute-start | bytes 786440 | tf_op jit(solution)/shard_map/ppermute | solution.py:426
  37.1 15.7 %copy-start.3 = (bf16[256,256]{1,0:T(8,128)(2,1)S(1)}, bf16[256,256]{1,0:T(8,128)(2,1)}, u32[]{:S(2)}) copy-start(bf16[256,256]{1,0:T(8,128)(2,1)} %out_w_ref.1) | copy-start | bytes 393220
  38.5 14.3 %copy-start.1 = (bf16[256,256]{1,0:T(8,128)(2,1)S(1)}, bf16[256,256]{1,0:T(8,128)(2,1)}, u32[]{:S(2)}) copy-start(bf16[256,256]{1,0:T(8,128)(2,1)} %query_w_ref.1) | copy-start | bytes 393220
  38.5 14.3 %copy-start.2 = (bf16[256,256]{1,0:T(8,128)(2,1)S(1)}, bf16[256,256]{1,0:T(8,128)(2,1)}, u32[]{:S(2)}) copy-start(bf16[256,256]{1,0:T(8,128)(2,1)} %key_w_ref.1) | copy-start | bytes 393220
  40.6 12.2 %all-to-all-start.1 = ((bf16[32,2,8,128]{3,2,1,0:T(8,128)(2,1)}), bf16[32,2,8,128]{3,2,1,0:T(8,128)(2,1)S(1)}, u32[]{:S(2)}, u32[]{:S(2)}) async-start(bf16[32,2,8,128]{3,2,1,0:T(8,128)(2,1)} %shard_map.142), calls=%async_computation.1 | async-start | bytes 262144 | tf_op jit(solution)/shard_map/all_to_all | solution.py:429
  44.2 11.5 %collective-permute-start.2 = (bf16[32,4,8,128]{3,2,1,0:T(8,128)(2,1)S(1)}, bf16[32,4,8,128]{3,2,1,0:T(8,128)(2,1)S(1)}, u32[]{:S(2)}, u32[]{:S(2)}) collective-permute-start(bf16[32,4,8,128]{3,2,1,0:T(8,128)(2,1)S(1)} %all-to-all-done.2.own_right_ref), channel_id=1, source_target_pairs={{0,2},{1,3},{2,0},{3,1},{4,6},{5,7},{6,4},{7,5},{8,10},{9,11},{10,... | collective-permute-start | bytes 786440 | tf_op jit(solution)/shard_map/ppermute | solution.py:426

commit v8 on v7

--- a/solution.py
+++ b/solution.py
@@ -116,7 +116,7 @@
                     rows_ref[part * groups + group, own * halves + half] = tile
 
 
-def factor_kernel(groups, x_ref, keep_ref, left_w_ref, right_w_ref, right_ref, left_ref):
+def factor_kernel(x_ref, keep_ref, left_w_ref, right_w_ref, right_ref, left_ref):
     sequences, residues, width = x_ref.shape
     total = sequences * residues
     channels = left_w_ref.shape[0]
@@ -151,10 +151,7 @@
         )
         expanded = jnp.where(same_sequence, matmul(right, select), 0.0).astype(BF16)
         result = (matmul(residue_pick, expanded) * keep_spread).astype(BF16)
-        core, slot = divmod(tile, right_ref.shape[1])
-        for target in range(right_ref.shape[0]):
-            if target // groups % 2 == core:
-                right_ref[target, slot] = result
+        right_ref[tile] = result
 
 
 def attend_half(
@@ -268,32 +265,30 @@
 
 
 def outer_kernel(
-    sizes, place_ref, keep_all_ref, own_right_ref, other_right_ref, left_ref, keep_ref,
-    weight_ref, out_ref, mixed_s,
-):
-    groups, sequences, pair = sizes
+    sizes, place_ref, keep_all_ref, *refs
+):
+    groups, sequences, pair, masks = sizes
+    right_refs = refs[: len(masks)]
+    left_ref, keep_ref, weight_ref, out_ref, mixed_s, right_s = refs[len(masks) :]
     residues = keep_ref.shape[0]
     channels, _, depth = weight_ref.shape
-    core = quotient(place_ref[0], groups) & 1
     left = left_ref[...]
-    half_channels = channels // 2
-    for at in range(0, channels, 2):
-        channel = (core ^ (at // half_channels)) * half_channels + at % half_channels
+    for channel in range(0, channels, 2):
         weights = jnp.concatenate([weight_ref[channel], weight_ref[channel + 1]], axis=1)
         product = matmul(left, weights).astype(BF16)
         for residue in range(residues):
             for step in range(2):
-                mixed_s[residue, (at + step) * sequences : (at + step + 1) * sequences, :] = product[
+                mixed_s[
+                    residue, (channel + step) * sequences : (channel + step + 1) * sequences, :
+                ] = product[
                     residue * sequences : (residue + 1) * sequences,
                     step * depth : (step + 1) * depth,
                 ]
+    for mask, right_ref in zip(masks, right_refs):
+        for at in range(right_ref.shape[0]):
+            right_s[place_ref[0] ^ (mask + at * 4 * groups)] = right_ref[at]
     right = jnp.concatenate(
-        [
-            flat_rows(right_ref[:, tile])
-            for right_ref in (own_right_ref, other_right_ref)
-            for tile in range(right_ref.shape[1])
-        ],
-        axis=1,
+        [flat_rows(right_s[:, tile]) for tile in range(right_s.shape[1])], axis=1
     )
     keep_all = keep_all_ref[...]
     for first in range(0, residues, pair):
@@ -456,21 +451,31 @@
     )
     rows_in = to_all(rows_out)
     right_out, left = call(
-        functools.partial(factor_kernel, groups),
+        factor_kernel,
         (
-            shape((devices, right_tiles // 2, residues, LANES), BF16),
+            shape((right_tiles, residues, LANES), BF16),
             shape((sequences * residues, channels), BF16),
         ),
         (homolog_activity, keep, first_operand_matrix.T, second_operand_matrix.T),
         mib=56 if large else 32,
     )
-    own_right = to_all(right_out)
+    right = right_out[None]
+    mask = 4 * groups
+    while mask < devices:
+        right = jnp.concatenate([right, exchange(right, mask)])
+        mask *= 2
 
     row_weight = horizontal_projection_matrix.transpose(1, 0, 2)
     outer_weight = outer_output_weight.reshape(channels, channels, depth).transpose(1, 0, 2)
     content_weight = vertical_content_sigmoid_matrix.transpose(1, 0, 2)
-    rows_in, row_weight, outer_weight, content_weight, row_out_weight = lax.optimization_barrier(
-        (rows_in, row_weight, outer_weight, content_weight, row_out_weight)
+    right_masks, right_parts = [0], [right]
+    for mask in (2 * groups, *range(1, groups)):
+        right_masks.append(mask)
+        right_parts.append(exchange(right, mask))
+    rows_in, row_weight, outer_weight, content_weight, row_out_weight, _ = (
+        lax.optimization_barrier(
+            (rows_in, row_weight, outer_weight, content_weight, row_out_weight, right)
+        )
     )
     other_bias = exchange(rows_in[:, row_slots:-1], groups)
 
@@ -501,22 +506,28 @@
         micros=0.1,
     )
     mix_in = to_all(mix_out)
-    late_right, _ = lax.optimization_barrier((own_right, mix_out))
-    other_right = exchange(late_right, groups)
+    *late_parts, _ = lax.optimization_barrier((*right_parts, mix_out))
+    for mask in range(1, groups):
+        right_masks.append(2 * groups + mask)
+        late_parts.append(exchange(late_parts[1], mask))
+    right_masks += [mask + groups for mask in right_masks]
+    late_parts += [exchange(late_part, groups) for late_part in late_parts]
 
     pairwise_update = call(
-        functools.partial(outer_kernel, (groups, sequences, 2)),
+        functools.partial(outer_kernel, (groups, sequences, 2, tuple(right_masks))),
         shape((residues, residues_overall, depth), BF16),
         (
             place,
             keep_all,
-            own_right,
-            other_right,
+            *late_parts,
             left,
             keep,
             outer_weight,
         ),
-        scratch=[pltpu.VMEM((residues, channels * sequences, depth), BF16)],
+        scratch=[
+            pltpu.VMEM((residues, channels * sequences, depth), BF16),
+            pltpu.VMEM((devices, right_tiles, residues, LANES), BF16),
+        ],
         scalars=1,
         mib=60 if large else 32,
     )

time: 58.2 us -> 51.1 us (0.88)
  waiting for transfers between devices: 26.3 us -> 13.3 us
  starting transfers between devices: 16.8 us -> 23.4 us
  Pallas kernels: 12.2 us -> 11.5 us
    all_to_all x3 -> x2, waiting for transfers between devices: 23.4 us -> 4.46 us  [to_all(): return lax.all_to_all(value, both, split_axis=0, concat_axis=0, tiled=True)]
    ppermute x3 -> x11, starting transfers between devices: 2.22 us -> 13.6 us  [exchange(): return lax.ppermute(value, both, [(at, at ^ mask) for at in range(devices)])]
    ppermute x3 -> x11, waiting for transfers between devices: 2.91 us -> 8.84 us  [exchange(): return lax.ppermute(value, both, [(at, at ^ mask) for at in range(devices)])]
    all_to_all x3 -> x2, starting transfers between devices: 14.5 us -> 9.88 us  [to_all(): return lax.all_to_all(value, both, split_axis=0, concat_axis=0, tiled=True)]
    pallas_call x6, Pallas kernels: 12.2 us -> 11.5 us  [call(): pl.pallas_call(kernel, out_shape=outs, in_specs=[smem] * scalars + [read]...]
  transfers between devices with their start and end apart: 6 -> 13, of which waited for: 5 -> 8; matrix products, arithmetic and copies ran while one was open for 0% -> 0% of each run, Pallas kernels for 14% -> 13%
where the time goes in v8:
time: 51.1 us; the launch traced here: 50.8 us
  starting transfers between devices  23.4 us (46%)
  waiting for transfers between devices  13.3 us (26%)
  Pallas kernels  11.5 us (23%)
  local copies, waits for them, and re-layouts  1.72 us (3%)
  between operations  0.81 us (2%)
    ppermute x11, starting transfers between devices, exchange(): return lax.ppermute(value, both, [(at, at ^ mask) for at in range(devices)])  13.6 us
    pallas_call x6, Pallas kernels, call(): pl.pallas_call(kernel, out_shape=outs, in_specs=[smem] * scalars + [read]...  11.5 us
    all_to_all x2, starting transfers between devices, to_all(): return lax.all_to_all(value, both, split_axis=0, concat_axis=0, tiled=True)  9.88 us
    ppermute x11, waiting for transfers between devices, exchange(): return lax.ppermute(value, both, [(at, at ^ mask) for at in range(devices)])  8.84 us
    all_to_all x2, waiting for transfers between devices, to_all(): return lax.all_to_all(value, both, split_axis=0, concat_axis=0, tiled=True)  4.46 us
    unnamed x24, local copies, waits for them, and re-layouts  1.59 us
  transfers between devices with their start and end apart: 13, of which 8 were waited for; matrix products, arithmetic and copies ran while one was open for 0% of the time, Pallas kernels for 13%

profile of v8, /device:TPU:0, one launch (start us, length us, event | category | flops | bytes accessed | tf_op | source)
XLA Modules:
  0.0 50.8 jit_solution(12564646286666939336)
XLA Ops:
  0.6 1.9 %shard_map.140 = (bf16[32,9,8,128]{3,2,1,0:T(8,128)(2,1)}, f32[8,128]{1,0:T(8,128)}) custom-call(bf16[8,16,128]{2,1,0:T(8,128)(2,1)} %bias_hbm.1, s32[8,32]{1,0:T(8,128)} %bitcast.31, s32[1,32]{1,0:T(1,128)} %bitcast.32, bf16[32,8,256]{2,1,0:T(8,128)(2,1)} %x_ref.3), custom_call_target="tpu_custom_call" | custom-call | flops 2000000000 | bytes 2000000 | tf_op jit(solution)/shard_map/pallas_call | solution.py:377
  2.5 0.0 copy-start
  2.5 0.0 copy-start.4
  2.5 0.0 copy-start.5
  2.5 7.3 %all-to-all-start = ((bf16[32,9,8,128]{3,2,1,0:T(8,128)(2,1)}), bf16[32,9,8,128]{3,2,1,0:T(8,128)(2,1)S(1)}, u32[]{:S(2)}, u32[]{:S(2)}) async-start(bf16[32,9,8,128]{3,2,1,0:T(8,128)(2,1)} %get-tuple-element.21), calls=%async_computation | async-start | bytes 1179648 | tf_op jit(solution)/shard_map/all_to_all | solution.py:424
  9.9 0.0 copy-start.6
  9.9 0.0 copy-done
  9.9 0.0 copy-done.4
  9.9 0.0 copy-done.5
  9.9 0.6 %copy-done.6 = f32[8,128]{1,0:T(8,128)S(1)} copy-done((f32[8,128]{1,0:T(8,128)S(1)}, f32[8,128]{1,0:T(8,128)}, u32[]{:S(2)}) %copy-start.6) | copy-done | bytes 4120
  10.6 1.9 %shard_map.141 = (bf16[8,8,128]{2,1,0:T(8,128)(2,1)S(1)}, bf16[256,32]{1,0:T(8,128)(2,1)S(1)}) custom-call(bf16[32,8,256]{2,1,0:T(8,128)(2,1)S(1)} %copy-done, f32[8,128]{1,0:T(8,128)S(1)} %copy-done.6, bf16[32,256]{1,0:T(8,128)(2,1)S(1)} %bitcast.26, bf16[32,256]{1,0:T(8,128)(2,1)S(1)} %bitcast.27), custom_call_target="tpu_custom_call" | custom-call | flops 2000000000 | bytes 2000000 | tf_op jit(solution)/shard_map/pallas_call | solution.py:377
  12.5 1.8 %collective-permute-start.1 = (bf16[1,8,8,128]{3,2,1,0:T(8,128)(2,1)S(1)}, bf16[1,8,8,128]{3,2,1,0:T(8,128)(2,1)S(1)}, u32[]{:S(2)}, u32[]{:S(2)}) collective-permute-start(bf16[1,8,8,128]{3,2,1,0:T(8,128)(2,1)S(1)} %bitcast.23), channel_id=1, source_target_pairs={{0,8},{1,9},{2,10},{3,11},{4,12},{5,13},{6,14},{7,15},{8,0},{9,1},... | collective-permute-start | bytes 49160 | tf_op jit(solution)/shard_map/ppermute | solution.py:421
  14.3 6.1 %collective-permute-done.1 = bf16[1,8,8,128]{3,2,1,0:T(8,128)(2,1)S(1)} collective-permute-done((bf16[1,8,8,128]{3,2,1,0:T(8,128)(2,1)S(1)}, bf16[1,8,8,128]{3,2,1,0:T(8,128)(2,1)S(1)}, u32[]{:S(2)}, u32[]{:S(2)}) %collective-permute-start.1) | collective-permute-done | bytes 16416 | tf_op jit(solution)/shard_map/ppermute | solution.py:421
  20.4 4.6 %collective-permute-start.2 = (bf16[2,8,8,128]{3,2,1,0:T(8,128)(2,1)S(1)}, bf16[2,8,8,128]{3,2,1,0:T(8,128)(2,1)S(1)}, u32[]{:S(2)}, u32[]{:S(2)}) collective-permute-start(bf16[2,8,8,128]{3,2,1,0:T(8,128)(2,1)S(1)} %pad_maximum_fusion.2), channel_id=1, source_target_pairs={{0,16},{1,17},{2,18},{3,19},{4,20},{5,21},{6,22},{7,23},{8,24},{9,... | collective-permute-start | bytes 98312 | tf_op jit(solution)/shard_map/ppermute | solution.py:421
  25.0 0.0 copy-done.10
  25.0 1.5 %collective-permute-start = (bf16[128,256]{1,0:T(8,128)(2,1)S(1)}, bf16[128,256]{1,0:T(8,128)(2,1)S(1)}, u32[]{:S(2)}, u32[]{:S(2)}) collective-permute-start(bf16[128,256]{1,0:T(8,128)(2,1)S(1)} %copy-done.10), channel_id=1, source_target_pairs={{0,1},{1,0},{2,3},{3,2},{4,5},{5,4},{6,7},{7,6},{8,9},{9,8},{10,11... | collective-permute-start | bytes 196616 | tf_op jit(solution)/shard_map/ppermute | solution.py:421
  26.5 0.0 copy-done.7
  26.6 0.0 copy-done.8
  26.6 0.0 copy-start.9
  26.6 0.1 copy.24
  26.7 0.8 %copy-done.9 = bf16[256,4,128]{2,1,0:T(4,128)(2,1)S(1)} copy-done((bf16[256,4,128]{2,1,0:T(4,128)(2,1)S(1)}, bf16[256,4,128]{2,1,0:T(4,128)(2,1)}, u32[]{:S(2)}) %copy-start.9) | copy-done | bytes 262168
  27.6 0.1 collective-permute-done.2
  27.7 1.6 %collective-permute-done = bf16[128,256]{1,0:T(8,128)(2,1)S(1)} collective-permute-done((bf16[128,256]{1,0:T(8,128)(2,1)S(1)}, bf16[128,256]{1,0:T(8,128)(2,1)S(1)}, u32[]{:S(2)}, u32[]{:S(2)}) %collective-permute-start) | collective-permute-done | bytes 65568 | tf_op jit(solution)/shard_map/ppermute | solution.py:421
  29.3 0.0 all-to-all-done.rows_ref
  29.4 0.1 collective-permute-start.3
  29.4 1.5 %collective-permute-start.4 = (bf16[4,8,8,128]{3,2,1,0:T(8,128)(2,1)S(1)}, bf16[4,8,8,128]{3,2,1,0:T(8,128)(2,1)S(1)}, u32[]{:S(2)}, u32[]{:S(2)}) collective-permute-start(bf16[4,8,8,128]{3,2,1,0:T(8,128)(2,1)S(1)} %pad_maximum_fusion.1.refs_0_), channel_id=1, source_target_pairs={{0,4},{1,5},{2,6},{3,7},{4,0},{5,1},{6,2},{7,3},{8,12},{9,13},{10,... | collective-permute-start | bytes 196616 | tf_op jit(solution)/shard_map/ppermute | solution.py:421
  31.0 1.5 %collective-permute-start.5 = (bf16[4,8,8,128]{3,2,1,0:T(8,128)(2,1)S(1)}, bf16[4,8,8,128]{3,2,1,0:T(8,128)(2,1)S(1)}, u32[]{:S(2)}, u32[]{:S(2)}) collective-permute-start(bf16[4,8,8,128]{3,2,1,0:T(8,128)(2,1)S(1)} %pad_maximum_fusion.1.refs_0_), channel_id=1, source_target_pairs={{0,1},{1,0},{2,3},{3,2},{4,5},{5,4},{6,7},{7,6},{8,9},{9,8},{10,11... | collective-permute-start | bytes 196616 | tf_op jit(solution)/shard_map/ppermute | solution.py:421
  32.5 1.3 %shard_map.142 = (f32[2,256,128]{2,1,0:T(8,128)S(1)}, bf16[256,128]{1,0:T(8,128)(2,1)S(1)}, f32[8,256]{1,0:T(8,128)S(1)}, bf16[2,256,128]{2,1,0:T(8,128)(2,1)S(1...) custom-call(s32[1]{0:T(128)} %bitcast.place_ref, ...), custom_call_target="tpu_custom_call" | custom-call | flops 100000000 | bytes 100000 | tf_op jit(solution)/shard_map/pallas_call | solution.py:377
  33.8 0.0 collective-permute-done.3.swapped_ref
  33.8 1.4 %shard_map.143 = bf16[32,2,8,128]{3,2,1,0:T(8,128)(2,1)} custom-call(s32[1]{0:T(128)} %bitcast.place_ref, bf16[32,4,8,128]{3,2,1,0:T(8,128)(2,1)S(1)} %collective-permute-done.3.swapped_ref, f32[2,256,128]{2,1,0:T(8,128)S(1)} %get-tuple-element.26.part_ref, f32[8,256]{1,0:T(8,128)S(1)} %get-tuple-element.27.key_keep_ref, ...), custom_call_target="tpu_custom_call" | custom-call | flops 100000000 | bytes 100000 | tf_op jit(solution)/shard_map/pallas_call | solution.py:377
  35.2 0.0 collective-permute-done.4.refs_1_
  35.2 0.1 collective-permute-done.5.refs_2_
  35.2 1.5 %collective-permute-start.6 = (bf16[4,8,8,128]{3,2,1,0:T(8,128)(2,1)S(1)}, bf16[4,8,8,128]{3,2,1,0:T(8,128)(2,1)S(1)}, u32[]{:S(2)}, u32[]{:S(2)}) collective-permute-start(bf16[4,8,8,128]{3,2,1,0:T(8,128)(2,1)S(1)} %collective-permute-done.4.refs_1_), channel_id=1, source_target_pairs={{0,1},{1,0},{2,3},{3,2},{4,5},{5,4},{6,7},{7,6},{8,9},{9,8},{10,11... | collective-permute-start | bytes 196616 | tf_op jit(solution)/shard_map/ppermute | solution.py:421
  36.7 2.6 %all-to-all-start.1 = ((bf16[32,2,8,128]{3,2,1,0:T(8,128)(2,1)}), bf16[32,2,8,128]{3,2,1,0:T(8,128)(2,1)S(1)}, u32[]{:S(2)}, u32[]{:S(2)}) async-start(bf16[32,2,8,128]{3,2,1,0:T(8,128)(2,1)} %shard_map.143), calls=%async_computation.1 | async-start | bytes 262144 | tf_op jit(solution)/shard_map/all_to_all | solution.py:424
  39.3 0.2 collective-permute-start.8
  39.5 0.4 collective-permute-start.7
  39.9 0.1 collective-permute-start.9
  40.0 0.0 collective-permute-done.6.refs_3_
  40.0 0.4 collective-permute-start.10
  40.4 0.4 collective-permute-done.7.refs_4_
  40.8 0.0 collective-permute-done.8.refs_5_
  40.8 0.3 collective-permute-done.9.refs_6_
  41.2 0.2 collective-permute-done.10.refs_7_
  41.3 2.2 %shard_map.145 = bf16[8,256,128]{2,1,0:T(8,128)(2,1)} custom-call(s32[1]{0:T(128)} %bitcast.place_ref, bf16[256,128]{1,0:T(8,128)(2,1)S(1)} %get-tuple-element.34.keep_all_ref, bf16[4,8,8,128]{3,2,1,0:T(8,128)(2,1)S(1)} %pad_maximum_fusion.1.refs_0_, bf16[4,8,8,128]{3,2,1,0:T(8,128)(2,1)S(1)} %collective-permute-done.4.refs_1_, ...), custom_call_target="tpu_custom_call" | custom-call | flops 2000000000 | bytes 2000000 | tf_op jit(solution)/shard_map/pallas_call | solution.py:377
  43.5 4.5 %all-to-all-done.1 = bf16[32,2,8,128]{3,2,1,0:T(8,128)(2,1)S(1)} async-done(((bf16[32,2,8,128]{3,2,1,0:T(8,128)(2,1)}), bf16[32,2,8,128]{3,2,1,0:T(8,128)(2,1)S(1)}, u32[]{:S(2)}, u32[]{:S(2)}) %all-to-all-start.1) | async-done | bytes 131104 | tf_op jit(solution)/shard_map/all_to_all | solution.py:424
  48.0 0.0 copy-done.1
  48.0 0.0 copy-done.2
  48.0 2.8 %shard_map.144 = bf16[32,8,256]{2,1,0:T(8,128)(2,1)} custom-call(s32[1]{0:T(128)} %bitcast.place_ref, bf16[32,8,256]{2,1,0:T(8,128)(2,1)S(1)} %copy-done, bf16[16,2,2,8,128]{4,3,2,1,0:T(8,128)(2,1)S(1)} %bitcast.22, f32[8,128]{1,0:T(8,128)S(1)} %copy-done.6, bf16[2,128,256]{2,1,0:T(8,128)(2,1)S(1)} %pad_maximum_fusion.row_out_ref, ...), custom_call_target="tpu_custom_call" | custom-call | flops 3000000000 | bytes 3000000 | tf_op jit(solution)/shard_map/pallas_call | solution.py:377
  (13 shorter events, 0.1 us)
Async XLA Ops:
  2.5 7.4 %copy-start = (bf16[32,8,256]{2,1,0:T(8,128)(2,1)S(1)}, bf16[32,8,256]{2,1,0:T(8,128)(2,1)}, u32[]{:S(2)}) copy-start(bf16[32,8,256]{2,1,0:T(8,128)(2,1)} %x_ref.3) | copy-start | bytes 393220
  2.5 7.4 %copy-start.4 = (bf16[256,32]{0,1:T(8,128)(2,1)S(1)}, bf16[256,32]{0,1:T(8,128)(2,1)}, u32[]{:S(2)}) copy-start(bf16[256,32]{0,1:T(8,128)(2,1)} %param.23) | copy-start | bytes 49156
  2.5 7.4 %copy-start.5 = (bf16[256,32]{0,1:T(8,128)(2,1)S(1)}, bf16[256,32]{0,1:T(8,128)(2,1)}, u32[]{:S(2)}) copy-start(bf16[256,32]{0,1:T(8,128)(2,1)} %param.24) | copy-start | bytes 49156
  2.5 26.8 %all-to-all-start = ((bf16[32,9,8,128]{3,2,1,0:T(8,128)(2,1)}), bf16[32,9,8,128]{3,2,1,0:T(8,128)(2,1)S(1)}, u32[]{:S(2)}, u32[]{:S(2)}) async-start(bf16[32,9,8,128]{3,2,1,0:T(8,128)(2,1)} %get-tuple-element.21), calls=%async_computation | async-start | bytes 1179648 | tf_op jit(solution)/shard_map/all_to_all | solution.py:424
  9.9 0.7 %copy-start.6 = (f32[8,128]{1,0:T(8,128)S(1)}, f32[8,128]{1,0:T(8,128)}, u32[]{:S(2)}) copy-start(f32[8,128]{1,0:T(8,128)} %get-tuple-element.22.keep_ref.refs_9_) | copy-start | bytes 12292
  10.6 16.0 %copy-start.7 = (bf16[256,2,256]{2,1,0:T(2,128)(2,1)S(1)}, bf16[256,2,256]{2,1,0:T(2,128)(2,1)}, u32[]{:S(2)}) copy-start(bf16[256,2,256]{2,1,0:T(2,128)(2,1)} %param.21) | copy-start | bytes 786436
  12.5 12.5 %copy-start.10 = (bf16[128,256]{1,0:T(8,128)(2,1)S(1)}, bf16[128,256]{1,0:T(8,128)(2,1)}, u32[]{:S(2)}) copy-start(bf16[128,256]{1,0:T(8,128)(2,1)} %param.18) | copy-start | bytes 196612
  12.5 7.9 %collective-permute-start.1 = (bf16[1,8,8,128]{3,2,1,0:T(8,128)(2,1)S(1)}, bf16[1,8,8,128]{3,2,1,0:T(8,128)(2,1)S(1)}, u32[]{:S(2)}, u32[]{:S(2)}) collective-permute-start(bf16[1,8,8,128]{3,2,1,0:T(8,128)(2,1)S(1)} %bitcast.23), channel_id=1, source_target_pairs={{0,8},{1,9},{2,10},{3,11},{4,12},{5,13},{6,14},{7,15},{8,0},{9,1},... | collective-permute-start | bytes 49160 | tf_op jit(solution)/shard_map/ppermute | solution.py:421
  20.4 6.1 %copy-start.8 = (bf16[1024,128]{1,0:T(8,128)(2,1)S(1)}, bf16[1024,128]{1,0:T(8,128)(2,1)}, u32[]{:S(2)}) copy-start(bf16[1024,128]{1,0:T(8,128)(2,1)} %param.25) | copy-start | bytes 786436
  20.4 7.2 %collective-permute-start.2 = (bf16[2,8,8,128]{3,2,1,0:T(8,128)(2,1)S(1)}, bf16[2,8,8,128]{3,2,1,0:T(8,128)(2,1)S(1)}, u32[]{:S(2)}, u32[]{:S(2)}) collective-permute-start(bf16[2,8,8,128]{3,2,1,0:T(8,128)(2,1)S(1)} %pad_maximum_fusion.2), channel_id=1, source_target_pairs={{0,16},{1,17},{2,18},{3,19},{4,20},{5,21},{6,22},{7,23},{8,24},{9,... | collective-permute-start | bytes 98312 | tf_op jit(solution)/shard_map/ppermute | solution.py:421
  25.0 4.3 %collective-permute-start = (bf16[128,256]{1,0:T(8,128)(2,1)S(1)}, bf16[128,256]{1,0:T(8,128)(2,1)S(1)}, u32[]{:S(2)}, u32[]{:S(2)}) collective-permute-start(bf16[128,256]{1,0:T(8,128)(2,1)S(1)} %copy-done.10), channel_id=1, source_target_pairs={{0,1},{1,0},{2,3},{3,2},{4,5},{5,4},{6,7},{7,6},{8,9},{9,8},{10,11... | collective-permute-start | bytes 196616 | tf_op jit(solution)/shard_map/ppermute | solution.py:421
  26.6 1.0 %copy-start.9 = (bf16[256,4,128]{2,1,0:T(4,128)(2,1)S(1)}, bf16[256,4,128]{2,1,0:T(4,128)(2,1)}, u32[]{:S(2)}) copy-start(bf16[256,4,128]{2,1,0:T(4,128)(2,1)} %param.17) | copy-start | bytes 786436
  29.4 4.4 %collective-permute-start.3 = (bf16[32,4,8,128]{3,2,1,0:T(8,128)(2,1)S(1)}, bf16[32,4,8,128]{3,2,1,0:T(8,128)(2,1)S(1)}, u32[]{:S(2)}, u32[]{:S(2)}) collective-permute-start(bf16[32,4,8,128]{3,2,1,0:T(8,128)(2,1)S(1)} %slice.3), channel_id=1, source_target_pairs={{0,2},{1,3},{2,0},{3,1},{4,6},{5,7},{6,4},{7,5},{8,10},{9,11},{10,... | collective-permute-start | bytes 786440 | tf_op jit(solution)/shard_map/ppermute | solution.py:421
  29.4 5.7 %collective-permute-start.4 = (bf16[4,8,8,128]{3,2,1,0:T(8,128)(2,1)S(1)}, bf16[4,8,8,128]{3,2,1,0:T(8,128)(2,1)S(1)}, u32[]{:S(2)}, u32[]{:S(2)}) collective-permute-start(bf16[4,8,8,128]{3,2,1,0:T(8,128)(2,1)S(1)} %pad_maximum_fusion.1.refs_0_), channel_id=1, source_target_pairs={{0,4},{1,5},{2,6},{3,7},{4,0},{5,1},{6,2},{7,3},{8,12},{9,13},{10,... | collective-permute-start | bytes 196616 | tf_op jit(solution)/shard_map/ppermute | solution.py:421
  31.0 4.3 %collective-permute-start.5 = (bf16[4,8,8,128]{3,2,1,0:T(8,128)(2,1)S(1)}, bf16[4,8,8,128]{3,2,1,0:T(8,128)(2,1)S(1)}, u32[]{:S(2)}, u32[]{:S(2)}) collective-permute-start(bf16[4,8,8,128]{3,2,1,0:T(8,128)(2,1)S(1)} %pad_maximum_fusion.1.refs_0_), channel_id=1, source_target_pairs={{0,1},{1,0},{2,3},{3,2},{4,5},{5,4},{6,7},{7,6},{8,9},{9,8},{10,11... | collective-permute-start | bytes 196616 | tf_op jit(solution)/shard_map/ppermute | solution.py:421
  35.2 4.8 %collective-permute-start.6 = (bf16[4,8,8,128]{3,2,1,0:T(8,128)(2,1)S(1)}, bf16[4,8,8,128]{3,2,1,0:T(8,128)(2,1)S(1)}, u32[]{:S(2)}, u32[]{:S(2)}) collective-permute-start(bf16[4,8,8,128]{3,2,1,0:T(8,128)(2,1)S(1)} %collective-permute-done.4.refs_1_), channel_id=1, source_target_pairs={{0,1},{1,0},{2,3},{3,2},{4,5},{5,4},{6,7},{7,6},{8,9},{9,8},{10,11... | collective-permute-start | bytes 196616 | tf_op jit(solution)/shard_map/ppermute | solution.py:421
  36.7 11.2 %all-to-all-start.1 = ((bf16[32,2,8,128]{3,2,1,0:T(8,128)(2,1)}), bf16[32,2,8,128]{3,2,1,0:T(8,128)(2,1)S(1)}, u32[]{:S(2)}, u32[]{:S(2)}) async-start(bf16[32,2,8,128]{3,2,1,0:T(8,128)(2,1)} %shard_map.143), calls=%async_computation.1 | async-start | bytes 262144 | tf_op jit(solution)/shard_map/all_to_all | solution.py:424
  39.3 1.5 %collective-permute-start.8 = (bf16[4,8,8,128]{3,2,1,0:T(8,128)(2,1)S(1)}, bf16[4,8,8,128]{3,2,1,0:T(8,128)(2,1)S(1)}, u32[]{:S(2)}, u32[]{:S(2)}) collective-permute-start(bf16[4,8,8,128]{3,2,1,0:T(8,128)(2,1)S(1)} %collective-permute-done.4.refs_1_), channel_id=1, source_target_pairs={{0,2},{1,3},{2,0},{3,1},{4,6},{5,7},{6,4},{7,5},{8,10},{9,11},{10,... | collective-permute-start | bytes 196616 | tf_op jit(solution)/shard_map/ppermute | solution.py:421
  39.5 1.3 %collective-permute-start.7 = (bf16[4,8,8,128]{3,2,1,0:T(8,128)(2,1)S(1)}, bf16[4,8,8,128]{3,2,1,0:T(8,128)(2,1)S(1)}, u32[]{:S(2)}, u32[]{:S(2)}) collective-permute-start(bf16[4,8,8,128]{3,2,1,0:T(8,128)(2,1)S(1)} %pad_maximum_fusion.1.refs_0_), channel_id=1, source_target_pairs={{0,2},{1,3},{2,0},{3,1},{4,6},{5,7},{6,4},{7,5},{8,10},{9,11},{10,... | collective-permute-start | bytes 196616 | tf_op jit(solution)/shard_map/ppermute | solution.py:421
  39.9 1.3 %collective-permute-start.9 = (bf16[4,8,8,128]{3,2,1,0:T(8,128)(2,1)S(1)}, bf16[4,8,8,128]{3,2,1,0:T(8,128)(2,1)S(1)}, u32[]{:S(2)}, u32[]{:S(2)}) collective-permute-start(bf16[4,8,8,128]{3,2,1,0:T(8,128)(2,1)S(1)} %collective-permute-done.5.refs_2_), channel_id=1, source_target_pairs={{0,2},{1,3},{2,0},{3,1},{4,6},{5,7},{6,4},{7,5},{8,10},{9,11},{10,... | collective-permute-start | bytes 196616 | tf_op jit(solution)/shard_map/ppermute | solution.py:421
  40.0 1.3 %collective-permute-start.10 = (bf16[4,8,8,128]{3,2,1,0:T(8,128)(2,1)S(1)}, bf16[4,8,8,128]{3,2,1,0:T(8,128)(2,1)S(1)}, u32[]{:S(2)}, u32[]{:S(2)}) collective-permute-start(bf16[4,8,8,128]{3,2,1,0:T(8,128)(2,1)S(1)} %collective-permute-done.6.refs_3_), channel_id=1, source_target_pairs={{0,2},{1,3},{2,0},{3,1},{4,6},{5,7},{6,4},{7,5},{8,10},{9,11},{10,... | collective-permute-start | bytes 196616 | tf_op jit(solution)/shard_map/ppermute | solution.py:421
  41.3 6.6 %copy-start.1 = (bf16[256,256]{1,0:T(8,128)(2,1)S(1)}, bf16[256,256]{1,0:T(8,128)(2,1)}, u32[]{:S(2)}) copy-start(bf16[256,256]{1,0:T(8,128)(2,1)} %query_w_ref.1) | copy-start | bytes 393220
  41.3 6.6 %copy-start.2 = (bf16[256,256]{1,0:T(8,128)(2,1)S(1)}, bf16[256,256]{1,0:T(8,128)(2,1)}, u32[]{:S(2)}) copy-start(bf16[256,256]{1,0:T(8,128)(2,1)} %key_w_ref.1) | copy-start | bytes 393220
  41.3 6.6 %copy-start.3 = (bf16[256,256]{1,0:T(8,128)(2,1)S(1)}, bf16[256,256]{1,0:T(8,128)(2,1)}, u32[]{:S(2)}) copy-start(bf16[256,256]{1,0:T(8,128)(2,1)} %out_w_ref.1) | copy-start | bytes 393220

commit v9 on v8

--- a/solution.py
+++ b/solution.py
@@ -423,11 +423,6 @@
     def to_all(value):
         return lax.all_to_all(value, both, split_axis=0, concat_axis=0, tiled=True)
 
-    row_out_weight = jnp.stack(
-        [horizontal_final_matrix]
-        + [exchange(horizontal_final_matrix, relative) for relative in range(1, groups)]
-    )
-
     right_tiles = channels * sequences // LANES
     row_slots = sequences_here * (width // LANES)
     half_tiles = heads_here // 2 * row_tiles * column_tiles
@@ -468,14 +463,8 @@
     row_weight = horizontal_projection_matrix.transpose(1, 0, 2)
     outer_weight = outer_output_weight.reshape(channels, channels, depth).transpose(1, 0, 2)
     content_weight = vertical_content_sigmoid_matrix.transpose(1, 0, 2)
-    right_masks, right_parts = [0], [right]
-    for mask in (2 * groups, *range(1, groups)):
-        right_masks.append(mask)
-        right_parts.append(exchange(right, mask))
-    rows_in, row_weight, outer_weight, content_weight, row_out_weight, _ = (
-        lax.optimization_barrier(
-            (rows_in, row_weight, outer_weight, content_weight, row_out_weight, right)
-        )
+    rows_in, row_weight, outer_weight, content_weight, right = lax.optimization_barrier(
+        (rows_in, row_weight, outer_weight, content_weight, right)
     )
     other_bias = exchange(rows_in[:, row_slots:-1], groups)
 
@@ -506,7 +495,14 @@
         micros=0.1,
     )
     mix_in = to_all(mix_out)
-    *late_parts, _ = lax.optimization_barrier((*right_parts, mix_out))
+    right, own_final, _ = lax.optimization_barrier((right, horizontal_final_matrix, mix_out))
+    right_masks, late_parts = [0], [right]
+    for mask in (2 * groups, *range(1, groups)):
+        right_masks.append(mask)
+        late_parts.append(exchange(right, mask))
+    row_out_weight = jnp.stack(
+        [own_final] + [exchange(own_final, relative) for relative in range(1, groups)]
+    )
     for mask in range(1, groups):
         right_masks.append(2 * groups + mask)
         late_parts.append(exchange(late_parts[1], mask))

time: 51.1 us -> 53.3 us (1.043)
  waiting for transfers between devices: 13.3 us -> 14.9 us
  starting transfers between devices: 23.4 us -> 24.1 us
    all_to_all x2, starting transfers between devices: 9.88 us -> 11.8 us  [to_all(): return lax.all_to_all(value, both, split_axis=0, concat_axis=0, tiled=True)]
    ppermute x11, waiting for transfers between devices: 8.84 us -> 10.3 us  [exchange(): return lax.ppermute(value, both, [(at, at ^ mask) for at in range(devices)])]
    ppermute x11, starting transfers between devices: 13.6 us -> 12.3 us  [exchange(): return lax.ppermute(value, both, [(at, at ^ mask) for at in range(devices)])]
  transfers between devices with their start and end apart: 13 -> 13, of which waited for: 8 -> 8; matrix products, arithmetic and copies ran while one was open for 0% -> 0% of each run, Pallas kernels for 13% -> 10%
where the time goes in v9:
time: 53.3 us; the launch traced here: 53 us
  starting transfers between devices  24.1 us (45%)
  waiting for transfers between devices  14.9 us (28%)
  Pallas kernels  11.5 us (22%)
  local copies, waits for them, and re-layouts  1.72 us (3%)
  between operations  0.81 us (2%)
    ppermute x11, starting transfers between devices, exchange(): return lax.ppermute(value, both, [(at, at ^ mask) for at in range(devices)])  12.3 us
    all_to_all x2, starting transfers between devices, to_all(): return lax.all_to_all(value, both, split_axis=0, concat_axis=0, tiled=True)  11.8 us
    pallas_call x6, Pallas kernels, call(): pl.pallas_call(kernel, out_shape=outs, in_specs=[smem] * scalars + [read]...  11.5 us
    ppermute x11, waiting for transfers between devices, exchange(): return lax.ppermute(value, both, [(at, at ^ mask) for at in range(devices)])  10.3 us
    all_to_all x2, waiting for transfers between devices, to_all(): return lax.all_to_all(value, both, split_axis=0, concat_axis=0, tiled=True)  4.62 us
    unnamed x24, local copies, waits for them, and re-layouts  1.59 us
  transfers between devices with their start and end apart: 13, of which 8 were waited for; matrix products, arithmetic and copies ran while one was open for 0% of the time, Pallas kernels for 10%

profile of v9, /device:TPU:0, one launch (start us, length us, event | category | flops | bytes accessed | tf_op | source)
XLA Modules:
  0.0 53.0 jit_solution(1518202896624693306)
XLA Ops:
  0.6 1.9 %shard_map.140 = (bf16[32,9,8,128]{3,2,1,0:T(8,128)(2,1)}, f32[8,128]{1,0:T(8,128)}) custom-call(bf16[8,16,128]{2,1,0:T(8,128)(2,1)} %bias_hbm.1, s32[8,32]{1,0:T(8,128)} %bitcast.31, s32[1,32]{1,0:T(1,128)} %bitcast.32, bf16[32,8,256]{2,1,0:T(8,128)(2,1)} %x_ref.3), custom_call_target="tpu_custom_call" | custom-call | flops 2000000000 | bytes 2000000 | tf_op jit(solution)/shard_map/pallas_call | solution.py:377
  2.5 0.0 copy-start
  2.5 0.0 copy-start.4
  2.5 0.0 copy-start.5
  2.5 7.3 %all-to-all-start = ((bf16[32,9,8,128]{3,2,1,0:T(8,128)(2,1)}), bf16[32,9,8,128]{3,2,1,0:T(8,128)(2,1)S(1)}, u32[]{:S(2)}, u32[]{:S(2)}) async-start(bf16[32,9,8,128]{3,2,1,0:T(8,128)(2,1)} %get-tuple-element.20), calls=%async_computation | async-start | bytes 1179648 | tf_op jit(solution)/shard_map/all_to_all | solution.py:424
  9.9 0.0 copy-start.6
  9.9 0.0 copy-done
  9.9 0.0 copy-done.4
  9.9 0.0 copy-done.5
  9.9 0.6 %copy-done.6 = f32[8,128]{1,0:T(8,128)S(1)} copy-done((f32[8,128]{1,0:T(8,128)S(1)}, f32[8,128]{1,0:T(8,128)}, u32[]{:S(2)}) %copy-start.6) | copy-done | bytes 4120
  10.6 1.9 %shard_map.141 = (bf16[8,8,128]{2,1,0:T(8,128)(2,1)S(1)}, bf16[256,32]{1,0:T(8,128)(2,1)S(1)}) custom-call(bf16[32,8,256]{2,1,0:T(8,128)(2,1)S(1)} %copy-done, f32[8,128]{1,0:T(8,128)S(1)} %copy-done.6, bf16[32,256]{1,0:T(8,128)(2,1)S(1)} %bitcast.26, bf16[32,256]{1,0:T(8,128)(2,1)S(1)} %bitcast.27), custom_call_target="tpu_custom_call" | custom-call | flops 2000000000 | bytes 2000000 | tf_op jit(solution)/shard_map/pallas_call | solution.py:377
  12.5 1.8 %collective-permute-start = (bf16[1,8,8,128]{3,2,1,0:T(8,128)(2,1)S(1)}, bf16[1,8,8,128]{3,2,1,0:T(8,128)(2,1)S(1)}, u32[]{:S(2)}, u32[]{:S(2)}) collective-permute-start(bf16[1,8,8,128]{3,2,1,0:T(8,128)(2,1)S(1)} %bitcast.23), channel_id=1, source_target_pairs={{0,8},{1,9},{2,10},{3,11},{4,12},{5,13},{6,14},{7,15},{8,0},{9,1},... | collective-permute-start | bytes 49160 | tf_op jit(solution)/shard_map/ppermute | solution.py:421
  14.3 6.1 %collective-permute-done = bf16[1,8,8,128]{3,2,1,0:T(8,128)(2,1)S(1)} collective-permute-done((bf16[1,8,8,128]{3,2,1,0:T(8,128)(2,1)S(1)}, bf16[1,8,8,128]{3,2,1,0:T(8,128)(2,1)S(1)}, u32[]{:S(2)}, u32[]{:S(2)}) %collective-permute-start) | collective-permute-done | bytes 16416 | tf_op jit(solution)/shard_map/ppermute | solution.py:421
  20.4 4.6 %collective-permute-start.1 = (bf16[2,8,8,128]{3,2,1,0:T(8,128)(2,1)S(1)}, bf16[2,8,8,128]{3,2,1,0:T(8,128)(2,1)S(1)}, u32[]{:S(2)}, u32[]{:S(2)}) collective-permute-start(bf16[2,8,8,128]{3,2,1,0:T(8,128)(2,1)S(1)} %pad_maximum_fusion.2), channel_id=1, source_target_pairs={{0,16},{1,17},{2,18},{3,19},{4,20},{5,21},{6,22},{7,23},{8,24},{9,... | collective-permute-start | bytes 98312 | tf_op jit(solution)/shard_map/ppermute | solution.py:421
  25.0 0.0 copy-done.7
  25.1 0.0 copy-done.8
  25.1 0.0 copy-start.9
  25.1 0.1 copy.24
  25.2 0.8 %copy-done.9 = bf16[256,4,128]{2,1,0:T(4,128)(2,1)S(1)} copy-done((bf16[256,4,128]{2,1,0:T(4,128)(2,1)S(1)}, bf16[256,4,128]{2,1,0:T(4,128)(2,1)}, u32[]{:S(2)}) %copy-start.9) | copy-done | bytes 262168
  26.1 1.6 %collective-permute-done.1 = bf16[2,8,8,128]{3,2,1,0:T(8,128)(2,1)S(1)} collective-permute-done((bf16[2,8,8,128]{3,2,1,0:T(8,128)(2,1)S(1)}, bf16[2,8,8,128]{3,2,1,0:T(8,128)(2,1)S(1)}, u32[]{:S(2)}, u32[]{:S(2)}) %collective-permute-start.1) | collective-permute-done | bytes 32800 | tf_op jit(solution)/shard_map/ppermute | solution.py:421
  27.7 0.0 all-to-all-done.rows_ref
  27.7 0.1 collective-permute-start.2
  27.8 1.3 %shard_map.142 = (f32[2,256,128]{2,1,0:T(8,128)S(1)}, bf16[256,128]{1,0:T(8,128)(2,1)S(1)}, f32[8,256]{1,0:T(8,128)S(1)}, bf16[2,256,128]{2,1,0:T(8,128)(2,1)S(1...) custom-call(s32[1]{0:T(128)} %bitcast.place_ref, ...), custom_call_target="tpu_custom_call" | custom-call | flops 100000000 | bytes 100000 | tf_op jit(solution)/shard_map/pallas_call | solution.py:377
  29.1 0.2 collective-permute-done.2.swapped_ref
  29.3 1.4 %shard_map.143 = bf16[32,2,8,128]{3,2,1,0:T(8,128)(2,1)} custom-call(s32[1]{0:T(128)} %bitcast.place_ref, bf16[32,4,8,128]{3,2,1,0:T(8,128)(2,1)S(1)} %collective-permute-done.2.swapped_ref, f32[2,256,128]{2,1,0:T(8,128)S(1)} %get-tuple-element.25.part_ref, f32[8,256]{1,0:T(8,128)S(1)} %get-tuple-element.26.key_keep_ref, ...), custom_call_target="tpu_custom_call" | custom-call | flops 100000000 | bytes 100000 | tf_op jit(solution)/shard_map/pallas_call | solution.py:377
  30.7 1.5 %collective-permute-start.4 = (bf16[4,8,8,128]{3,2,1,0:T(8,128)(2,1)S(1)}, bf16[4,8,8,128]{3,2,1,0:T(8,128)(2,1)S(1)}, u32[]{:S(2)}, u32[]{:S(2)}) collective-permute-start(bf16[4,8,8,128]{3,2,1,0:T(8,128)(2,1)S(1)} %pad_maximum_fusion.1.refs_0_), channel_id=1, source_target_pairs={{0,4},{1,5},{2,6},{3,7},{4,0},{5,1},{6,2},{7,3},{8,12},{9,13},{10,... | collective-permute-start | bytes 196616 | tf_op jit(solution)/shard_map/ppermute | solution.py:421
  32.2 1.5 %collective-permute-start.5 = (bf16[4,8,8,128]{3,2,1,0:T(8,128)(2,1)S(1)}, bf16[4,8,8,128]{3,2,1,0:T(8,128)(2,1)S(1)}, u32[]{:S(2)}, u32[]{:S(2)}) collective-permute-start(bf16[4,8,8,128]{3,2,1,0:T(8,128)(2,1)S(1)} %pad_maximum_fusion.1.refs_0_), channel_id=1, source_target_pairs={{0,1},{1,0},{2,3},{3,2},{4,5},{5,4},{6,7},{7,6},{8,9},{9,8},{10,11... | collective-permute-start | bytes 196616 | tf_op jit(solution)/shard_map/ppermute | solution.py:421
  33.7 1.3 %collective-permute-done.4.refs_1_ = bf16[4,8,8,128]{3,2,1,0:T(8,128)(2,1)S(1)} collective-permute-done((bf16[4,8,8,128]{3,2,1,0:T(8,128)(2,1)S(1)}, bf16[4,8,8,128]{3,2,1,0:T(8,128)(2,1)S(1)}, u32[]{:S(2)}, u32[]{:S(2)}) %collective-permute-start.4) | collective-permute-done | bytes 65568 | tf_op jit(solution)/shard_map/ppermute | solution.py:421
  35.0 1.5 %collective-permute-start.6 = (bf16[4,8,8,128]{3,2,1,0:T(8,128)(2,1)S(1)}, bf16[4,8,8,128]{3,2,1,0:T(8,128)(2,1)S(1)}, u32[]{:S(2)}, u32[]{:S(2)}) collective-permute-start(bf16[4,8,8,128]{3,2,1,0:T(8,128)(2,1)S(1)} %collective-permute-done.4.refs_1_), channel_id=1, source_target_pairs={{0,1},{1,0},{2,3},{3,2},{4,5},{5,4},{6,7},{7,6},{8,9},{9,8},{10,11... | collective-permute-start | bytes 196616 | tf_op jit(solution)/shard_map/ppermute | solution.py:421
  36.5 0.0 copy-done.10
  36.5 0.6 %collective-permute-start.3 = (bf16[128,256]{1,0:T(8,128)(2,1)S(1)}, bf16[128,256]{1,0:T(8,128)(2,1)S(1)}, u32[]{:S(2)}, u32[]{:S(2)}) collective-permute-start(bf16[128,256]{1,0:T(8,128)(2,1)S(1)} %copy-done.10), channel_id=1, source_target_pairs={{0,1},{1,0},{2,3},{3,2},{4,5},{5,4},{6,7},{7,6},{8,9},{9,8},{10,11... | collective-permute-start | bytes 196616 | tf_op jit(solution)/shard_map/ppermute | solution.py:421
  37.0 0.0 collective-permute-start.7
  37.0 4.5 %all-to-all-start.1 = ((bf16[32,2,8,128]{3,2,1,0:T(8,128)(2,1)}), bf16[32,2,8,128]{3,2,1,0:T(8,128)(2,1)S(1)}, u32[]{:S(2)}, u32[]{:S(2)}) async-start(bf16[32,2,8,128]{3,2,1,0:T(8,128)(2,1)} %shard_map.143), calls=%async_computation.1 | async-start | bytes 262144 | tf_op jit(solution)/shard_map/all_to_all | solution.py:424
  41.5 0.3 collective-permute-start.8
  41.9 0.0 collective-permute-done.5.refs_2_
  41.9 0.3 collective-permute-start.9
  42.1 0.0 collective-permute-done.6.refs_3_
  42.1 0.3 collective-permute-start.10
  42.4 0.0 collective-permute-done.3
  42.4 0.0 collective-permute-done.7.refs_4_
  42.4 0.5 collective-permute-done.8.refs_5_
  42.9 0.3 collective-permute-done.9.refs_6_
  43.1 0.3 collective-permute-done.10.refs_7_
  43.4 2.2 %shard_map.145 = bf16[8,256,128]{2,1,0:T(8,128)(2,1)} custom-call(s32[1]{0:T(128)} %bitcast.place_ref, bf16[256,128]{1,0:T(8,128)(2,1)S(1)} %get-tuple-element.34.keep_all_ref, bf16[4,8,8,128]{3,2,1,0:T(8,128)(2,1)S(1)} %pad_maximum_fusion.1.refs_0_, bf16[4,8,8,128]{3,2,1,0:T(8,128)(2,1)S(1)} %collective-permute-done.4.refs_1_, ...), custom_call_target="tpu_custom_call" | custom-call | flops 2000000000 | bytes 2000000 | tf_op jit(solution)/shard_map/pallas_call | solution.py:377
  45.6 4.6 %all-to-all-done.1 = bf16[32,2,8,128]{3,2,1,0:T(8,128)(2,1)S(1)} async-done(((bf16[32,2,8,128]{3,2,1,0:T(8,128)(2,1)}), bf16[32,2,8,128]{3,2,1,0:T(8,128)(2,1)S(1)}, u32[]{:S(2)}, u32[]{:S(2)}) %all-to-all-start.1) | async-done | bytes 131104 | tf_op jit(solution)/shard_map/all_to_all | solution.py:424
  50.2 0.0 copy-done.1
  50.2 0.0 copy-done.2
  50.2 2.8 %shard_map.144 = bf16[32,8,256]{2,1,0:T(8,128)(2,1)} custom-call(s32[1]{0:T(128)} %bitcast.place_ref, bf16[32,8,256]{2,1,0:T(8,128)(2,1)S(1)} %copy-done, bf16[16,2,2,8,128]{4,3,2,1,0:T(8,128)(2,1)S(1)} %bitcast.22, f32[8,128]{1,0:T(8,128)S(1)} %copy-done.6, bf16[2,128,256]{2,1,0:T(8,128)(2,1)S(1)} %pad_maximum_fusion.row_out_ref, ...), custom_call_target="tpu_custom_call" | custom-call | flops 3000000000 | bytes 3000000 | tf_op jit(solution)/shard_map/pallas_call | solution.py:377
  (13 shorter events, 0.1 us)
Async XLA Ops:
  2.5 7.4 %copy-start = (bf16[32,8,256]{2,1,0:T(8,128)(2,1)S(1)}, bf16[32,8,256]{2,1,0:T(8,128)(2,1)}, u32[]{:S(2)}) copy-start(bf16[32,8,256]{2,1,0:T(8,128)(2,1)} %x_ref.3) | copy-start | bytes 393220
  2.5 7.4 %copy-start.4 = (bf16[256,32]{0,1:T(8,128)(2,1)S(1)}, bf16[256,32]{0,1:T(8,128)(2,1)}, u32[]{:S(2)}) copy-start(bf16[256,32]{0,1:T(8,128)(2,1)} %param.23) | copy-start | bytes 49156
  2.5 7.4 %copy-start.5 = (bf16[256,32]{0,1:T(8,128)(2,1)S(1)}, bf16[256,32]{0,1:T(8,128)(2,1)}, u32[]{:S(2)}) copy-start(bf16[256,32]{0,1:T(8,128)(2,1)} %param.24) | copy-start | bytes 49156
  2.5 25.1 %all-to-all-start = ((bf16[32,9,8,128]{3,2,1,0:T(8,128)(2,1)}), bf16[32,9,8,128]{3,2,1,0:T(8,128)(2,1)S(1)}, u32[]{:S(2)}, u32[]{:S(2)}) async-start(bf16[32,9,8,128]{3,2,1,0:T(8,128)(2,1)} %get-tuple-element.20), calls=%async_computation | async-start | bytes 1179648 | tf_op jit(solution)/shard_map/all_to_all | solution.py:424
  9.9 0.7 %copy-start.6 = (f32[8,128]{1,0:T(8,128)S(1)}, f32[8,128]{1,0:T(8,128)}, u32[]{:S(2)}) copy-start(f32[8,128]{1,0:T(8,128)} %get-tuple-element.21.keep_ref.refs_9_) | copy-start | bytes 12292
  10.6 14.5 %copy-start.7 = (bf16[256,2,256]{2,1,0:T(2,128)(2,1)S(1)}, bf16[256,2,256]{2,1,0:T(2,128)(2,1)}, u32[]{:S(2)}) copy-start(bf16[256,2,256]{2,1,0:T(2,128)(2,1)} %param.21) | copy-start | bytes 786436
  12.5 7.9 %collective-permute-start = (bf16[1,8,8,128]{3,2,1,0:T(8,128)(2,1)S(1)}, bf16[1,8,8,128]{3,2,1,0:T(8,128)(2,1)S(1)}, u32[]{:S(2)}, u32[]{:S(2)}) collective-permute-start(bf16[1,8,8,128]{3,2,1,0:T(8,128)(2,1)S(1)} %bitcast.23), channel_id=1, source_target_pairs={{0,8},{1,9},{2,10},{3,11},{4,12},{5,13},{6,14},{7,15},{8,0},{9,1},... | collective-permute-start | bytes 49160 | tf_op jit(solution)/shard_map/ppermute | solution.py:421
  20.4 4.6 %copy-start.8 = (bf16[1024,128]{1,0:T(8,128)(2,1)S(1)}, bf16[1024,128]{1,0:T(8,128)(2,1)}, u32[]{:S(2)}) copy-start(bf16[1024,128]{1,0:T(8,128)(2,1)} %param.25) | copy-start | bytes 786436
  20.4 7.2 %collective-permute-start.1 = (bf16[2,8,8,128]{3,2,1,0:T(8,128)(2,1)S(1)}, bf16[2,8,8,128]{3,2,1,0:T(8,128)(2,1)S(1)}, u32[]{:S(2)}, u32[]{:S(2)}) collective-permute-start(bf16[2,8,8,128]{3,2,1,0:T(8,128)(2,1)S(1)} %pad_maximum_fusion.2), channel_id=1, source_target_pairs={{0,16},{1,17},{2,18},{3,19},{4,20},{5,21},{6,22},{7,23},{8,24},{9,... | collective-permute-start | bytes 98312 | tf_op jit(solution)/shard_map/ppermute | solution.py:421
  25.1 1.0 %copy-start.9 = (bf16[256,4,128]{2,1,0:T(4,128)(2,1)S(1)}, bf16[256,4,128]{2,1,0:T(4,128)(2,1)}, u32[]{:S(2)}) copy-start(bf16[256,4,128]{2,1,0:T(4,128)(2,1)} %param.17) | copy-start | bytes 786436
  27.7 1.6 %collective-permute-start.2 = (bf16[32,4,8,128]{3,2,1,0:T(8,128)(2,1)S(1)}, bf16[32,4,8,128]{3,2,1,0:T(8,128)(2,1)S(1)}, u32[]{:S(2)}, u32[]{:S(2)}) collective-permute-start(bf16[32,4,8,128]{3,2,1,0:T(8,128)(2,1)S(1)} %slice.3), channel_id=1, source_target_pairs={{0,2},{1,3},{2,0},{3,1},{4,6},{5,7},{6,4},{7,5},{8,10},{9,11},{10,... | collective-permute-start | bytes 786440 | tf_op jit(solution)/shard_map/ppermute | solution.py:421
  29.3 7.2 %copy-start.10 = (bf16[128,256]{1,0:T(8,128)(2,1)S(1)}, bf16[128,256]{1,0:T(8,128)(2,1)}, u32[]{:S(2)}) copy-start(bf16[128,256]{1,0:T(8,128)(2,1)} %param.18) | copy-start | bytes 196612
  30.7 4.3 %collective-permute-start.4 = (bf16[4,8,8,128]{3,2,1,0:T(8,128)(2,1)S(1)}, bf16[4,8,8,128]{3,2,1,0:T(8,128)(2,1)S(1)}, u32[]{:S(2)}, u32[]{:S(2)}) collective-permute-start(bf16[4,8,8,128]{3,2,1,0:T(8,128)(2,1)S(1)} %pad_maximum_fusion.1.refs_0_), channel_id=1, source_target_pairs={{0,4},{1,5},{2,6},{3,7},{4,0},{5,1},{6,2},{7,3},{8,12},{9,13},{10,... | collective-permute-start | bytes 196616 | tf_op jit(solution)/shard_map/ppermute | solution.py:421
  32.2 9.7 %collective-permute-start.5 = (bf16[4,8,8,128]{3,2,1,0:T(8,128)(2,1)S(1)}, bf16[4,8,8,128]{3,2,1,0:T(8,128)(2,1)S(1)}, u32[]{:S(2)}, u32[]{:S(2)}) collective-permute-start(bf16[4,8,8,128]{3,2,1,0:T(8,128)(2,1)S(1)} %pad_maximum_fusion.1.refs_0_), channel_id=1, source_target_pairs={{0,1},{1,0},{2,3},{3,2},{4,5},{5,4},{6,7},{7,6},{8,9},{9,8},{10,11... | collective-permute-start | bytes 196616 | tf_op jit(solution)/shard_map/ppermute | solution.py:421
  35.0 7.1 %collective-permute-start.6 = (bf16[4,8,8,128]{3,2,1,0:T(8,128)(2,1)S(1)}, bf16[4,8,8,128]{3,2,1,0:T(8,128)(2,1)S(1)}, u32[]{:S(2)}, u32[]{:S(2)}) collective-permute-start(bf16[4,8,8,128]{3,2,1,0:T(8,128)(2,1)S(1)} %collective-permute-done.4.refs_1_), channel_id=1, source_target_pairs={{0,1},{1,0},{2,3},{3,2},{4,5},{5,4},{6,7},{7,6},{8,9},{9,8},{10,11... | collective-permute-start | bytes 196616 | tf_op jit(solution)/shard_map/ppermute | solution.py:421
  36.5 5.9 %collective-permute-start.3 = (bf16[128,256]{1,0:T(8,128)(2,1)S(1)}, bf16[128,256]{1,0:T(8,128)(2,1)S(1)}, u32[]{:S(2)}, u32[]{:S(2)}) collective-permute-start(bf16[128,256]{1,0:T(8,128)(2,1)S(1)} %copy-done.10), channel_id=1, source_target_pairs={{0,1},{1,0},{2,3},{3,2},{4,5},{5,4},{6,7},{7,6},{8,9},{9,8},{10,11... | collective-permute-start | bytes 196616 | tf_op jit(solution)/shard_map/ppermute | solution.py:421
  37.0 5.4 %collective-permute-start.7 = (bf16[4,8,8,128]{3,2,1,0:T(8,128)(2,1)S(1)}, bf16[4,8,8,128]{3,2,1,0:T(8,128)(2,1)S(1)}, u32[]{:S(2)}, u32[]{:S(2)}) collective-permute-start(bf16[4,8,8,128]{3,2,1,0:T(8,128)(2,1)S(1)} %pad_maximum_fusion.1.refs_0_), channel_id=1, source_target_pairs={{0,2},{1,3},{2,0},{3,1},{4,6},{5,7},{6,4},{7,5},{8,10},{9,11},{10,... | collective-permute-start | bytes 196616 | tf_op jit(solution)/shard_map/ppermute | solution.py:421
  37.0 13.1 %all-to-all-start.1 = ((bf16[32,2,8,128]{3,2,1,0:T(8,128)(2,1)}), bf16[32,2,8,128]{3,2,1,0:T(8,128)(2,1)S(1)}, u32[]{:S(2)}, u32[]{:S(2)}) async-start(bf16[32,2,8,128]{3,2,1,0:T(8,128)(2,1)} %shard_map.143), calls=%async_computation.1 | async-start | bytes 262144 | tf_op jit(solution)/shard_map/all_to_all | solution.py:424
  41.5 1.3 %collective-permute-start.8 = (bf16[4,8,8,128]{3,2,1,0:T(8,128)(2,1)S(1)}, bf16[4,8,8,128]{3,2,1,0:T(8,128)(2,1)S(1)}, u32[]{:S(2)}, u32[]{:S(2)}) collective-permute-start(bf16[4,8,8,128]{3,2,1,0:T(8,128)(2,1)S(1)} %collective-permute-done.4.refs_1_), channel_id=1, source_target_pairs={{0,2},{1,3},{2,0},{3,1},{4,6},{5,7},{6,4},{7,5},{8,10},{9,11},{10,... | collective-permute-start | bytes 196616 | tf_op jit(solution)/shard_map/ppermute | solution.py:421
  41.9 1.3 %collective-permute-start.9 = (bf16[4,8,8,128]{3,2,1,0:T(8,128)(2,1)S(1)}, bf16[4,8,8,128]{3,2,1,0:T(8,128)(2,1)S(1)}, u32[]{:S(2)}, u32[]{:S(2)}) collective-permute-start(bf16[4,8,8,128]{3,2,1,0:T(8,128)(2,1)S(1)} %collective-permute-done.5.refs_2_), channel_id=1, source_target_pairs={{0,2},{1,3},{2,0},{3,1},{4,6},{5,7},{6,4},{7,5},{8,10},{9,11},{10,... | collective-permute-start | bytes 196616 | tf_op jit(solution)/shard_map/ppermute | solution.py:421
  42.1 1.3 %collective-permute-start.10 = (bf16[4,8,8,128]{3,2,1,0:T(8,128)(2,1)S(1)}, bf16[4,8,8,128]{3,2,1,0:T(8,128)(2,1)S(1)}, u32[]{:S(2)}, u32[]{:S(2)}) collective-permute-start(bf16[4,8,8,128]{3,2,1,0:T(8,128)(2,1)S(1)} %collective-permute-done.6.refs_3_), channel_id=1, source_target_pairs={{0,2},{1,3},{2,0},{3,1},{4,6},{5,7},{6,4},{7,5},{8,10},{9,11},{10,... | collective-permute-start | bytes 196616 | tf_op jit(solution)/shard_map/ppermute | solution.py:421
  43.4 6.8 %copy-start.1 = (bf16[256,256]{1,0:T(8,128)(2,1)S(1)}, bf16[256,256]{1,0:T(8,128)(2,1)}, u32[]{:S(2)}) copy-start(bf16[256,256]{1,0:T(8,128)(2,1)} %query_w_ref.1) | copy-start | bytes 393220
  43.4 6.8 %copy-start.2 = (bf16[256,256]{1,0:T(8,128)(2,1)S(1)}, bf16[256,256]{1,0:T(8,128)(2,1)}, u32[]{:S(2)}) copy-start(bf16[256,256]{1,0:T(8,128)(2,1)} %key_w_ref.1) | copy-start | bytes 393220
  43.4 6.8 %copy-start.3 = (bf16[256,256]{1,0:T(8,128)(2,1)S(1)}, bf16[256,256]{1,0:T(8,128)(2,1)}, u32[]{:S(2)}) copy-start(bf16[256,256]{1,0:T(8,128)(2,1)} %out_w_ref.1) | copy-start | bytes 393220

commit v10 on v8

--- a/solution.py
+++ b/solution.py
@@ -423,11 +423,6 @@
     def to_all(value):
         return lax.all_to_all(value, both, split_axis=0, concat_axis=0, tiled=True)
 
-    row_out_weight = jnp.stack(
-        [horizontal_final_matrix]
-        + [exchange(horizontal_final_matrix, relative) for relative in range(1, groups)]
-    )
-
     right_tiles = channels * sequences // LANES
     row_slots = sequences_here * (width // LANES)
     half_tiles = heads_here // 2 * row_tiles * column_tiles
@@ -459,22 +454,23 @@
         (homolog_activity, keep, first_operand_matrix.T, second_operand_matrix.T),
         mib=56 if large else 32,
     )
-    right = right_out[None]
-    mask = 4 * groups
-    while mask < devices:
-        right = jnp.concatenate([right, exchange(right, mask)])
-        mask *= 2
+    pieces = [right_out] + [
+        exchange(right_out, near * 4 * groups) for near in range(1, parallel // 4)
+    ]
+    right = jnp.stack(pieces)
+    right_masks = [across * 2 * groups + mask for across in range(2) for mask in range(groups)]
+    right_parts = [right] + [exchange(right, mask) for mask in right_masks[1:]]
+    row_out_weight = jnp.stack(
+        [horizontal_final_matrix]
+        + [exchange(horizontal_final_matrix, relative) for relative in range(1, groups)]
+    )
 
     row_weight = horizontal_projection_matrix.transpose(1, 0, 2)
     outer_weight = outer_output_weight.reshape(channels, channels, depth).transpose(1, 0, 2)
     content_weight = vertical_content_sigmoid_matrix.transpose(1, 0, 2)
-    right_masks, right_parts = [0], [right]
-    for mask in (2 * groups, *range(1, groups)):
-        right_masks.append(mask)
-        right_parts.append(exchange(right, mask))
-    rows_in, row_weight, outer_weight, content_weight, row_out_weight, _ = (
+    rows_in, row_weight, outer_weight, content_weight, row_out_weight, *right_parts = (
         lax.optimization_barrier(
-            (rows_in, row_weight, outer_weight, content_weight, row_out_weight, right)
+            (rows_in, row_weight, outer_weight, content_weight, row_out_weight, *right_parts)
         )
     )
     other_bias = exchange(rows_in[:, row_slots:-1], groups)
@@ -507,9 +503,6 @@
     )
     mix_in = to_all(mix_out)
     *late_parts, _ = lax.optimization_barrier((*right_parts, mix_out))
-    for mask in range(1, groups):
-        right_masks.append(2 * groups + mask)
-        late_parts.append(exchange(late_parts[1], mask))
     right_masks += [mask + groups for mask in right_masks]
     late_parts += [exchange(late_part, groups) for late_part in late_parts]
 

time: 51.1 us -> 53.1 us (1.039)
  waiting for transfers between devices: 13.3 us -> 18 us
  starting transfers between devices: 23.4 us -> 20.8 us
    ppermute x11 -> x12, waiting for transfers between devices: 8.84 us -> 13.5 us  [exchange(): return lax.ppermute(value, both, [(at, at ^ mask) for at in range(devices)])]
    ppermute x11 -> x12, starting transfers between devices: 13.6 us -> 10.9 us  [exchange(): return lax.ppermute(value, both, [(at, at ^ mask) for at in range(devices)])]
  transfers between devices with their start and end apart: 13 -> 14, of which waited for: 8 -> 11; matrix products, arithmetic and copies ran while one was open for 0% -> 0% of each run, Pallas kernels for 13% -> 10%
where the time goes in v10:
time: 53.1 us; the launch traced here: 52.7 us
  starting transfers between devices  20.8 us (39%)
  waiting for transfers between devices  18 us (34%)
  Pallas kernels  11.5 us (22%)
  local copies, waits for them, and re-layouts  1.71 us (3%)
  between operations  0.8 us (2%)
    ppermute x12, waiting for transfers between devices, exchange(): return lax.ppermute(value, both, [(at, at ^ mask) for at in range(devices)])  13.5 us
    pallas_call x6, Pallas kernels, call(): pl.pallas_call(kernel, out_shape=outs, in_specs=[smem] * scalars + [read]...  11.5 us
    ppermute x12, starting transfers between devices, exchange(): return lax.ppermute(value, both, [(at, at ^ mask) for at in range(devices)])  10.9 us
    all_to_all x2, starting transfers between devices, to_all(): return lax.all_to_all(value, both, split_axis=0, concat_axis=0, tiled=True)  9.88 us
    all_to_all x2, waiting for transfers between devices, to_all(): return lax.all_to_all(value, both, split_axis=0, concat_axis=0, tiled=True)  4.47 us
    unnamed x24, local copies, waits for them, and re-layouts  1.59 us
  transfers between devices with their start and end apart: 14, of which 11 were waited for; matrix products, arithmetic and copies ran while one was open for 0% of the time, Pallas kernels for 10%

profile of v10, /device:TPU:0, one launch (start us, length us, event | category | flops | bytes accessed | tf_op | source)
XLA Modules:
  0.0 52.7 jit_solution(14428218499623969534)
XLA Ops:
  0.6 1.9 %shard_map.140 = (bf16[32,9,8,128]{3,2,1,0:T(8,128)(2,1)}, f32[8,128]{1,0:T(8,128)}) custom-call(bf16[8,16,128]{2,1,0:T(8,128)(2,1)} %bias_hbm.1, s32[8,32]{1,0:T(8,128)} %bitcast.35, s32[1,32]{1,0:T(1,128)} %bitcast.36, bf16[32,8,256]{2,1,0:T(8,128)(2,1)} %x_ref.3), custom_call_target="tpu_custom_call" | custom-call | flops 2000000000 | bytes 2000000 | tf_op jit(solution)/shard_map/pallas_call | solution.py:377
  2.5 0.0 copy-start
  2.5 0.0 copy-start.4
  2.5 0.0 copy-start.5
  2.5 7.3 %all-to-all-start = ((bf16[32,9,8,128]{3,2,1,0:T(8,128)(2,1)}), bf16[32,9,8,128]{3,2,1,0:T(8,128)(2,1)S(1)}, u32[]{:S(2)}, u32[]{:S(2)}) async-start(bf16[32,9,8,128]{3,2,1,0:T(8,128)(2,1)} %get-tuple-element.26), calls=%async_computation | async-start | bytes 1179648 | tf_op jit(solution)/shard_map/all_to_all | solution.py:424
  9.8 0.0 copy-start.6
  9.9 0.0 copy-done
  9.9 0.0 copy-done.4
  9.9 0.0 copy-done.5
  9.9 0.6 %copy-done.6 = f32[8,128]{1,0:T(8,128)S(1)} copy-done((f32[8,128]{1,0:T(8,128)S(1)}, f32[8,128]{1,0:T(8,128)}, u32[]{:S(2)}) %copy-start.6) | copy-done | bytes 4120
  10.5 1.9 %shard_map.141 = (bf16[8,8,128]{2,1,0:T(8,128)(2,1)S(1)}, bf16[256,32]{1,0:T(8,128)(2,1)S(1)}) custom-call(bf16[32,8,256]{2,1,0:T(8,128)(2,1)S(1)} %copy-done, f32[8,128]{1,0:T(8,128)S(1)} %copy-done.6, bf16[32,256]{1,0:T(8,128)(2,1)S(1)} %bitcast.27, bf16[32,256]{1,0:T(8,128)(2,1)S(1)} %bitcast.28), custom_call_target="tpu_custom_call" | custom-call | flops 2000000000 | bytes 2000000 | tf_op jit(solution)/shard_map/pallas_call | solution.py:377
  12.5 1.8 %collective-permute-start.1 = (bf16[8,8,128]{2,1,0:T(8,128)(2,1)S(1)}, bf16[8,8,128]{2,1,0:T(8,128)(2,1)S(1)}, u32[]{:S(2)}, u32[]{:S(2)}) collective-permute-start(bf16[8,8,128]{2,1,0:T(8,128)(2,1)S(1)} %get-tuple-element.28), channel_id=1, source_target_pairs={{0,8},{1,9},{2,10},{3,11},{4,12},{5,13},{6,14},{7,15},{8,0},{9,1},... | collective-permute-start | bytes 49160 | tf_op jit(solution)/shard_map/ppermute | solution.py:421
  14.3 2.4 %collective-permute-start.2 = (bf16[8,8,128]{2,1,0:T(8,128)(2,1)S(1)}, bf16[8,8,128]{2,1,0:T(8,128)(2,1)S(1)}, u32[]{:S(2)}, u32[]{:S(2)}) collective-permute-start(bf16[8,8,128]{2,1,0:T(8,128)(2,1)S(1)} %get-tuple-element.28), channel_id=1, source_target_pairs={{0,16},{1,17},{2,18},{3,19},{4,20},{5,21},{6,22},{7,23},{8,24},{9,... | collective-permute-start | bytes 49160 | tf_op jit(solution)/shard_map/ppermute | solution.py:421
  16.7 0.2 collective-permute-start.3
  16.9 0.0 copy-done.10
  16.9 1.8 %collective-permute-start = (bf16[128,256]{1,0:T(8,128)(2,1)S(1)}, bf16[128,256]{1,0:T(8,128)(2,1)S(1)}, u32[]{:S(2)}, u32[]{:S(2)}) collective-permute-start(bf16[128,256]{1,0:T(8,128)(2,1)S(1)} %copy-done.10), channel_id=1, source_target_pairs={{0,1},{1,0},{2,3},{3,2},{4,5},{5,4},{6,7},{7,6},{8,9},{9,8},{10,11... | collective-permute-start | bytes 196616 | tf_op jit(solution)/shard_map/ppermute | solution.py:421
  18.7 0.0 copy-done.7
  18.7 0.0 copy-start.9
  18.7 0.1 copy.24
  18.8 0.8 %copy-done.9 = bf16[256,4,128]{2,1,0:T(4,128)(2,1)S(1)} copy-done((bf16[256,4,128]{2,1,0:T(4,128)(2,1)S(1)}, bf16[256,4,128]{2,1,0:T(4,128)(2,1)}, u32[]{:S(2)}) %copy-start.9) | copy-done | bytes 262168
  19.7 1.0 %collective-permute-done.1 = bf16[8,8,128]{2,1,0:T(8,128)(2,1)S(1)} collective-permute-done((bf16[8,8,128]{2,1,0:T(8,128)(2,1)S(1)}, bf16[8,8,128]{2,1,0:T(8,128)(2,1)S(1)}, u32[]{:S(2)}, u32[]{:S(2)}) %collective-permute-start.1) | collective-permute-done | bytes 16416 | tf_op jit(solution)/shard_map/ppermute | solution.py:421
  20.7 6.8 %collective-permute-done.2 = bf16[8,8,128]{2,1,0:T(8,128)(2,1)S(1)} collective-permute-done((bf16[8,8,128]{2,1,0:T(8,128)(2,1)S(1)}, bf16[8,8,128]{2,1,0:T(8,128)(2,1)S(1)}, u32[]{:S(2)}, u32[]{:S(2)}) %collective-permute-start.2) | collective-permute-done | bytes 16416 | tf_op jit(solution)/shard_map/ppermute | solution.py:421
  27.5 0.0 collective-permute-done.3
  27.5 1.5 %collective-permute-start.4 = (bf16[4,8,8,128]{3,2,1,0:T(8,128)(2,1)S(1)}, bf16[4,8,8,128]{3,2,1,0:T(8,128)(2,1)S(1)}, u32[]{:S(2)}, u32[]{:S(2)}) collective-permute-start(bf16[4,8,8,128]{3,2,1,0:T(8,128)(2,1)S(1)} %pad_maximum_fusion.1.refs_0_), channel_id=1, source_target_pairs={{0,1},{1,0},{2,3},{3,2},{4,5},{5,4},{6,7},{7,6},{8,9},{9,8},{10,11... | collective-permute-start | bytes 196616 | tf_op jit(solution)/shard_map/ppermute | solution.py:421
  29.0 1.5 %collective-permute-start.5 = (bf16[4,8,8,128]{3,2,1,0:T(8,128)(2,1)S(1)}, bf16[4,8,8,128]{3,2,1,0:T(8,128)(2,1)S(1)}, u32[]{:S(2)}, u32[]{:S(2)}) collective-permute-start(bf16[4,8,8,128]{3,2,1,0:T(8,128)(2,1)S(1)} %pad_maximum_fusion.1.refs_0_), channel_id=1, source_target_pairs={{0,4},{1,5},{2,6},{3,7},{4,0},{5,1},{6,2},{7,3},{8,12},{9,13},{10,... | collective-permute-start | bytes 196616 | tf_op jit(solution)/shard_map/ppermute | solution.py:421
  30.5 0.5 %collective-permute-start.6 = (bf16[4,8,8,128]{3,2,1,0:T(8,128)(2,1)S(1)}, bf16[4,8,8,128]{3,2,1,0:T(8,128)(2,1)S(1)}, u32[]{:S(2)}, u32[]{:S(2)}) collective-permute-start(bf16[4,8,8,128]{3,2,1,0:T(8,128)(2,1)S(1)} %pad_maximum_fusion.1.refs_0_), channel_id=1, source_target_pairs={{0,5},{1,4},{2,7},{3,6},{4,1},{5,0},{6,3},{7,2},{8,13},{9,12},{10,... | collective-permute-start | bytes 196616 | tf_op jit(solution)/shard_map/ppermute | solution.py:421
  31.0 0.0 collective-permute-done
  31.1 0.8 %collective-permute-done.4.refs_1_ = bf16[4,8,8,128]{3,2,1,0:T(8,128)(2,1)S(1)} collective-permute-done((bf16[4,8,8,128]{3,2,1,0:T(8,128)(2,1)S(1)}, bf16[4,8,8,128]{3,2,1,0:T(8,128)(2,1)S(1)}, u32[]{:S(2)}, u32[]{:S(2)}) %collective-permute-start.4) | collective-permute-done | bytes 65568 | tf_op jit(solution)/shard_map/ppermute | solution.py:421
  31.8 1.5 %collective-permute-done.5.refs_2_ = bf16[4,8,8,128]{3,2,1,0:T(8,128)(2,1)S(1)} collective-permute-done((bf16[4,8,8,128]{3,2,1,0:T(8,128)(2,1)S(1)}, bf16[4,8,8,128]{3,2,1,0:T(8,128)(2,1)S(1)}, u32[]{:S(2)}, u32[]{:S(2)}) %collective-permute-start.5) | collective-permute-done | bytes 65568 | tf_op jit(solution)/shard_map/ppermute | solution.py:421
  33.3 2.4 %collective-permute-done.6.refs_3_ = bf16[4,8,8,128]{3,2,1,0:T(8,128)(2,1)S(1)} collective-permute-done((bf16[4,8,8,128]{3,2,1,0:T(8,128)(2,1)S(1)}, bf16[4,8,8,128]{3,2,1,0:T(8,128)(2,1)S(1)}, u32[]{:S(2)}, u32[]{:S(2)}) %collective-permute-start.6) | collective-permute-done | bytes 65568 | tf_op jit(solution)/shard_map/ppermute | solution.py:421
  35.7 0.0 all-to-all-done.rows_ref
  35.7 0.1 collective-permute-start.7
  35.8 1.3 %shard_map.142 = (f32[2,256,128]{2,1,0:T(8,128)S(1)}, bf16[256,128]{1,0:T(8,128)(2,1)S(1)}, f32[8,256]{1,0:T(8,128)S(1)}, bf16[2,256,128]{2,1,0:T(8,128)(2,1)S(1...) custom-call(s32[1]{0:T(128)} %bitcast.place_ref, ...), custom_call_target="tpu_custom_call" | custom-call | flops 100000000 | bytes 100000 | tf_op jit(solution)/shard_map/pallas_call | solution.py:377
  37.1 0.2 collective-permute-done.7.swapped_ref
  37.3 1.4 %shard_map.143 = bf16[32,2,8,128]{3,2,1,0:T(8,128)(2,1)} custom-call(s32[1]{0:T(128)} %bitcast.place_ref, bf16[32,4,8,128]{3,2,1,0:T(8,128)(2,1)S(1)} %collective-permute-done.7.swapped_ref, f32[2,256,128]{2,1,0:T(8,128)S(1)} %get-tuple-element.31.part_ref, f32[8,256]{1,0:T(8,128)S(1)} %get-tuple-element.32.key_keep_ref, ...), custom_call_target="tpu_custom_call" | custom-call | flops 100000000 | bytes 100000 | tf_op jit(solution)/shard_map/pallas_call | solution.py:377
  38.7 2.6 %all-to-all-start.1 = ((bf16[32,2,8,128]{3,2,1,0:T(8,128)(2,1)}), bf16[32,2,8,128]{3,2,1,0:T(8,128)(2,1)S(1)}, u32[]{:S(2)}, u32[]{:S(2)}) async-start(bf16[32,2,8,128]{3,2,1,0:T(8,128)(2,1)} %shard_map.143), calls=%async_computation.1 | async-start | bytes 262144 | tf_op jit(solution)/shard_map/all_to_all | solution.py:424
  41.3 0.2 collective-permute-start.10
  41.5 0.4 collective-permute-start.11
  41.9 0.1 collective-permute-start.8
  42.0 0.4 collective-permute-start.9
  42.4 0.2 collective-permute-done.10.refs_6_
  42.6 0.2 collective-permute-done.11.refs_7_
  42.8 0.4 collective-permute-done.8.refs_4_
  43.1 0.2 collective-permute-done.9.refs_5_
  43.3 2.2 %shard_map.145 = bf16[8,256,128]{2,1,0:T(8,128)(2,1)} custom-call(s32[1]{0:T(128)} %bitcast.place_ref, bf16[256,128]{1,0:T(8,128)(2,1)S(1)} %get-tuple-element.39.keep_all_ref, bf16[4,8,8,128]{3,2,1,0:T(8,128)(2,1)S(1)} %pad_maximum_fusion.1.refs_0_, bf16[4,8,8,128]{3,2,1,0:T(8,128)(2,1)S(1)} %collective-permute-done.4.refs_1_, ...), custom_call_target="tpu_custom_call" | custom-call | flops 2000000000 | bytes 2000000 | tf_op jit(solution)/shard_map/pallas_call | solution.py:377
  45.4 4.5 %all-to-all-done.1 = bf16[32,2,8,128]{3,2,1,0:T(8,128)(2,1)S(1)} async-done(((bf16[32,2,8,128]{3,2,1,0:T(8,128)(2,1)}), bf16[32,2,8,128]{3,2,1,0:T(8,128)(2,1)S(1)}, u32[]{:S(2)}, u32[]{:S(2)}) %all-to-all-start.1) | async-done | bytes 131104 | tf_op jit(solution)/shard_map/all_to_all | solution.py:424
  49.9 0.0 copy-done.3
  49.9 2.8 %shard_map.144 = bf16[32,8,256]{2,1,0:T(8,128)(2,1)} custom-call(s32[1]{0:T(128)} %bitcast.place_ref, bf16[32,8,256]{2,1,0:T(8,128)(2,1)S(1)} %copy-done, bf16[16,2,2,8,128]{4,3,2,1,0:T(8,128)(2,1)S(1)} %bitcast.25, f32[8,128]{1,0:T(8,128)S(1)} %copy-done.6, bf16[2,128,256]{2,1,0:T(8,128)(2,1)S(1)} %pad_maximum_fusion.row_out_ref, ...), custom_call_target="tpu_custom_call" | custom-call | flops 3000000000 | bytes 3000000 | tf_op jit(solution)/shard_map/pallas_call | solution.py:377
  (14 shorter events, 0.1 us)
Async XLA Ops:
  2.5 7.4 %copy-start = (bf16[32,8,256]{2,1,0:T(8,128)(2,1)S(1)}, bf16[32,8,256]{2,1,0:T(8,128)(2,1)}, u32[]{:S(2)}) copy-start(bf16[32,8,256]{2,1,0:T(8,128)(2,1)} %x_ref.3) | copy-start | bytes 393220
  2.5 7.4 %copy-start.4 = (bf16[256,32]{0,1:T(8,128)(2,1)S(1)}, bf16[256,32]{0,1:T(8,128)(2,1)}, u32[]{:S(2)}) copy-start(bf16[256,32]{0,1:T(8,128)(2,1)} %param.23) | copy-start | bytes 49156
  2.5 7.4 %copy-start.5 = (bf16[256,32]{0,1:T(8,128)(2,1)S(1)}, bf16[256,32]{0,1:T(8,128)(2,1)}, u32[]{:S(2)}) copy-start(bf16[256,32]{0,1:T(8,128)(2,1)} %param.24) | copy-start | bytes 49156
  2.5 33.2 %all-to-all-start = ((bf16[32,9,8,128]{3,2,1,0:T(8,128)(2,1)}), bf16[32,9,8,128]{3,2,1,0:T(8,128)(2,1)S(1)}, u32[]{:S(2)}, u32[]{:S(2)}) async-start(bf16[32,9,8,128]{3,2,1,0:T(8,128)(2,1)} %get-tuple-element.26), calls=%async_computation | async-start | bytes 1179648 | tf_op jit(solution)/shard_map/all_to_all | solution.py:424
  9.8 0.7 %copy-start.6 = (f32[8,128]{1,0:T(8,128)S(1)}, f32[8,128]{1,0:T(8,128)}, u32[]{:S(2)}) copy-start(f32[8,128]{1,0:T(8,128)} %get-tuple-element.27.keep_ref.refs_9_) | copy-start | bytes 12292
  10.5 6.4 %copy-start.10 = (bf16[128,256]{1,0:T(8,128)(2,1)S(1)}, bf16[128,256]{1,0:T(8,128)(2,1)}, u32[]{:S(2)}) copy-start(bf16[128,256]{1,0:T(8,128)(2,1)} %param.18) | copy-start | bytes 196612
  10.5 8.1 %copy-start.7 = (bf16[256,2,256]{2,1,0:T(2,128)(2,1)S(1)}, bf16[256,2,256]{2,1,0:T(2,128)(2,1)}, u32[]{:S(2)}) copy-start(bf16[256,2,256]{2,1,0:T(2,128)(2,1)} %param.21) | copy-start | bytes 786436
  12.5 6.2 %copy-start.8 = (bf16[1024,128]{1,0:T(8,128)(2,1)S(1)}, bf16[1024,128]{1,0:T(8,128)(2,1)}, u32[]{:S(2)}) copy-start(bf16[1024,128]{1,0:T(8,128)(2,1)} %param.25) | copy-start | bytes 786436
  12.5 8.2 %collective-permute-start.1 = (bf16[8,8,128]{2,1,0:T(8,128)(2,1)S(1)}, bf16[8,8,128]{2,1,0:T(8,128)(2,1)S(1)}, u32[]{:S(2)}, u32[]{:S(2)}) collective-permute-start(bf16[8,8,128]{2,1,0:T(8,128)(2,1)S(1)} %get-tuple-element.28), channel_id=1, source_target_pairs={{0,8},{1,9},{2,10},{3,11},{4,12},{5,13},{6,14},{7,15},{8,0},{9,1},... | collective-permute-start | bytes 49160 | tf_op jit(solution)/shard_map/ppermute | solution.py:421
  14.3 13.2 %collective-permute-start.2 = (bf16[8,8,128]{2,1,0:T(8,128)(2,1)S(1)}, bf16[8,8,128]{2,1,0:T(8,128)(2,1)S(1)}, u32[]{:S(2)}, u32[]{:S(2)}) collective-permute-start(bf16[8,8,128]{2,1,0:T(8,128)(2,1)S(1)} %get-tuple-element.28), channel_id=1, source_target_pairs={{0,16},{1,17},{2,18},{3,19},{4,20},{5,21},{6,22},{7,23},{8,24},{9,... | collective-permute-start | bytes 49160 | tf_op jit(solution)/shard_map/ppermute | solution.py:421
  16.7 10.8 %collective-permute-start.3 = (bf16[8,8,128]{2,1,0:T(8,128)(2,1)S(1)}, bf16[8,8,128]{2,1,0:T(8,128)(2,1)S(1)}, u32[]{:S(2)}, u32[]{:S(2)}) collective-permute-start(bf16[8,8,128]{2,1,0:T(8,128)(2,1)S(1)} %get-tuple-element.28), channel_id=1, source_target_pairs={{0,24},{1,25},{2,26},{3,27},{4,28},{5,29},{6,30},{7,31},{8,16},{9,... | collective-permute-start | bytes 49160 | tf_op jit(solution)/shard_map/ppermute | solution.py:421
  16.9 14.2 %collective-permute-start = (bf16[128,256]{1,0:T(8,128)(2,1)S(1)}, bf16[128,256]{1,0:T(8,128)(2,1)S(1)}, u32[]{:S(2)}, u32[]{:S(2)}) collective-permute-start(bf16[128,256]{1,0:T(8,128)(2,1)S(1)} %copy-done.10), channel_id=1, source_target_pairs={{0,1},{1,0},{2,3},{3,2},{4,5},{5,4},{6,7},{7,6},{8,9},{9,8},{10,11... | collective-permute-start | bytes 196616 | tf_op jit(solution)/shard_map/ppermute | solution.py:421
  18.7 1.0 %copy-start.9 = (bf16[256,4,128]{2,1,0:T(4,128)(2,1)S(1)}, bf16[256,4,128]{2,1,0:T(4,128)(2,1)}, u32[]{:S(2)}) copy-start(bf16[256,4,128]{2,1,0:T(4,128)(2,1)} %param.17) | copy-start | bytes 786436
  27.5 4.3 %collective-permute-start.4 = (bf16[4,8,8,128]{3,2,1,0:T(8,128)(2,1)S(1)}, bf16[4,8,8,128]{3,2,1,0:T(8,128)(2,1)S(1)}, u32[]{:S(2)}, u32[]{:S(2)}) collective-permute-start(bf16[4,8,8,128]{3,2,1,0:T(8,128)(2,1)S(1)} %pad_maximum_fusion.1.refs_0_), channel_id=1, source_target_pairs={{0,1},{1,0},{2,3},{3,2},{4,5},{5,4},{6,7},{7,6},{8,9},{9,8},{10,11... | collective-permute-start | bytes 196616 | tf_op jit(solution)/shard_map/ppermute | solution.py:421
  29.0 4.3 %collective-permute-start.5 = (bf16[4,8,8,128]{3,2,1,0:T(8,128)(2,1)S(1)}, bf16[4,8,8,128]{3,2,1,0:T(8,128)(2,1)S(1)}, u32[]{:S(2)}, u32[]{:S(2)}) collective-permute-start(bf16[4,8,8,128]{3,2,1,0:T(8,128)(2,1)S(1)} %pad_maximum_fusion.1.refs_0_), channel_id=1, source_target_pairs={{0,4},{1,5},{2,6},{3,7},{4,0},{5,1},{6,2},{7,3},{8,12},{9,13},{10,... | collective-permute-start | bytes 196616 | tf_op jit(solution)/shard_map/ppermute | solution.py:421
  30.5 5.2 %collective-permute-start.6 = (bf16[4,8,8,128]{3,2,1,0:T(8,128)(2,1)S(1)}, bf16[4,8,8,128]{3,2,1,0:T(8,128)(2,1)S(1)}, u32[]{:S(2)}, u32[]{:S(2)}) collective-permute-start(bf16[4,8,8,128]{3,2,1,0:T(8,128)(2,1)S(1)} %pad_maximum_fusion.1.refs_0_), channel_id=1, source_target_pairs={{0,5},{1,4},{2,7},{3,6},{4,1},{5,0},{6,3},{7,2},{8,13},{9,12},{10,... | collective-permute-start | bytes 196616 | tf_op jit(solution)/shard_map/ppermute | solution.py:421
  35.7 1.6 %collective-permute-start.7 = (bf16[32,4,8,128]{3,2,1,0:T(8,128)(2,1)S(1)}, bf16[32,4,8,128]{3,2,1,0:T(8,128)(2,1)S(1)}, u32[]{:S(2)}, u32[]{:S(2)}) collective-permute-start(bf16[32,4,8,128]{3,2,1,0:T(8,128)(2,1)S(1)} %slice.3), channel_id=1, source_target_pairs={{0,2},{1,3},{2,0},{3,1},{4,6},{5,7},{6,4},{7,5},{8,10},{9,11},{10,... | collective-permute-start | bytes 786440 | tf_op jit(solution)/shard_map/ppermute | solution.py:421
  38.7 11.2 %all-to-all-start.1 = ((bf16[32,2,8,128]{3,2,1,0:T(8,128)(2,1)}), bf16[32,2,8,128]{3,2,1,0:T(8,128)(2,1)S(1)}, u32[]{:S(2)}, u32[]{:S(2)}) async-start(bf16[32,2,8,128]{3,2,1,0:T(8,128)(2,1)} %shard_map.143), calls=%async_computation.1 | async-start | bytes 262144 | tf_op jit(solution)/shard_map/all_to_all | solution.py:424
  41.3 1.3 %collective-permute-start.10 = (bf16[4,8,8,128]{3,2,1,0:T(8,128)(2,1)S(1)}, bf16[4,8,8,128]{3,2,1,0:T(8,128)(2,1)S(1)}, u32[]{:S(2)}, u32[]{:S(2)}) collective-permute-start(bf16[4,8,8,128]{3,2,1,0:T(8,128)(2,1)S(1)} %collective-permute-done.5.refs_2_), channel_id=1, source_target_pairs={{0,2},{1,3},{2,0},{3,1},{4,6},{5,7},{6,4},{7,5},{8,10},{9,11},{10,... | collective-permute-start | bytes 196616 | tf_op jit(solution)/shard_map/ppermute | solution.py:421
  41.5 1.3 %collective-permute-start.11 = (bf16[4,8,8,128]{3,2,1,0:T(8,128)(2,1)S(1)}, bf16[4,8,8,128]{3,2,1,0:T(8,128)(2,1)S(1)}, u32[]{:S(2)}, u32[]{:S(2)}) collective-permute-start(bf16[4,8,8,128]{3,2,1,0:T(8,128)(2,1)S(1)} %collective-permute-done.6.refs_3_), channel_id=1, source_target_pairs={{0,2},{1,3},{2,0},{3,1},{4,6},{5,7},{6,4},{7,5},{8,10},{9,11},{10,... | collective-permute-start | bytes 196616 | tf_op jit(solution)/shard_map/ppermute | solution.py:421
  41.9 1.3 %collective-permute-start.8 = (bf16[4,8,8,128]{3,2,1,0:T(8,128)(2,1)S(1)}, bf16[4,8,8,128]{3,2,1,0:T(8,128)(2,1)S(1)}, u32[]{:S(2)}, u32[]{:S(2)}) collective-permute-start(bf16[4,8,8,128]{3,2,1,0:T(8,128)(2,1)S(1)} %pad_maximum_fusion.1.refs_0_), channel_id=1, source_target_pairs={{0,2},{1,3},{2,0},{3,1},{4,6},{5,7},{6,4},{7,5},{8,10},{9,11},{10,... | collective-permute-start | bytes 196616 | tf_op jit(solution)/shard_map/ppermute | solution.py:421
  42.0 1.3 %collective-permute-start.9 = (bf16[4,8,8,128]{3,2,1,0:T(8,128)(2,1)S(1)}, bf16[4,8,8,128]{3,2,1,0:T(8,128)(2,1)S(1)}, u32[]{:S(2)}, u32[]{:S(2)}) collective-permute-start(bf16[4,8,8,128]{3,2,1,0:T(8,128)(2,1)S(1)} %collective-permute-done.4.refs_1_), channel_id=1, source_target_pairs={{0,2},{1,3},{2,0},{3,1},{4,6},{5,7},{6,4},{7,5},{8,10},{9,11},{10,... | collective-permute-start | bytes 196616 | tf_op jit(solution)/shard_map/ppermute | solution.py:421
  43.3 6.6 %copy-start.1 = (bf16[256,256]{1,0:T(8,128)(2,1)S(1)}, bf16[256,256]{1,0:T(8,128)(2,1)}, u32[]{:S(2)}) copy-start(bf16[256,256]{1,0:T(8,128)(2,1)} %query_w_ref.1) | copy-start | bytes 393220
  43.3 6.6 %copy-start.2 = (bf16[256,256]{1,0:T(8,128)(2,1)S(1)}, bf16[256,256]{1,0:T(8,128)(2,1)}, u32[]{:S(2)}) copy-start(bf16[256,256]{1,0:T(8,128)(2,1)} %key_w_ref.1) | copy-start | bytes 393220
  43.3 6.6 %copy-start.3 = (bf16[256,256]{1,0:T(8,128)(2,1)S(1)}, bf16[256,256]{1,0:T(8,128)(2,1)}, u32[]{:S(2)}) copy-start(bf16[256,256]{1,0:T(8,128)(2,1)} %out_w_ref.1) | copy-start | bytes 393220

commit v11 on v9

--- a/solution.py
+++ b/solution.py
@@ -463,7 +463,8 @@
     row_weight = horizontal_projection_matrix.transpose(1, 0, 2)
     outer_weight = outer_output_weight.reshape(channels, channels, depth).transpose(1, 0, 2)
     content_weight = vertical_content_sigmoid_matrix.transpose(1, 0, 2)
-    rows_in, row_weight, outer_weight, content_weight, right = lax.optimization_barrier(
+    across = exchange(right, 2 * groups)
+    rows_in, row_weight, outer_weight, content_weight, _ = lax.optimization_barrier(
         (rows_in, row_weight, outer_weight, content_weight, right)
     )
     other_bias = exchange(rows_in[:, row_slots:-1], groups)
@@ -495,17 +496,16 @@
         micros=0.1,
     )
     mix_in = to_all(mix_out)
-    right, own_final, _ = lax.optimization_barrier((right, horizontal_final_matrix, mix_out))
-    right_masks, late_parts = [0], [right]
-    for mask in (2 * groups, *range(1, groups)):
-        right_masks.append(mask)
-        late_parts.append(exchange(right, mask))
-    row_out_weight = jnp.stack(
-        [own_final] + [exchange(own_final, relative) for relative in range(1, groups)]
-    )
+    right, across, own_final, _ = lax.optimization_barrier(
+        (right, across, horizontal_final_matrix, mix_out)
+    )
+    right_masks, late_parts = [0, 2 * groups], [right, across]
+    final_parts = [own_final]
     for mask in range(1, groups):
-        right_masks.append(2 * groups + mask)
-        late_parts.append(exchange(late_parts[1], mask))
+        right_masks += [mask, 2 * groups + mask]
+        late_parts += [exchange(right, mask), exchange(across, mask)]
+        final_parts.append(exchange(own_final, mask))
+    row_out_weight = jnp.stack(final_parts)
     right_masks += [mask + groups for mask in right_masks]
     late_parts += [exchange(late_part, groups) for late_part in late_parts]
 

time: 53.3 us -> 51.6 us (0.968)
  waiting for transfers between devices: 14.9 us -> 13.9 us
  starting transfers between devices: 24.1 us -> 23.3 us
    ppermute x11, waiting for transfers between devices: 10.3 us -> 8.99 us  [exchange(): return lax.ppermute(value, both, [(at, at ^ mask) for at in range(devices)])]
    all_to_all x2, starting transfers between devices: 11.8 us -> 10.8 us  [to_all(): return lax.all_to_all(value, both, split_axis=0, concat_axis=0, tiled=True)]
  transfers between devices with their start and end apart: 13 -> 13, of which waited for: 8 -> 6; matrix products, arithmetic and copies ran while one was open for 0% -> 0% of each run, Pallas kernels for 10% -> 13%
where the time goes in v11:
time: 51.6 us; the launch traced here: 51.3 us
  starting transfers between devices  23.3 us (45%)
  waiting for transfers between devices  13.9 us (27%)
  Pallas kernels  11.5 us (22%)
  local copies, waits for them, and re-layouts  1.72 us (3%)
  between operations  0.84 us (2%)
    ppermute x11, starting transfers between devices, exchange(): return lax.ppermute(value, both, [(at, at ^ mask) for at in range(devices)])  12.6 us
    pallas_call x6, Pallas kernels, call(): pl.pallas_call(kernel, out_shape=outs, in_specs=[smem] * scalars + [read]...  11.5 us
    all_to_all x2, starting transfers between devices, to_all(): return lax.all_to_all(value, both, split_axis=0, concat_axis=0, tiled=True)  10.8 us
    ppermute x11, waiting for transfers between devices, exchange(): return lax.ppermute(value, both, [(at, at ^ mask) for at in range(devices)])  8.99 us
    all_to_all x2, waiting for transfers between devices, to_all(): return lax.all_to_all(value, both, split_axis=0, concat_axis=0, tiled=True)  4.87 us
    unnamed x24, local copies, waits for them, and re-layouts  1.59 us
  transfers between devices with their start and end apart: 13, of which 6 were waited for; matrix products, arithmetic and copies ran while one was open for 0% of the time, Pallas kernels for 13%

profile of v11, /device:TPU:0, one launch (start us, length us, event | category | flops | bytes accessed | tf_op | source)
XLA Modules:
  0.0 51.3 jit_solution(1181294601695139811)
XLA Ops:
  0.6 1.9 %shard_map.140 = (bf16[32,9,8,128]{3,2,1,0:T(8,128)(2,1)}, f32[8,128]{1,0:T(8,128)}) custom-call(bf16[8,16,128]{2,1,0:T(8,128)(2,1)} %bias_hbm.1, s32[8,32]{1,0:T(8,128)} %bitcast.31, s32[1,32]{1,0:T(1,128)} %bitcast.32, bf16[32,8,256]{2,1,0:T(8,128)(2,1)} %x_ref.3), custom_call_target="tpu_custom_call" | custom-call | flops 2000000000 | bytes 2000000 | tf_op jit(solution)/shard_map/pallas_call | solution.py:377
  2.5 0.0 copy-start
  2.5 0.0 copy-start.4
  2.5 0.0 copy-start.5
  2.5 7.3 %all-to-all-start = ((bf16[32,9,8,128]{3,2,1,0:T(8,128)(2,1)}), bf16[32,9,8,128]{3,2,1,0:T(8,128)(2,1)S(1)}, u32[]{:S(2)}, u32[]{:S(2)}) async-start(bf16[32,9,8,128]{3,2,1,0:T(8,128)(2,1)} %get-tuple-element.20), calls=%async_computation | async-start | bytes 1179648 | tf_op jit(solution)/shard_map/all_to_all | solution.py:424
  9.9 0.0 copy-start.6
  9.9 0.0 copy-done
  9.9 0.0 copy-done.4
  9.9 0.0 copy-done.5
  9.9 0.6 %copy-done.6 = f32[8,128]{1,0:T(8,128)S(1)} copy-done((f32[8,128]{1,0:T(8,128)S(1)}, f32[8,128]{1,0:T(8,128)}, u32[]{:S(2)}) %copy-start.6) | copy-done | bytes 4120
  10.6 1.9 %shard_map.141 = (bf16[8,8,128]{2,1,0:T(8,128)(2,1)S(1)}, bf16[256,32]{1,0:T(8,128)(2,1)S(1)}) custom-call(bf16[32,8,256]{2,1,0:T(8,128)(2,1)S(1)} %copy-done, f32[8,128]{1,0:T(8,128)S(1)} %copy-done.6, bf16[32,256]{1,0:T(8,128)(2,1)S(1)} %bitcast.26, bf16[32,256]{1,0:T(8,128)(2,1)S(1)} %bitcast.27), custom_call_target="tpu_custom_call" | custom-call | flops 2000000000 | bytes 2000000 | tf_op jit(solution)/shard_map/pallas_call | solution.py:377
  12.5 1.8 %collective-permute-start = (bf16[1,8,8,128]{3,2,1,0:T(8,128)(2,1)S(1)}, bf16[1,8,8,128]{3,2,1,0:T(8,128)(2,1)S(1)}, u32[]{:S(2)}, u32[]{:S(2)}) collective-permute-start(bf16[1,8,8,128]{3,2,1,0:T(8,128)(2,1)S(1)} %bitcast.23), channel_id=1, source_target_pairs={{0,8},{1,9},{2,10},{3,11},{4,12},{5,13},{6,14},{7,15},{8,0},{9,1},... | collective-permute-start | bytes 49160 | tf_op jit(solution)/shard_map/ppermute | solution.py:421
  14.3 6.1 %collective-permute-done = bf16[1,8,8,128]{3,2,1,0:T(8,128)(2,1)S(1)} collective-permute-done((bf16[1,8,8,128]{3,2,1,0:T(8,128)(2,1)S(1)}, bf16[1,8,8,128]{3,2,1,0:T(8,128)(2,1)S(1)}, u32[]{:S(2)}, u32[]{:S(2)}) %collective-permute-start) | collective-permute-done | bytes 16416 | tf_op jit(solution)/shard_map/ppermute | solution.py:421
  20.4 4.6 %collective-permute-start.1 = (bf16[2,8,8,128]{3,2,1,0:T(8,128)(2,1)S(1)}, bf16[2,8,8,128]{3,2,1,0:T(8,128)(2,1)S(1)}, u32[]{:S(2)}, u32[]{:S(2)}) collective-permute-start(bf16[2,8,8,128]{3,2,1,0:T(8,128)(2,1)S(1)} %pad_maximum_fusion.2), channel_id=1, source_target_pairs={{0,16},{1,17},{2,18},{3,19},{4,20},{5,21},{6,22},{7,23},{8,24},{9,... | collective-permute-start | bytes 98312 | tf_op jit(solution)/shard_map/ppermute | solution.py:421
  25.0 0.0 copy-done.7
  25.1 0.0 copy-done.8
  25.1 0.0 copy-start.9
  25.1 0.1 copy.24
  25.2 0.8 %copy-done.9 = bf16[256,4,128]{2,1,0:T(4,128)(2,1)S(1)} copy-done((bf16[256,4,128]{2,1,0:T(4,128)(2,1)S(1)}, bf16[256,4,128]{2,1,0:T(4,128)(2,1)}, u32[]{:S(2)}) %copy-start.9) | copy-done | bytes 262168
  26.1 1.6 %collective-permute-done.1 = bf16[2,8,8,128]{3,2,1,0:T(8,128)(2,1)S(1)} collective-permute-done((bf16[2,8,8,128]{3,2,1,0:T(8,128)(2,1)S(1)}, bf16[2,8,8,128]{3,2,1,0:T(8,128)(2,1)S(1)}, u32[]{:S(2)}, u32[]{:S(2)}) %collective-permute-start.1) | collective-permute-done | bytes 32800 | tf_op jit(solution)/shard_map/ppermute | solution.py:421
  27.7 0.0 all-to-all-done.rows_ref
  27.7 0.1 collective-permute-start.2
  27.8 1.5 %collective-permute-start.3 = (bf16[4,8,8,128]{3,2,1,0:T(8,128)(2,1)S(1)}, bf16[4,8,8,128]{3,2,1,0:T(8,128)(2,1)S(1)}, u32[]{:S(2)}, u32[]{:S(2)}) collective-permute-start(bf16[4,8,8,128]{3,2,1,0:T(8,128)(2,1)S(1)} %pad_maximum_fusion.1.refs_0_), channel_id=1, source_target_pairs={{0,4},{1,5},{2,6},{3,7},{4,0},{5,1},{6,2},{7,3},{8,12},{9,13},{10,... | collective-permute-start | bytes 196616 | tf_op jit(solution)/shard_map/ppermute | solution.py:421
  29.3 1.3 %shard_map.142 = (f32[2,256,128]{2,1,0:T(8,128)S(1)}, bf16[256,128]{1,0:T(8,128)(2,1)S(1)}, f32[8,256]{1,0:T(8,128)S(1)}, bf16[2,256,128]{2,1,0:T(8,128)(2,1)S(1...) custom-call(s32[1]{0:T(128)} %bitcast.place_ref, ...), custom_call_target="tpu_custom_call" | custom-call | flops 100000000 | bytes 100000 | tf_op jit(solution)/shard_map/pallas_call | solution.py:377
  30.6 0.0 collective-permute-done.2.swapped_ref
  30.6 0.0 copy-start.10
  30.6 1.4 %shard_map.143 = bf16[32,2,8,128]{3,2,1,0:T(8,128)(2,1)} custom-call(s32[1]{0:T(128)} %bitcast.place_ref, bf16[32,4,8,128]{3,2,1,0:T(8,128)(2,1)S(1)} %collective-permute-done.2.swapped_ref, f32[2,256,128]{2,1,0:T(8,128)S(1)} %get-tuple-element.25.part_ref, f32[8,256]{1,0:T(8,128)S(1)} %get-tuple-element.26.key_keep_ref, ...), custom_call_target="tpu_custom_call" | custom-call | flops 100000000 | bytes 100000 | tf_op jit(solution)/shard_map/pallas_call | solution.py:377
  32.0 0.3 collective-permute-done.3.refs_1_
  32.3 1.5 %collective-permute-start.6 = (bf16[4,8,8,128]{3,2,1,0:T(8,128)(2,1)S(1)}, bf16[4,8,8,128]{3,2,1,0:T(8,128)(2,1)S(1)}, u32[]{:S(2)}, u32[]{:S(2)}) collective-permute-start(bf16[4,8,8,128]{3,2,1,0:T(8,128)(2,1)S(1)} %collective-permute-done.3.refs_1_), channel_id=1, source_target_pairs={{0,1},{1,0},{2,3},{3,2},{4,5},{5,4},{6,7},{7,6},{8,9},{9,8},{10,11... | collective-permute-start | bytes 196616 | tf_op jit(solution)/shard_map/ppermute | solution.py:421
  33.8 0.5 %collective-permute-start.5 = (bf16[4,8,8,128]{3,2,1,0:T(8,128)(2,1)S(1)}, bf16[4,8,8,128]{3,2,1,0:T(8,128)(2,1)S(1)}, u32[]{:S(2)}, u32[]{:S(2)}) collective-permute-start(bf16[4,8,8,128]{3,2,1,0:T(8,128)(2,1)S(1)} %pad_maximum_fusion.1.refs_0_), channel_id=1, source_target_pairs={{0,1},{1,0},{2,3},{3,2},{4,5},{5,4},{6,7},{7,6},{8,9},{9,8},{10,11... | collective-permute-start | bytes 196616 | tf_op jit(solution)/shard_map/ppermute | solution.py:421
  34.3 0.0 copy-done.10
  34.3 1.5 %collective-permute-start.4 = (bf16[128,256]{1,0:T(8,128)(2,1)S(1)}, bf16[128,256]{1,0:T(8,128)(2,1)S(1)}, u32[]{:S(2)}, u32[]{:S(2)}) collective-permute-start(bf16[128,256]{1,0:T(8,128)(2,1)S(1)} %copy-done.10), channel_id=1, source_target_pairs={{0,1},{1,0},{2,3},{3,2},{4,5},{5,4},{6,7},{7,6},{8,9},{9,8},{10,11... | collective-permute-start | bytes 196616 | tf_op jit(solution)/shard_map/ppermute | solution.py:421
  35.8 0.0 collective-permute-start.7
  35.8 0.5 collective-permute-start.8
  36.3 3.5 %all-to-all-start.1 = ((bf16[32,2,8,128]{3,2,1,0:T(8,128)(2,1)}), bf16[32,2,8,128]{3,2,1,0:T(8,128)(2,1)S(1)}, u32[]{:S(2)}, u32[]{:S(2)}) async-start(bf16[32,2,8,128]{3,2,1,0:T(8,128)(2,1)} %shard_map.143), calls=%async_computation.1 | async-start | bytes 262144 | tf_op jit(solution)/shard_map/all_to_all | solution.py:424
  39.8 0.0 collective-permute-done.6.refs_3_
  39.8 0.3 collective-permute-start.10
  40.1 0.0 collective-permute-done.5.refs_2_
  40.1 0.3 collective-permute-start.9
  40.4 0.0 collective-permute-done.4
  40.4 0.0 collective-permute-done.7.refs_4_
  40.4 0.0 collective-permute-done.8.refs_5_
  40.4 0.7 %collective-permute-done.10.refs_7_ = bf16[4,8,8,128]{3,2,1,0:T(8,128)(2,1)S(1)} collective-permute-done((bf16[4,8,8,128]{3,2,1,0:T(8,128)(2,1)S(1)}, bf16[4,8,8,128]{3,2,1,0:T(8,128)(2,1)S(1)}, u32[]{:S(2)}, u32[]{:S(2)}) %collective-permute-start.10) | collective-permute-done | bytes 65568 | tf_op jit(solution)/shard_map/ppermute | solution.py:421
  41.1 0.3 collective-permute-done.9.refs_6_
  41.4 2.2 %shard_map.145 = bf16[8,256,128]{2,1,0:T(8,128)(2,1)} custom-call(s32[1]{0:T(128)} %bitcast.place_ref, bf16[256,128]{1,0:T(8,128)(2,1)S(1)} %get-tuple-element.33.keep_all_ref, bf16[4,8,8,128]{3,2,1,0:T(8,128)(2,1)S(1)} %pad_maximum_fusion.1.refs_0_, bf16[4,8,8,128]{3,2,1,0:T(8,128)(2,1)S(1)} %collective-permute-done.3.refs_1_, ...), custom_call_target="tpu_custom_call" | custom-call | flops 2000000000 | bytes 2000000 | tf_op jit(solution)/shard_map/pallas_call | solution.py:377
  43.6 4.9 %all-to-all-done.1 = bf16[32,2,8,128]{3,2,1,0:T(8,128)(2,1)S(1)} async-done(((bf16[32,2,8,128]{3,2,1,0:T(8,128)(2,1)}), bf16[32,2,8,128]{3,2,1,0:T(8,128)(2,1)S(1)}, u32[]{:S(2)}, u32[]{:S(2)}) %all-to-all-start.1) | async-done | bytes 131104 | tf_op jit(solution)/shard_map/all_to_all | solution.py:424
  48.4 0.0 copy-done.1
  48.4 2.8 %shard_map.144 = bf16[32,8,256]{2,1,0:T(8,128)(2,1)} custom-call(s32[1]{0:T(128)} %bitcast.place_ref, bf16[32,8,256]{2,1,0:T(8,128)(2,1)S(1)} %copy-done, bf16[16,2,2,8,128]{4,3,2,1,0:T(8,128)(2,1)S(1)} %bitcast.22, f32[8,128]{1,0:T(8,128)S(1)} %copy-done.6, bf16[2,128,256]{2,1,0:T(8,128)(2,1)S(1)} %pad_maximum_fusion.row_out_ref, ...), custom_call_target="tpu_custom_call" | custom-call | flops 3000000000 | bytes 3000000 | tf_op jit(solution)/shard_map/pallas_call | solution.py:377
  (13 shorter events, 0.1 us)
Async XLA Ops:
  2.5 7.4 %copy-start = (bf16[32,8,256]{2,1,0:T(8,128)(2,1)S(1)}, bf16[32,8,256]{2,1,0:T(8,128)(2,1)}, u32[]{:S(2)}) copy-start(bf16[32,8,256]{2,1,0:T(8,128)(2,1)} %x_ref.3) | copy-start | bytes 393220
  2.5 7.4 %copy-start.4 = (bf16[256,32]{0,1:T(8,128)(2,1)S(1)}, bf16[256,32]{0,1:T(8,128)(2,1)}, u32[]{:S(2)}) copy-start(bf16[256,32]{0,1:T(8,128)(2,1)} %param.23) | copy-start | bytes 49156
  2.5 7.4 %copy-start.5 = (bf16[256,32]{0,1:T(8,128)(2,1)S(1)}, bf16[256,32]{0,1:T(8,128)(2,1)}, u32[]{:S(2)}) copy-start(bf16[256,32]{0,1:T(8,128)(2,1)} %param.24) | copy-start | bytes 49156
  2.5 25.1 %all-to-all-start = ((bf16[32,9,8,128]{3,2,1,0:T(8,128)(2,1)}), bf16[32,9,8,128]{3,2,1,0:T(8,128)(2,1)S(1)}, u32[]{:S(2)}, u32[]{:S(2)}) async-start(bf16[32,9,8,128]{3,2,1,0:T(8,128)(2,1)} %get-tuple-element.20), calls=%async_computation | async-start | bytes 1179648 | tf_op jit(solution)/shard_map/all_to_all | solution.py:424
  9.9 0.7 %copy-start.6 = (f32[8,128]{1,0:T(8,128)S(1)}, f32[8,128]{1,0:T(8,128)}, u32[]{:S(2)}) copy-start(f32[8,128]{1,0:T(8,128)} %get-tuple-element.21.keep_ref.refs_9_) | copy-start | bytes 12292
  10.6 14.5 %copy-start.7 = (bf16[256,2,256]{2,1,0:T(2,128)(2,1)S(1)}, bf16[256,2,256]{2,1,0:T(2,128)(2,1)}, u32[]{:S(2)}) copy-start(bf16[256,2,256]{2,1,0:T(2,128)(2,1)} %param.21) | copy-start | bytes 786436
  12.5 7.9 %collective-permute-start = (bf16[1,8,8,128]{3,2,1,0:T(8,128)(2,1)S(1)}, bf16[1,8,8,128]{3,2,1,0:T(8,128)(2,1)S(1)}, u32[]{:S(2)}, u32[]{:S(2)}) collective-permute-start(bf16[1,8,8,128]{3,2,1,0:T(8,128)(2,1)S(1)} %bitcast.23), channel_id=1, source_target_pairs={{0,8},{1,9},{2,10},{3,11},{4,12},{5,13},{6,14},{7,15},{8,0},{9,1},... | collective-permute-start | bytes 49160 | tf_op jit(solution)/shard_map/ppermute | solution.py:421
  20.4 4.6 %copy-start.8 = (bf16[1024,128]{1,0:T(8,128)(2,1)S(1)}, bf16[1024,128]{1,0:T(8,128)(2,1)}, u32[]{:S(2)}) copy-start(bf16[1024,128]{1,0:T(8,128)(2,1)} %param.25) | copy-start | bytes 786436
  20.4 7.2 %collective-permute-start.1 = (bf16[2,8,8,128]{3,2,1,0:T(8,128)(2,1)S(1)}, bf16[2,8,8,128]{3,2,1,0:T(8,128)(2,1)S(1)}, u32[]{:S(2)}, u32[]{:S(2)}) collective-permute-start(bf16[2,8,8,128]{3,2,1,0:T(8,128)(2,1)S(1)} %pad_maximum_fusion.2), channel_id=1, source_target_pairs={{0,16},{1,17},{2,18},{3,19},{4,20},{5,21},{6,22},{7,23},{8,24},{9,... | collective-permute-start | bytes 98312 | tf_op jit(solution)/shard_map/ppermute | solution.py:421
  25.1 1.0 %copy-start.9 = (bf16[256,4,128]{2,1,0:T(4,128)(2,1)S(1)}, bf16[256,4,128]{2,1,0:T(4,128)(2,1)}, u32[]{:S(2)}) copy-start(bf16[256,4,128]{2,1,0:T(4,128)(2,1)} %param.17) | copy-start | bytes 786436
  27.7 2.9 %collective-permute-start.2 = (bf16[32,4,8,128]{3,2,1,0:T(8,128)(2,1)S(1)}, bf16[32,4,8,128]{3,2,1,0:T(8,128)(2,1)S(1)}, u32[]{:S(2)}, u32[]{:S(2)}) collective-permute-start(bf16[32,4,8,128]{3,2,1,0:T(8,128)(2,1)S(1)} %slice.3), channel_id=1, source_target_pairs={{0,2},{1,3},{2,0},{3,1},{4,6},{5,7},{6,4},{7,5},{8,10},{9,11},{10,... | collective-permute-start | bytes 786440 | tf_op jit(solution)/shard_map/ppermute | solution.py:421
  27.8 4.5 %collective-permute-start.3 = (bf16[4,8,8,128]{3,2,1,0:T(8,128)(2,1)S(1)}, bf16[4,8,8,128]{3,2,1,0:T(8,128)(2,1)S(1)}, u32[]{:S(2)}, u32[]{:S(2)}) collective-permute-start(bf16[4,8,8,128]{3,2,1,0:T(8,128)(2,1)S(1)} %pad_maximum_fusion.1.refs_0_), channel_id=1, source_target_pairs={{0,4},{1,5},{2,6},{3,7},{4,0},{5,1},{6,2},{7,3},{8,12},{9,13},{10,... | collective-permute-start | bytes 196616 | tf_op jit(solution)/shard_map/ppermute | solution.py:421
  30.6 3.7 %copy-start.10 = (bf16[128,256]{1,0:T(8,128)(2,1)S(1)}, bf16[128,256]{1,0:T(8,128)(2,1)}, u32[]{:S(2)}) copy-start(bf16[128,256]{1,0:T(8,128)(2,1)} %param.18) | copy-start | bytes 196612
  32.3 7.5 %collective-permute-start.6 = (bf16[4,8,8,128]{3,2,1,0:T(8,128)(2,1)S(1)}, bf16[4,8,8,128]{3,2,1,0:T(8,128)(2,1)S(1)}, u32[]{:S(2)}, u32[]{:S(2)}) collective-permute-start(bf16[4,8,8,128]{3,2,1,0:T(8,128)(2,1)S(1)} %collective-permute-done.3.refs_1_), channel_id=1, source_target_pairs={{0,1},{1,0},{2,3},{3,2},{4,5},{5,4},{6,7},{7,6},{8,9},{9,8},{10,11... | collective-permute-start | bytes 196616 | tf_op jit(solution)/shard_map/ppermute | solution.py:421
  33.8 6.4 %collective-permute-start.5 = (bf16[4,8,8,128]{3,2,1,0:T(8,128)(2,1)S(1)}, bf16[4,8,8,128]{3,2,1,0:T(8,128)(2,1)S(1)}, u32[]{:S(2)}, u32[]{:S(2)}) collective-permute-start(bf16[4,8,8,128]{3,2,1,0:T(8,128)(2,1)S(1)} %pad_maximum_fusion.1.refs_0_), channel_id=1, source_target_pairs={{0,1},{1,0},{2,3},{3,2},{4,5},{5,4},{6,7},{7,6},{8,9},{9,8},{10,11... | collective-permute-start | bytes 196616 | tf_op jit(solution)/shard_map/ppermute | solution.py:421
  34.3 6.1 %collective-permute-start.4 = (bf16[128,256]{1,0:T(8,128)(2,1)S(1)}, bf16[128,256]{1,0:T(8,128)(2,1)S(1)}, u32[]{:S(2)}, u32[]{:S(2)}) collective-permute-start(bf16[128,256]{1,0:T(8,128)(2,1)S(1)} %copy-done.10), channel_id=1, source_target_pairs={{0,1},{1,0},{2,3},{3,2},{4,5},{5,4},{6,7},{7,6},{8,9},{9,8},{10,11... | collective-permute-start | bytes 196616 | tf_op jit(solution)/shard_map/ppermute | solution.py:421
  35.8 4.6 %collective-permute-start.7 = (bf16[4,8,8,128]{3,2,1,0:T(8,128)(2,1)S(1)}, bf16[4,8,8,128]{3,2,1,0:T(8,128)(2,1)S(1)}, u32[]{:S(2)}, u32[]{:S(2)}) collective-permute-start(bf16[4,8,8,128]{3,2,1,0:T(8,128)(2,1)S(1)} %pad_maximum_fusion.1.refs_0_), channel_id=1, source_target_pairs={{0,2},{1,3},{2,0},{3,1},{4,6},{5,7},{6,4},{7,5},{8,10},{9,11},{10,... | collective-permute-start | bytes 196616 | tf_op jit(solution)/shard_map/ppermute | solution.py:421
  35.8 4.6 %collective-permute-start.8 = (bf16[4,8,8,128]{3,2,1,0:T(8,128)(2,1)S(1)}, bf16[4,8,8,128]{3,2,1,0:T(8,128)(2,1)S(1)}, u32[]{:S(2)}, u32[]{:S(2)}) collective-permute-start(bf16[4,8,8,128]{3,2,1,0:T(8,128)(2,1)S(1)} %collective-permute-done.3.refs_1_), channel_id=1, source_target_pairs={{0,2},{1,3},{2,0},{3,1},{4,6},{5,7},{6,4},{7,5},{8,10},{9,11},{10,... | collective-permute-start | bytes 196616 | tf_op jit(solution)/shard_map/ppermute | solution.py:421
  36.3 12.1 %all-to-all-start.1 = ((bf16[32,2,8,128]{3,2,1,0:T(8,128)(2,1)}), bf16[32,2,8,128]{3,2,1,0:T(8,128)(2,1)S(1)}, u32[]{:S(2)}, u32[]{:S(2)}) async-start(bf16[32,2,8,128]{3,2,1,0:T(8,128)(2,1)} %shard_map.143), calls=%async_computation.1 | async-start | bytes 262144 | tf_op jit(solution)/shard_map/all_to_all | solution.py:424
  39.8 1.3 %collective-permute-start.10 = (bf16[4,8,8,128]{3,2,1,0:T(8,128)(2,1)S(1)}, bf16[4,8,8,128]{3,2,1,0:T(8,128)(2,1)S(1)}, u32[]{:S(2)}, u32[]{:S(2)}) collective-permute-start(bf16[4,8,8,128]{3,2,1,0:T(8,128)(2,1)S(1)} %collective-permute-done.6.refs_3_), channel_id=1, source_target_pairs={{0,2},{1,3},{2,0},{3,1},{4,6},{5,7},{6,4},{7,5},{8,10},{9,11},{10,... | collective-permute-start | bytes 196616 | tf_op jit(solution)/shard_map/ppermute | solution.py:421
  40.1 1.3 %collective-permute-start.9 = (bf16[4,8,8,128]{3,2,1,0:T(8,128)(2,1)S(1)}, bf16[4,8,8,128]{3,2,1,0:T(8,128)(2,1)S(1)}, u32[]{:S(2)}, u32[]{:S(2)}) collective-permute-start(bf16[4,8,8,128]{3,2,1,0:T(8,128)(2,1)S(1)} %collective-permute-done.5.refs_2_), channel_id=1, source_target_pairs={{0,2},{1,3},{2,0},{3,1},{4,6},{5,7},{6,4},{7,5},{8,10},{9,11},{10,... | collective-permute-start | bytes 196616 | tf_op jit(solution)/shard_map/ppermute | solution.py:421
  41.4 7.0 %copy-start.1 = (bf16[256,256]{1,0:T(8,128)(2,1)S(1)}, bf16[256,256]{1,0:T(8,128)(2,1)}, u32[]{:S(2)}) copy-start(bf16[256,256]{1,0:T(8,128)(2,1)} %query_w_ref.1) | copy-start | bytes 393220
  41.4 7.0 %copy-start.2 = (bf16[256,256]{1,0:T(8,128)(2,1)S(1)}, bf16[256,256]{1,0:T(8,128)(2,1)}, u32[]{:S(2)}) copy-start(bf16[256,256]{1,0:T(8,128)(2,1)} %key_w_ref.1) | copy-start | bytes 393220
  41.4 7.0 %copy-start.3 = (bf16[256,256]{1,0:T(8,128)(2,1)S(1)}, bf16[256,256]{1,0:T(8,128)(2,1)}, u32[]{:S(2)}) copy-start(bf16[256,256]{1,0:T(8,128)(2,1)} %out_w_ref.1) | copy-start | bytes 393220
